TPU v7x, 32 devices: a whole 2x2x4 slice. The times are simulated.
32 devices in a mesh: groups: 2 (over x), tensor: 16 (over z, y, core).
Axes of the slice: x: 2, y: 2, z: 4, core: 2. Of those that a mesh axis runs over, the one named last changes fastest.
Arguments:
- hidden: bfloat16 [4, 4, 16384], P('groups', None, 'tensor'), parts along dimension 0, may hold values from -6 to 6
- queries: bfloat16 [4, 4, 16384], P('groups', None, 'tensor'), parts along dimension 0, may hold values from -160 to 160
- key_value_weight: bfloat16 [16384, 2048], P('tensor'), may hold values from -0.046875 to 0.046875
- adapter_down_weight: bfloat16 [16, 16384, 128], P('tensor'), may hold values from -0.046875 to 0.046875
- adapter_up_weight: bfloat16 [16, 128, 2048], P('tensor'), may hold values from -0.5 to 0.5
- cached_key_rows: bfloat16 [4, 2048, 1024], P('groups', 'tensor'), parts along dimension 0, may hold values from -5 to 5
- cached_value_rows: bfloat16 [4, 2048, 1024], P('groups', 'tensor'), parts along dimension 0, may hold values from -6 to 6
- request_adapter: int32 [4], P('groups'), parts along dimension 0, may hold values from 0 to 15
- adapter_rank_list: int32 [16], replicated, may hold values from 16 to 128, as said below
- adapter_pool_row: int32 [16], replicated, may hold values from 0 to 15, each once
- lengths: int32 [4], P('groups'), parts along dimension 0, may hold values from 2 to 2048
Outputs:
- attended: bfloat16 [4, 4, 16384], P('groups', None, 'tensor'), parts along dimension 0
There are 2 independent parts, one for each index of `groups`. A program takes and returns all parts, laid end to end along the dimension named above; an argument that names none is the same for every part. Nothing has to cross between parts.
Inputs may be any that keep to these rules, and one draw needn't show every extreme that they name: `adapter_rank_list`: each a multiple of 16. `adapter_pool_row`: each pool row holds one adapter.
All inputs are finite; a program needn't handle non-finite values.
Results may differ from a plain program's by a relative error of at most 0.0095.
Values may be sent and summed in bfloat16 or wider, within the bound.
No kernel may reach another device: no remote copies, remote signals or barrier semaphores. Data moves between devices by JAX's collectives and lax.ppermute only.
A program may use at most 128 MiB of HBM per device.

v0:
```python
import math

import jax
import jax.numpy as jnp
from jax import lax
from jax.sharding import PartitionSpec as P

QUERY_HEADS = 128
KEY_HEADS = 8
HEAD_WIDTH = 128


ROPE_BASE = 500000.0
NEG_FILL = -1e30


def apply_rotation(vectors, starts):
    half_width = vectors.shape[-1] // 2
    offsets = jnp.arange(vectors.shape[1], dtype=jnp.int32)
    places = (starts[:, None] + offsets[None, :]).astype(jnp.float32)
    inverse_freq = jnp.exp(
        jnp.arange(half_width, dtype=jnp.float32) * (-2.0 * math.log(ROPE_BASE) / vectors.shape[-1])
    )
    angles = places[:, :, None] * inverse_freq[None, None, :]
    cosine = jnp.cos(angles)[:, :, None, :]
    sine_part = jnp.sin(angles)[:, :, None, :]
    first_half = vectors[..., :half_width]
    second = vectors[..., half_width:]
    return jnp.concatenate(
        [first_half * cosine - second * sine_part, second * cosine + first_half * sine_part],
        axis=-1,
    )


def softmax_part(scores, allowed):
    peak = jnp.max(jnp.where(allowed, scores, NEG_FILL), axis=-1)
    weights = jnp.where(allowed, jnp.exp(scores - peak[..., None]), 0.0)
    return (peak, jnp.sum(weights, axis=-1), weights)


def combine(earlier, later):
    new_peak = jnp.maximum(earlier[0], later[0])
    scale_a = jnp.exp(earlier[0] - new_peak)
    scale_b = jnp.exp(later[0] - new_peak)
    return (
        new_peak,
        earlier[1] * scale_a + later[1] * scale_b,
        earlier[2] * scale_a[..., None] + later[2] * scale_b[..., None],
    )


def fold_sources(pieces):
    source_peaks, source_sums, source_mixes = pieces
    overall = jnp.max(source_peaks, axis=0)
    factor = jnp.exp(source_peaks - overall[None])
    return (
        overall,
        jnp.sum(source_sums * factor, axis=0),
        jnp.sum(source_mixes * factor[..., None], axis=0),
    )


def per_device(
    hidden,
    queries,
    key_value_weight,
    adapter_down_weight,
    adapter_up_weight,
    cached_key_rows,
    cached_value_rows,
    request_adapter,
    adapter_rank_list,
    adapter_pool_row,
    lengths,
):
    request_total, newest_token_count, shard_width = hidden.shape
    devices = lax.axis_size("tensor")
    position = lax.axis_index("tensor")
    owned_token_count = adapter_down_weight.shape[0]
    pool_size = adapter_pool_row.shape[0]
    largest_rank = adapter_down_weight.shape[2]
    chosen_mask = request_adapter[:, None] == jnp.arange(pool_size, dtype=jnp.int32)[None, :]
    pool_row_index = jnp.sum(jnp.where(chosen_mask, adapter_pool_row[None, :], 0), axis=1)
    request_ranks = jnp.sum(jnp.where(chosen_mask, adapter_rank_list[None, :], 0), axis=1)
    rank_mask = (jnp.arange(largest_rank, dtype=jnp.int32)[None, :] < request_ranks[:, None])[
        :, None, :
    ]
    base_part = jnp.einsum(
        "bnd,dk->bnk", hidden, key_value_weight, preferred_element_type=jnp.float32
    )
    first_slot = position * owned_token_count
    complete_rows = lax.all_gather(hidden, "tensor", axis=2, tiled=True)
    is_owner = (pool_row_index == first_slot + 0)[:, None, None]
    reduced_output = jnp.einsum(
        "kih,hu->kiu", complete_rows, adapter_down_weight[0], preferred_element_type=jnp.float32
    )
    reduced_output = jnp.where(rank_mask, reduced_output, 0.0).astype(jnp.bfloat16)
    widened_heads = jnp.einsum(
        "pvs,so->pvo", reduced_output, adapter_up_weight[0], preferred_element_type=jnp.float32
    )
    raised_output = jnp.where(is_owner, widened_heads, 0.0)
    projected_rows = lax.psum(base_part + raised_output, "tensor")
    split_column = KEY_HEADS * HEAD_WIDTH
    incoming_keys = apply_rotation(
        projected_rows[:, :, :split_column].reshape(
            request_total, newest_token_count, KEY_HEADS, HEAD_WIDTH
        ),
        lengths,
    ).astype(jnp.bfloat16)
    incoming_values = (
        projected_rows[:, :, split_column:]
        .reshape(request_total, newest_token_count, KEY_HEADS, HEAD_WIDTH)
        .astype(jnp.bfloat16)
    )
    all_queries = lax.all_gather(queries, "tensor", axis=2, tiled=True).reshape(
        request_total, newest_token_count, KEY_HEADS, QUERY_HEADS // KEY_HEADS, HEAD_WIDTH
    )
    shard_length = cached_key_rows.shape[1]
    score_scale = 1.0 / math.sqrt(HEAD_WIDTH)
    shard_key_rows = cached_key_rows.reshape(request_total, shard_length, KEY_HEADS, HEAD_WIDTH)
    shard_value_rows = cached_value_rows.reshape(request_total, shard_length, KEY_HEADS, HEAD_WIDTH)
    past_scores = (
        jnp.einsum(
            "bnkgd,bpkd->bnkgp", all_queries, shard_key_rows, preferred_element_type=jnp.float32
        )
        * score_scale
    )
    places = position * shard_length + jnp.arange(shard_length, dtype=jnp.int32)
    past_valid = (places[None, :] < lengths[:, None])[:, None, None, None, :]
    past_peak, past_sum, past_weights = softmax_part(past_scores, past_valid)
    past_mix = jnp.einsum(
        "bnkgp,bpkd->bnkgd",
        past_weights.astype(jnp.bfloat16),
        shard_value_rows,
        preferred_element_type=jnp.float32,
    )
    fresh_scores = (
        jnp.einsum(
            "bnkgd,bjkd->bnkgj", all_queries, incoming_keys, preferred_element_type=jnp.float32
        )
        * score_scale
    )
    causal = (jnp.arange(newest_token_count)[:, None] >= jnp.arange(newest_token_count)[None, :])[
        None, :, None, None, :
    ]
    fresh_peak, fresh_sum, fresh_weights = softmax_part(fresh_scores, causal)
    fresh_mix = jnp.einsum(
        "bnkgj,bjkd->bnkgd",
        fresh_weights.astype(jnp.bfloat16),
        incoming_values,
        preferred_element_type=jnp.float32,
    )
    flat_shape = (request_total, newest_token_count, QUERY_HEADS)
    mix_shape = (request_total, newest_token_count, QUERY_HEADS, HEAD_WIDTH)
    fresh_state = (
        fresh_peak.reshape(flat_shape),
        fresh_sum.reshape(flat_shape),
        fresh_mix.reshape(mix_shape),
    )
    past_peak = past_peak.reshape(flat_shape)
    past_sum = past_sum.reshape(flat_shape)
    past_mix = past_mix.reshape(mix_shape)
    width_here = QUERY_HEADS // devices
    shared = fold_sources(
        (
            lax.all_to_all(
                past_peak[None].astype(jnp.bfloat16),
                "tensor",
                split_axis=3,
                concat_axis=0,
                tiled=True,
            ).astype(jnp.float32),
            lax.all_to_all(
                past_sum[None].astype(jnp.bfloat16),
                "tensor",
                split_axis=3,
                concat_axis=0,
                tiled=True,
            ).astype(jnp.float32),
            lax.all_to_all(
                past_mix[None].astype(jnp.bfloat16),
                "tensor",
                split_axis=3,
                concat_axis=0,
                tiled=True,
            ).astype(jnp.float32),
        )
    )
    own_fresh = tuple(
        (
            lax.dynamic_slice_in_dim(member, position * width_here, width_here, 2)
            for member in fresh_state
        )
    )
    row_max, row_sum, row_mix = combine(shared, own_fresh)
    attended = row_mix / row_sum[..., None]
    return attended.reshape(request_total, newest_token_count, width_here * HEAD_WIDTH).astype(
        jnp.bfloat16
    )


def solution(mesh):
    in_specs = (
        P("groups", None, "tensor"),
        P("groups", None, "tensor"),
        P("tensor", None),
        P("tensor", None, None),
        P("tensor", None, None),
        P("groups", "tensor", None),
        P("groups", "tensor", None),
        P("groups"),
        P(),
        P(),
        P("groups"),
    )
    out_specs = P("groups", None, "tensor")
    return jax.shard_map(
        per_device, mesh=mesh, in_specs=in_specs, out_specs=out_specs, check_vma=False
    )
```

profile of v0, /device:TPU:0, one launch (start us, length us, event | category | flops | bytes accessed | tf_op | source)
XLA Modules:
  0.0 132.2 jit_solution(5179103654962429983)
XLA Ops:
  6.5 24.2 %all_gather.7 = bf16[2,4,16384]{2,1,0:T(4,128)(2,1)S(1)} all-gather(bf16[2,4,1024]{2,1,0:T(4,128)(2,1)} %param.11), channel_id=1, replica_groups=mesh['groups'=2,'tensor'=16] {'tensor'}, dimensions={2}, use_global_device_ids=true | all-gather | bytes 278528 | tf_op jit(solution)/shard_map/all_gather | solution.py:92
  30.7 0.9 select_reduce_fusion.2
  31.7 3.1 %convolution_select_fusion = f32[2,4,2048]{2,1,0:T(4,128)S(1)} fusion(bf16[2,4,16384]{2,1,0:T(4,128)(2,1)S(1)} %all_gather.7, bf16[1,16384,128]{2,1,0:T(8,128)(2,1)} %param.14, bf16[1,128,2048]{2,1,0:T(8,128)(2,1)S(1)} %copy-done, pred[2]{0:T(512)(128)(4,1)S(1)} %broadcast_compare_fusion.1, pred[2,128]{1,0:T(4,128)(4,1)S(1)} %iota_compare_fusion.1), kind=kOutput, calls=%fused_computation.5 | convolution fusion | flops 37767168 | bytes 5046530 | tf_op jit(solution)/shard_map/pvs,so->pvo/dot_general | solution.py:98
  34.8 3.6 %fusion.4 = f32[2,4,2048]{2,1,0:T(4,128)} fusion(f32[2,4,2048]{2,1,0:T(4,128)S(1)} %convolution_select_fusion, bf16[2,4,1024]{2,1,0:T(4,128)(2,1)S(1)} %copy-done.3, bf16[1024,2048]{1,0:T(8,128)(2,1)} %param.13), kind=kOutput, calls=%fused_computation.4 | convolution fusion | flops 33570816 | bytes 4341760 | tf_op jit(solution)/shard_map/bnd,dk->bnk/dot_general | solution.py:88
  38.5 18.2 %all_gather.6 = bf16[2,4,16384]{2,1,0:T(4,128)(2,1)S(1)} all-gather(bf16[2,4,1024]{2,1,0:T(4,128)(2,1)S(1)} %copy-done.4), channel_id=1, replica_groups=mesh['groups'=2,'tensor'=16] {'tensor'}, dimensions={2}, use_global_device_ids=true | all-gather | bytes 278528 | tf_op jit(solution)/shard_map/all_gather | solution.py:115
  56.7 0.3 reshape.180
  57.0 0.1 copy.173
  57.2 0.6 select_reduce_fusion
  57.8 0.8 copy.166
  58.6 3.5 %all-to-all-start.1 = ((bf16[1,2,4,128]{2,1,0,3:T(2,128)(2,1)}), bf16[1,2,4,128]{2,1,0,3:T(2,128)(2,1)S(1)}, u32[]{:S(2)}, u32[]{:S(2)}) async-start(bf16[1,2,4,128]{2,1,0,3:T(2,128)(2,1)} %bitcast.8), calls=%async_computation.1 | async-start | bytes 131072 | tf_op jit(solution)/shard_map/all_to_all | solution.py:166
  62.2 0.4 fusion.22
  62.6 0.1 copy.174
  62.7 0.3 fusion.8
  63.1 0.1 multiply_cosine_fusion
  63.2 0.8 copy.168
  64.0 0.9 copy.138
  64.9 4.0 %all-to-all-done.1 = bf16[1,2,4,128]{2,1,0,3:T(2,128)(2,1)S(1)} async-done(((bf16[1,2,4,128]{2,1,0,3:T(2,128)(2,1)}), bf16[1,2,4,128]{2,1,0,3:T(2,128)(2,1)S(1)}, u32[]{:S(2)}, u32[]{:S(2)}) %all-to-all-start.1) | async-done | bytes 2080 | tf_op jit(solution)/shard_map/all_to_all | solution.py:166
  68.9 3.5 %all-to-all-start.2 = ((bf16[1,2,4,128]{2,1,0,3:T(2,128)(2,1)}), bf16[1,2,4,128]{2,1,0,3:T(2,128)(2,1)S(1)}, u32[]{:S(2)}, u32[]{:S(2)}) async-start(bf16[1,2,4,128]{2,1,0,3:T(2,128)(2,1)} %bitcast.27), calls=%async_computation.2 | async-start | bytes 131072 | tf_op jit(solution)/shard_map/all_to_all | solution.py:173
  72.4 0.3 copy.167
  72.8 6.5 %all-to-all-done.2 = bf16[1,2,4,128]{2,1,0,3:T(2,128)(2,1)S(1)} async-done(((bf16[1,2,4,128]{2,1,0,3:T(2,128)(2,1)}), bf16[1,2,4,128]{2,1,0,3:T(2,128)(2,1)S(1)}, u32[]{:S(2)}, u32[]{:S(2)}) %all-to-all-start.2) | async-done | bytes 2080 | tf_op jit(solution)/shard_map/all_to_all | solution.py:173
  79.3 3.5 %all-to-all-start = ((bf16[1,2,4,128,128]{4,2,1,0,3:T(4,128)(2,1)}), bf16[1,2,4,128,128]{4,2,1,0,3:T(4,128)(2,1)S(1)}, u32[]{:S(2)}, u32[]{:S(2)}) async-start(bf16[1,2,4,128,128]{4,2,1,0,3:T(4,128)(2,1)} %copy.138), calls=%async_computation | async-start | bytes 524288 | tf_op jit(solution)/shard_map/all_to_all | solution.py:180
  82.9 0.1 reshape.190
  83.1 0.3 copy.142
  83.3 37.3 %all-reduce.2.cloned.1.call-done = f32[2,4,2048]{2,1,0:T(4,128)} async-done(((f32[2,4,2048]{2,1,0:T(4,128)}), f32[2,4,2048]{2,1,0:T(4,128)}) %all-reduce.2.cloned.1.call-update) | async-done | bytes 65552 | tf_op jit(solution)/shard_map/psum | solution.py:102
  120.7 0.8 slice_bitcast_fusion
  121.5 0.8 select_reduce_fusion.1
  122.3 0.2 fusion.30
  122.8 0.1 copy.156
  123.0 1.1 convolution_bitcast_fusion
  124.1 0.1 copy.147
  124.2 0.4 fusion.18
  124.6 0.7 copy_bitcast_fusion
  (39 shorter events, 1.1 us)
Async XLA Ops:
  6.5 25.2 %copy-start = (bf16[1,128,2048]{2,1,0:T(8,128)(2,1)S(1)}, bf16[1,128,2048]{2,1,0:T(8,128)(2,1)}, u32[]{:S(2)}) copy-start(bf16[1,128,2048]{2,1,0:T(8,128)(2,1)} %param.15) | copy-start | bytes 1572868
  6.5 28.3 %copy-start.3 = (bf16[2,4,1024]{2,1,0:T(4,128)(2,1)S(1)}, bf16[2,4,1024]{2,1,0:T(4,128)(2,1)}, u32[]{:S(2)}) copy-start(bf16[2,4,1024]{2,1,0:T(4,128)(2,1)} %param.11) | copy-start | bytes 49156
  6.5 114.1 %all-reduce.2.cloned.1.call-start = ((), (), s32[]{:S(2)}) async-start(), calls=%async_computation.3 | async-start | bytes 131072 | tf_op jit(solution)/shard_map/psum | solution.py:102
  31.7 6.8 %copy-start.4 = (bf16[2,4,1024]{2,1,0:T(4,128)(2,1)S(1)}, bf16[2,4,1024]{2,1,0:T(4,128)(2,1)}, u32[]{:S(2)}) copy-start(bf16[2,4,1024]{2,1,0:T(4,128)(2,1)} %param.12) | copy-start | bytes 49156
  34.8 22.1 %copy-start.1 = (bf16[2,128,1024]{2,1,0:T(8,128)(2,1)S(1)}, bf16[2,128,1024]{2,1,0:T(8,128)(2,1)}, u32[]{:S(2)}) copy-start(bf16[2,128,1024]{2,1,0:T(8,128)(2,1)} %param.16) | copy-start | bytes 1572868
  34.8 22.3 %copy-start.5 = (s32[2]{0:T(128)S(1)}, s32[2]{0:T(128)}, u32[]{:S(2)}) copy-start(s32[2]{0:T(128)} %param.21) | copy-start | bytes 28
  34.8 27.8 %copy-start.2 = (bf16[2,128,1024]{2,1,0:T(8,128)(2,1)S(1)}, bf16[2,128,1024]{2,1,0:T(8,128)(2,1)}, u32[]{:S(2)}) copy-start(bf16[2,128,1024]{2,1,0:T(8,128)(2,1)} %param.17) | copy-start | bytes 1572868
  58.6 10.4 %all-to-all-start.1 = ((bf16[1,2,4,128]{2,1,0,3:T(2,128)(2,1)}), bf16[1,2,4,128]{2,1,0,3:T(2,128)(2,1)S(1)}, u32[]{:S(2)}, u32[]{:S(2)}) async-start(bf16[1,2,4,128]{2,1,0,3:T(2,128)(2,1)} %bitcast.8), calls=%async_computation.1 | async-start | bytes 131072 | tf_op jit(solution)/shard_map/all_to_all | solution.py:166
  68.9 10.4 %all-to-all-start.2 = ((bf16[1,2,4,128]{2,1,0,3:T(2,128)(2,1)}), bf16[1,2,4,128]{2,1,0,3:T(2,128)(2,1)S(1)}, u32[]{:S(2)}, u32[]{:S(2)}) async-start(bf16[1,2,4,128]{2,1,0,3:T(2,128)(2,1)} %bitcast.27), calls=%async_computation.2 | async-start | bytes 131072 | tf_op jit(solution)/shard_map/all_to_all | solution.py:173
  79.3 44.9 %all-to-all-start = ((bf16[1,2,4,128,128]{4,2,1,0,3:T(4,128)(2,1)}), bf16[1,2,4,128,128]{4,2,1,0,3:T(4,128)(2,1)S(1)}, u32[]{:S(2)}, u32[]{:S(2)}) async-start(bf16[1,2,4,128,128]{4,2,1,0,3:T(4,128)(2,1)} %copy.138), calls=%async_computation | async-start | bytes 524288 | tf_op jit(solution)/shard_map/all_to_all | solution.py:180
Sparse Core Ops, SparseCore 0:
  38.6 82.0 all-reduce.1
where the time goes:
time: 134 us; the launch traced here: 132 us
  waiting for transfers between devices  47.9 us (36%)
  blocking collectives  42.3 us (32%)
  between operations  13.6 us (10%)
  starting transfers between devices  10.5 us (8%)
  matrix products  9.48 us (7%)
  local copies, waits for them, and re-layouts  5.1 us (4%)
  other arithmetic  3.21 us (2%)
    psum x1, waiting for transfers between devices, per_device(): projected_rows = lax.psum(base_part + raised_output, 'tensor')  37.3 us
    all_gather x1, blocking collectives, per_device(): complete_rows = lax.all_gather(hidden, 'tensor', axis=2, tiled=True)  24.2 us
    all_gather x1, blocking collectives, per_device(): lax.all_gather(queries, 'tensor', axis=2, tiled=True)  18.2 us
    all_to_all x1, waiting for transfers between devices, per_device(): lax.all_to_all(past_sum[None].astype(jnp.bfloat16), 'tensor', split_axis=...  6.53 us
    all_to_all x1, waiting for transfers between devices, per_device(): lax.all_to_all(past_peak[None].astype(jnp.bfloat16), 'tensor', split_axis...  4 us
    dot_general x1, matrix products, per_device(): jnp.einsum('bnd,dk->bnk', hidden, key_value_weight, preferred_element_typ...  3.59 us
    all_to_all x1, starting transfers between devices, per_device(): lax.all_to_all(past_mix[None].astype(jnp.bfloat16), 'tensor', split_axis=...  3.53 us
    all_to_all x1, starting transfers between devices, per_device(): lax.all_to_all(past_peak[None].astype(jnp.bfloat16), 'tensor', split_axis...  3.49 us
  transfers between devices with their start and end apart: 4, of which 3 were waited for; matrix products, arithmetic and copies ran while one was open for 7% of the time, Pallas kernels for 0%

commit v1 on v0

v1 whole, which is shorter than its diff:
```python
import functools
import math

import jax
import jax.numpy as jnp
from jax import lax
from jax.experimental import pallas as pl
from jax.experimental.pallas import tpu as pltpu
from jax.sharding import PartitionSpec as P

QUERY_HEADS = 128
KEY_HEADS = 8
HEAD_WIDTH = 128
ROPE_BASE = 500000.0
NEG_FILL = -1e30
SCALE = 1.0 / math.sqrt(HEAD_WIDTH)
PROJ_ROWS = 32
STAT_ROWS = 16


def dot(a, b, dims):
    return lax.dot_general(a, b, (dims, ((), ())), preferred_element_type=jnp.float32)


def partial_kernel(devices, requests, tokens, *refs):
    (index_ref, adapter_ref, rank_ref, pool_ref, length_ref) = refs[:5]
    base_ref, down_ref, up_ref, key_ref, value_ref, out_ref = refs[-6:]
    gathered = refs[5:-6]
    here = index_ref[0]
    rows = requests * tokens
    heads = QUERY_HEADS // devices
    per_key_head = devices // KEY_HEADS
    chunks = down_ref.shape[0] // devices // HEAD_WIDTH
    positions = key_ref.shape[0] // requests
    mix_rows = heads * rows

    flat = [ref.at[s] for ref in gathered for s in range(ref.shape[0])]
    bits = devices.bit_length() - 1
    slots = [flat[int(format(r, f"0{bits}b")[::-1], 2)] for r in range(devices)]

    lowered = jnp.zeros((rows, down_ref.shape[1]), jnp.float32)
    for r in range(devices):
        hidden = jnp.concatenate([slots[r][heads + c] for c in range(chunks)], axis=1)
        source = here ^ r
        depth = chunks * HEAD_WIDTH
        factor = down_ref[pl.ds(pl.multiple_of(source * depth, depth), depth), :]
        lowered += dot(hidden, factor, ((1,), (0,)))
    row_request = lax.broadcasted_iota(jnp.int32, (rows, 1), 0) // tokens
    ranks = jnp.zeros((rows, 1), jnp.int32)
    owners = jnp.zeros((rows, 1), jnp.int32)
    for b in range(requests):
        adapter = adapter_ref[b]
        ranks = jnp.where(row_request == b, rank_ref[adapter], ranks)
        owners = jnp.where(row_request == b, pool_ref[adapter], owners)
    lane = lax.broadcasted_iota(jnp.int32, lowered.shape, 1)
    lowered = jnp.where(lane < ranks, lowered, 0.0).astype(jnp.bfloat16)
    lifted = dot(lowered, up_ref[...], ((1,), (0,)))
    projected = base_ref[...] + jnp.where(owners == here, lifted, 0.0)
    high = projected.astype(jnp.bfloat16)
    low = (projected - high.astype(jnp.float32)).astype(jnp.bfloat16)
    split = KEY_HEADS * HEAD_WIDTH
    for head in range(KEY_HEADS):
        at = head * HEAD_WIDTH
        block = jnp.concatenate(
            [
                high[:, at : at + HEAD_WIDTH],
                high[:, split + at : split + at + HEAD_WIDTH],
                low[:, at : at + HEAD_WIDTH],
                low[:, split + at : split + at + HEAD_WIDTH],
            ],
            axis=0,
        )
        for t in range(per_key_head):
            out_ref[head * per_key_head + t, mix_rows : mix_rows + PROJ_ROWS, :] = block

    stacked = requests * positions
    place = lax.broadcasted_iota(jnp.int32, (stacked, HEAD_WIDTH), 0)
    column = lax.broadcasted_iota(jnp.int32, (stacked, HEAD_WIDTH), 1)
    place_request = place // positions
    limit = jnp.zeros_like(place)
    for b in range(requests):
        limit = jnp.where(place_request == b, length_ref[b], limit)
    allowed = (here * positions + place % positions < limit) & (
        place_request == (column // tokens) % requests
    )
    stat_row = lax.broadcasted_iota(jnp.int32, (STAT_ROWS, mix_rows), 0)
    pad = jnp.zeros((STAT_ROWS, HEAD_WIDTH - mix_rows), jnp.float32)
    for j in range(KEY_HEADS):
        key_head = (here // per_key_head) ^ j
        at = pl.multiple_of(key_head * HEAD_WIDTH, HEAD_WIDTH)
        query = jnp.concatenate(
            [
                slots[j * per_key_head + t][h]
                for t in range(per_key_head)
                for h in range(heads)
            ],
            axis=0,
        )
        scores = dot(key_ref[:, pl.ds(at, HEAD_WIDTH)], query, ((1,), (1,))) * SCALE
        peak = jnp.max(jnp.where(allowed, scores, NEG_FILL), axis=0, keepdims=True)
        peak = peak.astype(jnp.bfloat16).astype(jnp.float32)
        weights = jnp.where(allowed, jnp.exp(scores - peak), 0.0)
        total = jnp.sum(weights, axis=0, keepdims=True)
        total_high = total.astype(jnp.bfloat16).astype(jnp.float32)
        mix = dot(weights.astype(jnp.bfloat16), value_ref[:, pl.ds(at, HEAD_WIDTH)], ((0,), (0,)))
        mix = mix.astype(jnp.bfloat16)
        for t in range(per_key_head):
            owner = here ^ (j * per_key_head + t)
            own = slice(t * mix_rows, (t + 1) * mix_rows)
            out_ref[owner, 0:mix_rows, :] = mix[own]
            stats = jnp.where(
                stat_row == 0,
                peak[:, own],
                jnp.where(
                    stat_row == 1,
                    total_high[:, own],
                    jnp.where(stat_row == 2, (total - total_high)[:, own], 0.0),
                ),
            )
            out_ref[owner, mix_rows + PROJ_ROWS :, :] = jnp.concatenate([stats, pad], axis=1).astype(
                jnp.bfloat16
            )


def merge_kernel(devices, requests, tokens, query_ref, cos_ref, sin_ref, got_ref, out_ref):
    rows = requests * tokens
    heads = QUERY_HEADS // devices
    mix_rows = heads * rows
    projected = jnp.sum(got_ref[:, mix_rows : mix_rows + PROJ_ROWS, :].astype(jnp.float32), axis=0)
    projected = projected[: 2 * rows] + projected[2 * rows :]
    keys, values = projected[:rows], projected[rows:].astype(jnp.bfloat16)
    turned = pltpu.roll(keys, HEAD_WIDTH // 2, 1)
    keys = (keys * cos_ref[...] + turned * sin_ref[...]).astype(jnp.bfloat16)
    query = jnp.concatenate([query_ref[h] for h in range(heads)], axis=0)
    fresh = dot(keys, query, ((1,), (1,))) * SCALE
    source = lax.broadcasted_iota(jnp.int32, fresh.shape, 0)
    column = lax.broadcasted_iota(jnp.int32, fresh.shape, 1) % rows
    allowed = (source // tokens == column // tokens) & (source % tokens <= column % tokens)
    stats = got_ref[:, mix_rows + PROJ_ROWS :, :].astype(jnp.float32)[:, :, :mix_rows]
    peaks = stats[:, 0, :]
    totals = stats[:, 1, :] + stats[:, 2, :]
    peak = jnp.maximum(
        jnp.max(peaks, axis=0, keepdims=True),
        jnp.max(jnp.where(allowed, fresh, NEG_FILL), axis=0, keepdims=True),
    )
    weights = jnp.where(allowed, jnp.exp(fresh - peak), 0.0)
    factors = jnp.exp(peaks - peak)
    total = jnp.sum(factors * totals, axis=0, keepdims=True) + jnp.sum(
        weights, axis=0, keepdims=True
    )
    inverse = 1.0 / total
    filler = jnp.zeros((128 - devices - 8, mix_rows), jnp.float32)
    table = jnp.concatenate(
        [factors * inverse, jnp.broadcast_to(inverse, (8, mix_rows)), filler], axis=0
    )
    if mix_rows < 128:
        table = jnp.concatenate([table, jnp.zeros((128, 128 - mix_rows), jnp.float32)], axis=1)
    table = jnp.transpose(table)[:mix_rows]
    mix = dot(weights.astype(jnp.bfloat16), values, ((0,), (0,))) * table[:, devices : devices + 1]
    for s in range(devices):
        mix += got_ref[s, 0:mix_rows, :].astype(jnp.float32) * table[:, s : s + 1]
    for h in range(heads):
        out_ref[:, h * HEAD_WIDTH : (h + 1) * HEAD_WIDTH] = mix[h * rows : (h + 1) * rows].astype(
            jnp.bfloat16
        )


def rotation(lengths, tokens):
    half = HEAD_WIDTH // 2
    places = (lengths[:, None] + jnp.arange(tokens, dtype=jnp.int32)[None, :]).astype(jnp.float32)
    inverse_freq = jnp.exp(
        jnp.arange(half, dtype=jnp.float32) * (-2.0 * math.log(ROPE_BASE) / HEAD_WIDTH)
    )
    angles = places.reshape(-1, 1) * inverse_freq[None, :]
    cosine, sine = jnp.cos(angles), jnp.sin(angles)
    return jnp.concatenate([cosine, cosine], axis=1), jnp.concatenate([-sine, sine], axis=1)


def vmem():
    return pl.BlockSpec(memory_space=pltpu.VMEM)


def smem():
    return pl.BlockSpec(memory_space=pltpu.SMEM)


def per_device(
    hidden,
    queries,
    key_value_weight,
    adapter_down_weight,
    adapter_up_weight,
    cached_key_rows,
    cached_value_rows,
    request_adapter,
    adapter_rank_list,
    adapter_pool_row,
    lengths,
):
    requests, tokens, width = hidden.shape
    rows = requests * tokens
    devices = lax.axis_size("tensor")
    here = lax.axis_index("tensor")
    heads = QUERY_HEADS // devices
    chunks = width // HEAD_WIDTH

    def tiles(x):
        return x.reshape(rows, -1, HEAD_WIDTH).transpose(1, 0, 2)

    own_queries = tiles(queries)
    own = jnp.concatenate([own_queries, tiles(hidden)], axis=0)[None]
    gathered = [own]
    bit = devices // 2
    while bit:
        sent = gathered[0] if len(gathered) == 1 else jnp.concatenate(gathered, axis=0)
        pairs = [(d, d ^ bit) for d in range(devices)]
        gathered = [sent, lax.ppermute(sent, "tensor", pairs)]
        bit //= 2
    held = jnp.concatenate(gathered, axis=0)
    base = dot(hidden.reshape(rows, width), key_value_weight, ((1,), (0,)))
    flat = requests * cached_key_rows.shape[1]
    mix_rows = heads * rows
    packet_rows = mix_rows + PROJ_ROWS + STAT_ROWS
    packets = pl.pallas_call(
        functools.partial(partial_kernel, devices, requests, tokens),
        out_shape=jax.ShapeDtypeStruct((devices, packet_rows, HEAD_WIDTH), jnp.bfloat16),
        in_specs=[smem()] * 5 + [vmem()] * 6,
        out_specs=vmem(),
        compiler_params=pltpu.CompilerParams(vmem_limit_bytes=24 * 2**20),
        name="partial_states",
    )(
        here.reshape(1).astype(jnp.int32),
        request_adapter,
        adapter_rank_list,
        adapter_pool_row,
        lengths,
        held,
        base,
        adapter_down_weight[0],
        adapter_up_weight[0],
        cached_key_rows.reshape(flat, -1),
        cached_value_rows.reshape(flat, -1),
    )
    got = lax.all_to_all(packets, "tensor", split_axis=0, concat_axis=0, tiled=True)
    cosine, sine = rotation(lengths, tokens)
    out = pl.pallas_call(
        functools.partial(merge_kernel, devices, requests, tokens),
        out_shape=jax.ShapeDtypeStruct((rows, heads * HEAD_WIDTH), jnp.bfloat16),
        in_specs=[vmem()] * 4,
        out_specs=vmem(),
        compiler_params=pltpu.CompilerParams(vmem_limit_bytes=16 * 2**20),
        name="merge_states",
    )(own_queries, cosine, sine, got)
    return out.reshape(requests, tokens, -1)


def solution(mesh):
    in_specs = (
        P("groups", None, "tensor"),
        P("groups", None, "tensor"),
        P("tensor", None),
        P("tensor", None, None),
        P("tensor", None, None),
        P("groups", "tensor", None),
        P("groups", "tensor", None),
        P("groups"),
        P(),
        P(),
        P("groups"),
    )
    out_specs = P("groups", None, "tensor")
    return jax.shard_map(
        per_device, mesh=mesh, in_specs=in_specs, out_specs=out_specs, check_vma=False
    )
```

time: 134 us -> 45.5 us (0.34); the launches traced: 132 us -> 45.1 us
  blocking collectives: 42.3 us -> 0 us
  waiting for transfers between devices: 47.9 us -> 19 us
  between operations: 13.6 us -> 0.16 us
  matrix products: 9.48 us -> 2.84 us
  Pallas kernels: 0 us -> 3.7 us
  starting transfers between devices: 10.5 us -> 13.8 us
  other arithmetic: 3.21 us -> 0.33 us
    all_gather x2 -> x0, blocking collectives: 42.3 us -> none  [the longest x1 24.2 us: per_device(): complete_rows = lax.all_gather(hidden, 'tensor', axis=2, tiled=True)]
    psum x1 -> x0, waiting for transfers between devices: 37.3 us -> none  [per_device(): projected_rows = lax.psum(base_part + raised_output, 'tensor')]
    ppermute x0 -> x4, starting transfers between devices: none -> 7.6 us  [per_device(): gathered = [sent, lax.ppermute(sent, 'tensor', pairs)]]
    dot_general x6 -> x1, matrix products: 9.48 us -> 2.84 us  [dot(): lax.dot_general(a, b, (dims, ((), ())), preferred_element_type=jnp.float32)]
    ppermute x0 -> x4, waiting for transfers between devices: none -> 6.08 us  [per_device(): gathered = [sent, lax.ppermute(sent, 'tensor', pairs)]]
    all_to_all x3 -> x1, starting transfers between devices: 10.5 us -> 6.15 us  [per_device(): lax.all_to_all(packets, 'tensor', split_axis=0, concat_axis=0, tiled=True)]
    pallas_call x0 -> x2, Pallas kernels: none -> 3.7 us  [the longest x1 3.09 us: per_device(): pl.pallas_call(functools.partial(partial_kernel, devices, requests, token...]
    convert_element_type x5 -> x1, local copies, waits for them, and re-layouts: 2.63 us -> 0.08 us  [rotation(): (lengths[:, None] + jnp.arange(tokens, dtype=jnp.int32)[None, :]).astype(...]
  transfers between devices with their start and end apart: 4 -> 5, of which waited for: 3 -> 5; matrix products, arithmetic and copies ran while one was open for 7% -> 9% of each run, Pallas kernels for 0% -> 0%
where the time goes in v1:
time: 45.5 us; the launch traced here: 45.1 us
  waiting for transfers between devices  19 us (42%)
  starting transfers between devices  13.8 us (30%)
  local copies, waits for them, and re-layouts  5.31 us (12%)
  Pallas kernels  3.7 us (8%)
  matrix products  2.84 us (6%)
    all_to_all x1, waiting for transfers between devices, per_device(): lax.all_to_all(packets, 'tensor', split_axis=0, concat_axis=0, tiled=True)  12.9 us
    ppermute x4, starting transfers between devices, per_device(): gathered = [sent, lax.ppermute(sent, 'tensor', pairs)]  7.6 us
    all_to_all x1, starting transfers between devices, per_device(): lax.all_to_all(packets, 'tensor', split_axis=0, concat_axis=0, tiled=True)  6.15 us
    ppermute x4, waiting for transfers between devices, per_device(): gathered = [sent, lax.ppermute(sent, 'tensor', pairs)]  6.08 us
    pallas_call x1, Pallas kernels, per_device(): pl.pallas_call(functools.partial(partial_kernel, devices, requests, token...  3.09 us
    dot_general x1, matrix products, dot(): lax.dot_general(a, b, (dims, ((), ())), preferred_element_type=jnp.float32)  2.84 us
    unnamed x19, local copies, waits for them, and re-layouts  2.25 us
    reshape x2, local copies, waits for them, and re-layouts, tiles(): return x.reshape(rows, -1, HEAD_WIDTH).transpose(1, 0, 2)  1.58 us
  transfers between devices with their start and end apart: 5, of which 5 were waited for; matrix products, arithmetic and copies ran while one was open for 9% of the time, Pallas kernels for 0%

profile of v1, /device:TPU:0, one launch (start us, length us, event | category | flops | bytes accessed | tf_op | source)
XLA Modules:
  0.0 45.1 jit_solution(5703675993075962233)
XLA Ops:
  0.0 0.0 copy-start.6
  0.0 0.0 copy-start.7
  0.0 0.8 %reshape.44 = bf16[8,8,128]{2,1,0:T(8,128)(2,1)S(1)} reshape(bf16[2,4,1024]{2,1,0:T(4,128)(2,1)} %param.12) | data formatting | bytes 32768 | tf_op jit(solution)/shard_map/reshape | solution.py:208
  0.9 0.7 %reshape.46 = bf16[8,8,128]{2,1,0:T(8,128)(2,1)S(1)} reshape(bf16[2,4,1024]{2,1,0:T(4,128)(2,1)} %param.11) | data formatting | bytes 32768 | tf_op jit(solution)/shard_map/reshape | solution.py:208
  1.6 4.1 %collective-permute-start = (bf16[1,16,8,128]{3,2,1,0:T(8,128)(2,1)S(1)}, bf16[1,16,8,128]{3,2,1,0:T(8,128)(2,1)S(1)}, u32[]{:S(2)}, u32[]{:S(2)}) collective-permute-start(bf16[1,16,8,128]{3,2,1,0:T(8,128)(2,1)S(1)} %maximum_bitcast_fusion), channel_id=1, source_target_pairs={{0,8},{1,9},{2,10},{3,11},{4,12},{5,13},{6,14},{7,15},{8,0},{9,1},... | collective-permute-start | bytes 98312 | tf_op jit(solution)/shard_map/ppermute | solution.py:217
  5.8 2.2 %collective-permute-done = bf16[1,16,8,128]{3,2,1,0:T(8,128)(2,1)S(1)} collective-permute-done((bf16[1,16,8,128]{3,2,1,0:T(8,128)(2,1)S(1)}, bf16[1,16,8,128]{3,2,1,0:T(8,128)(2,1)S(1)}, u32[]{:S(2)}, u32[]{:S(2)}) %collective-permute-start) | collective-permute-done | bytes 32800 | tf_op jit(solution)/shard_map/ppermute | solution.py:217
  8.0 1.6 %collective-permute-start.1 = (bf16[2,16,8,128]{3,2,1,0:T(8,128)(2,1)S(1)}, bf16[2,16,8,128]{3,2,1,0:T(8,128)(2,1)S(1)}, u32[]{:S(2)}, u32[]{:S(2)}) collective-permute-start(bf16[2,16,8,128]{3,2,1,0:T(8,128)(2,1)S(1)} %pad_maximum_fusion.2), channel_id=1, source_target_pairs={{0,4},{1,5},{2,6},{3,7},{4,0},{5,1},{6,2},{7,3},{8,12},{9,13},{10,... | collective-permute-start | bytes 196616 | tf_op jit(solution)/shard_map/ppermute | solution.py:217
  9.6 0.7 %reshape.47 = bf16[8,1024]{1,0:T(8,128)(2,1)S(1)} reshape(bf16[2,4,1024]{2,1,0:T(4,128)(2,1)} %param.11) | data formatting | bytes 32768 | tf_op jit(solution)/shard_map/reshape | solution.py:220
  10.4 2.0 %collective-permute-done.1 = bf16[2,16,8,128]{3,2,1,0:T(8,128)(2,1)S(1)} collective-permute-done((bf16[2,16,8,128]{3,2,1,0:T(8,128)(2,1)S(1)}, bf16[2,16,8,128]{3,2,1,0:T(8,128)(2,1)S(1)}, u32[]{:S(2)}, u32[]{:S(2)}) %collective-permute-start.1) | collective-permute-done | bytes 65568 | tf_op jit(solution)/shard_map/ppermute | solution.py:217
  12.4 1.8 %collective-permute-start.2 = (bf16[4,16,8,128]{3,2,1,0:T(8,128)(2,1)S(1)}, bf16[4,16,8,128]{3,2,1,0:T(8,128)(2,1)S(1)}, u32[]{:S(2)}, u32[]{:S(2)}) collective-permute-start(bf16[4,16,8,128]{3,2,1,0:T(8,128)(2,1)S(1)} %pad_maximum_fusion.1), channel_id=1, source_target_pairs={{0,2},{1,3},{2,0},{3,1},{4,6},{5,7},{6,4},{7,5},{8,10},{9,11},{10,... | collective-permute-start | bytes 393224 | tf_op jit(solution)/shard_map/ppermute | solution.py:217
  14.2 2.8 %fusion.1.refs_6_ = f32[8,2048]{1,0:T(8,128)S(1)} fusion(bf16[8,1024]{1,0:T(8,128)(2,1)S(1)} %reshape.47, bf16[1024,2048]{1,0:T(8,128)(2,1)} %param.13), kind=kOutput, calls=%fused_computation.18 | convolution fusion | flops 33554432 | bytes 4276224 | tf_op jit(solution)/shard_map/dot_general | solution.py:22
  17.0 0.4 collective-permute-done.2
  17.4 0.1 collective-permute-start.3
  17.6 1.5 %collective-permute-done.3 = bf16[8,16,8,128]{3,2,1,0:T(8,128)(2,1)S(1)} collective-permute-done((bf16[8,16,8,128]{3,2,1,0:T(8,128)(2,1)S(1)}, bf16[8,16,8,128]{3,2,1,0:T(8,128)(2,1)S(1)}, u32[]{:S(2)}, u32[]{:S(2)}) %collective-permute-start.3) | collective-permute-done | bytes 262176 | tf_op jit(solution)/shard_map/ppermute | solution.py:217
  19.1 0.0 copy-done.1
  19.1 0.0 copy-done.2
  19.1 0.0 copy-done.3
  19.1 0.0 copy-done.4
  19.1 0.0 copy-done.5
  19.1 0.0 copy-done.6
  19.1 0.0 copy-done.7
  19.1 0.0 copy-start
  19.2 2.2 %copy-done = bf16[1,16384,128]{2,1,0:T(8,128)(2,1)S(1)} copy-done((bf16[1,16384,128]{2,1,0:T(8,128)(2,1)S(1)}, bf16[1,16384,128]{2,1,0:T(8,128)(2,1)}, u32[]{:S(2)}) %copy-start) | copy-done | bytes 4194328
  21.3 3.1 %partial_states.1 = bf16[16,112,128]{2,1,0:T(8,128)(2,1)} custom-call(s32[1]{0:T(128)} %bitcast.1.refs_0_, s32[2]{0:T(128)S(1)} %copy-done.4, s32[16]{0:T(128)S(1)} %copy-done.5, s32[16]{0:T(128)S(1)} %copy-done.6, s32[2]{0:T(128)S(1)} %copy-done.7, bf16[16,16,8,128]{3,2,1,0:T(8,128)(2,1)S(1)} %constant_dynamic-update-slice_fusion.refs_5_, ...), custom_call_target="tpu_custom_call" | custom-call | tf_op jit(solution)/shard_map/partial_states/pallas_call | solution.py:224
  24.4 6.2 %all-to-all-start = ((bf16[16,112,128]{2,1,0:T(8,128)(2,1)}), bf16[16,112,128]{2,1,0:T(8,128)(2,1)S(1)}, u32[]{:S(2)}, u32[]{:S(2)}) async-start(bf16[16,112,128]{2,1,0:T(8,128)(2,1)} %partial_states.1), calls=%async_computation | async-start | bytes 917504 | tf_op jit(solution)/shard_map/all_to_all | solution.py:244
  30.6 0.1 add_convert_fusion
  30.7 0.1 convert_element_type.11
  30.8 0.1 fusion
  30.9 0.1 pad_maximum_fusion.3
  30.9 12.9 %all-to-all-done.got_ref = bf16[16,112,128]{2,1,0:T(8,128)(2,1)S(1)} async-done(((bf16[16,112,128]{2,1,0:T(8,128)(2,1)}), bf16[16,112,128]{2,1,0:T(8,128)(2,1)S(1)}, u32[]{:S(2)}, u32[]{:S(2)}) %all-to-all-start) | async-done | bytes 458784 | tf_op jit(solution)/shard_map/all_to_all | solution.py:244
  43.8 0.6 %merge_states.1 = bf16[8,1024]{1,0:T(8,128)(2,1)S(1)} custom-call(bf16[8,8,128]{2,1,0:T(8,128)(2,1)S(1)} %get-tuple-element.11.query_ref, f32[8,128]{1,0:T(8,128)S(1)} %get-tuple-element.8.cos_ref, f32[8,128]{1,0:T(8,128)S(1)} %get-tuple-element.9.sin_ref, bf16[16,112,128]{2,1,0:T(8,128)(2,1)S(1)} %all-to-all-done.got_ref), custom_call_target="tpu_custom_call" | custom-call | tf_op jit(solution)/shard_map/merge_states/pallas_call | solution.py:246
  44.4 0.6 %reshape.50 = bf16[2,4,1024]{2,1,0:T(4,128)(2,1)} reshape(bf16[8,1024]{1,0:T(8,128)(2,1)S(1)} %merge_states.1) | data formatting | bytes 32768 | tf_op jit(solution)/shard_map/reshape | solution.py:254
  (16 shorter events, 0.2 us)
Async XLA Ops:
  0.0 19.1 %copy-start.1 = (bf16[1,128,2048]{2,1,0:T(8,128)(2,1)S(1)}, bf16[1,128,2048]{2,1,0:T(8,128)(2,1)}, u32[]{:S(2)}) copy-start(bf16[1,128,2048]{2,1,0:T(8,128)(2,1)} %param.15) | copy-start | bytes 1572868
  0.0 19.1 %copy-start.2 = (bf16[2,128,1024]{2,1,0:T(8,128)(2,1)S(1)}, bf16[2,128,1024]{2,1,0:T(8,128)(2,1)}, u32[]{:S(2)}) copy-start(bf16[2,128,1024]{2,1,0:T(8,128)(2,1)} %param.16) | copy-start | bytes 1572868
  0.0 19.1 %copy-start.3 = (bf16[2,128,1024]{2,1,0:T(8,128)(2,1)S(1)}, bf16[2,128,1024]{2,1,0:T(8,128)(2,1)}, u32[]{:S(2)}) copy-start(bf16[2,128,1024]{2,1,0:T(8,128)(2,1)} %param.17) | copy-start | bytes 1572868
  0.0 19.1 %copy-start.4 = (s32[2]{0:T(128)S(1)}, s32[2]{0:T(128)}, u32[]{:S(2)}) copy-start(s32[2]{0:T(128)} %refs_1_.1) | copy-start | bytes 28
  0.0 19.1 %copy-start.5 = (s32[16]{0:T(128)S(1)}, s32[16]{0:T(128)}, u32[]{:S(2)}) copy-start(s32[16]{0:T(128)} %refs_2_.1) | copy-start | bytes 196
  0.0 19.1 %copy-start.6 = (s32[16]{0:T(128)S(1)}, s32[16]{0:T(128)}, u32[]{:S(2)}) copy-start(s32[16]{0:T(128)} %refs_3_.1) | copy-start | bytes 196
  0.0 19.1 %copy-start.7 = (s32[2]{0:T(128)S(1)}, s32[2]{0:T(128)}, u32[]{:S(2)}) copy-start(s32[2]{0:T(128)} %refs_4_.1) | copy-start | bytes 28
  1.6 6.4 %collective-permute-start = (bf16[1,16,8,128]{3,2,1,0:T(8,128)(2,1)S(1)}, bf16[1,16,8,128]{3,2,1,0:T(8,128)(2,1)S(1)}, u32[]{:S(2)}, u32[]{:S(2)}) collective-permute-start(bf16[1,16,8,128]{3,2,1,0:T(8,128)(2,1)S(1)} %maximum_bitcast_fusion), channel_id=1, source_target_pairs={{0,8},{1,9},{2,10},{3,11},{4,12},{5,13},{6,14},{7,15},{8,0},{9,1},... | collective-permute-start | bytes 98312 | tf_op jit(solution)/shard_map/ppermute | solution.py:217
  8.0 4.3 %collective-permute-start.1 = (bf16[2,16,8,128]{3,2,1,0:T(8,128)(2,1)S(1)}, bf16[2,16,8,128]{3,2,1,0:T(8,128)(2,1)S(1)}, u32[]{:S(2)}, u32[]{:S(2)}) collective-permute-start(bf16[2,16,8,128]{3,2,1,0:T(8,128)(2,1)S(1)} %pad_maximum_fusion.2), channel_id=1, source_target_pairs={{0,4},{1,5},{2,6},{3,7},{4,0},{5,1},{6,2},{7,3},{8,12},{9,13},{10,... | collective-permute-start | bytes 196616 | tf_op jit(solution)/shard_map/ppermute | solution.py:217
  12.4 5.0 %collective-permute-start.2 = (bf16[4,16,8,128]{3,2,1,0:T(8,128)(2,1)S(1)}, bf16[4,16,8,128]{3,2,1,0:T(8,128)(2,1)S(1)}, u32[]{:S(2)}, u32[]{:S(2)}) collective-permute-start(bf16[4,16,8,128]{3,2,1,0:T(8,128)(2,1)S(1)} %pad_maximum_fusion.1), channel_id=1, source_target_pairs={{0,2},{1,3},{2,0},{3,1},{4,6},{5,7},{6,4},{7,5},{8,10},{9,11},{10,... | collective-permute-start | bytes 393224 | tf_op jit(solution)/shard_map/ppermute | solution.py:217
  17.4 1.6 %collective-permute-start.3 = (bf16[8,16,8,128]{3,2,1,0:T(8,128)(2,1)S(1)}, bf16[8,16,8,128]{3,2,1,0:T(8,128)(2,1)S(1)}, u32[]{:S(2)}, u32[]{:S(2)}) collective-permute-start(bf16[8,16,8,128]{3,2,1,0:T(8,128)(2,1)S(1)} %pad_maximum_fusion), channel_id=1, source_target_pairs={{0,1},{1,0},{2,3},{3,2},{4,5},{5,4},{6,7},{7,6},{8,9},{9,8},{10,11... | collective-permute-start | bytes 786440 | tf_op jit(solution)/shard_map/ppermute | solution.py:217
  19.1 2.2 %copy-start = (bf16[1,16384,128]{2,1,0:T(8,128)(2,1)S(1)}, bf16[1,16384,128]{2,1,0:T(8,128)(2,1)}, u32[]{:S(2)}) copy-start(bf16[1,16384,128]{2,1,0:T(8,128)(2,1)} %param.14) | copy-start | bytes 12582916
  24.4 19.4 %all-to-all-start = ((bf16[16,112,128]{2,1,0:T(8,128)(2,1)}), bf16[16,112,128]{2,1,0:T(8,128)(2,1)S(1)}, u32[]{:S(2)}, u32[]{:S(2)}) async-start(bf16[16,112,128]{2,1,0:T(8,128)(2,1)} %partial_states.1), calls=%async_computation | async-start | bytes 917504 | tf_op jit(solution)/shard_map/all_to_all | solution.py:244

commit v2 on v1

v2 whole, which is shorter than its diff:
```python
import functools
import math

import jax
import jax.numpy as jnp
from jax import lax
from jax.experimental import pallas as pl
from jax.experimental.pallas import tpu as pltpu
from jax.sharding import PartitionSpec as P

QUERY_HEADS = 128
KEY_HEADS = 8
HEAD_WIDTH = 128
ROPE_BASE = 500000.0
NEG_FILL = -1e30
SCALE = 1.0 / math.sqrt(HEAD_WIDTH)
PAIRS = KEY_HEADS // 2
STAT_ROWS = 16
MIB = 2**20


def dot(a, b, dims):
    return lax.dot_general(a, b, (dims, ((), ())), preferred_element_type=jnp.float32)


def round_bf16(x):
    return x.astype(jnp.bfloat16).astype(jnp.float32)


def pack_kernel(requests, query_ref, hidden_ref, out_ref):
    at = 0
    for ref in (query_ref, hidden_ref):
        rows = jnp.concatenate([ref[b].astype(jnp.float32) for b in range(requests)], axis=0)
        for c in range(rows.shape[1] // HEAD_WIDTH):
            tile = rows[:, c * HEAD_WIDTH : (c + 1) * HEAD_WIDTH]
            out_ref[at] = tile.astype(jnp.bfloat16)
            at += 1


def base_kernel(heads, packed_ref, weight_ref, base_ref):
    chunks = weight_ref.shape[0] // HEAD_WIDTH
    hidden = jnp.concatenate([packed_ref[heads + c] for c in range(chunks)], axis=1)
    base_ref[...] = dot(hidden, weight_ref[...], ((1,), (0,)))


def partial_kernel(devices, requests, tokens, *refs):
    (index_ref, adapter_ref, rank_ref, pool_ref, length_ref) = refs[:5]
    (lane_ref, other_ref, base_ref, down_ref, up_ref, key_ref, value_ref) = refs[5:12]
    (send_ref, mix_ref, stat_ref, proj_ref, all_ref) = refs[12:]
    here = index_ref[0]
    rows = requests * tokens
    heads = QUERY_HEADS // devices
    lanes = devices // 2
    per_key_head = devices // KEY_HEADS
    per_lane = per_key_head // 2
    chunks = down_ref.shape[0] // devices // HEAD_WIDTH
    positions = key_ref.shape[0] // requests
    depth = chunks * HEAD_WIDTH

    lowered = jnp.zeros((rows, down_ref.shape[1]), jnp.float32)
    for side, ref in enumerate((lane_ref, other_ref)):
        for m in range(lanes):
            hidden = jnp.concatenate([ref[m, heads + c] for c in range(chunks)], axis=1)
            source = here ^ (2 * m + side)
            factor = down_ref[pl.ds(pl.multiple_of(source * depth, depth), depth), :]
            lowered += dot(hidden, factor, ((1,), (0,)))
    row_request = lax.broadcasted_iota(jnp.int32, (rows, 1), 0) // tokens
    ranks = jnp.zeros((rows, 1), jnp.int32)
    owners = jnp.zeros((rows, 1), jnp.int32)
    for b in range(requests):
        adapter = adapter_ref[b]
        ranks = jnp.where(row_request == b, rank_ref[adapter], ranks)
        owners = jnp.where(row_request == b, pool_ref[adapter], owners)
    column = lax.broadcasted_iota(jnp.int32, lowered.shape, 1)
    lowered = jnp.where(column < ranks, lowered, 0.0).astype(jnp.bfloat16)
    lifted = dot(lowered, up_ref[...], ((1,), (0,)))
    all_ref[...] = base_ref[...] + jnp.where(owners == here, lifted, 0.0)

    split = KEY_HEADS * HEAD_WIDTH
    mix_total = KEY_HEADS * 64
    for j in range(KEY_HEADS):
        at = ((here // per_key_head) ^ j) * HEAD_WIDTH
        keys = all_ref[:, pl.ds(pl.multiple_of(at, HEAD_WIDTH), HEAD_WIDTH)]
        values = all_ref[:, pl.ds(pl.multiple_of(split + at, HEAD_WIDTH), HEAD_WIDTH)]
        proj_ref[0, j] = keys
        proj_ref[1, j] = values
    keys = proj_ref[0].reshape(KEY_HEADS * rows, HEAD_WIDTH)
    high = keys.astype(jnp.bfloat16)
    step = KEY_HEADS * rows
    send_ref[mix_total : mix_total + step] = high
    send_ref[mix_total + step : mix_total + 2 * step] = (keys - high.astype(jnp.float32)).astype(
        jnp.bfloat16
    )
    send_ref[mix_total + 2 * step : mix_total + 3 * step] = (
        proj_ref[1].reshape(step, HEAD_WIDTH).astype(jnp.bfloat16)
    )

    stacked = requests * positions
    place = lax.broadcasted_iota(jnp.int32, (stacked, HEAD_WIDTH), 0)
    column = lax.broadcasted_iota(jnp.int32, (stacked, HEAD_WIDTH), 1)
    place_request = place // positions
    limit = jnp.zeros_like(place)
    for b in range(requests):
        limit = jnp.where(place_request == b, length_ref[b], limit)
    allowed = (here * positions + place % positions < limit) & (
        place_request == (column // tokens) % requests
    )
    first = column < 64
    stat_row = lax.broadcasted_iota(jnp.int32, (STAT_ROWS, HEAD_WIDTH), 0)
    for side, ref in enumerate((other_ref, lane_ref)):
        stats = jnp.zeros((STAT_ROWS, HEAD_WIDTH), jnp.float32)
        for p in range(PAIRS):
            spots = [
                pl.multiple_of(((here // per_key_head) ^ j) * HEAD_WIDTH, HEAD_WIDTH)
                for j in (2 * p, 2 * p + 1)
            ]
            query = jnp.concatenate(
                [ref[2 * p * per_lane + t, h] for t in range(2 * per_lane) for h in range(heads)],
                axis=0,
            )
            scores = [
                dot(key_ref[:, pl.ds(at, HEAD_WIDTH)], query, ((1,), (1,))) for at in spots
            ]
            scores = jnp.where(first, scores[0], scores[1]) * SCALE
            peak = jnp.max(jnp.where(allowed, scores, NEG_FILL), axis=0, keepdims=True)
            peak = round_bf16(peak)
            weights = jnp.where(allowed, jnp.exp(scores - peak), 0.0)
            total = jnp.sum(weights, axis=0, keepdims=True)
            weights = jnp.transpose(weights.astype(jnp.bfloat16))
            mix = [
                dot(weights[64 * i : 64 * i + 64], value_ref[:, pl.ds(at, HEAD_WIDTH)], ((1,), (0,)))
                for i, at in enumerate(spots)
            ]
            at = p * 128
            for i in range(2):
                if side == 0:
                    send_ref[at + 64 * i : at + 64 * i + 64] = mix[i].astype(jnp.bfloat16)
                else:
                    mix_ref[at + 64 * i : at + 64 * i + 64] = mix[i]
            stats = jnp.where(stat_row == p, peak, stats)
            high = round_bf16(total)
            if side == 0:
                stats = jnp.where(stat_row == PAIRS + p, high, stats)
                stats = jnp.where(stat_row == 2 * PAIRS + p, total - high, stats)
            else:
                stats = jnp.where(stat_row == PAIRS + p, total, stats)
        if side == 0:
            send_ref[mix_total + 3 * step :] = stats.astype(jnp.bfloat16)
        else:
            stat_ref[...] = stats


def join_kernel(devices, requests, tokens, mix_ref, stat_ref, proj_ref, got_ref, *out_refs):
    rows = requests * tokens
    heads = QUERY_HEADS // devices
    mix_rows = heads * rows
    per_lane = devices // KEY_HEADS // 2
    mix_total = KEY_HEADS * 64
    step = KEY_HEADS * rows
    got = got_ref[mix_total + 3 * step :, :].astype(jnp.float32)
    own = stat_ref[...]
    own_peak, got_peak = own[:PAIRS], got[:PAIRS]
    peak = jnp.maximum(own_peak, got_peak)
    own_factor = jnp.exp(own_peak - peak)
    got_factor = jnp.exp(got_peak - peak)
    total = own_factor * own[PAIRS : 2 * PAIRS] + got_factor * (
        got[PAIRS : 2 * PAIRS] + got[2 * PAIRS : 3 * PAIRS]
    )
    high = round_bf16(total)
    filler = jnp.zeros((128 - 2 * PAIRS, 128), jnp.float32)
    table = jnp.transpose(jnp.concatenate([own_factor, got_factor, filler], axis=0))
    keys = got_ref[mix_total : mix_total + step].astype(jnp.float32) + got_ref[
        mix_total + step : mix_total + 2 * step
    ].astype(jnp.float32)
    keys += proj_ref[0].reshape(step, HEAD_WIDTH)
    values = got_ref[mix_total + 2 * step : mix_total + 3 * step].astype(jnp.float32)
    values += proj_ref[1].reshape(step, HEAD_WIDTH)
    keys_high = round_bf16(keys)
    keys_low = keys - keys_high
    stat_row = lax.broadcasted_iota(jnp.int32, (rows, HEAD_WIDTH), 0)
    for p in range(PAIRS):
        mix = mix_ref[p * 128 : p * 128 + 128] * table[:, p : p + 1] + got_ref[
            p * 128 : p * 128 + 128
        ].astype(jnp.float32) * table[:, PAIRS + p : PAIRS + p + 1]
        stats = jnp.where(
            stat_row == 0,
            peak[p : p + 1],
            jnp.where(
                stat_row == 1,
                high[p : p + 1],
                jnp.where(stat_row == 2, (total - high)[p : p + 1], 0.0),
            ),
        )
        for t in range(2 * per_lane):
            j = 2 * p + t // per_lane
            out_ref = out_refs[2 * p * per_lane + t]
            out_ref[:mix_rows] = mix[t * mix_rows : (t + 1) * mix_rows].astype(jnp.bfloat16)
            shifted = stats if t == 0 else pltpu.roll(stats, HEAD_WIDTH - t * mix_rows, 1)
            own = slice(j * rows, (j + 1) * rows)
            out_ref[mix_rows:] = jnp.concatenate(
                [keys_high[own], keys_low[own], values[own], shifted], axis=0
            ).astype(jnp.bfloat16)


def merge_kernel(devices, requests, tokens, packed_ref, cos_ref, sin_ref, *refs):
    got_refs, out_ref = refs[:-1], refs[-1]
    rows = requests * tokens
    heads = QUERY_HEADS // devices
    mix_rows = heads * rows
    sources = len(got_refs)
    tails = [ref[mix_rows:].astype(jnp.float32) for ref in got_refs]
    sums = functools.reduce(jnp.add, [tail[: 3 * rows] for tail in tails])
    keys = sums[:rows] + sums[rows : 2 * rows]
    values = sums[2 * rows :].astype(jnp.bfloat16)
    turned = pltpu.roll(keys, HEAD_WIDTH // 2, 1)
    keys = (keys * cos_ref[...] + turned * sin_ref[...]).astype(jnp.bfloat16)
    query = jnp.concatenate([packed_ref[h] for h in range(heads)], axis=0)
    if mix_rows < 128:
        query = jnp.concatenate(
            [query, jnp.zeros((128 - mix_rows, HEAD_WIDTH), jnp.bfloat16)], axis=0
        )
    fresh = dot(keys, query, ((1,), (1,))) * SCALE
    source = lax.broadcasted_iota(jnp.int32, fresh.shape, 0)
    column = lax.broadcasted_iota(jnp.int32, fresh.shape, 1) % rows
    allowed = (source // tokens == column // tokens) & (source % tokens <= column % tokens)
    fresh_peak = jnp.max(jnp.where(allowed, fresh, NEG_FILL), axis=0, keepdims=True)
    stats = [tail[3 * rows :] for tail in tails]
    peak = functools.reduce(jnp.maximum, [stat[0:1] for stat in stats], fresh_peak)
    weights = jnp.where(allowed, jnp.exp(fresh - peak), 0.0)
    factors = [jnp.exp(stat[0:1] - peak) for stat in stats]
    total = functools.reduce(
        jnp.add,
        [factor * (stat[1:2] + stat[2:3]) for factor, stat in zip(factors, stats)],
        jnp.sum(weights, axis=0, keepdims=True),
    )
    inverse = 1.0 / total
    filler = jnp.zeros((128 - sources - 1, 128), jnp.float32)
    table = jnp.concatenate([factor * inverse for factor in factors] + [inverse, filler], axis=0)
    table = jnp.transpose(table)[:mix_rows]
    weights = jnp.transpose(
        jnp.concatenate([weights, jnp.zeros((128 - rows, 128), jnp.float32)], axis=0)
    )[:mix_rows].astype(jnp.bfloat16)
    values = jnp.concatenate(
        [values, jnp.zeros((128 - rows, HEAD_WIDTH), jnp.bfloat16)], axis=0
    )
    mix = dot(weights, values, ((1,), (0,))) * table[:, sources : sources + 1]
    for s, ref in enumerate(got_refs):
        mix += ref[:mix_rows].astype(jnp.float32) * table[:, s : s + 1]
    for h in range(heads):
        tile = mix[h * rows : (h + 1) * rows]
        for b in range(requests):
            out_ref[b, :, h * HEAD_WIDTH : (h + 1) * HEAD_WIDTH] = tile[
                b * tokens : (b + 1) * tokens
            ].astype(jnp.bfloat16)


def rotation(lengths, tokens):
    half = HEAD_WIDTH // 2
    places = (lengths[:, None] + jnp.arange(tokens, dtype=jnp.int32)[None, :]).astype(jnp.float32)
    inverse_freq = jnp.exp(
        jnp.arange(half, dtype=jnp.float32) * (-2.0 * math.log(ROPE_BASE) / HEAD_WIDTH)
    )
    angles = places.reshape(-1, 1) * inverse_freq[None, :]
    cosine, sine = jnp.cos(angles), jnp.sin(angles)
    return jnp.concatenate([cosine, cosine], axis=1), jnp.concatenate([-sine, sine], axis=1)


def vmem():
    return pl.BlockSpec(memory_space=pltpu.VMEM)


def smem():
    return pl.BlockSpec(memory_space=pltpu.SMEM)


def hbm():
    return pl.BlockSpec(memory_space=pltpu.HBM)


def cost(flops, moved):
    return pl.CostEstimate(flops=int(flops), bytes_accessed=int(moved), transcendentals=0)


def swap(x, devices, bit):
    return lax.ppermute(x, "tensor", [(d, d ^ bit) for d in range(devices)])


def per_device(
    hidden,
    queries,
    key_value_weight,
    adapter_down_weight,
    adapter_up_weight,
    cached_key_rows,
    cached_value_rows,
    request_adapter,
    adapter_rank_list,
    adapter_pool_row,
    lengths,
):
    requests, tokens, width = hidden.shape
    rows = requests * tokens
    devices = lax.axis_size("tensor")
    here = lax.axis_index("tensor")
    heads = QUERY_HEADS // devices
    chunks = width // HEAD_WIDTH
    lanes = devices // 2
    tiles = heads + chunks
    mix_rows = heads * rows

    packed = pl.pallas_call(
        functools.partial(pack_kernel, requests),
        out_shape=jax.ShapeDtypeStruct((tiles, rows, HEAD_WIDTH), jnp.bfloat16),
        in_specs=[vmem()] * 2,
        out_specs=vmem(),
        cost_estimate=cost(10**10, 0),
        name="pack",
    )(queries, hidden)
    lane = [packed] + [swap(packed, devices, 2 * m) for m in range(1, lanes)]
    lane = jnp.concatenate([x[None] for x in lane], axis=0)

    base = pl.pallas_call(
        functools.partial(base_kernel, heads),
        out_shape=jax.ShapeDtypeStruct((rows, key_value_weight.shape[1]), jnp.float32),
        in_specs=[vmem()] * 2,
        out_specs=vmem(),
        compiler_params=pltpu.CompilerParams(vmem_limit_bytes=16 * MIB),
        cost_estimate=cost(2 * rows * key_value_weight.size, 2 * key_value_weight.size),
        name="base",
    )(packed, key_value_weight)
    lane, base = lax.optimization_barrier((lane, base))
    other = swap(lane, devices, 1)

    flat = requests * cached_key_rows.shape[1]
    mix_total = KEY_HEADS * 64
    send_rows = mix_total + 3 * KEY_HEADS * rows + STAT_ROWS
    send, mix, stats, proj = pl.pallas_call(
        functools.partial(partial_kernel, devices, requests, tokens),
        out_shape=(
            jax.ShapeDtypeStruct((send_rows, HEAD_WIDTH), jnp.bfloat16),
            jax.ShapeDtypeStruct((mix_total, HEAD_WIDTH), jnp.float32),
            jax.ShapeDtypeStruct((STAT_ROWS, HEAD_WIDTH), jnp.float32),
            jax.ShapeDtypeStruct((2, KEY_HEADS, rows, HEAD_WIDTH), jnp.float32),
        ),
        in_specs=[smem()] * 5 + [vmem()] * 7,
        out_specs=(vmem(),) * 4,
        scratch_shapes=[pltpu.VMEM(base.shape, jnp.float32)],
        compiler_params=pltpu.CompilerParams(vmem_limit_bytes=20 * MIB),
        name="partial_states",
    )(
        here.reshape(1).astype(jnp.int32),
        request_adapter,
        adapter_rank_list,
        adapter_pool_row,
        lengths,
        lane,
        other,
        base,
        adapter_down_weight[0],
        adapter_up_weight[0],
        cached_key_rows.reshape(flat, -1),
        cached_value_rows.reshape(flat, -1),
    )
    got = swap(send, devices, 1)
    packet = jax.ShapeDtypeStruct((mix_rows + 4 * rows, HEAD_WIDTH), jnp.bfloat16)
    packets = pl.pallas_call(
        functools.partial(join_kernel, devices, requests, tokens),
        out_shape=(packet,) * lanes,
        in_specs=[vmem()] * 4,
        out_specs=(vmem(),) * lanes,
        name="join",
    )(mix, stats, proj, got)
    packets = [packets[0]] + [swap(packets[m], devices, 2 * m) for m in range(1, lanes)]
    cosine, sine = rotation(lengths, tokens)
    return pl.pallas_call(
        functools.partial(merge_kernel, devices, requests, tokens),
        out_shape=jax.ShapeDtypeStruct((requests, tokens, heads * HEAD_WIDTH), jnp.bfloat16),
        in_specs=[vmem()] * (3 + lanes),
        out_specs=vmem(),
        name="merge_states",
    )(packed, cosine, sine, *packets)


def solution(mesh):
    in_specs = (
        P("groups", None, "tensor"),
        P("groups", None, "tensor"),
        P("tensor", None),
        P("tensor", None, None),
        P("tensor", None, None),
        P("groups", "tensor", None),
        P("groups", "tensor", None),
        P("groups"),
        P(),
        P(),
        P("groups"),
    )
    out_specs = P("groups", None, "tensor")
    return jax.shard_map(
        per_device, mesh=mesh, in_specs=in_specs, out_specs=out_specs, check_vma=False
    )
```

time: 45.5 us -> 55.7 us (1.22)
  starting transfers between devices: 13.8 us -> 23.9 us
  waiting for transfers between devices: 19 us -> 11 us
  Pallas kernels: 3.7 us -> 9.98 us
  local copies, waits for them, and re-layouts: 5.31 us -> 9.3 us
  matrix products: 2.84 us -> 0 us
    ppermute x4 -> x16, starting transfers between devices: 7.6 us -> 23.9 us  [swap(): return lax.ppermute(x, 'tensor', [(d, d ^ bit) for d in range(devices)])]
    all_to_all x1 -> x0, waiting for transfers between devices: 12.9 us -> none  [per_device(): lax.all_to_all(packets, 'tensor', split_axis=0, concat_axis=0, tiled=True)]
    unnamed x19 -> x49, local copies, waits for them, and re-layouts: 2.25 us -> 9.2 us
    all_to_all x1 -> x0, starting transfers between devices: 6.15 us -> none  [per_device(): lax.all_to_all(packets, 'tensor', split_axis=0, concat_axis=0, tiled=True)]
    ppermute x4 -> x16, waiting for transfers between devices: 6.08 us -> 11 us  [swap(): return lax.ppermute(x, 'tensor', [(d, d ^ bit) for d in range(devices)])]
    pallas_call x0 -> x3, Pallas kernels: none -> 4.12 us  [the longest x1 2.01 us: per_device(): pl.pallas_call(functools.partial(join_kernel, devices, requests, tokens),...]
    reshape x4 -> x0, local copies, waits for them, and re-layouts: 2.93 us -> none  [the longest x2 1.58 us: tiles(): return x.reshape(rows, -1, HEAD_WIDTH).transpose(1, 0, 2)]
    dot_general x1 -> x0, matrix products: 2.84 us -> none  [dot(): lax.dot_general(a, b, (dims, ((), ())), preferred_element_type=jnp.float32)]
  transfers between devices with their start and end apart: 5 -> 16, of which waited for: 5 -> 6; matrix products, arithmetic and copies ran while one was open for 9% -> 3% of each run, Pallas kernels for 0% -> 1%
where the time goes in v2:
time: 55.7 us; the launch traced here: 55.2 us
  starting transfers between devices  23.9 us (43%)
  waiting for transfers between devices  11 us (20%)
  Pallas kernels  9.98 us (18%)
  local copies, waits for them, and re-layouts  9.3 us (17%)
  other arithmetic  0.85 us (2%)
    ppermute x16, starting transfers between devices, swap(): return lax.ppermute(x, 'tensor', [(d, d ^ bit) for d in range(devices)])  23.9 us
    ppermute x16, waiting for transfers between devices, swap(): return lax.ppermute(x, 'tensor', [(d, d ^ bit) for d in range(devices)])  11 us
    unnamed x49, local copies, waits for them, and re-layouts  9.2 us
    pallas_call x1, Pallas kernels, per_device(): pl.pallas_call(functools.partial(partial_kernel, devices, requests, token...  3.86 us
    pallas_call x1, Pallas kernels, per_device(): pl.pallas_call(functools.partial(join_kernel, devices, requests, tokens),...  2.01 us
    pallas_call x1, Pallas kernels, per_device(): pl.pallas_call(functools.partial(merge_kernel, devices, requests, tokens)...  2 us
    pallas_call x1, Pallas kernels, per_device(): pl.pallas_call(functools.partial(pack_kernel, requests), out_shape=jax.Sh...  1.47 us
  transfers between devices with their start and end apart: 16, of which 6 were waited for; matrix products, arithmetic and copies ran while one was open for 3% of the time, Pallas kernels for 1%

profile of v2, /device:TPU:0, one launch (start us, length us, event | category | flops | bytes accessed | tf_op | source)
XLA Modules:
  0.0 55.2 jit_solution(13419258659818547515)
XLA Ops:
  0.0 1.5 %pack.1.packed_ref = bf16[16,8,128]{2,1,0:T(8,128)(2,1)} custom-call(bf16[2,4,1024]{2,1,0:T(4,128)(2,1)} %query_ref.1, bf16[2,4,1024]{2,1,0:T(4,128)(2,1)} %hidden_ref.1), custom_call_target="tpu_custom_call" | custom-call | flops 10000000000 | tf_op jit(solution)/shard_map/pack/pallas_call | solution.py:311
  1.5 3.0 %collective-permute-start = (bf16[16,8,128]{2,1,0:T(8,128)(2,1)}, bf16[16,8,128]{2,1,0:T(8,128)(2,1)S(1)}, u32[]{:S(2)}, u32[]{:S(2)}) collective-permute-start(bf16[16,8,128]{2,1,0:T(8,128)(2,1)} %pack.1.packed_ref), channel_id=1, source_target_pairs={{0,2},{1,3},{2,0},{3,1},{4,6},{5,7},{6,4},{7,5},{8,10},{9,11},{10,... | collective-permute-start | bytes 98312 | tf_op jit(solution)/shard_map/ppermute | solution.py:285
  4.5 1.6 %collective-permute-start.1 = (bf16[16,8,128]{2,1,0:T(8,128)(2,1)}, bf16[16,8,128]{2,1,0:T(8,128)(2,1)S(1)}, u32[]{:S(2)}, u32[]{:S(2)}) collective-permute-start(bf16[16,8,128]{2,1,0:T(8,128)(2,1)} %pack.1.packed_ref), channel_id=1, source_target_pairs={{0,4},{1,5},{2,6},{3,7},{4,0},{5,1},{6,2},{7,3},{8,12},{9,13},{10,... | collective-permute-start | bytes 98312 | tf_op jit(solution)/shard_map/ppermute | solution.py:285
  6.1 3.0 %collective-permute-start.3 = (bf16[16,8,128]{2,1,0:T(8,128)(2,1)}, bf16[16,8,128]{2,1,0:T(8,128)(2,1)S(1)}, u32[]{:S(2)}, u32[]{:S(2)}) collective-permute-start(bf16[16,8,128]{2,1,0:T(8,128)(2,1)} %pack.1.packed_ref), channel_id=1, source_target_pairs={{0,8},{1,9},{2,10},{3,11},{4,12},{5,13},{6,14},{7,15},{8,0},{9,1},... | collective-permute-start | bytes 98312 | tf_op jit(solution)/shard_map/ppermute | solution.py:285
  9.1 1.3 %collective-permute-start.4 = (bf16[16,8,128]{2,1,0:T(8,128)(2,1)}, bf16[16,8,128]{2,1,0:T(8,128)(2,1)S(1)}, u32[]{:S(2)}, u32[]{:S(2)}) collective-permute-start(bf16[16,8,128]{2,1,0:T(8,128)(2,1)} %pack.1.packed_ref), channel_id=1, source_target_pairs={{0,10},{1,11},{2,8},{3,9},{4,14},{5,15},{6,12},{7,13},{8,2},{9,3},... | collective-permute-start | bytes 98312 | tf_op jit(solution)/shard_map/ppermute | solution.py:285
  10.4 0.8 %bitcast_dynamic-update-slice_fusion.7 = bf16[8,16,8,128]{3,2,1,0:T(8,128)(2,1)S(1)} fusion(bf16[16,8,128]{2,1,0:T(8,128)(2,1)} %pack.1.packed_ref), kind=kLoop, calls=%fused_computation.7 | loop fusion | bytes 65536
  11.2 2.2 %copy-done.1 = bf16[1024,2048]{1,0:T(8,128)(2,1)S(1)} copy-done((bf16[1024,2048]{1,0:T(8,128)(2,1)S(1)}, bf16[1024,2048]{1,0:T(8,128)(2,1)}, u32[]{:S(2)}) %copy-start.1) | copy-done | bytes 4194328
  13.4 0.8 %copy-done.5 = bf16[16,8,128]{2,1,0:T(8,128)(2,1)S(1)} copy-done((bf16[16,8,128]{2,1,0:T(8,128)(2,1)S(1)}, bf16[16,8,128]{2,1,0:T(8,128)(2,1)}, u32[]{:S(2)}) %copy-start.5) | copy-done | bytes 32792
  14.1 0.6 %base.1.refs_7_ = f32[8,2048]{1,0:T(8,128)S(1)} custom-call(bf16[16,8,128]{2,1,0:T(8,128)(2,1)S(1)} %copy-done.5, bf16[1024,2048]{1,0:T(8,128)(2,1)S(1)} %copy-done.1), custom_call_target="tpu_custom_call" | custom-call | flops 33554432 | bytes 4194304 | tf_op jit(solution)/shard_map/base/pallas_call | solution.py:322
  14.8 3.6 %collective-permute-start.5 = (bf16[16,8,128]{2,1,0:T(8,128)(2,1)S(1)}, bf16[16,8,128]{2,1,0:T(8,128)(2,1)S(1)}, u32[]{:S(2)}, u32[]{:S(2)}) collective-permute-start(bf16[16,8,128]{2,1,0:T(8,128)(2,1)S(1)} %copy-done.5), channel_id=1, source_target_pairs={{0,12},{1,13},{2,14},{3,15},{4,8},{5,9},{6,10},{7,11},{8,4},{9,5},... | collective-permute-start | bytes 98312 | tf_op jit(solution)/shard_map/ppermute | solution.py:285
  18.6 1.9 %collective-permute-done.5 = bf16[16,8,128]{2,1,0:T(8,128)(2,1)S(1)} collective-permute-done((bf16[16,8,128]{2,1,0:T(8,128)(2,1)S(1)}, bf16[16,8,128]{2,1,0:T(8,128)(2,1)S(1)}, u32[]{:S(2)}, u32[]{:S(2)}) %collective-permute-start.5) | collective-permute-done | bytes 32800 | tf_op jit(solution)/shard_map/ppermute | solution.py:285
  20.5 4.6 %collective-permute-done.6 = bf16[16,8,128]{2,1,0:T(8,128)(2,1)S(1)} collective-permute-done((bf16[16,8,128]{2,1,0:T(8,128)(2,1)S(1)}, bf16[16,8,128]{2,1,0:T(8,128)(2,1)S(1)}, u32[]{:S(2)}, u32[]{:S(2)}) %collective-permute-start.6) | collective-permute-done | bytes 32800 | tf_op jit(solution)/shard_map/ppermute | solution.py:285
  25.1 1.5 %collective-permute-done.7.refs_6_ = bf16[8,16,8,128]{3,2,1,0:T(8,128)(2,1)S(1)} collective-permute-done((bf16[8,16,8,128]{3,2,1,0:T(8,128)(2,1)S(1)}, bf16[8,16,8,128]{3,2,1,0:T(8,128)(2,1)S(1)}, u32[]{:S(2)}, u32[]{:S(2)}) %collective-permute-start.7) | collective-permute-done | bytes 262176 | tf_op jit(solution)/shard_map/ppermute | solution.py:285
  26.7 2.2 %copy-done = bf16[1,16384,128]{2,1,0:T(8,128)(2,1)S(1)} copy-done((bf16[1,16384,128]{2,1,0:T(8,128)(2,1)S(1)}, bf16[1,16384,128]{2,1,0:T(8,128)(2,1)}, u32[]{:S(2)}) %copy-start) | copy-done | bytes 4194328
  28.9 3.9 %partial_states.1 = (bf16[720,128]{1,0:T(8,128)(2,1)S(1)}, f32[512,128]{1,0:T(8,128)S(1)}, f32[16,128]{1,0:T(8,128)S(1)}, f32[2,8,8,128]{3,2,1,0:T(8,128)S(1)}) custom-call(s32[1]{0:T(128)} %bitcast.refs_0_, s32[2]{0:T(128)S(1)} %copy-done.9, s32[16]{0:T(128)S(1)} %copy-done.10, s32[16]{0:T(128)S(1)} %copy-done.11, s32[2]{0:T(128)S(1)} %copy-done.12, ...), custom_call_target="tpu_custom_call" | custom-call | tf_op jit(solution)/shard_map/partial_states/pallas_call | solution.py:337
  32.7 0.7 %copy-done.6 = f32[512,128]{1,0:T(8,128)} copy-done((f32[512,128]{1,0:T(8,128)}, f32[512,128]{1,0:T(8,128)S(1)}, u32[]{:S(2)}) %copy-start.6) | copy-done | bytes 262168
  33.4 0.6 %copy-done.7 = f32[2,8,8,128]{3,2,1,0:T(8,128)} copy-done((f32[2,8,8,128]{3,2,1,0:T(8,128)}, f32[2,8,8,128]{3,2,1,0:T(8,128)S(1)}, u32[]{:S(2)}) %copy-start.7) | copy-done | bytes 65560
  34.1 0.6 %copy-done.8 = f32[16,128]{1,0:T(8,128)} copy-done((f32[16,128]{1,0:T(8,128)}, f32[16,128]{1,0:T(8,128)S(1)}, u32[]{:S(2)}) %copy-start.8) | copy-done | bytes 8216
  34.7 0.1 collective-permute-start.8
  35.0 1.1 %collective-permute-done.8.got_ref = bf16[720,128]{1,0:T(8,128)(2,1)S(1)} collective-permute-done((bf16[720,128]{1,0:T(8,128)(2,1)S(1)}, bf16[720,128]{1,0:T(8,128)(2,1)S(1)}, u32[]{:S(2)}, u32[]{:S(2)}) %collective-permute-start.8) | collective-permute-done | bytes 184352 | tf_op jit(solution)/shard_map/ppermute | solution.py:285
  36.1 0.7 %copy-done.13 = bf16[720,128]{1,0:T(8,128)(2,1)} copy-done((bf16[720,128]{1,0:T(8,128)(2,1)}, bf16[720,128]{1,0:T(8,128)(2,1)S(1)}, u32[]{:S(2)}) %copy-start.13) | copy-done | bytes 184344
  36.8 2.0 %join.1 = (bf16[96,128]{1,0:T(8,128)(2,1)}, bf16[96,128]{1,0:T(8,128)(2,1)}, bf16[96,128]{1,0:T(8,128)(2,1)}, bf16[96,128]{1,0:T(8,128)(2,1)}, bf16[96,128]{1,0:...) custom-call(f32[512,128]{1,0:T(8,128)} %copy-done.6, ...), custom_call_target="tpu_custom_call" | custom-call | tf_op jit(solution)/shard_map/join/pallas_call | solution.py:366
  38.8 1.9 %collective-permute-start.11 = (bf16[96,128]{1,0:T(8,128)(2,1)}, bf16[96,128]{1,0:T(8,128)(2,1)S(1)}, u32[]{:S(2)}, u32[]{:S(2)}) collective-permute-start(bf16[96,128]{1,0:T(8,128)(2,1)} %get-tuple-element.28), channel_id=1, source_target_pairs={{0,6},{1,7},{2,4},{3,5},{4,2},{5,3},{6,0},{7,1},{8,14},{9,15},{10,... | collective-permute-start | bytes 73736 | tf_op jit(solution)/shard_map/ppermute | solution.py:285
  40.9 3.9 %collective-permute-start.13 = (bf16[96,128]{1,0:T(8,128)(2,1)}, bf16[96,128]{1,0:T(8,128)(2,1)S(1)}, u32[]{:S(2)}, u32[]{:S(2)}) collective-permute-start(bf16[96,128]{1,0:T(8,128)(2,1)} %get-tuple-element.30), channel_id=1, source_target_pairs={{0,10},{1,11},{2,8},{3,9},{4,14},{5,15},{6,12},{7,13},{8,2},{9,3},... | collective-permute-start | bytes 73736 | tf_op jit(solution)/shard_map/ppermute | solution.py:285
  44.8 0.2 collective-permute-start.14
  45.0 3.5 %collective-permute-start.15 = (bf16[96,128]{1,0:T(8,128)(2,1)}, bf16[96,128]{1,0:T(8,128)(2,1)S(1)}, u32[]{:S(2)}, u32[]{:S(2)}) collective-permute-start(bf16[96,128]{1,0:T(8,128)(2,1)} %get-tuple-element.32), channel_id=1, source_target_pairs={{0,14},{1,15},{2,12},{3,13},{4,10},{5,11},{6,8},{7,9},{8,6},{9,7},... | collective-permute-start | bytes 73736 | tf_op jit(solution)/shard_map/ppermute | solution.py:285
  48.6 1.5 %collective-permute-start.9 = (bf16[96,128]{1,0:T(8,128)(2,1)}, bf16[96,128]{1,0:T(8,128)(2,1)S(1)}, u32[]{:S(2)}, u32[]{:S(2)}) collective-permute-start(bf16[96,128]{1,0:T(8,128)(2,1)} %get-tuple-element.26), channel_id=1, source_target_pairs={{0,2},{1,3},{2,0},{3,1},{4,6},{5,7},{6,4},{7,5},{8,10},{9,11},{10,... | collective-permute-start | bytes 73736 | tf_op jit(solution)/shard_map/ppermute | solution.py:285
  50.1 0.7 %pad_maximum_fusion = (f32[8,128]{1,0:T(8,128)}, f32[8,128]{1,0:T(8,128)}) fusion(f32[8,64]{1,0:T(8,128)S(1)} %get-tuple-element.35, f32[8,64]{1,0:T(8,128)S(1)} %get-tuple-element.34, f32[8,64]{1,0:T(8,128)S(1)} %get-tuple-element.33), kind=kLoop, calls=%fused_computation.10 | loop fusion | flops 2048 | bytes 14336 | tf_op jit(solution)/shard_map/concatenate | solution.py:265
  50.8 1.0 %collective-permute-done.15.refs_7_ = bf16[96,128]{1,0:T(8,128)(2,1)S(1)} collective-permute-done((bf16[96,128]{1,0:T(8,128)(2,1)}, bf16[96,128]{1,0:T(8,128)(2,1)S(1)}, u32[]{:S(2)}, u32[]{:S(2)}) %collective-permute-start.15) | collective-permute-done | bytes 24608 | tf_op jit(solution)/shard_map/ppermute | solution.py:285
  51.8 0.8 %collective-permute-done.9.refs_1_ = bf16[96,128]{1,0:T(8,128)(2,1)S(1)} collective-permute-done((bf16[96,128]{1,0:T(8,128)(2,1)}, bf16[96,128]{1,0:T(8,128)(2,1)S(1)}, u32[]{:S(2)}, u32[]{:S(2)}) %collective-permute-start.9) | collective-permute-done | bytes 24608 | tf_op jit(solution)/shard_map/ppermute | solution.py:285
  52.7 0.6 %copy-done.20 = bf16[96,128]{1,0:T(8,128)(2,1)} copy-done((bf16[96,128]{1,0:T(8,128)(2,1)}, bf16[96,128]{1,0:T(8,128)(2,1)S(1)}, u32[]{:S(2)}) %copy-start.20) | copy-done | bytes 24600
  53.2 2.0 %merge_states.1 = bf16[2,4,1024]{2,1,0:T(4,128)(2,1)} custom-call(bf16[16,8,128]{2,1,0:T(8,128)(2,1)} %pack.1.packed_ref, f32[8,128]{1,0:T(8,128)} %get-tuple-element.36.cos_ref, f32[8,128]{1,0:T(8,128)} %get-tuple-element.37.sin_ref, bf16[96,128]{1,0:T(8,128)(2,1)} %get-tuple-element.25.refs_0_, bf16[96,128]{1,0:T(8,128)(2,1)} %copy-done.20, ...), custom_call_target="tpu_custom_call" | custom-call | tf_op jit(solution)/shard_map/merge_states/pallas_call | solution.py:375
  (60 shorter events, 0.6 us)
Async XLA Ops:
  0.0 26.6 %copy-start.2 = (bf16[1,128,2048]{2,1,0:T(8,128)(2,1)S(1)}, bf16[1,128,2048]{2,1,0:T(8,128)(2,1)}, u32[]{:S(2)}) copy-start(bf16[1,128,2048]{2,1,0:T(8,128)(2,1)} %param.15) | copy-start | bytes 1572868
  0.0 26.6 %copy-start.3 = (bf16[2,128,1024]{2,1,0:T(8,128)(2,1)S(1)}, bf16[2,128,1024]{2,1,0:T(8,128)(2,1)}, u32[]{:S(2)}) copy-start(bf16[2,128,1024]{2,1,0:T(8,128)(2,1)} %param.16) | copy-start | bytes 1572868
  0.0 26.6 %copy-start.4 = (bf16[2,128,1024]{2,1,0:T(8,128)(2,1)S(1)}, bf16[2,128,1024]{2,1,0:T(8,128)(2,1)}, u32[]{:S(2)}) copy-start(bf16[2,128,1024]{2,1,0:T(8,128)(2,1)} %param.17) | copy-start | bytes 1572868
  1.5 25.2 %copy-start.9 = (s32[2]{0:T(128)S(1)}, s32[2]{0:T(128)}, u32[]{:S(2)}) copy-start(s32[2]{0:T(128)} %refs_1_.1) | copy-start | bytes 28
  1.5 25.2 %copy-start.10 = (s32[16]{0:T(128)S(1)}, s32[16]{0:T(128)}, u32[]{:S(2)}) copy-start(s32[16]{0:T(128)} %refs_2_.1) | copy-start | bytes 196
  1.5 25.2 %copy-start.11 = (s32[16]{0:T(128)S(1)}, s32[16]{0:T(128)}, u32[]{:S(2)}) copy-start(s32[16]{0:T(128)} %refs_3_.1) | copy-start | bytes 196
  1.5 25.2 %copy-start.12 = (s32[2]{0:T(128)S(1)}, s32[2]{0:T(128)}, u32[]{:S(2)}) copy-start(s32[2]{0:T(128)} %refs_4_.1) | copy-start | bytes 28
  1.5 13.3 %collective-permute-start = (bf16[16,8,128]{2,1,0:T(8,128)(2,1)}, bf16[16,8,128]{2,1,0:T(8,128)(2,1)S(1)}, u32[]{:S(2)}, u32[]{:S(2)}) collective-permute-start(bf16[16,8,128]{2,1,0:T(8,128)(2,1)} %pack.1.packed_ref), channel_id=1, source_target_pairs={{0,2},{1,3},{2,0},{3,1},{4,6},{5,7},{6,4},{7,5},{8,10},{9,11},{10,... | collective-permute-start | bytes 98312 | tf_op jit(solution)/shard_map/ppermute | solution.py:285
  4.5 13.9 %collective-permute-start.1 = (bf16[16,8,128]{2,1,0:T(8,128)(2,1)}, bf16[16,8,128]{2,1,0:T(8,128)(2,1)S(1)}, u32[]{:S(2)}, u32[]{:S(2)}) collective-permute-start(bf16[16,8,128]{2,1,0:T(8,128)(2,1)} %pack.1.packed_ref), channel_id=1, source_target_pairs={{0,4},{1,5},{2,6},{3,7},{4,0},{5,1},{6,2},{7,3},{8,12},{9,13},{10,... | collective-permute-start | bytes 98312 | tf_op jit(solution)/shard_map/ppermute | solution.py:285
  6.1 12.4 %collective-permute-start.2 = (bf16[16,8,128]{2,1,0:T(8,128)(2,1)}, bf16[16,8,128]{2,1,0:T(8,128)(2,1)S(1)}, u32[]{:S(2)}, u32[]{:S(2)}) collective-permute-start(bf16[16,8,128]{2,1,0:T(8,128)(2,1)} %pack.1.packed_ref), channel_id=1, source_target_pairs={{0,6},{1,7},{2,4},{3,5},{4,2},{5,3},{6,0},{7,1},{8,14},{9,15},{10,... | collective-permute-start | bytes 98312 | tf_op jit(solution)/shard_map/ppermute | solution.py:285
  6.1 12.4 %collective-permute-start.3 = (bf16[16,8,128]{2,1,0:T(8,128)(2,1)}, bf16[16,8,128]{2,1,0:T(8,128)(2,1)S(1)}, u32[]{:S(2)}, u32[]{:S(2)}) collective-permute-start(bf16[16,8,128]{2,1,0:T(8,128)(2,1)} %pack.1.packed_ref), channel_id=1, source_target_pairs={{0,8},{1,9},{2,10},{3,11},{4,12},{5,13},{6,14},{7,15},{8,0},{9,1},... | collective-permute-start | bytes 98312 | tf_op jit(solution)/shard_map/ppermute | solution.py:285
  9.1 9.5 %collective-permute-start.4 = (bf16[16,8,128]{2,1,0:T(8,128)(2,1)}, bf16[16,8,128]{2,1,0:T(8,128)(2,1)S(1)}, u32[]{:S(2)}, u32[]{:S(2)}) collective-permute-start(bf16[16,8,128]{2,1,0:T(8,128)(2,1)} %pack.1.packed_ref), channel_id=1, source_target_pairs={{0,10},{1,11},{2,8},{3,9},{4,14},{5,15},{6,12},{7,13},{8,2},{9,3},... | collective-permute-start | bytes 98312 | tf_op jit(solution)/shard_map/ppermute | solution.py:285
  11.2 2.2 %copy-start.1 = (bf16[1024,2048]{1,0:T(8,128)(2,1)S(1)}, bf16[1024,2048]{1,0:T(8,128)(2,1)}, u32[]{:S(2)}) copy-start(bf16[1024,2048]{1,0:T(8,128)(2,1)} %weight_ref.1) | copy-start | bytes 12582916
  13.4 0.8 %copy-start.5 = (bf16[16,8,128]{2,1,0:T(8,128)(2,1)S(1)}, bf16[16,8,128]{2,1,0:T(8,128)(2,1)}, u32[]{:S(2)}) copy-start(bf16[16,8,128]{2,1,0:T(8,128)(2,1)} %pack.1.packed_ref) | copy-start | bytes 98308
  14.8 5.7 %collective-permute-start.5 = (bf16[16,8,128]{2,1,0:T(8,128)(2,1)S(1)}, bf16[16,8,128]{2,1,0:T(8,128)(2,1)S(1)}, u32[]{:S(2)}, u32[]{:S(2)}) collective-permute-start(bf16[16,8,128]{2,1,0:T(8,128)(2,1)S(1)} %copy-done.5), channel_id=1, source_target_pairs={{0,12},{1,13},{2,14},{3,15},{4,8},{5,9},{6,10},{7,11},{8,4},{9,5},... | collective-permute-start | bytes 98312 | tf_op jit(solution)/shard_map/ppermute | solution.py:285
  18.4 6.7 %collective-permute-start.6 = (bf16[16,8,128]{2,1,0:T(8,128)(2,1)S(1)}, bf16[16,8,128]{2,1,0:T(8,128)(2,1)S(1)}, u32[]{:S(2)}, u32[]{:S(2)}) collective-permute-start(bf16[16,8,128]{2,1,0:T(8,128)(2,1)S(1)} %copy-done.5), channel_id=1, source_target_pairs={{0,14},{1,15},{2,12},{3,13},{4,10},{5,11},{6,8},{7,9},{8,6},{9,7},... | collective-permute-start | bytes 98312 | tf_op jit(solution)/shard_map/ppermute | solution.py:285
  25.1 1.5 %collective-permute-start.7 = (bf16[8,16,8,128]{3,2,1,0:T(8,128)(2,1)S(1)}, bf16[8,16,8,128]{3,2,1,0:T(8,128)(2,1)S(1)}, u32[]{:S(2)}, u32[]{:S(2)}) collective-permute-start(bf16[8,16,8,128]{3,2,1,0:T(8,128)(2,1)S(1)} %bitcast_dynamic-update-slice_fusion.refs_5_), channel_id=1, source_target_pairs={{0,1},{1,0},{2,3},{3,2},{4,5},{5,4},{6,7},{7,6},{8,9},{9,8},{10,11... | collective-permute-start | bytes 786440 | tf_op jit(solution)/shard_map/ppermute | solution.py:285
  26.7 2.2 %copy-start = (bf16[1,16384,128]{2,1,0:T(8,128)(2,1)S(1)}, bf16[1,16384,128]{2,1,0:T(8,128)(2,1)}, u32[]{:S(2)}) copy-start(bf16[1,16384,128]{2,1,0:T(8,128)(2,1)} %param.14) | copy-start | bytes 12582916
  34.7 1.4 %collective-permute-start.8 = (bf16[720,128]{1,0:T(8,128)(2,1)S(1)}, bf16[720,128]{1,0:T(8,128)(2,1)S(1)}, u32[]{:S(2)}, u32[]{:S(2)}) collective-permute-start(bf16[720,128]{1,0:T(8,128)(2,1)S(1)} %get-tuple-element.24), channel_id=1, source_target_pairs={{0,1},{1,0},{2,3},{3,2},{4,5},{5,4},{6,7},{7,6},{8,9},{9,8},{10,11... | collective-permute-start | bytes 552968 | tf_op jit(solution)/shard_map/ppermute | solution.py:285
  38.8 6.3 %collective-permute-start.10 = (bf16[96,128]{1,0:T(8,128)(2,1)}, bf16[96,128]{1,0:T(8,128)(2,1)S(1)}, u32[]{:S(2)}, u32[]{:S(2)}) collective-permute-start(bf16[96,128]{1,0:T(8,128)(2,1)} %get-tuple-element.27), channel_id=1, source_target_pairs={{0,4},{1,5},{2,6},{3,7},{4,0},{5,1},{6,2},{7,3},{8,12},{9,13},{10,... | collective-permute-start | bytes 73736 | tf_op jit(solution)/shard_map/ppermute | solution.py:285
  38.8 9.8 %collective-permute-start.11 = (bf16[96,128]{1,0:T(8,128)(2,1)}, bf16[96,128]{1,0:T(8,128)(2,1)S(1)}, u32[]{:S(2)}, u32[]{:S(2)}) collective-permute-start(bf16[96,128]{1,0:T(8,128)(2,1)} %get-tuple-element.28), channel_id=1, source_target_pairs={{0,6},{1,7},{2,4},{3,5},{4,2},{5,3},{6,0},{7,1},{8,14},{9,15},{10,... | collective-permute-start | bytes 73736 | tf_op jit(solution)/shard_map/ppermute | solution.py:285
  40.9 9.9 %collective-permute-start.12 = (bf16[96,128]{1,0:T(8,128)(2,1)}, bf16[96,128]{1,0:T(8,128)(2,1)S(1)}, u32[]{:S(2)}, u32[]{:S(2)}) collective-permute-start(bf16[96,128]{1,0:T(8,128)(2,1)} %get-tuple-element.29), channel_id=1, source_target_pairs={{0,8},{1,9},{2,10},{3,11},{4,12},{5,13},{6,14},{7,15},{8,0},{9,1},... | collective-permute-start | bytes 73736 | tf_op jit(solution)/shard_map/ppermute | solution.py:285
  40.9 9.8 %collective-permute-start.13 = (bf16[96,128]{1,0:T(8,128)(2,1)}, bf16[96,128]{1,0:T(8,128)(2,1)S(1)}, u32[]{:S(2)}, u32[]{:S(2)}) collective-permute-start(bf16[96,128]{1,0:T(8,128)(2,1)} %get-tuple-element.30), channel_id=1, source_target_pairs={{0,10},{1,11},{2,8},{3,9},{4,14},{5,15},{6,12},{7,13},{8,2},{9,3},... | collective-permute-start | bytes 73736 | tf_op jit(solution)/shard_map/ppermute | solution.py:285
  44.8 6.0 %collective-permute-start.14 = (bf16[96,128]{1,0:T(8,128)(2,1)}, bf16[96,128]{1,0:T(8,128)(2,1)S(1)}, u32[]{:S(2)}, u32[]{:S(2)}) collective-permute-start(bf16[96,128]{1,0:T(8,128)(2,1)} %get-tuple-element.31), channel_id=1, source_target_pairs={{0,12},{1,13},{2,14},{3,15},{4,8},{5,9},{6,10},{7,11},{8,4},{9,5},... | collective-permute-start | bytes 73736 | tf_op jit(solution)/shard_map/ppermute | solution.py:285
  45.0 7.6 %copy-start.14 = (bf16[96,128]{1,0:T(8,128)(2,1)}, bf16[96,128]{1,0:T(8,128)(2,1)S(1)}, u32[]{:S(2)}) copy-start(bf16[96,128]{1,0:T(8,128)(2,1)S(1)} %collective-permute-done.10.refs_2_) | copy-start | bytes 73732
  45.0 6.7 %collective-permute-start.15 = (bf16[96,128]{1,0:T(8,128)(2,1)}, bf16[96,128]{1,0:T(8,128)(2,1)S(1)}, u32[]{:S(2)}, u32[]{:S(2)}) collective-permute-start(bf16[96,128]{1,0:T(8,128)(2,1)} %get-tuple-element.32), channel_id=1, source_target_pairs={{0,14},{1,15},{2,12},{3,13},{4,10},{5,11},{6,8},{7,9},{8,6},{9,7},... | collective-permute-start | bytes 73736 | tf_op jit(solution)/shard_map/ppermute | solution.py:285
  48.6 4.0 %copy-start.15 = (bf16[96,128]{1,0:T(8,128)(2,1)}, bf16[96,128]{1,0:T(8,128)(2,1)S(1)}, u32[]{:S(2)}) copy-start(bf16[96,128]{1,0:T(8,128)(2,1)S(1)} %collective-permute-done.11.refs_3_) | copy-start | bytes 73732
  48.6 4.0 %collective-permute-start.9 = (bf16[96,128]{1,0:T(8,128)(2,1)}, bf16[96,128]{1,0:T(8,128)(2,1)S(1)}, u32[]{:S(2)}, u32[]{:S(2)}) collective-permute-start(bf16[96,128]{1,0:T(8,128)(2,1)} %get-tuple-element.26), channel_id=1, source_target_pairs={{0,2},{1,3},{2,0},{3,1},{4,6},{5,7},{6,4},{7,5},{8,10},{9,11},{10,... | collective-permute-start | bytes 73736 | tf_op jit(solution)/shard_map/ppermute | solution.py:285
  50.8 1.9 %copy-start.16 = (bf16[96,128]{1,0:T(8,128)(2,1)}, bf16[96,128]{1,0:T(8,128)(2,1)S(1)}, u32[]{:S(2)}) copy-start(bf16[96,128]{1,0:T(8,128)(2,1)S(1)} %collective-permute-done.12.refs_4_) | copy-start | bytes 73732
  50.8 1.8 %copy-start.17 = (bf16[96,128]{1,0:T(8,128)(2,1)}, bf16[96,128]{1,0:T(8,128)(2,1)S(1)}, u32[]{:S(2)}) copy-start(bf16[96,128]{1,0:T(8,128)(2,1)S(1)} %collective-permute-done.13.refs_5_) | copy-start | bytes 73732
  50.8 1.8 %copy-start.18 = (bf16[96,128]{1,0:T(8,128)(2,1)}, bf16[96,128]{1,0:T(8,128)(2,1)S(1)}, u32[]{:S(2)}) copy-start(bf16[96,128]{1,0:T(8,128)(2,1)S(1)} %collective-permute-done.14.refs_6_) | copy-start | bytes 73732
  51.8 0.9 %copy-start.19 = (bf16[96,128]{1,0:T(8,128)(2,1)}, bf16[96,128]{1,0:T(8,128)(2,1)S(1)}, u32[]{:S(2)}) copy-start(bf16[96,128]{1,0:T(8,128)(2,1)S(1)} %collective-permute-done.15.refs_7_) | copy-start | bytes 73732
  (5 other events, 3.2 us)

commit v3 on v2

--- a/solution.py
+++ b/solution.py
@@ -33,20 +33,21 @@
         rows = jnp.concatenate([ref[b].astype(jnp.float32) for b in range(requests)], axis=0)
         for c in range(rows.shape[1] // HEAD_WIDTH):
             tile = rows[:, c * HEAD_WIDTH : (c + 1) * HEAD_WIDTH]
-            out_ref[at] = tile.astype(jnp.bfloat16)
+            for copy in range(out_ref.shape[0]):
+                out_ref[copy, at] = tile.astype(jnp.bfloat16)
             at += 1
 
 
 def base_kernel(heads, packed_ref, weight_ref, base_ref):
     chunks = weight_ref.shape[0] // HEAD_WIDTH
-    hidden = jnp.concatenate([packed_ref[heads + c] for c in range(chunks)], axis=1)
+    hidden = jnp.concatenate([packed_ref[0, heads + c] for c in range(chunks)], axis=1)
     base_ref[...] = dot(hidden, weight_ref[...], ((1,), (0,)))
 
 
 def partial_kernel(devices, requests, tokens, *refs):
     (index_ref, adapter_ref, rank_ref, pool_ref, length_ref) = refs[:5]
     (lane_ref, other_ref, base_ref, down_ref, up_ref, key_ref, value_ref) = refs[5:12]
-    (send_ref, mix_ref, stat_ref, proj_ref, all_ref) = refs[12:]
+    (send_ref, mix_ref, stat_ref, proj_ref) = refs[12:]
     here = index_ref[0]
     rows = requests * tokens
     heads = QUERY_HEADS // devices
@@ -61,7 +62,7 @@
     for side, ref in enumerate((lane_ref, other_ref)):
         for m in range(lanes):
             hidden = jnp.concatenate([ref[m, heads + c] for c in range(chunks)], axis=1)
-            source = here ^ (2 * m + side)
+            source = 2 * m + (here % 2 ^ side)
             factor = down_ref[pl.ds(pl.multiple_of(source * depth, depth), depth), :]
             lowered += dot(hidden, factor, ((1,), (0,)))
     row_request = lax.broadcasted_iota(jnp.int32, (rows, 1), 0) // tokens
@@ -74,16 +75,14 @@
     column = lax.broadcasted_iota(jnp.int32, lowered.shape, 1)
     lowered = jnp.where(column < ranks, lowered, 0.0).astype(jnp.bfloat16)
     lifted = dot(lowered, up_ref[...], ((1,), (0,)))
-    all_ref[...] = base_ref[...] + jnp.where(owners == here, lifted, 0.0)
+    projected = base_ref[...] + jnp.where(owners == here, lifted, 0.0)
 
     split = KEY_HEADS * HEAD_WIDTH
     mix_total = KEY_HEADS * 64
     for j in range(KEY_HEADS):
-        at = ((here // per_key_head) ^ j) * HEAD_WIDTH
-        keys = all_ref[:, pl.ds(pl.multiple_of(at, HEAD_WIDTH), HEAD_WIDTH)]
-        values = all_ref[:, pl.ds(pl.multiple_of(split + at, HEAD_WIDTH), HEAD_WIDTH)]
-        proj_ref[0, j] = keys
-        proj_ref[1, j] = values
+        at = j * HEAD_WIDTH
+        proj_ref[0, j] = projected[:, at : at + HEAD_WIDTH]
+        proj_ref[1, j] = projected[:, split + at : split + at + HEAD_WIDTH]
     keys = proj_ref[0].reshape(KEY_HEADS * rows, HEAD_WIDTH)
     high = keys.astype(jnp.bfloat16)
     step = KEY_HEADS * rows
@@ -110,16 +109,13 @@
     for side, ref in enumerate((other_ref, lane_ref)):
         stats = jnp.zeros((STAT_ROWS, HEAD_WIDTH), jnp.float32)
         for p in range(PAIRS):
-            spots = [
-                pl.multiple_of(((here // per_key_head) ^ j) * HEAD_WIDTH, HEAD_WIDTH)
-                for j in (2 * p, 2 * p + 1)
-            ]
+            spots = [2 * p * HEAD_WIDTH, (2 * p + 1) * HEAD_WIDTH]
             query = jnp.concatenate(
                 [ref[2 * p * per_lane + t, h] for t in range(2 * per_lane) for h in range(heads)],
                 axis=0,
             )
             scores = [
-                dot(key_ref[:, pl.ds(at, HEAD_WIDTH)], query, ((1,), (1,))) for at in spots
+                dot(key_ref[:, at : at + HEAD_WIDTH], query, ((1,), (1,))) for at in spots
             ]
             scores = jnp.where(first, scores[0], scores[1]) * SCALE
             peak = jnp.max(jnp.where(allowed, scores, NEG_FILL), axis=0, keepdims=True)
@@ -128,7 +124,7 @@
             total = jnp.sum(weights, axis=0, keepdims=True)
             weights = jnp.transpose(weights.astype(jnp.bfloat16))
             mix = [
-                dot(weights[64 * i : 64 * i + 64], value_ref[:, pl.ds(at, HEAD_WIDTH)], ((1,), (0,)))
+                dot(weights[64 * i : 64 * i + 64], value_ref[:, at : at + HEAD_WIDTH], ((1,), (0,)))
                 for i, at in enumerate(spots)
             ]
             at = p * 128
@@ -150,7 +146,7 @@
             stat_ref[...] = stats
 
 
-def join_kernel(devices, requests, tokens, mix_ref, stat_ref, proj_ref, got_ref, *out_refs):
+def join_kernel(devices, requests, tokens, mix_ref, stat_ref, proj_ref, got_ref, packet_ref):
     rows = requests * tokens
     heads = QUERY_HEADS // devices
     mix_rows = heads * rows
@@ -193,7 +189,7 @@
         )
         for t in range(2 * per_lane):
             j = 2 * p + t // per_lane
-            out_ref = out_refs[2 * p * per_lane + t]
+            out_ref = packet_ref.at[2 * p * per_lane + t]
             out_ref[:mix_rows] = mix[t * mix_rows : (t + 1) * mix_rows].astype(jnp.bfloat16)
             shifted = stats if t == 0 else pltpu.roll(stats, HEAD_WIDTH - t * mix_rows, 1)
             own = slice(j * rows, (j + 1) * rows)
@@ -202,8 +198,8 @@
             ).astype(jnp.bfloat16)
 
 
-def merge_kernel(devices, requests, tokens, packed_ref, cos_ref, sin_ref, *refs):
-    got_refs, out_ref = refs[:-1], refs[-1]
+def merge_kernel(devices, requests, tokens, packed_ref, cos_ref, sin_ref, got_ref, out_ref):
+    got_refs = [got_ref.at[s] for s in range(got_ref.shape[0])]
     rows = requests * tokens
     heads = QUERY_HEADS // devices
     mix_rows = heads * rows
@@ -214,7 +210,7 @@
     values = sums[2 * rows :].astype(jnp.bfloat16)
     turned = pltpu.roll(keys, HEAD_WIDTH // 2, 1)
     keys = (keys * cos_ref[...] + turned * sin_ref[...]).astype(jnp.bfloat16)
-    query = jnp.concatenate([packed_ref[h] for h in range(heads)], axis=0)
+    query = jnp.concatenate([packed_ref[0, h] for h in range(heads)], axis=0)
     if mix_rows < 128:
         query = jnp.concatenate(
             [query, jnp.zeros((128 - mix_rows, HEAD_WIDTH), jnp.bfloat16)], axis=0
@@ -308,16 +304,21 @@
     tiles = heads + chunks
     mix_rows = heads * rows
 
+    lane_groups = [list(range(core, devices, 2)) for core in range(2)]
+
+    def exchange(x):
+        return lax.all_to_all(x, "tensor", 0, 0, axis_index_groups=lane_groups, tiled=True)
+
     packed = pl.pallas_call(
         functools.partial(pack_kernel, requests),
-        out_shape=jax.ShapeDtypeStruct((tiles, rows, HEAD_WIDTH), jnp.bfloat16),
+        out_shape=jax.ShapeDtypeStruct((lanes, tiles, rows, HEAD_WIDTH), jnp.bfloat16),
         in_specs=[vmem()] * 2,
         out_specs=vmem(),
+        compiler_params=pltpu.CompilerParams(vmem_limit_bytes=8 * MIB),
         cost_estimate=cost(10**10, 0),
         name="pack",
     )(queries, hidden)
-    lane = [packed] + [swap(packed, devices, 2 * m) for m in range(1, lanes)]
-    lane = jnp.concatenate([x[None] for x in lane], axis=0)
+    lane = exchange(packed)
 
     base = pl.pallas_call(
         functools.partial(base_kernel, heads),
@@ -344,8 +345,7 @@
         ),
         in_specs=[smem()] * 5 + [vmem()] * 7,
         out_specs=(vmem(),) * 4,
-        scratch_shapes=[pltpu.VMEM(base.shape, jnp.float32)],
-        compiler_params=pltpu.CompilerParams(vmem_limit_bytes=20 * MIB),
+        compiler_params=pltpu.CompilerParams(vmem_limit_bytes=16 * MIB),
         name="partial_states",
     )(
         here.reshape(1).astype(jnp.int32),
@@ -362,23 +362,24 @@
         cached_value_rows.reshape(flat, -1),
     )
     got = swap(send, devices, 1)
-    packet = jax.ShapeDtypeStruct((mix_rows + 4 * rows, HEAD_WIDTH), jnp.bfloat16)
     packets = pl.pallas_call(
         functools.partial(join_kernel, devices, requests, tokens),
-        out_shape=(packet,) * lanes,
+        out_shape=jax.ShapeDtypeStruct((lanes, mix_rows + 4 * rows, HEAD_WIDTH), jnp.bfloat16),
         in_specs=[vmem()] * 4,
-        out_specs=(vmem(),) * lanes,
+        out_specs=vmem(),
+        compiler_params=pltpu.CompilerParams(vmem_limit_bytes=8 * MIB),
         name="join",
     )(mix, stats, proj, got)
-    packets = [packets[0]] + [swap(packets[m], devices, 2 * m) for m in range(1, lanes)]
+    packets = exchange(packets)
     cosine, sine = rotation(lengths, tokens)
     return pl.pallas_call(
         functools.partial(merge_kernel, devices, requests, tokens),
         out_shape=jax.ShapeDtypeStruct((requests, tokens, heads * HEAD_WIDTH), jnp.bfloat16),
-        in_specs=[vmem()] * (3 + lanes),
+        in_specs=[vmem()] * 4,
         out_specs=vmem(),
+        compiler_params=pltpu.CompilerParams(vmem_limit_bytes=8 * MIB),
         name="merge_states",
-    )(packed, cosine, sine, *packets)
+    )(packed, cosine, sine, packets)
 
 
 def solution(mesh):

time: 55.7 us -> 43.1 us (0.77)
  starting transfers between devices: 23.9 us -> 11.2 us
  waiting for transfers between devices: 11 us -> 15.8 us
  local copies, waits for them, and re-layouts: 9.3 us -> 5.91 us
  Pallas kernels: 9.98 us -> 9.3 us
  other arithmetic: 0.85 us -> 0.27 us
    ppermute x16 -> x2, starting transfers between devices: 23.9 us -> 0.2 us  [swap(): return lax.ppermute(x, 'tensor', [(d, d ^ bit) for d in range(devices)])]
    all_to_all x0 -> x2, waiting for transfers between devices: none -> 13 us  [exchange(): lax.all_to_all(x, 'tensor', 0, 0, axis_index_groups=lane_groups, tiled=True)]
    all_to_all x0 -> x2, starting transfers between devices: none -> 11 us  [exchange(): lax.all_to_all(x, 'tensor', 0, 0, axis_index_groups=lane_groups, tiled=True)]
    ppermute x16 -> x2, waiting for transfers between devices: 11 us -> 2.75 us  [swap(): return lax.ppermute(x, 'tensor', [(d, d ^ bit) for d in range(devices)])]
    unnamed x49 -> x22, local copies, waits for them, and re-layouts: 9.2 us -> 5.83 us
    pallas_call x1, Pallas kernels: 0.64 us -> 1.68 us  [per_device(): pl.pallas_call(functools.partial(base_kernel, heads), out_shape=jax.Shape...]
    pallas_call x1, Pallas kernels: 2.01 us -> 1.02 us  [per_device(): pl.pallas_call(functools.partial(join_kernel, devices, requests, tokens),...]
    pallas_call x1, Pallas kernels: 1.47 us -> 0.73 us  [per_device(): pl.pallas_call(functools.partial(pack_kernel, requests), out_shape=jax.Sh...]
  transfers between devices with their start and end apart: 16 -> 4, of which waited for: 6 -> 4; matrix products, arithmetic and copies ran while one was open for 3% -> 1% of each run, Pallas kernels for 1% -> 4%
where the time goes in v3:
time: 43.1 us; the launch traced here: 42.5 us
  waiting for transfers between devices  15.8 us (37%)
  starting transfers between devices  11.2 us (26%)
  Pallas kernels  9.3 us (22%)
  local copies, waits for them, and re-layouts  5.91 us (14%)
    all_to_all x2, waiting for transfers between devices, exchange(): lax.all_to_all(x, 'tensor', 0, 0, axis_index_groups=lane_groups, tiled=True)  13 us
    all_to_all x2, starting transfers between devices, exchange(): lax.all_to_all(x, 'tensor', 0, 0, axis_index_groups=lane_groups, tiled=True)  11 us
    unnamed x22, local copies, waits for them, and re-layouts  5.83 us
    pallas_call x1, Pallas kernels, per_device(): pl.pallas_call(functools.partial(partial_kernel, devices, requests, token...  3.81 us
    ppermute x2, waiting for transfers between devices, swap(): return lax.ppermute(x, 'tensor', [(d, d ^ bit) for d in range(devices)])  2.75 us
    pallas_call x1, Pallas kernels, per_device(): pl.pallas_call(functools.partial(merge_kernel, devices, requests, tokens)...  2.07 us
    pallas_call x1, Pallas kernels, per_device(): pl.pallas_call(functools.partial(base_kernel, heads), out_shape=jax.Shape...  1.68 us
    pallas_call x1, Pallas kernels, per_device(): pl.pallas_call(functools.partial(join_kernel, devices, requests, tokens),...  1.02 us
  transfers between devices with their start and end apart: 4, of which 4 were waited for; matrix products, arithmetic and copies ran while one was open for 1% of the time, Pallas kernels for 4%

profile of v3, /device:TPU:0, one launch (start us, length us, event | category | flops | bytes accessed | tf_op | source)
XLA Modules:
  0.0 42.5 jit_solution(9711251775975658177)
XLA Ops:
  0.0 0.0 copy-start.9
  0.0 0.7 %copy-done.9 = bf16[2,4,1024]{2,1,0:T(4,128)(2,1)S(1)} copy-done((bf16[2,4,1024]{2,1,0:T(4,128)(2,1)S(1)}, bf16[2,4,1024]{2,1,0:T(4,128)(2,1)}, u32[]{:S(2)}) %copy-start.9) | copy-done | bytes 16408
  0.7 0.7 %copy-done.10 = bf16[2,4,1024]{2,1,0:T(4,128)(2,1)S(1)} copy-done((bf16[2,4,1024]{2,1,0:T(4,128)(2,1)S(1)}, bf16[2,4,1024]{2,1,0:T(4,128)(2,1)}, u32[]{:S(2)}) %copy-start.10) | copy-done | bytes 16408
  1.4 0.7 %pack.1.packed_ref = bf16[8,16,8,128]{3,2,1,0:T(8,128)(2,1)} custom-call(bf16[2,4,1024]{2,1,0:T(4,128)(2,1)S(1)} %copy-done.9, bf16[2,4,1024]{2,1,0:T(4,128)(2,1)S(1)} %copy-done.10), custom_call_target="tpu_custom_call" | custom-call | flops 10000000000 | tf_op jit(solution)/shard_map/pack/pallas_call | solution.py:312
  2.2 7.4 %all-to-all-start = ((bf16[8,16,8,128]{3,2,1,0:T(8,128)(2,1)}), bf16[8,16,8,128]{3,2,1,0:T(8,128)(2,1)S(1)}, u32[]{:S(2)}, u32[]{:S(2)}) async-start(bf16[8,16,8,128]{3,2,1,0:T(8,128)(2,1)} %pack.1.packed_ref), calls=%async_computation | async-start | bytes 524288 | tf_op jit(solution)/shard_map/all_to_all | solution.py:310
  9.6 2.2 %copy-done.1 = bf16[1024,2048]{1,0:T(8,128)(2,1)S(1)} copy-done((bf16[1024,2048]{1,0:T(8,128)(2,1)S(1)}, bf16[1024,2048]{1,0:T(8,128)(2,1)}, u32[]{:S(2)}) %copy-start.1) | copy-done | bytes 4194328
  11.8 0.0 copy-start.7
  11.8 0.0 copy-start.8
  11.8 1.7 %base.1.refs_7_ = f32[8,2048]{1,0:T(8,128)S(1)} custom-call(bf16[8,16,8,128]{3,2,1,0:T(8,128)(2,1)} %pack.1.packed_ref, bf16[1024,2048]{1,0:T(8,128)(2,1)S(1)} %copy-done.1), custom_call_target="tpu_custom_call" | custom-call | flops 33554432 | bytes 4194304 | tf_op jit(solution)/shard_map/base/pallas_call | solution.py:323
  13.5 5.0 %all-to-all-done.refs_5_ = bf16[8,16,8,128]{3,2,1,0:T(8,128)(2,1)S(1)} async-done(((bf16[8,16,8,128]{3,2,1,0:T(8,128)(2,1)}), bf16[8,16,8,128]{3,2,1,0:T(8,128)(2,1)S(1)}, u32[]{:S(2)}, u32[]{:S(2)}) %all-to-all-start) | async-done | bytes 262176 | tf_op jit(solution)/shard_map/all_to_all | solution.py:310
  18.5 0.0 collective-permute-start
  18.5 1.5 %collective-permute-done.refs_6_ = bf16[8,16,8,128]{3,2,1,0:T(8,128)(2,1)S(1)} collective-permute-done((bf16[8,16,8,128]{3,2,1,0:T(8,128)(2,1)S(1)}, bf16[8,16,8,128]{3,2,1,0:T(8,128)(2,1)S(1)}, u32[]{:S(2)}, u32[]{:S(2)}) %collective-permute-start) | collective-permute-done | bytes 262176 | tf_op jit(solution)/shard_map/ppermute | solution.py:281
  20.0 0.0 copy-done.2
  20.0 0.0 copy-done.3
  20.0 0.0 copy-done.4
  20.0 0.0 copy-done.5
  20.1 0.0 copy-done.6
  20.1 0.0 copy-done.7
  20.1 0.0 copy-done.8
  20.1 0.0 copy-start
  20.1 2.2 %copy-done = bf16[1,16384,128]{2,1,0:T(8,128)(2,1)S(1)} copy-done((bf16[1,16384,128]{2,1,0:T(8,128)(2,1)S(1)}, bf16[1,16384,128]{2,1,0:T(8,128)(2,1)}, u32[]{:S(2)}) %copy-start) | copy-done | bytes 4194328
  22.3 3.8 %partial_states.1 = (bf16[720,128]{1,0:T(8,128)(2,1)S(1)}, f32[512,128]{1,0:T(8,128)S(1)}, f32[16,128]{1,0:T(8,128)S(1)}, f32[2,8,8,128]{3,2,1,0:T(8,128)S(1)}) custom-call(s32[1]{0:T(128)} %bitcast.refs_0_, s32[2]{0:T(128)S(1)} %copy-done.5, s32[16]{0:T(128)S(1)} %copy-done.6, s32[16]{0:T(128)S(1)} %copy-done.7, s32[2]{0:T(128)S(1)} %copy-done.8, ...), custom_call_target="tpu_custom_call" | custom-call | tf_op jit(solution)/shard_map/partial_states/pallas_call | solution.py:338
  26.1 0.2 collective-permute-start.1
  26.3 0.1 add_convert_fusion
  26.4 1.2 %collective-permute-done.1.got_ref = bf16[720,128]{1,0:T(8,128)(2,1)S(1)} collective-permute-done((bf16[720,128]{1,0:T(8,128)(2,1)S(1)}, bf16[720,128]{1,0:T(8,128)(2,1)S(1)}, u32[]{:S(2)}, u32[]{:S(2)}) %collective-permute-start.1) | collective-permute-done | bytes 184352 | tf_op jit(solution)/shard_map/ppermute | solution.py:281
  27.6 1.0 %join.1 = bf16[8,96,128]{2,1,0:T(8,128)(2,1)} custom-call(f32[512,128]{1,0:T(8,128)S(1)} %get-tuple-element.13.mix_ref, f32[16,128]{1,0:T(8,128)S(1)} %get-tuple-element.14.stat_ref, f32[2,8,8,128]{3,2,1,0:T(8,128)S(1)} %get-tuple-element.15.proj_ref, bf16[720,128]{1,0:T(8,128)(2,1)S(1)} %collective-permute-done.1.got_ref), custom_call_target="tpu_custom_call" | custom-call | tf_op jit(solution)/shard_map/join/pallas_call | solution.py:365
  28.6 3.6 %all-to-all-start.1 = ((bf16[8,96,128]{2,1,0:T(8,128)(2,1)}), bf16[8,96,128]{2,1,0:T(8,128)(2,1)S(1)}, u32[]{:S(2)}, u32[]{:S(2)}) async-start(bf16[8,96,128]{2,1,0:T(8,128)(2,1)} %join.1), calls=%async_computation.1 | async-start | bytes 393216 | tf_op jit(solution)/shard_map/all_to_all | solution.py:310
  32.2 0.1 convert_element_type.11
  32.3 0.1 fusion
  32.4 0.1 pad_maximum_fusion
  32.5 8.0 %all-to-all-done.1.got_ref = bf16[8,96,128]{2,1,0:T(8,128)(2,1)S(1)} async-done(((bf16[8,96,128]{2,1,0:T(8,128)(2,1)}), bf16[8,96,128]{2,1,0:T(8,128)(2,1)S(1)}, u32[]{:S(2)}, u32[]{:S(2)}) %all-to-all-start.1) | async-done | bytes 196640 | tf_op jit(solution)/shard_map/all_to_all | solution.py:310
  40.5 2.1 %merge_states.1 = bf16[2,4,1024]{2,1,0:T(4,128)(2,1)} custom-call(bf16[8,16,8,128]{3,2,1,0:T(8,128)(2,1)} %pack.1.packed_ref, f32[8,128]{1,0:T(8,128)S(1)} %get-tuple-element.20.cos_ref, f32[8,128]{1,0:T(8,128)S(1)} %get-tuple-element.21.sin_ref, bf16[8,96,128]{2,1,0:T(8,128)(2,1)S(1)} %all-to-all-done.1.got_ref), custom_call_target="tpu_custom_call" | custom-call | tf_op jit(solution)/shard_map/merge_states/pallas_call | solution.py:375
  (8 shorter events, 0.0 us)
Async XLA Ops:
  0.0 0.7 %copy-start.9 = (bf16[2,4,1024]{2,1,0:T(4,128)(2,1)S(1)}, bf16[2,4,1024]{2,1,0:T(4,128)(2,1)}, u32[]{:S(2)}) copy-start(bf16[2,4,1024]{2,1,0:T(4,128)(2,1)} %query_ref.1) | copy-start | bytes 49156
  0.7 0.7 %copy-start.10 = (bf16[2,4,1024]{2,1,0:T(4,128)(2,1)S(1)}, bf16[2,4,1024]{2,1,0:T(4,128)(2,1)}, u32[]{:S(2)}) copy-start(bf16[2,4,1024]{2,1,0:T(4,128)(2,1)} %hidden_ref.1) | copy-start | bytes 49156
  2.2 17.9 %copy-start.2 = (bf16[1,128,2048]{2,1,0:T(8,128)(2,1)S(1)}, bf16[1,128,2048]{2,1,0:T(8,128)(2,1)}, u32[]{:S(2)}) copy-start(bf16[1,128,2048]{2,1,0:T(8,128)(2,1)} %param.15) | copy-start | bytes 1572868
  2.2 16.3 %all-to-all-start = ((bf16[8,16,8,128]{3,2,1,0:T(8,128)(2,1)}), bf16[8,16,8,128]{3,2,1,0:T(8,128)(2,1)S(1)}, u32[]{:S(2)}, u32[]{:S(2)}) async-start(bf16[8,16,8,128]{3,2,1,0:T(8,128)(2,1)} %pack.1.packed_ref), calls=%async_computation | async-start | bytes 524288 | tf_op jit(solution)/shard_map/all_to_all | solution.py:310
  9.6 2.2 %copy-start.1 = (bf16[1024,2048]{1,0:T(8,128)(2,1)S(1)}, bf16[1024,2048]{1,0:T(8,128)(2,1)}, u32[]{:S(2)}) copy-start(bf16[1024,2048]{1,0:T(8,128)(2,1)} %weight_ref.1) | copy-start | bytes 12582916
  11.8 8.3 %copy-start.3 = (bf16[2,128,1024]{2,1,0:T(8,128)(2,1)S(1)}, bf16[2,128,1024]{2,1,0:T(8,128)(2,1)}, u32[]{:S(2)}) copy-start(bf16[2,128,1024]{2,1,0:T(8,128)(2,1)} %param.16) | copy-start | bytes 1572868
  11.8 8.3 %copy-start.4 = (bf16[2,128,1024]{2,1,0:T(8,128)(2,1)S(1)}, bf16[2,128,1024]{2,1,0:T(8,128)(2,1)}, u32[]{:S(2)}) copy-start(bf16[2,128,1024]{2,1,0:T(8,128)(2,1)} %param.17) | copy-start | bytes 1572868
  11.8 8.3 %copy-start.5 = (s32[2]{0:T(128)S(1)}, s32[2]{0:T(128)}, u32[]{:S(2)}) copy-start(s32[2]{0:T(128)} %refs_1_.1) | copy-start | bytes 28
  11.8 8.3 %copy-start.6 = (s32[16]{0:T(128)S(1)}, s32[16]{0:T(128)}, u32[]{:S(2)}) copy-start(s32[16]{0:T(128)} %refs_2_.1) | copy-start | bytes 196
  11.8 8.3 %copy-start.7 = (s32[16]{0:T(128)S(1)}, s32[16]{0:T(128)}, u32[]{:S(2)}) copy-start(s32[16]{0:T(128)} %refs_3_.1) | copy-start | bytes 196
  11.8 8.3 %copy-start.8 = (s32[2]{0:T(128)S(1)}, s32[2]{0:T(128)}, u32[]{:S(2)}) copy-start(s32[2]{0:T(128)} %refs_4_.1) | copy-start | bytes 28
  18.5 1.5 %collective-permute-start = (bf16[8,16,8,128]{3,2,1,0:T(8,128)(2,1)S(1)}, bf16[8,16,8,128]{3,2,1,0:T(8,128)(2,1)S(1)}, u32[]{:S(2)}, u32[]{:S(2)}) collective-permute-start(bf16[8,16,8,128]{3,2,1,0:T(8,128)(2,1)S(1)} %all-to-all-done.refs_5_), channel_id=1, source_target_pairs={{0,1},{1,0},{2,3},{3,2},{4,5},{5,4},{6,7},{7,6},{8,9},{9,8},{10,11... | collective-permute-start | bytes 786440 | tf_op jit(solution)/shard_map/ppermute | solution.py:281
  20.1 2.2 %copy-start = (bf16[1,16384,128]{2,1,0:T(8,128)(2,1)S(1)}, bf16[1,16384,128]{2,1,0:T(8,128)(2,1)}, u32[]{:S(2)}) copy-start(bf16[1,16384,128]{2,1,0:T(8,128)(2,1)} %param.14) | copy-start | bytes 12582916
  26.1 1.5 %collective-permute-start.1 = (bf16[720,128]{1,0:T(8,128)(2,1)S(1)}, bf16[720,128]{1,0:T(8,128)(2,1)S(1)}, u32[]{:S(2)}, u32[]{:S(2)}) collective-permute-start(bf16[720,128]{1,0:T(8,128)(2,1)S(1)} %get-tuple-element.16), channel_id=1, source_target_pairs={{0,1},{1,0},{2,3},{3,2},{4,5},{5,4},{6,7},{7,6},{8,9},{9,8},{10,11... | collective-permute-start | bytes 552968 | tf_op jit(solution)/shard_map/ppermute | solution.py:281
  28.6 11.9 %all-to-all-start.1 = ((bf16[8,96,128]{2,1,0:T(8,128)(2,1)}), bf16[8,96,128]{2,1,0:T(8,128)(2,1)S(1)}, u32[]{:S(2)}, u32[]{:S(2)}) async-start(bf16[8,96,128]{2,1,0:T(8,128)(2,1)} %join.1), calls=%async_computation.1 | async-start | bytes 393216 | tf_op jit(solution)/shard_map/all_to_all | solution.py:310

commit v4 on v3

--- a/solution.py
+++ b/solution.py
@@ -27,44 +27,119 @@
     return x.astype(jnp.bfloat16).astype(jnp.float32)
 
 
-def pack_kernel(requests, query_ref, hidden_ref, out_ref):
+def pack_kernel(requests, heads, query_ref, hidden_ref, copies_ref, own_ref, query_buf, hidden_buf, sems):
+    loads = [
+        pltpu.make_async_copy(query_ref, query_buf, sems.at[0]),
+        pltpu.make_async_copy(hidden_ref, hidden_buf, sems.at[1]),
+    ]
+    for load in loads:
+        load.start()
     at = 0
-    for ref in (query_ref, hidden_ref):
+    for load, ref in zip(loads, (query_buf, hidden_buf)):
+        load.wait()
         rows = jnp.concatenate([ref[b].astype(jnp.float32) for b in range(requests)], axis=0)
         for c in range(rows.shape[1] // HEAD_WIDTH):
-            tile = rows[:, c * HEAD_WIDTH : (c + 1) * HEAD_WIDTH]
-            for copy in range(out_ref.shape[0]):
-                out_ref[copy, at] = tile.astype(jnp.bfloat16)
+            tile = rows[:, c * HEAD_WIDTH : (c + 1) * HEAD_WIDTH].astype(jnp.bfloat16)
+            own_ref[at] = tile
+            for copy in range(copies_ref.shape[0]):
+                copies_ref[copy, at] = tile
             at += 1
 
 
-def base_kernel(heads, packed_ref, weight_ref, base_ref):
-    chunks = weight_ref.shape[0] // HEAD_WIDTH
-    hidden = jnp.concatenate([packed_ref[0, heads + c] for c in range(chunks)], axis=1)
-    base_ref[...] = dot(hidden, weight_ref[...], ((1,), (0,)))
-
-
-def partial_kernel(devices, requests, tokens, *refs):
+def base_kernel(heads, own_ref, weight_ref, *refs):
+    count = (len(refs) - 3) // 2
+    sources, base_ref, held = refs[:count], refs[count], refs[count + 1 : -2]
+    buffer, sems = refs[-2:]
+    parts, depth = buffer.shape[:2]
+    loads = [
+        pltpu.make_async_copy(weight_ref.at[pl.ds(p * depth, depth)], buffer.at[p], sems.at[p])
+        for p in range(parts)
+    ]
+    others = [
+        pltpu.make_async_copy(source, place, sems.at[parts + i])
+        for i, (source, place) in enumerate(zip(sources, held))
+    ]
+    for load in loads + others:
+        load.start()
+    tiles = depth // HEAD_WIDTH
+    total = jnp.zeros(base_ref.shape, jnp.float32)
+    for p in range(parts):
+        hidden = jnp.concatenate([own_ref[heads + p * tiles + c] for c in range(tiles)], axis=1)
+        loads[p].wait()
+        total += dot(hidden, buffer[p], ((1,), (0,)))
+    base_ref[...] = total
+    for load in others:
+        load.wait()
+
+
+def lower(side, heads, index_ref, gathered_ref, down_ref):
+    lanes = gathered_ref.shape[0]
+    depth = down_ref.shape[0] // lanes // 2
+    total = None
+    for m in range(lanes):
+        hidden = jnp.concatenate(
+            [gathered_ref[m, heads + c] for c in range(depth // HEAD_WIDTH)], axis=1
+        )
+        source = 2 * m + (index_ref[0] % 2 ^ side)
+        factor = down_ref[pl.ds(pl.multiple_of(source * depth, depth), depth), :]
+        term = dot(hidden, factor, ((1,), (0,)))
+        total = term if total is None else total + term
+    return total
+
+
+def attend(requests, tokens, heads, index_ref, length_ref, query_ref, key_ref, value_ref, put):
+    here = index_ref[0]
+    per_lane = query_ref.shape[0] // KEY_HEADS
+    positions = key_ref.shape[0] // requests
+    place = lax.broadcasted_iota(jnp.int32, (requests * positions, HEAD_WIDTH), 0)
+    column = lax.broadcasted_iota(jnp.int32, (requests * positions, HEAD_WIDTH), 1)
+    place_request = place // positions
+    limit = jnp.zeros_like(place)
+    for b in range(requests):
+        limit = jnp.where(place_request == b, length_ref[b], limit)
+    allowed = (here * positions + place % positions < limit) & (
+        place_request == (column // tokens) % requests
+    )
+    first = column < 64
+    peaks, totals = [], []
+    for p in range(PAIRS):
+        spots = [2 * p * HEAD_WIDTH, (2 * p + 1) * HEAD_WIDTH]
+        query = jnp.concatenate(
+            [query_ref[2 * p * per_lane + t, h] for t in range(2 * per_lane) for h in range(heads)],
+            axis=0,
+        )
+        scores = [dot(key_ref[:, at : at + HEAD_WIDTH], query, ((1,), (1,))) for at in spots]
+        scores = jnp.where(first, scores[0], scores[1]) * SCALE
+        peak = jnp.max(jnp.where(allowed, scores, NEG_FILL), axis=0, keepdims=True)
+        peak = round_bf16(peak)
+        weights = jnp.where(allowed, jnp.exp(scores - peak), 0.0)
+        peaks.append(peak)
+        totals.append(jnp.sum(weights, axis=0, keepdims=True))
+        weights = jnp.transpose(weights.astype(jnp.bfloat16))
+        for i, at in enumerate(spots):
+            mix = dot(weights[64 * i : 64 * i + 64], value_ref[:, at : at + HEAD_WIDTH], ((1,), (0,)))
+            put(p, i, mix)
+    return peaks, totals
+
+
+def rows_of(items, count):
+    row = lax.broadcasted_iota(jnp.int32, (count, HEAD_WIDTH), 0)
+    out = jnp.zeros((count, HEAD_WIDTH), jnp.float32)
+    for i, item in enumerate(items):
+        out = jnp.where(row == i, item, out)
+    return out
+
+
+def lower_kernel(heads, index_ref, lane_ref, down_ref, out_ref):
+    out_ref[...] = lower(0, heads, index_ref, lane_ref, down_ref)
+
+
+def other_kernel(requests, tokens, heads, *refs):
     (index_ref, adapter_ref, rank_ref, pool_ref, length_ref) = refs[:5]
-    (lane_ref, other_ref, base_ref, down_ref, up_ref, key_ref, value_ref) = refs[5:12]
-    (send_ref, mix_ref, stat_ref, proj_ref) = refs[12:]
-    here = index_ref[0]
+    (other_ref, lowered_ref, base_ref, down_ref, up_ref, key_ref, value_ref) = refs[5:12]
+    (send_ref, proj_ref) = refs[12:]
     rows = requests * tokens
-    heads = QUERY_HEADS // devices
-    lanes = devices // 2
-    per_key_head = devices // KEY_HEADS
-    per_lane = per_key_head // 2
-    chunks = down_ref.shape[0] // devices // HEAD_WIDTH
-    positions = key_ref.shape[0] // requests
-    depth = chunks * HEAD_WIDTH
-
-    lowered = jnp.zeros((rows, down_ref.shape[1]), jnp.float32)
-    for side, ref in enumerate((lane_ref, other_ref)):
-        for m in range(lanes):
-            hidden = jnp.concatenate([ref[m, heads + c] for c in range(chunks)], axis=1)
-            source = 2 * m + (here % 2 ^ side)
-            factor = down_ref[pl.ds(pl.multiple_of(source * depth, depth), depth), :]
-            lowered += dot(hidden, factor, ((1,), (0,)))
+    lowered = lowered_ref[...] + lower(1, heads, index_ref, other_ref, down_ref)
     row_request = lax.broadcasted_iota(jnp.int32, (rows, 1), 0) // tokens
     ranks = jnp.zeros((rows, 1), jnp.int32)
     owners = jnp.zeros((rows, 1), jnp.int32)
@@ -75,17 +150,16 @@
     column = lax.broadcasted_iota(jnp.int32, lowered.shape, 1)
     lowered = jnp.where(column < ranks, lowered, 0.0).astype(jnp.bfloat16)
     lifted = dot(lowered, up_ref[...], ((1,), (0,)))
-    projected = base_ref[...] + jnp.where(owners == here, lifted, 0.0)
-
+    projected = base_ref[...] + jnp.where(owners == index_ref[0], lifted, 0.0)
     split = KEY_HEADS * HEAD_WIDTH
-    mix_total = KEY_HEADS * 64
     for j in range(KEY_HEADS):
         at = j * HEAD_WIDTH
         proj_ref[0, j] = projected[:, at : at + HEAD_WIDTH]
         proj_ref[1, j] = projected[:, split + at : split + at + HEAD_WIDTH]
-    keys = proj_ref[0].reshape(KEY_HEADS * rows, HEAD_WIDTH)
+    mix_total = KEY_HEADS * 64
+    step = KEY_HEADS * rows
+    keys = proj_ref[0].reshape(step, HEAD_WIDTH)
     high = keys.astype(jnp.bfloat16)
-    step = KEY_HEADS * rows
     send_ref[mix_total : mix_total + step] = high
     send_ref[mix_total + step : mix_total + 2 * step] = (keys - high.astype(jnp.float32)).astype(
         jnp.bfloat16
@@ -94,56 +168,29 @@
         proj_ref[1].reshape(step, HEAD_WIDTH).astype(jnp.bfloat16)
     )
 
-    stacked = requests * positions
-    place = lax.broadcasted_iota(jnp.int32, (stacked, HEAD_WIDTH), 0)
-    column = lax.broadcasted_iota(jnp.int32, (stacked, HEAD_WIDTH), 1)
-    place_request = place // positions
-    limit = jnp.zeros_like(place)
-    for b in range(requests):
-        limit = jnp.where(place_request == b, length_ref[b], limit)
-    allowed = (here * positions + place % positions < limit) & (
-        place_request == (column // tokens) % requests
-    )
-    first = column < 64
-    stat_row = lax.broadcasted_iota(jnp.int32, (STAT_ROWS, HEAD_WIDTH), 0)
-    for side, ref in enumerate((other_ref, lane_ref)):
-        stats = jnp.zeros((STAT_ROWS, HEAD_WIDTH), jnp.float32)
-        for p in range(PAIRS):
-            spots = [2 * p * HEAD_WIDTH, (2 * p + 1) * HEAD_WIDTH]
-            query = jnp.concatenate(
-                [ref[2 * p * per_lane + t, h] for t in range(2 * per_lane) for h in range(heads)],
-                axis=0,
-            )
-            scores = [
-                dot(key_ref[:, at : at + HEAD_WIDTH], query, ((1,), (1,))) for at in spots
-            ]
-            scores = jnp.where(first, scores[0], scores[1]) * SCALE
-            peak = jnp.max(jnp.where(allowed, scores, NEG_FILL), axis=0, keepdims=True)
-            peak = round_bf16(peak)
-            weights = jnp.where(allowed, jnp.exp(scores - peak), 0.0)
-            total = jnp.sum(weights, axis=0, keepdims=True)
-            weights = jnp.transpose(weights.astype(jnp.bfloat16))
-            mix = [
-                dot(weights[64 * i : 64 * i + 64], value_ref[:, at : at + HEAD_WIDTH], ((1,), (0,)))
-                for i, at in enumerate(spots)
-            ]
-            at = p * 128
-            for i in range(2):
-                if side == 0:
-                    send_ref[at + 64 * i : at + 64 * i + 64] = mix[i].astype(jnp.bfloat16)
-                else:
-                    mix_ref[at + 64 * i : at + 64 * i + 64] = mix[i]
-            stats = jnp.where(stat_row == p, peak, stats)
-            high = round_bf16(total)
-            if side == 0:
-                stats = jnp.where(stat_row == PAIRS + p, high, stats)
-                stats = jnp.where(stat_row == 2 * PAIRS + p, total - high, stats)
-            else:
-                stats = jnp.where(stat_row == PAIRS + p, total, stats)
-        if side == 0:
-            send_ref[mix_total + 3 * step :] = stats.astype(jnp.bfloat16)
-        else:
-            stat_ref[...] = stats
+    def put(p, i, mix):
+        at = p * 128 + i * 64
+        send_ref[at : at + 64] = mix.astype(jnp.bfloat16)
+
+    peaks, totals = attend(
+        requests, tokens, heads, index_ref, length_ref, other_ref, key_ref, value_ref, put
+    )
+    highs = [round_bf16(total) for total in totals]
+    lows = [total - high for total, high in zip(totals, highs)]
+    send_ref[mix_total + 3 * step :] = rows_of(peaks + highs + lows, STAT_ROWS).astype(jnp.bfloat16)
+
+
+def own_kernel(
+    requests, tokens, heads, index_ref, length_ref, lane_ref, key_ref, value_ref, mix_ref, stat_ref
+):
+    def put(p, i, mix):
+        at = p * 128 + i * 64
+        mix_ref[at : at + 64] = mix
+
+    peaks, totals = attend(
+        requests, tokens, heads, index_ref, length_ref, lane_ref, key_ref, value_ref, put
+    )
+    stat_ref[...] = rows_of(peaks + totals, STAT_ROWS)
 
 
 def join_kernel(devices, requests, tokens, mix_ref, stat_ref, proj_ref, got_ref, packet_ref):
@@ -198,7 +245,7 @@
             ).astype(jnp.bfloat16)
 
 
-def merge_kernel(devices, requests, tokens, packed_ref, cos_ref, sin_ref, got_ref, out_ref):
+def merge_kernel(devices, requests, tokens, own_ref, cos_ref, sin_ref, got_ref, out_ref):
     got_refs = [got_ref.at[s] for s in range(got_ref.shape[0])]
     rows = requests * tokens
     heads = QUERY_HEADS // devices
@@ -210,7 +257,7 @@
     values = sums[2 * rows :].astype(jnp.bfloat16)
     turned = pltpu.roll(keys, HEAD_WIDTH // 2, 1)
     keys = (keys * cos_ref[...] + turned * sin_ref[...]).astype(jnp.bfloat16)
-    query = jnp.concatenate([packed_ref[0, h] for h in range(heads)], axis=0)
+    query = jnp.concatenate([own_ref[h] for h in range(heads)], axis=0)
     if mix_rows < 128:
         query = jnp.concatenate(
             [query, jnp.zeros((128 - mix_rows, HEAD_WIDTH), jnp.bfloat16)], axis=0
@@ -271,6 +318,10 @@
 
 def hbm():
     return pl.BlockSpec(memory_space=pltpu.HBM)
+
+
+def pinned(x):
+    return pltpu.with_memory_space_constraint(x, pltpu.HBM)
 
 
 def cost(flops, moved):
@@ -309,59 +360,100 @@
     def exchange(x):
         return lax.all_to_all(x, "tensor", 0, 0, axis_index_groups=lane_groups, tiled=True)
 
-    packed = pl.pallas_call(
-        functools.partial(pack_kernel, requests),
-        out_shape=jax.ShapeDtypeStruct((lanes, tiles, rows, HEAD_WIDTH), jnp.bfloat16),
-        in_specs=[vmem()] * 2,
-        out_specs=vmem(),
-        compiler_params=pltpu.CompilerParams(vmem_limit_bytes=8 * MIB),
-        cost_estimate=cost(10**10, 0),
+    tile_shape = (tiles, rows, HEAD_WIDTH)
+    copies, own = pl.pallas_call(
+        functools.partial(pack_kernel, requests, heads),
+        out_shape=(
+            jax.ShapeDtypeStruct((lanes,) + tile_shape, jnp.bfloat16),
+            pltpu.VMEM(tile_shape, jnp.bfloat16),
+        ),
+        in_specs=[hbm()] * 2,
+        out_specs=(vmem(),) * 2,
+        scratch_shapes=[
+            pltpu.VMEM(queries.shape, jnp.bfloat16),
+            pltpu.VMEM(hidden.shape, jnp.bfloat16),
+            pltpu.SemaphoreType.DMA((2,)),
+        ],
+        compiler_params=pltpu.CompilerParams(vmem_limit_bytes=4 * MIB),
         name="pack",
-    )(queries, hidden)
-    lane = exchange(packed)
-
-    base = pl.pallas_call(
+    )(pinned(queries), pinned(hidden))
+    lane = exchange(copies)
+
+    flat = requests * cached_key_rows.shape[1]
+    big = (
+        adapter_down_weight[0],
+        cached_key_rows.reshape(flat, -1),
+        cached_value_rows.reshape(flat, -1),
+        adapter_up_weight[0],
+    )
+    out_width = key_value_weight.shape[1]
+    parts = 4 if width % (4 * HEAD_WIDTH) == 0 else 1
+    base, down, keys, values, up = pl.pallas_call(
         functools.partial(base_kernel, heads),
-        out_shape=jax.ShapeDtypeStruct((rows, key_value_weight.shape[1]), jnp.float32),
-        in_specs=[vmem()] * 2,
-        out_specs=vmem(),
-        compiler_params=pltpu.CompilerParams(vmem_limit_bytes=16 * MIB),
-        cost_estimate=cost(2 * rows * key_value_weight.size, 2 * key_value_weight.size),
+        out_shape=(pltpu.VMEM((rows, out_width), jnp.float32),)
+        + tuple(pltpu.VMEM(x.shape, x.dtype) for x in big),
+        in_specs=[vmem()] + [hbm()] * 5,
+        out_specs=(vmem(),) * 5,
+        scratch_shapes=[
+            pltpu.VMEM((parts, width // parts, out_width), jnp.bfloat16),
+            pltpu.SemaphoreType.DMA((parts + 4,)),
+        ],
+        compiler_params=pltpu.CompilerParams(vmem_limit_bytes=12 * MIB),
+        cost_estimate=cost(10**9, 0),
         name="base",
-    )(packed, key_value_weight)
+    )(own, pinned(key_value_weight), *[pinned(x) for x in big])
     lane, base = lax.optimization_barrier((lane, base))
     other = swap(lane, devices, 1)
 
-    flat = requests * cached_key_rows.shape[1]
+    index = here.reshape(1).astype(jnp.int32)
+    lowered = pl.pallas_call(
+        functools.partial(lower_kernel, heads),
+        out_shape=pltpu.VMEM((rows, down.shape[1]), jnp.float32),
+        in_specs=[smem()] + [vmem()] * 2,
+        out_specs=vmem(),
+        compiler_params=pltpu.CompilerParams(vmem_limit_bytes=12 * MIB),
+        cost_estimate=cost(10**9, 0),
+        name="lower",
+    )(index, lane, down)
     mix_total = KEY_HEADS * 64
     send_rows = mix_total + 3 * KEY_HEADS * rows + STAT_ROWS
-    send, mix, stats, proj = pl.pallas_call(
-        functools.partial(partial_kernel, devices, requests, tokens),
+    send, proj = pl.pallas_call(
+        functools.partial(other_kernel, requests, tokens, heads),
         out_shape=(
-            jax.ShapeDtypeStruct((send_rows, HEAD_WIDTH), jnp.bfloat16),
-            jax.ShapeDtypeStruct((mix_total, HEAD_WIDTH), jnp.float32),
-            jax.ShapeDtypeStruct((STAT_ROWS, HEAD_WIDTH), jnp.float32),
-            jax.ShapeDtypeStruct((2, KEY_HEADS, rows, HEAD_WIDTH), jnp.float32),
+            pltpu.VMEM((send_rows, HEAD_WIDTH), jnp.bfloat16),
+            pltpu.VMEM((2, KEY_HEADS, rows, HEAD_WIDTH), jnp.float32),
         ),
         in_specs=[smem()] * 5 + [vmem()] * 7,
-        out_specs=(vmem(),) * 4,
-        compiler_params=pltpu.CompilerParams(vmem_limit_bytes=16 * MIB),
-        name="partial_states",
+        out_specs=(vmem(),) * 2,
+        compiler_params=pltpu.CompilerParams(vmem_limit_bytes=12 * MIB),
+        name="other_lane",
     )(
-        here.reshape(1).astype(jnp.int32),
+        index,
         request_adapter,
         adapter_rank_list,
         adapter_pool_row,
         lengths,
-        lane,
         other,
+        lowered,
         base,
-        adapter_down_weight[0],
-        adapter_up_weight[0],
-        cached_key_rows.reshape(flat, -1),
-        cached_value_rows.reshape(flat, -1),
+        down,
+        up,
+        keys,
+        values,
     )
     got = swap(send, devices, 1)
+    mix, stats = pl.pallas_call(
+        functools.partial(own_kernel, requests, tokens, heads),
+        out_shape=(
+            pltpu.VMEM((mix_total, HEAD_WIDTH), jnp.float32),
+            pltpu.VMEM((STAT_ROWS, HEAD_WIDTH), jnp.float32),
+        ),
+        in_specs=[smem()] * 2 + [vmem()] * 3,
+        out_specs=(vmem(),) * 2,
+        compiler_params=pltpu.CompilerParams(vmem_limit_bytes=8 * MIB),
+        cost_estimate=cost(10**9, 0),
+        name="own_lane",
+    )(index, lengths, lane, keys, values)
     packets = pl.pallas_call(
         functools.partial(join_kernel, devices, requests, tokens),
         out_shape=jax.ShapeDtypeStruct((lanes, mix_rows + 4 * rows, HEAD_WIDTH), jnp.bfloat16),
@@ -379,7 +471,7 @@
         out_specs=vmem(),
         compiler_params=pltpu.CompilerParams(vmem_limit_bytes=8 * MIB),
         name="merge_states",
-    )(packed, cosine, sine, packets)
+    )(own, cosine, sine, packets)
 
 
 def solution(mesh):

time: 43.1 us -> 41.3 us (0.958)
  waiting for transfers between devices: 15.8 us -> 11 us
  Pallas kernels: 9.3 us -> 12.1 us
    pallas_call x3 -> x5, Pallas kernels: 6.21 us -> 9.94 us  [the longest x1 3.86 us: per_device(): pl.pallas_call(functools.partial(base_kernel, heads), out_shape=(pltpu.VM...]
    ppermute x2, waiting for transfers between devices: 2.75 us -> 0.01 us  [swap(): return lax.ppermute(x, 'tensor', [(d, d ^ bit) for d in range(devices)])]
    all_to_all x2, waiting for transfers between devices: 13 us -> 11 us  [exchange(): lax.all_to_all(x, 'tensor', 0, 0, axis_index_groups=lane_groups, tiled=True)]
    pallas_call x1, Pallas kernels: 2.07 us -> 1.12 us  [per_device(): pl.pallas_call(functools.partial(merge_kernel, devices, requests, tokens)...]
    unnamed x22 -> x14, local copies, waits for them, and re-layouts: 5.83 us -> 5.91 us
  transfers between devices with their start and end apart: 4 -> 4, of which waited for: 4 -> 2; matrix products, arithmetic and copies ran while one was open for 1% -> 1% of each run, Pallas kernels for 4% -> 15%
where the time goes in v4:
time: 41.3 us; the launch traced here: 40.9 us
  Pallas kernels  12.1 us (29%)
  starting transfers between devices  11.5 us (28%)
  waiting for transfers between devices  11 us (27%)
  local copies, waits for them, and re-layouts  6 us (15%)
    all_to_all x2, waiting for transfers between devices, exchange(): lax.all_to_all(x, 'tensor', 0, 0, axis_index_groups=lane_groups, tiled=True)  11 us
    all_to_all x2, starting transfers between devices, exchange(): lax.all_to_all(x, 'tensor', 0, 0, axis_index_groups=lane_groups, tiled=True)  10.9 us
    unnamed x14, local copies, waits for them, and re-layouts  5.91 us
    pallas_call x1, Pallas kernels, per_device(): pl.pallas_call(functools.partial(base_kernel, heads), out_shape=(pltpu.VM...  3.86 us
    pallas_call x1, Pallas kernels, per_device(): pl.pallas_call(functools.partial(other_kernel, requests, tokens, heads),...  2.34 us
    pallas_call x1, Pallas kernels, per_device(): pl.pallas_call(functools.partial(own_kernel, requests, tokens, heads), ou...  1.87 us
    pallas_call x1, Pallas kernels, per_device(): pl.pallas_call(functools.partial(pack_kernel, requests, heads), out_shape...  1.5 us
    pallas_call x1, Pallas kernels, per_device(): pl.pallas_call(functools.partial(merge_kernel, devices, requests, tokens)...  1.12 us
  transfers between devices with their start and end apart: 4, of which 2 were waited for; matrix products, arithmetic and copies ran while one was open for 1% of the time, Pallas kernels for 15%

profile of v4, /device:TPU:0, one launch (start us, length us, event | category | flops | bytes accessed | tf_op | source)
XLA Modules:
  0.0 40.9 jit_solution(3467941170928323237)
XLA Ops:
  0.0 1.5 %pack.1 = (bf16[8,16,8,128]{3,2,1,0:T(8,128)(2,1)}, bf16[16,8,128]{2,1,0:T(8,128)(2,1)S(1)}) custom-call(bf16[2,4,1024]{2,1,0:T(4,128)(2,1)} %query_ref.1, bf16[2,4,1024]{2,1,0:T(4,128)(2,1)} %hidden_ref.1), custom_call_target="tpu_custom_call" | custom-call | tf_op jit(solution)/shard_map/pack/pallas_call | solution.py:364
  1.5 7.3 %all-to-all-start = ((bf16[8,16,8,128]{3,2,1,0:T(8,128)(2,1)}), bf16[8,16,8,128]{3,2,1,0:T(8,128)(2,1)S(1)}, u32[]{:S(2)}, u32[]{:S(2)}) async-start(bf16[8,16,8,128]{3,2,1,0:T(8,128)(2,1)} %get-tuple-element.19), calls=%async_computation | async-start | bytes 524288 | tf_op jit(solution)/shard_map/all_to_all | solution.py:361
  8.8 3.9 %base.1 = (f32[8,2048]{1,0:T(8,128)S(1)}, bf16[16384,128]{1,0:T(8,128)(2,1)S(1)}, bf16[256,1024]{1,0:T(8,128)(2,1)S(1)}, bf16[256,1024]{1,0:T(8,128)(2,1)S(1)}, bf16[128,2048]{1,0:T(8,128)(2,1)S(1)}) custom-call(bf16[16,8,128]{2,1,0:T(8,128)(2,1)S(1)} %get-tuple-element.18.own_ref, bf16[1024,2048]{1,0:T(8,128)(2,1)} %weight_ref.1, ...), custom_call_target="tpu_custom_call" | custom-call | flops 1000000000 | tf_op jit(solution)/shard_map/base/pallas_call | solution.py:391
  12.7 0.0 copy-start
  12.7 1.9 %copy-done = bf16[16384,128]{1,0:T(8,128)(2,1)} copy-done((bf16[16384,128]{1,0:T(8,128)(2,1)}, bf16[16384,128]{1,0:T(8,128)(2,1)S(1)}, u32[]{:S(2)}) %copy-start) | copy-done | bytes 4194328
  14.6 0.0 copy-start.3
  14.6 0.0 copy-start.4
  14.6 0.0 copy-start.5
  14.6 0.0 copy-start.6
  14.6 3.1 %all-to-all-done.lane_ref = bf16[8,16,8,128]{3,2,1,0:T(8,128)(2,1)S(1)} async-done(((bf16[8,16,8,128]{3,2,1,0:T(8,128)(2,1)}), bf16[8,16,8,128]{3,2,1,0:T(8,128)(2,1)S(1)}, u32[]{:S(2)}, u32[]{:S(2)}) %all-to-all-start) | async-done | bytes 262176 | tf_op jit(solution)/shard_map/all_to_all | solution.py:361
  17.7 0.0 collective-permute-start
  17.7 0.0 copy-start.1
  17.7 2.2 %copy-done.1 = bf16[16384,128]{1,0:T(8,128)(2,1)S(1)} copy-done((bf16[16384,128]{1,0:T(8,128)(2,1)S(1)}, bf16[16384,128]{1,0:T(8,128)(2,1)}, u32[]{:S(2)}) %copy-start.1) | copy-done | bytes 4194328
  19.9 0.4 lower.1.refs_6_
  20.3 0.0 collective-permute-done.refs_5_
  20.3 0.0 copy-done.3
  20.3 0.0 copy-done.4
  20.3 0.0 copy-done.5
  20.3 0.0 copy-done.6
  20.3 1.8 %copy-done.2 = bf16[16384,128]{1,0:T(8,128)(2,1)S(1)} copy-done((bf16[16384,128]{1,0:T(8,128)(2,1)S(1)}, bf16[16384,128]{1,0:T(8,128)(2,1)}, u32[]{:S(2)}) %copy-start.2) | copy-done | bytes 4194328
  22.1 2.3 %other_lane.1 = (bf16[720,128]{1,0:T(8,128)(2,1)S(1)}, f32[2,8,8,128]{3,2,1,0:T(8,128)S(1)}) custom-call(s32[1]{0:T(128)} %bitcast.index_ref.refs_0_, s32[2]{0:T(128)S(1)} %copy-done.3, s32[16]{0:T(128)S(1)} %copy-done.4, s32[16]{0:T(128)S(1)} %copy-done.5, s32[2]{0:T(128)S(1)} %copy-done.6, bf16[8,16,8,128]{3,2,1,0:T(8,128)(2,1)S(1)} %collective-permute-done.refs_5_, ...), custom_call_target="tpu_custom_call" | custom-call | tf_op jit(solution)/shard_map/other_lane/pallas_call | solution.py:420
  24.4 0.6 %collective-permute-start.1 = (bf16[720,128]{1,0:T(8,128)(2,1)S(1)}, bf16[720,128]{1,0:T(8,128)(2,1)S(1)}, u32[]{:S(2)}, u32[]{:S(2)}) collective-permute-start(bf16[720,128]{1,0:T(8,128)(2,1)S(1)} %get-tuple-element.30), channel_id=1, source_target_pairs={{0,1},{1,0},{2,3},{3,2},{4,5},{5,4},{6,7},{7,6},{8,9},{9,8},{10,11... | collective-permute-start | bytes 552968 | tf_op jit(solution)/shard_map/ppermute | solution.py:332
  25.0 0.1 add_convert_fusion
  25.1 1.9 %own_lane.1 = (f32[512,128]{1,0:T(8,128)S(1)}, f32[16,128]{1,0:T(8,128)S(1)}) custom-call(s32[1]{0:T(128)} %bitcast.index_ref.refs_0_, s32[2]{0:T(128)S(1)} %copy-done.6, bf16[8,16,8,128]{3,2,1,0:T(8,128)(2,1)S(1)} %all-to-all-done.lane_ref, bf16[256,1024]{1,0:T(8,128)(2,1)S(1)} %get-tuple-element.22.key_ref.refs_10_, ...), custom_call_target="tpu_custom_call" | custom-call | flops 1000000000 | tf_op jit(solution)/shard_map/own_lane/pallas_call | solution.py:445
  27.0 0.0 collective-permute-done.1.got_ref
  27.0 1.0 %join.1 = bf16[8,96,128]{2,1,0:T(8,128)(2,1)} custom-call(f32[512,128]{1,0:T(8,128)S(1)} %get-tuple-element.24.mix_ref, f32[16,128]{1,0:T(8,128)S(1)} %get-tuple-element.25.stat_ref, f32[2,8,8,128]{3,2,1,0:T(8,128)S(1)} %get-tuple-element.29.proj_ref, bf16[720,128]{1,0:T(8,128)(2,1)S(1)} %collective-permute-done.1.got_ref), custom_call_target="tpu_custom_call" | custom-call | tf_op jit(solution)/shard_map/join/pallas_call | solution.py:457
  28.0 3.6 %all-to-all-start.1 = ((bf16[8,96,128]{2,1,0:T(8,128)(2,1)}), bf16[8,96,128]{2,1,0:T(8,128)(2,1)S(1)}, u32[]{:S(2)}, u32[]{:S(2)}) async-start(bf16[8,96,128]{2,1,0:T(8,128)(2,1)} %join.1), calls=%async_computation.1 | async-start | bytes 393216 | tf_op jit(solution)/shard_map/all_to_all | solution.py:361
  31.6 0.1 convert_element_type.11
  31.7 0.1 fusion
  31.8 0.1 pad_maximum_fusion
  31.9 7.9 %all-to-all-done.1.got_ref = bf16[8,96,128]{2,1,0:T(8,128)(2,1)S(1)} async-done(((bf16[8,96,128]{2,1,0:T(8,128)(2,1)}), bf16[8,96,128]{2,1,0:T(8,128)(2,1)S(1)}, u32[]{:S(2)}, u32[]{:S(2)}) %all-to-all-start.1) | async-done | bytes 196640 | tf_op jit(solution)/shard_map/all_to_all | solution.py:361
  39.7 1.1 %merge_states.1 = bf16[2,4,1024]{2,1,0:T(4,128)(2,1)} custom-call(bf16[16,8,128]{2,1,0:T(8,128)(2,1)S(1)} %get-tuple-element.18.own_ref, f32[8,128]{1,0:T(8,128)S(1)} %get-tuple-element.34.cos_ref, f32[8,128]{1,0:T(8,128)S(1)} %get-tuple-element.35.sin_ref, bf16[8,96,128]{2,1,0:T(8,128)(2,1)S(1)} %all-to-all-done.1.got_ref), custom_call_target="tpu_custom_call" | custom-call | tf_op jit(solution)/shard_map/merge_states/pallas_call | solution.py:467
  (2 shorter events, 0.0 us)
Async XLA Ops:
  1.5 16.2 %all-to-all-start = ((bf16[8,16,8,128]{3,2,1,0:T(8,128)(2,1)}), bf16[8,16,8,128]{3,2,1,0:T(8,128)(2,1)S(1)}, u32[]{:S(2)}, u32[]{:S(2)}) async-start(bf16[8,16,8,128]{3,2,1,0:T(8,128)(2,1)} %get-tuple-element.19), calls=%async_computation | async-start | bytes 524288 | tf_op jit(solution)/shard_map/all_to_all | solution.py:361
  12.7 2.0 %copy-start = (bf16[16384,128]{1,0:T(8,128)(2,1)}, bf16[16384,128]{1,0:T(8,128)(2,1)S(1)}, u32[]{:S(2)}) copy-start(bf16[16384,128]{1,0:T(8,128)(2,1)S(1)} %get-tuple-element.26.down_ref.refs_8_) | copy-start | bytes 12582916
  14.6 5.7 %copy-start.3 = (s32[2]{0:T(128)S(1)}, s32[2]{0:T(128)}, u32[]{:S(2)}) copy-start(s32[2]{0:T(128)} %refs_1_.1) | copy-start | bytes 28
  14.6 5.7 %copy-start.4 = (s32[16]{0:T(128)S(1)}, s32[16]{0:T(128)}, u32[]{:S(2)}) copy-start(s32[16]{0:T(128)} %refs_2_.1) | copy-start | bytes 196
  14.6 5.7 %copy-start.5 = (s32[16]{0:T(128)S(1)}, s32[16]{0:T(128)}, u32[]{:S(2)}) copy-start(s32[16]{0:T(128)} %refs_3_.1) | copy-start | bytes 196
  14.6 5.7 %copy-start.6 = (s32[2]{0:T(128)S(1)}, s32[2]{0:T(128)}, u32[]{:S(2)}) copy-start(s32[2]{0:T(128)} %refs_4_.1) | copy-start | bytes 28
  17.7 2.6 %collective-permute-start = (bf16[8,16,8,128]{3,2,1,0:T(8,128)(2,1)S(1)}, bf16[8,16,8,128]{3,2,1,0:T(8,128)(2,1)S(1)}, u32[]{:S(2)}, u32[]{:S(2)}) collective-permute-start(bf16[8,16,8,128]{3,2,1,0:T(8,128)(2,1)S(1)} %all-to-all-done.lane_ref), channel_id=1, source_target_pairs={{0,1},{1,0},{2,3},{3,2},{4,5},{5,4},{6,7},{7,6},{8,9},{9,8},{10,11... | collective-permute-start | bytes 786440 | tf_op jit(solution)/shard_map/ppermute | solution.py:332
  17.7 2.2 %copy-start.1 = (bf16[16384,128]{1,0:T(8,128)(2,1)S(1)}, bf16[16384,128]{1,0:T(8,128)(2,1)}, u32[]{:S(2)}) copy-start(bf16[16384,128]{1,0:T(8,128)(2,1)} %copy-done) | copy-start | bytes 12582916
  19.9 2.2 %copy-start.2 = (bf16[16384,128]{1,0:T(8,128)(2,1)S(1)}, bf16[16384,128]{1,0:T(8,128)(2,1)}, u32[]{:S(2)}) copy-start(bf16[16384,128]{1,0:T(8,128)(2,1)} %copy-done) | copy-start | bytes 12582916
  24.4 2.5 %collective-permute-start.1 = (bf16[720,128]{1,0:T(8,128)(2,1)S(1)}, bf16[720,128]{1,0:T(8,128)(2,1)S(1)}, u32[]{:S(2)}, u32[]{:S(2)}) collective-permute-start(bf16[720,128]{1,0:T(8,128)(2,1)S(1)} %get-tuple-element.30), channel_id=1, source_target_pairs={{0,1},{1,0},{2,3},{3,2},{4,5},{5,4},{6,7},{7,6},{8,9},{9,8},{10,11... | collective-permute-start | bytes 552968 | tf_op jit(solution)/shard_map/ppermute | solution.py:332
  28.0 11.7 %all-to-all-start.1 = ((bf16[8,96,128]{2,1,0:T(8,128)(2,1)}), bf16[8,96,128]{2,1,0:T(8,128)(2,1)S(1)}, u32[]{:S(2)}, u32[]{:S(2)}) async-start(bf16[8,96,128]{2,1,0:T(8,128)(2,1)} %join.1), calls=%async_computation.1 | async-start | bytes 393216 | tf_op jit(solution)/shard_map/all_to_all | solution.py:361

commit v5 on v4

--- a/solution.py
+++ b/solution.py
@@ -27,7 +27,7 @@
     return x.astype(jnp.bfloat16).astype(jnp.float32)
 
 
-def pack_kernel(requests, heads, query_ref, hidden_ref, copies_ref, own_ref, query_buf, hidden_buf, sems):
+def pack_kernel(requests, query_ref, hidden_ref, own_ref, query_buf, hidden_buf, sems):
     loads = [
         pltpu.make_async_copy(query_ref, query_buf, sems.at[0]),
         pltpu.make_async_copy(hidden_ref, hidden_buf, sems.at[1]),
@@ -41,8 +41,6 @@
         for c in range(rows.shape[1] // HEAD_WIDTH):
             tile = rows[:, c * HEAD_WIDTH : (c + 1) * HEAD_WIDTH].astype(jnp.bfloat16)
             own_ref[at] = tile
-            for copy in range(copies_ref.shape[0]):
-                copies_ref[copy, at] = tile
             at += 1
 
 
@@ -72,24 +70,41 @@
         load.wait()
 
 
-def lower(side, heads, index_ref, gathered_ref, down_ref):
-    lanes = gathered_ref.shape[0]
-    depth = down_ref.shape[0] // lanes // 2
+def stream(side, masks, index_ref, down_ref, buffer, sems, at):
+    depth = buffer.shape[1]
+    copies = []
+    for i, mask in enumerate(masks):
+        source = index_ref[0] ^ (2 * mask + side)
+        rows = pl.ds(pl.multiple_of(source * depth, depth), depth)
+        copies.append(pltpu.make_async_copy(down_ref.at[rows], buffer.at[at + i], sems.at[at + i]))
+    for copy in copies:
+        copy.start()
+    return copies
+
+
+def lower(heads, gathered_ref, copies, buffer, at):
     total = None
-    for m in range(lanes):
+    for i, copy in enumerate(copies):
         hidden = jnp.concatenate(
-            [gathered_ref[m, heads + c] for c in range(depth // HEAD_WIDTH)], axis=1
+            [gathered_ref[i, heads + c] for c in range(buffer.shape[1] // HEAD_WIDTH)], axis=1
         )
-        source = 2 * m + (index_ref[0] % 2 ^ side)
-        factor = down_ref[pl.ds(pl.multiple_of(source * depth, depth), depth), :]
-        term = dot(hidden, factor, ((1,), (0,)))
+        copy.wait()
+        term = dot(hidden, buffer[at + i], ((1,), (0,)))
         total = term if total is None else total + term
     return total
 
 
-def attend(requests, tokens, heads, index_ref, length_ref, query_ref, key_ref, value_ref, put):
+def chunks_of(masks, slots):
+    order = sorted(masks)
+    return [order[at : at + slots] for at in range(0, len(order), slots)]
+
+
+def attend(requests, tokens, devices, masks, index_ref, length_ref, query_ref, key_ref, value_ref, put):
     here = index_ref[0]
-    per_lane = query_ref.shape[0] // KEY_HEADS
+    heads = QUERY_HEADS // devices
+    tile = requests * tokens
+    slot_rows = heads * tile
+    per_lane = devices // 2 // KEY_HEADS
     positions = key_ref.shape[0] // requests
     place = lax.broadcasted_iota(jnp.int32, (requests * positions, HEAD_WIDTH), 0)
     column = lax.broadcasted_iota(jnp.int32, (requests * positions, HEAD_WIDTH), 1)
@@ -100,16 +115,22 @@
     allowed = (here * positions + place % positions < limit) & (
         place_request == (column // tokens) % requests
     )
-    first = column < 64
     peaks, totals = [], []
-    for p in range(PAIRS):
-        spots = [2 * p * HEAD_WIDTH, (2 * p + 1) * HEAD_WIDTH]
+    for number, chunk in enumerate(chunks_of(masks, HEAD_WIDTH // slot_rows)):
         query = jnp.concatenate(
-            [query_ref[2 * p * per_lane + t, h] for t in range(2 * per_lane) for h in range(heads)],
-            axis=0,
+            [query_ref[masks.index(mask), h] for mask in chunk for h in range(heads)], axis=0
         )
-        scores = [dot(key_ref[:, at : at + HEAD_WIDTH], query, ((1,), (1,))) for at in spots]
-        scores = jnp.where(first, scores[0], scores[1]) * SCALE
+        key_heads = sorted({mask // per_lane for mask in chunk})
+        spots = [
+            pl.multiple_of(((here // 2 // per_lane) ^ head) * HEAD_WIDTH, HEAD_WIDTH)
+            for head in key_heads
+        ]
+        share = HEAD_WIDTH // len(key_heads)
+        scores = None
+        for i, at in enumerate(spots):
+            part = dot(key_ref[:, pl.ds(at, HEAD_WIDTH)], query, ((1,), (1,)))
+            scores = part if scores is None else jnp.where(column < i * share, scores, part)
+        scores = scores * SCALE
         peak = jnp.max(jnp.where(allowed, scores, NEG_FILL), axis=0, keepdims=True)
         peak = round_bf16(peak)
         weights = jnp.where(allowed, jnp.exp(scores - peak), 0.0)
@@ -117,8 +138,8 @@
         totals.append(jnp.sum(weights, axis=0, keepdims=True))
         weights = jnp.transpose(weights.astype(jnp.bfloat16))
         for i, at in enumerate(spots):
-            mix = dot(weights[64 * i : 64 * i + 64], value_ref[:, at : at + HEAD_WIDTH], ((1,), (0,)))
-            put(p, i, mix)
+            value = value_ref[:, pl.ds(at, HEAD_WIDTH)]
+            put(number, i * share, dot(weights[i * share : (i + 1) * share], value, ((1,), (0,))))
     return peaks, totals
 
 
@@ -130,16 +151,80 @@
     return out
 
 
-def lower_kernel(heads, index_ref, lane_ref, down_ref, out_ref):
-    out_ref[...] = lower(0, heads, index_ref, lane_ref, down_ref)
-
-
-def other_kernel(requests, tokens, heads, *refs):
+def own_kernel(
+    sizes, masks, with_lora, index_ref, length_ref, lane_ref, key_ref, value_ref, *refs
+):
+    requests, tokens, devices = sizes
+    if with_lora:
+        down_ref, mix_ref, stat_ref, lowered_ref, buffer, sems = refs
+        copies = stream(0, masks, index_ref, down_ref, buffer, sems, 0)
+    else:
+        mix_ref, stat_ref = refs
+
+    def put(chunk, row, mix):
+        at = chunk * 128 + row
+        mix_ref[at : at + mix.shape[0]] = mix
+
+    peaks, totals = attend(
+        requests, tokens, devices, masks, index_ref, length_ref, lane_ref, key_ref, value_ref, put
+    )
+    stat_ref[...] = rows_of(peaks + totals, 8)
+    if with_lora:
+        lowered_ref[...] = lower(QUERY_HEADS // devices, lane_ref, copies, buffer, 0)
+
+
+def early_kernel(sizes, masks, *refs):
+    (index_ref, length_ref, lane_ref, other_ref, key_ref, value_ref, down_ref) = refs[:7]
+    (send_ref, stat_ref, lowered_ref, buffer, sems) = refs[7:]
+    requests, tokens, devices = sizes
+    heads = QUERY_HEADS // devices
+    count = len(masks)
+    lane_copies = stream(0, masks, index_ref, down_ref, buffer, sems, 0)
+    other_copies = stream(1, masks, index_ref, down_ref, buffer, sems, count)
+
+    def put(chunk, row, mix):
+        at = chunk * 128 + row
+        send_ref[at : at + mix.shape[0]] = mix.astype(jnp.bfloat16)
+
+    peaks, totals = attend(
+        requests, tokens, devices, masks, index_ref, length_ref, other_ref, key_ref, value_ref, put
+    )
+    stat_ref[...] = rows_of(peaks + totals, 8)
+    lowered_ref[...] = lower(heads, lane_ref, lane_copies, buffer, 0) + lower(
+        heads, other_ref, other_copies, buffer, count
+    )
+
+
+def late_kernel(sizes, masks, *refs):
     (index_ref, adapter_ref, rank_ref, pool_ref, length_ref) = refs[:5]
-    (other_ref, lowered_ref, base_ref, down_ref, up_ref, key_ref, value_ref) = refs[5:12]
-    (send_ref, proj_ref) = refs[12:]
+    (other_ref, key_ref, value_ref, down_ref, base_ref, up_ref) = refs[5:11]
+    (early_ref, early_stat_ref, early_lowered_ref, own_lowered_ref) = refs[11:15]
+    (send_ref, proj_ref, buffer, sems) = refs[15:]
+    requests, tokens, devices = sizes
     rows = requests * tokens
-    lowered = lowered_ref[...] + lower(1, heads, index_ref, other_ref, down_ref)
+    copies = stream(1, masks, index_ref, down_ref, buffer, sems, 0)
+    mix_total = KEY_HEADS * 64
+    half = mix_total // 2
+    step = KEY_HEADS * rows
+    send_ref[:half] = early_ref[...]
+
+    def put(chunk, row, mix):
+        at = half + chunk * 128 + row
+        send_ref[at : at + mix.shape[0]] = mix.astype(jnp.bfloat16)
+
+    peaks, totals = attend(
+        requests, tokens, devices, masks, index_ref, length_ref, other_ref, key_ref, value_ref, put
+    )
+    early = early_stat_ref[...]
+    count = PAIRS // 2
+    peaks = [early[i : i + 1] for i in range(count)] + peaks
+    totals = [early[count + i : count + i + 1] for i in range(count)] + totals
+    highs = [round_bf16(total) for total in totals]
+    lows = [total - high for total, high in zip(totals, highs)]
+    send_ref[mix_total + 3 * step :] = rows_of(peaks + highs + lows, STAT_ROWS).astype(jnp.bfloat16)
+
+    lowered = early_lowered_ref[...] + own_lowered_ref[...]
+    lowered += lower(QUERY_HEADS // devices, other_ref, copies, buffer, 0)
     row_request = lax.broadcasted_iota(jnp.int32, (rows, 1), 0) // tokens
     ranks = jnp.zeros((rows, 1), jnp.int32)
     owners = jnp.zeros((rows, 1), jnp.int32)
@@ -156,8 +241,6 @@
         at = j * HEAD_WIDTH
         proj_ref[0, j] = projected[:, at : at + HEAD_WIDTH]
         proj_ref[1, j] = projected[:, split + at : split + at + HEAD_WIDTH]
-    mix_total = KEY_HEADS * 64
-    step = KEY_HEADS * rows
     keys = proj_ref[0].reshape(step, HEAD_WIDTH)
     high = keys.astype(jnp.bfloat16)
     send_ref[mix_total : mix_total + step] = high
@@ -168,48 +251,30 @@
         proj_ref[1].reshape(step, HEAD_WIDTH).astype(jnp.bfloat16)
     )
 
-    def put(p, i, mix):
-        at = p * 128 + i * 64
-        send_ref[at : at + 64] = mix.astype(jnp.bfloat16)
-
-    peaks, totals = attend(
-        requests, tokens, heads, index_ref, length_ref, other_ref, key_ref, value_ref, put
-    )
-    highs = [round_bf16(total) for total in totals]
-    lows = [total - high for total, high in zip(totals, highs)]
-    send_ref[mix_total + 3 * step :] = rows_of(peaks + highs + lows, STAT_ROWS).astype(jnp.bfloat16)
-
-
-def own_kernel(
-    requests, tokens, heads, index_ref, length_ref, lane_ref, key_ref, value_ref, mix_ref, stat_ref
-):
-    def put(p, i, mix):
-        at = p * 128 + i * 64
-        mix_ref[at : at + 64] = mix
-
-    peaks, totals = attend(
-        requests, tokens, heads, index_ref, length_ref, lane_ref, key_ref, value_ref, put
-    )
-    stat_ref[...] = rows_of(peaks + totals, STAT_ROWS)
-
-
-def join_kernel(devices, requests, tokens, mix_ref, stat_ref, proj_ref, got_ref, packet_ref):
+
+def join_kernel(sizes, chunks, index_ref, *refs):
+    (first_ref, second_ref, first_stat_ref, second_stat_ref, proj_ref, got_ref) = refs[:6]
+    packet_ref, tail_ref = refs[6:]
+    requests, tokens, devices = sizes
+    chip = index_ref[0] // 2
     rows = requests * tokens
     heads = QUERY_HEADS // devices
     mix_rows = heads * rows
-    per_lane = devices // KEY_HEADS // 2
+    per_lane = devices // 2 // KEY_HEADS
     mix_total = KEY_HEADS * 64
     step = KEY_HEADS * rows
+    count = PAIRS // 2
     got = got_ref[mix_total + 3 * step :, :].astype(jnp.float32)
-    own = stat_ref[...]
-    own_peak, got_peak = own[:PAIRS], got[:PAIRS]
+    first, second = first_stat_ref[...], second_stat_ref[...]
+    own_peak = jnp.concatenate([first[:count], second[:count]], axis=0)
+    own_total = jnp.concatenate([first[count:PAIRS], second[count:PAIRS]], axis=0)
+    got_peak = got[:PAIRS]
     peak = jnp.maximum(own_peak, got_peak)
     own_factor = jnp.exp(own_peak - peak)
     got_factor = jnp.exp(got_peak - peak)
-    total = own_factor * own[PAIRS : 2 * PAIRS] + got_factor * (
-        got[PAIRS : 2 * PAIRS] + got[2 * PAIRS : 3 * PAIRS]
-    )
+    total = own_factor * own_total + got_factor * (got[PAIRS : 2 * PAIRS] + got[2 * PAIRS : 3 * PAIRS])
     high = round_bf16(total)
+    low = total - high
     filler = jnp.zeros((128 - 2 * PAIRS, 128), jnp.float32)
     table = jnp.transpose(jnp.concatenate([own_factor, got_factor, filler], axis=0))
     keys = got_ref[mix_total : mix_total + step].astype(jnp.float32) + got_ref[
@@ -219,30 +284,30 @@
     values = got_ref[mix_total + 2 * step : mix_total + 3 * step].astype(jnp.float32)
     values += proj_ref[1].reshape(step, HEAD_WIDTH)
     keys_high = round_bf16(keys)
-    keys_low = keys - keys_high
+    for j in range(KEY_HEADS):
+        own = slice(j * rows, (j + 1) * rows)
+        tail_ref[j, :rows] = keys_high[own]
+        tail_ref[j, rows : 2 * rows] = (keys - keys_high)[own]
+        tail_ref[j, 2 * rows :] = values[own]
     stat_row = lax.broadcasted_iota(jnp.int32, (rows, HEAD_WIDTH), 0)
-    for p in range(PAIRS):
-        mix = mix_ref[p * 128 : p * 128 + 128] * table[:, p : p + 1] + got_ref[
-            p * 128 : p * 128 + 128
-        ].astype(jnp.float32) * table[:, PAIRS + p : PAIRS + p + 1]
+    for c, chunk in enumerate(chunks):
+        own_ref, at = (first_ref, c * 128) if c < count else (second_ref, (c - count) * 128)
+        mix = own_ref[at : at + 128] * table[:, c : c + 1] + got_ref[
+            c * 128 : c * 128 + 128
+        ].astype(jnp.float32) * table[:, PAIRS + c : PAIRS + c + 1]
         stats = jnp.where(
             stat_row == 0,
-            peak[p : p + 1],
+            peak[c : c + 1],
             jnp.where(
-                stat_row == 1,
-                high[p : p + 1],
-                jnp.where(stat_row == 2, (total - high)[p : p + 1], 0.0),
+                stat_row == 1, high[c : c + 1], jnp.where(stat_row == 2, low[c : c + 1], 0.0)
             ),
         )
-        for t in range(2 * per_lane):
-            j = 2 * p + t // per_lane
-            out_ref = packet_ref.at[2 * p * per_lane + t]
-            out_ref[:mix_rows] = mix[t * mix_rows : (t + 1) * mix_rows].astype(jnp.bfloat16)
+        for t, mask in enumerate(chunk):
+            to = chip ^ mask
             shifted = stats if t == 0 else pltpu.roll(stats, HEAD_WIDTH - t * mix_rows, 1)
-            own = slice(j * rows, (j + 1) * rows)
-            out_ref[mix_rows:] = jnp.concatenate(
-                [keys_high[own], keys_low[own], values[own], shifted], axis=0
-            ).astype(jnp.bfloat16)
+            tail = jnp.concatenate([tail_ref[to // per_lane], shifted], axis=0)
+            packet_ref[to, :mix_rows] = mix[t * mix_rows : (t + 1) * mix_rows].astype(jnp.bfloat16)
+            packet_ref[to, mix_rows:] = tail.astype(jnp.bfloat16)
 
 
 def merge_kernel(devices, requests, tokens, own_ref, cos_ref, sin_ref, got_ref, out_ref):
@@ -361,14 +426,11 @@
         return lax.all_to_all(x, "tensor", 0, 0, axis_index_groups=lane_groups, tiled=True)
 
     tile_shape = (tiles, rows, HEAD_WIDTH)
-    copies, own = pl.pallas_call(
-        functools.partial(pack_kernel, requests, heads),
-        out_shape=(
-            jax.ShapeDtypeStruct((lanes,) + tile_shape, jnp.bfloat16),
-            pltpu.VMEM(tile_shape, jnp.bfloat16),
-        ),
+    own = pl.pallas_call(
+        functools.partial(pack_kernel, requests),
+        out_shape=jax.ShapeDtypeStruct(tile_shape, jnp.bfloat16),
         in_specs=[hbm()] * 2,
-        out_specs=(vmem(),) * 2,
+        out_specs=vmem(),
         scratch_shapes=[
             pltpu.VMEM(queries.shape, jnp.bfloat16),
             pltpu.VMEM(hidden.shape, jnp.bfloat16),
@@ -377,91 +439,130 @@
         compiler_params=pltpu.CompilerParams(vmem_limit_bytes=4 * MIB),
         name="pack",
     )(pinned(queries), pinned(hidden))
-    lane = exchange(copies)
-
     flat = requests * cached_key_rows.shape[1]
     big = (
-        adapter_down_weight[0],
         cached_key_rows.reshape(flat, -1),
         cached_value_rows.reshape(flat, -1),
         adapter_up_weight[0],
     )
     out_width = key_value_weight.shape[1]
     parts = 4 if width % (4 * HEAD_WIDTH) == 0 else 1
-    base, down, keys, values, up = pl.pallas_call(
+    base, keys, values, up = pl.pallas_call(
         functools.partial(base_kernel, heads),
         out_shape=(pltpu.VMEM((rows, out_width), jnp.float32),)
         + tuple(pltpu.VMEM(x.shape, x.dtype) for x in big),
-        in_specs=[vmem()] + [hbm()] * 5,
-        out_specs=(vmem(),) * 5,
+        in_specs=[vmem()] + [hbm()] * 4,
+        out_specs=(vmem(),) * 4,
         scratch_shapes=[
             pltpu.VMEM((parts, width // parts, out_width), jnp.bfloat16),
-            pltpu.SemaphoreType.DMA((parts + 4,)),
+            pltpu.SemaphoreType.DMA((parts + 3,)),
         ],
         compiler_params=pltpu.CompilerParams(vmem_limit_bytes=12 * MIB),
         cost_estimate=cost(10**9, 0),
         name="base",
     )(own, pinned(key_value_weight), *[pinned(x) for x in big])
+    down = pinned(adapter_down_weight[0])
+    sizes = (requests, tokens, devices)
+    index = here.reshape(1).astype(jnp.int32)
+    rank = adapter_down_weight.shape[2]
+    mix_total = KEY_HEADS * 64
+
+    masks, lane = [0], own[None]
+    bit = lanes // 2
+    while bit > 1:
+        masks += [mask ^ bit for mask in masks]
+        lane = jnp.concatenate([lane, swap(lane, devices, 2 * bit)], axis=0)
+        bit //= 2
+    late_masks = [mask ^ 1 for mask in masks]
     lane, base = lax.optimization_barrier((lane, base))
+    late_lane = swap(lane, devices, 2)
     other = swap(lane, devices, 1)
-
-    index = here.reshape(1).astype(jnp.int32)
-    lowered = pl.pallas_call(
-        functools.partial(lower_kernel, heads),
-        out_shape=pltpu.VMEM((rows, down.shape[1]), jnp.float32),
-        in_specs=[smem()] + [vmem()] * 2,
-        out_specs=vmem(),
-        compiler_params=pltpu.CompilerParams(vmem_limit_bytes=12 * MIB),
-        cost_estimate=cost(10**9, 0),
-        name="lower",
-    )(index, lane, down)
-    mix_total = KEY_HEADS * 64
+    slot_count = HEAD_WIDTH // mix_rows
+    chunks = chunks_of(masks, slot_count) + chunks_of(late_masks, slot_count)
+
+    def streamed(count):
+        return [pltpu.VMEM((count, width, rank), jnp.bfloat16), pltpu.SemaphoreType.DMA((count,))]
+
+    def call(kernel, operands, in_specs, out_shape, scratch, name):
+        return pl.pallas_call(
+            kernel,
+            out_shape=tuple(out_shape),
+            in_specs=in_specs,
+            out_specs=(vmem(),) * len(out_shape),
+            scratch_shapes=scratch,
+            compiler_params=pltpu.CompilerParams(vmem_limit_bytes=12 * MIB),
+            cost_estimate=cost(10**9, 0),
+            name=name,
+        )(*operands)
+
+    half_mix = pltpu.VMEM((mix_total // 2, HEAD_WIDTH), jnp.float32)
+    half_send = pltpu.VMEM((mix_total // 2, HEAD_WIDTH), jnp.bfloat16)
+    half_stat = pltpu.VMEM((8, HEAD_WIDTH), jnp.float32)
+    lowered = pltpu.VMEM((rows, rank), jnp.float32)
+    first_mix, first_stats = call(
+        functools.partial(own_kernel, sizes, masks, False),
+        (index, lengths, lane, keys, values),
+        [smem()] * 2 + [vmem()] * 3,
+        [half_mix, half_stat],
+        [],
+        "own_first",
+    )
+    early_send, early_stats, early_lowered = call(
+        functools.partial(early_kernel, sizes, masks),
+        (index, lengths, lane, other, keys, values, down),
+        [smem()] * 2 + [vmem()] * 4 + [hbm()],
+        [half_send, half_stat, lowered],
+        streamed(2 * len(masks)),
+        "other_first",
+    )
+    late_lane, early_send = lax.optimization_barrier((late_lane, early_send))
+    late_other = swap(late_lane, devices, 1)
+    second_mix, second_stats, own_lowered = call(
+        functools.partial(own_kernel, sizes, late_masks, True),
+        (index, lengths, late_lane, keys, values, down),
+        [smem()] * 2 + [vmem()] * 3 + [hbm()],
+        [half_mix, half_stat, lowered],
+        streamed(len(masks)),
+        "own_second",
+    )
     send_rows = mix_total + 3 * KEY_HEADS * rows + STAT_ROWS
-    send, proj = pl.pallas_call(
-        functools.partial(other_kernel, requests, tokens, heads),
-        out_shape=(
+    send, proj = call(
+        functools.partial(late_kernel, sizes, late_masks),
+        (
+            index,
+            request_adapter,
+            adapter_rank_list,
+            adapter_pool_row,
+            lengths,
+            late_other,
+            keys,
+            values,
+            down,
+            base,
+            up,
+            early_send,
+            early_stats,
+            early_lowered,
+            own_lowered,
+        ),
+        [smem()] * 5 + [vmem()] * 3 + [hbm()] + [vmem()] * 6,
+        [
             pltpu.VMEM((send_rows, HEAD_WIDTH), jnp.bfloat16),
             pltpu.VMEM((2, KEY_HEADS, rows, HEAD_WIDTH), jnp.float32),
-        ),
-        in_specs=[smem()] * 5 + [vmem()] * 7,
-        out_specs=(vmem(),) * 2,
-        compiler_params=pltpu.CompilerParams(vmem_limit_bytes=12 * MIB),
-        name="other_lane",
-    )(
-        index,
-        request_adapter,
-        adapter_rank_list,
-        adapter_pool_row,
-        lengths,
-        other,
-        lowered,
-        base,
-        down,
-        up,
-        keys,
-        values,
+        ],
+        streamed(len(masks)),
+        "other_second",
     )
     got = swap(send, devices, 1)
-    mix, stats = pl.pallas_call(
-        functools.partial(own_kernel, requests, tokens, heads),
-        out_shape=(
-            pltpu.VMEM((mix_total, HEAD_WIDTH), jnp.float32),
-            pltpu.VMEM((STAT_ROWS, HEAD_WIDTH), jnp.float32),
-        ),
-        in_specs=[smem()] * 2 + [vmem()] * 3,
-        out_specs=(vmem(),) * 2,
-        compiler_params=pltpu.CompilerParams(vmem_limit_bytes=8 * MIB),
-        cost_estimate=cost(10**9, 0),
-        name="own_lane",
-    )(index, lengths, lane, keys, values)
     packets = pl.pallas_call(
-        functools.partial(join_kernel, devices, requests, tokens),
+        functools.partial(join_kernel, sizes, chunks),
         out_shape=jax.ShapeDtypeStruct((lanes, mix_rows + 4 * rows, HEAD_WIDTH), jnp.bfloat16),
-        in_specs=[vmem()] * 4,
+        in_specs=[smem()] + [vmem()] * 6,
         out_specs=vmem(),
+        scratch_shapes=[pltpu.VMEM((KEY_HEADS, 3 * rows, HEAD_WIDTH), jnp.float32)],
         compiler_params=pltpu.CompilerParams(vmem_limit_bytes=8 * MIB),
         name="join",
-    )(mix, stats, proj, got)
+    )(index, first_mix, second_mix, first_stats, second_stats, proj, got)
     packets = exchange(packets)
     cosine, sine = rotation(lengths, tokens)
     return pl.pallas_call(

time: 41.3 us -> 41.5 us (level)
  local copies, waits for them, and re-layouts: 6 us -> 0.1 us
  Pallas kernels: 12.1 us -> 15.2 us
  starting transfers between devices: 11.5 us -> 14.2 us
    ppermute x2 -> x6, starting transfers between devices: 0.58 us -> 8.16 us  [swap(): return lax.ppermute(x, 'tensor', [(d, d ^ bit) for d in range(devices)])]
    unnamed x14 -> x8, local copies, waits for them, and re-layouts: 5.91 us -> 0.02 us
    all_to_all x2 -> x1, starting transfers between devices: 10.9 us -> 6.05 us  [exchange(): lax.all_to_all(x, 'tensor', 0, 0, axis_index_groups=lane_groups, tiled=True)]
    pallas_call x5 -> x6, Pallas kernels: 7.11 us -> 11.4 us  [the longest x4 9.58 us: call(): pl.pallas_call(kernel, out_shape=tuple(out_shape), in_specs=in_specs, out...]
    ppermute x2 -> x6, waiting for transfers between devices: 0.01 us -> 3.38 us  [swap(): return lax.ppermute(x, 'tensor', [(d, d ^ bit) for d in range(devices)])]
    all_to_all x2 -> x1, waiting for transfers between devices: 11 us -> 7.89 us  [exchange(): lax.all_to_all(x, 'tensor', 0, 0, axis_index_groups=lane_groups, tiled=True)]
    pallas_call x1, Pallas kernels: 3.86 us -> 2.68 us  [per_device(): pl.pallas_call(functools.partial(base_kernel, heads), out_shape=(pltpu.VM...]
  transfers between devices with their start and end apart: 4 -> 7, of which waited for: 2 -> 3; matrix products, arithmetic and copies ran while one was open for 1% -> 1% of each run, Pallas kernels for 15% -> 23%
where the time goes in v5:
time: 41.5 us; the launch traced here: 41.2 us
  Pallas kernels  15.2 us (37%)
  starting transfers between devices  14.2 us (34%)
  waiting for transfers between devices  11.3 us (27%)
    pallas_call x4, Pallas kernels, call(): pl.pallas_call(kernel, out_shape=tuple(out_shape), in_specs=in_specs, out...  9.58 us
    ppermute x6, starting transfers between devices, swap(): return lax.ppermute(x, 'tensor', [(d, d ^ bit) for d in range(devices)])  8.16 us
    all_to_all x1, waiting for transfers between devices, exchange(): lax.all_to_all(x, 'tensor', 0, 0, axis_index_groups=lane_groups, tiled=True)  7.89 us
    all_to_all x1, starting transfers between devices, exchange(): lax.all_to_all(x, 'tensor', 0, 0, axis_index_groups=lane_groups, tiled=True)  6.05 us
    ppermute x6, waiting for transfers between devices, swap(): return lax.ppermute(x, 'tensor', [(d, d ^ bit) for d in range(devices)])  3.38 us
    pallas_call x1, Pallas kernels, per_device(): pl.pallas_call(functools.partial(base_kernel, heads), out_shape=(pltpu.VM...  2.68 us
    pallas_call x1, Pallas kernels, per_device(): pl.pallas_call(functools.partial(merge_kernel, devices, requests, tokens)...  1.12 us
    pallas_call x1, Pallas kernels, per_device(): pl.pallas_call(functools.partial(join_kernel, sizes, chunks), out_shape=j...  1.04 us
  transfers between devices with their start and end apart: 7, of which 3 were waited for; matrix products, arithmetic and copies ran while one was open for 1% of the time, Pallas kernels for 23%

profile of v5, /device:TPU:0, one launch (start us, length us, event | category | flops | bytes accessed | tf_op | source)
XLA Modules:
  0.0 41.2 jit_solution(14247190893198069710)
XLA Ops:
  0.0 0.0 copy-start
  0.0 0.8 %pack.1.own_ref = bf16[16,8,128]{2,1,0:T(8,128)(2,1)S(1)} custom-call(bf16[2,4,1024]{2,1,0:T(4,128)(2,1)} %query_ref.1, bf16[2,4,1024]{2,1,0:T(4,128)(2,1)} %hidden_ref.1), custom_call_target="tpu_custom_call" | custom-call | tf_op jit(solution)/shard_map/pack/pallas_call | solution.py:429
  0.8 4.1 %collective-permute-start = (bf16[1,16,8,128]{3,2,1,0:T(8,128)(2,1)S(1)}, bf16[1,16,8,128]{3,2,1,0:T(8,128)(2,1)S(1)}, u32[]{:S(2)}, u32[]{:S(2)}) collective-permute-start(bf16[1,16,8,128]{3,2,1,0:T(8,128)(2,1)S(1)} %bitcast.6), channel_id=1, source_target_pairs={{0,8},{1,9},{2,10},{3,11},{4,12},{5,13},{6,14},{7,15},{8,0},{9,1},... | collective-permute-start | bytes 98312 | tf_op jit(solution)/shard_map/ppermute | solution.py:397
  4.9 2.2 %collective-permute-done = bf16[1,16,8,128]{3,2,1,0:T(8,128)(2,1)S(1)} collective-permute-done((bf16[1,16,8,128]{3,2,1,0:T(8,128)(2,1)S(1)}, bf16[1,16,8,128]{3,2,1,0:T(8,128)(2,1)S(1)}, u32[]{:S(2)}, u32[]{:S(2)}) %collective-permute-start) | collective-permute-done | bytes 32800 | tf_op jit(solution)/shard_map/ppermute | solution.py:397
  7.1 1.6 %collective-permute-start.1 = (bf16[2,16,8,128]{3,2,1,0:T(8,128)(2,1)S(1)}, bf16[2,16,8,128]{3,2,1,0:T(8,128)(2,1)S(1)}, u32[]{:S(2)}, u32[]{:S(2)}) collective-permute-start(bf16[2,16,8,128]{3,2,1,0:T(8,128)(2,1)S(1)} %pad_maximum_fusion.1), channel_id=1, source_target_pairs={{0,4},{1,5},{2,6},{3,7},{4,0},{5,1},{6,2},{7,3},{8,12},{9,13},{10,... | collective-permute-start | bytes 196616 | tf_op jit(solution)/shard_map/ppermute | solution.py:397
  8.8 2.7 %base.1 = (f32[8,2048]{1,0:T(8,128)S(1)}, bf16[256,1024]{1,0:T(8,128)(2,1)S(1)}, bf16[256,1024]{1,0:T(8,128)(2,1)S(1)}, bf16[128,2048]{1,0:T(8,128)(2,1)S(1)}) custom-call(bf16[16,8,128]{2,1,0:T(8,128)(2,1)S(1)} %pack.1.own_ref, bf16[1024,2048]{1,0:T(8,128)(2,1)} %weight_ref.1, bf16[256,1024]{1,0:T(8,128)(2,1)} %bitcast.12, bf16[256,1024]{1,0:T(8,128)(2,1)} %bitcast.13, ...), custom_call_target="tpu_custom_call" | custom-call | flops 1000000000 | tf_op jit(solution)/shard_map/base/pallas_call | solution.py:450
  11.4 0.0 collective-permute-done.1
  11.5 0.1 collective-permute-start.3
  11.6 1.8 %collective-permute-start.2 = (bf16[4,16,8,128]{3,2,1,0:T(8,128)(2,1)S(1)}, bf16[4,16,8,128]{3,2,1,0:T(8,128)(2,1)S(1)}, u32[]{:S(2)}, u32[]{:S(2)}) collective-permute-start(bf16[4,16,8,128]{3,2,1,0:T(8,128)(2,1)S(1)} %pad_maximum_fusion.lane_ref.refs_2_), channel_id=1, source_target_pairs={{0,2},{1,3},{2,0},{3,1},{4,6},{5,7},{6,4},{7,5},{8,10},{9,11},{10,... | collective-permute-start | bytes 393224 | tf_op jit(solution)/shard_map/ppermute | solution.py:397
  13.4 0.0 collective-permute-done.3.refs_3_
  13.4 0.0 copy-done
  13.4 0.0 copy-start.3
  13.4 3.0 %other_first.1 = (bf16[256,128]{1,0:T(8,128)(2,1)S(1)}, f32[8,128]{1,0:T(8,128)S(1)}, f32[8,128]{1,0:T(8,128)S(1)}) custom-call(s32[1]{0:T(128)} %bitcast.index_ref.refs_0_, s32[2]{0:T(128)S(1)} %copy-done, bf16[4,16,8,128]{3,2,1,0:T(8,128)(2,1)S(1)} %pad_maximum_fusion.lane_ref.refs_2_, bf16[4,16,8,128]{3,2,1,0:T(8,128)(2,1)S(1)} %collective-permute-done.3.refs_3_, ...), custom_call_target="tpu_custom_call" | custom-call | flops 1000000000 | tf_op jit(solution)/shard_map/other_first/pallas_call | solution.py:487
  16.4 1.1 %collective-permute-done.2.lane_ref = bf16[4,16,8,128]{3,2,1,0:T(8,128)(2,1)S(1)} collective-permute-done((bf16[4,16,8,128]{3,2,1,0:T(8,128)(2,1)S(1)}, bf16[4,16,8,128]{3,2,1,0:T(8,128)(2,1)S(1)}, u32[]{:S(2)}, u32[]{:S(2)}) %collective-permute-start.2) | collective-permute-done | bytes 131104 | tf_op jit(solution)/shard_map/ppermute | solution.py:397
  17.5 0.0 collective-permute-start.4
  17.5 2.5 %own_second.1 = (f32[256,128]{1,0:T(8,128)S(1)}, f32[8,128]{1,0:T(8,128)S(1)}, f32[8,128]{1,0:T(8,128)S(1)}) custom-call(s32[1]{0:T(128)} %bitcast.index_ref.refs_0_, s32[2]{0:T(128)S(1)} %copy-done, bf16[4,16,8,128]{3,2,1,0:T(8,128)(2,1)S(1)} %collective-permute-done.2.lane_ref, bf16[256,1024]{1,0:T(8,128)(2,1)S(1)} %get-tuple-element.25.key_ref.refs_4_.refs_6_, ...), custom_call_target="tpu_custom_call" | custom-call | flops 1000000000 | tf_op jit(solution)/shard_map/own_second/pallas_call | solution.py:487
  20.0 0.0 collective-permute-done.4.refs_5_
  20.0 0.0 copy-done.1
  20.0 0.0 copy-done.2
  20.0 0.0 copy-done.3
  20.0 2.9 %other_second.1 = (bf16[720,128]{1,0:T(8,128)(2,1)S(1)}, f32[2,8,8,128]{3,2,1,0:T(8,128)S(1)}) custom-call(s32[1]{0:T(128)} %bitcast.index_ref.refs_0_, s32[2]{0:T(128)S(1)} %copy-done.1, s32[16]{0:T(128)S(1)} %copy-done.2, s32[16]{0:T(128)S(1)} %copy-done.3, s32[2]{0:T(128)S(1)} %copy-done, bf16[4,16,8,128]{3,2,1,0:T(8,128)(2,1)S(1)} %collective-permute-done.4.refs_5_, ...), custom_call_target="tpu_custom_call" | custom-call | flops 1000000000 | tf_op jit(solution)/shard_map/other_second/pallas_call | solution.py:487
  22.9 0.6 %collective-permute-start.5 = (bf16[720,128]{1,0:T(8,128)(2,1)S(1)}, bf16[720,128]{1,0:T(8,128)(2,1)S(1)}, u32[]{:S(2)}, u32[]{:S(2)}) collective-permute-start(bf16[720,128]{1,0:T(8,128)(2,1)S(1)} %get-tuple-element.40), channel_id=1, source_target_pairs={{0,1},{1,0},{2,3},{3,2},{4,5},{5,4},{6,7},{7,6},{8,9},{9,8},{10,11... | collective-permute-start | bytes 552968 | tf_op jit(solution)/shard_map/ppermute | solution.py:397
  23.4 0.1 add_convert_fusion
  23.5 1.3 %own_first.1 = (f32[256,128]{1,0:T(8,128)S(1)}, f32[8,128]{1,0:T(8,128)S(1)}) custom-call(s32[1]{0:T(128)} %bitcast.index_ref.refs_0_, s32[2]{0:T(128)S(1)} %copy-done, bf16[4,16,8,128]{3,2,1,0:T(8,128)(2,1)S(1)} %pad_maximum_fusion.lane_ref.refs_2_, bf16[256,1024]{1,0:T(8,128)(2,1)S(1)} %get-tuple-element.25.key_ref.refs_4_.refs_6_, ...), custom_call_target="tpu_custom_call" | custom-call | flops 1000000000 | tf_op jit(solution)/shard_map/own_first/pallas_call | solution.py:487
  24.8 0.0 collective-permute-done.5.refs_5_
  24.8 1.0 %join.1 = bf16[8,96,128]{2,1,0:T(8,128)(2,1)} custom-call(s32[1]{0:T(128)} %bitcast.index_ref.refs_0_, f32[256,128]{1,0:T(8,128)S(1)} %get-tuple-element.27.refs_0_, f32[256,128]{1,0:T(8,128)S(1)} %get-tuple-element.30.refs_1_, f32[8,128]{1,0:T(8,128)S(1)} %get-tuple-element.31.refs_2_, f32[8,128]{1,0:T(8,128)S(1)} %get-tuple-element.32.refs_3_, ...), custom_call_target="tpu_custom_call" | custom-call | tf_op jit(solution)/shard_map/join/pallas_call | solution.py:557
  25.8 6.0 %all-to-all-start = ((bf16[8,96,128]{2,1,0:T(8,128)(2,1)}), bf16[8,96,128]{2,1,0:T(8,128)(2,1)S(1)}, u32[]{:S(2)}, u32[]{:S(2)}) async-start(bf16[8,96,128]{2,1,0:T(8,128)(2,1)} %join.1), calls=%async_computation | async-start | bytes 393216 | tf_op jit(solution)/shard_map/all_to_all | solution.py:426
  31.9 0.1 convert_element_type.11
  32.0 0.1 fusion
  32.1 0.1 pad_maximum_fusion.2
  32.2 7.9 %all-to-all-done.got_ref = bf16[8,96,128]{2,1,0:T(8,128)(2,1)S(1)} async-done(((bf16[8,96,128]{2,1,0:T(8,128)(2,1)}), bf16[8,96,128]{2,1,0:T(8,128)(2,1)S(1)}, u32[]{:S(2)}, u32[]{:S(2)}) %all-to-all-start) | async-done | bytes 196640 | tf_op jit(solution)/shard_map/all_to_all | solution.py:426
  40.1 1.1 %merge_states.1 = bf16[2,4,1024]{2,1,0:T(4,128)(2,1)} custom-call(bf16[16,8,128]{2,1,0:T(8,128)(2,1)S(1)} %pack.1.own_ref, f32[8,128]{1,0:T(8,128)S(1)} %get-tuple-element.44.cos_ref, f32[8,128]{1,0:T(8,128)S(1)} %get-tuple-element.45.sin_ref, bf16[8,96,128]{2,1,0:T(8,128)(2,1)S(1)} %all-to-all-done.got_ref), custom_call_target="tpu_custom_call" | custom-call | tf_op jit(solution)/shard_map/merge_states/pallas_call | solution.py:568
  (5 shorter events, 0.0 us)
Async XLA Ops:
  0.0 13.4 %copy-start = (s32[2]{0:T(128)S(1)}, s32[2]{0:T(128)}, u32[]{:S(2)}) copy-start(s32[2]{0:T(128)} %refs_4_.1) | copy-start | bytes 28
  0.8 6.3 %collective-permute-start = (bf16[1,16,8,128]{3,2,1,0:T(8,128)(2,1)S(1)}, bf16[1,16,8,128]{3,2,1,0:T(8,128)(2,1)S(1)}, u32[]{:S(2)}, u32[]{:S(2)}) collective-permute-start(bf16[1,16,8,128]{3,2,1,0:T(8,128)(2,1)S(1)} %bitcast.6), channel_id=1, source_target_pairs={{0,8},{1,9},{2,10},{3,11},{4,12},{5,13},{6,14},{7,15},{8,0},{9,1},... | collective-permute-start | bytes 98312 | tf_op jit(solution)/shard_map/ppermute | solution.py:397
  7.1 4.3 %collective-permute-start.1 = (bf16[2,16,8,128]{3,2,1,0:T(8,128)(2,1)S(1)}, bf16[2,16,8,128]{3,2,1,0:T(8,128)(2,1)S(1)}, u32[]{:S(2)}, u32[]{:S(2)}) collective-permute-start(bf16[2,16,8,128]{3,2,1,0:T(8,128)(2,1)S(1)} %pad_maximum_fusion.1), channel_id=1, source_target_pairs={{0,4},{1,5},{2,6},{3,7},{4,0},{5,1},{6,2},{7,3},{8,12},{9,13},{10,... | collective-permute-start | bytes 196616 | tf_op jit(solution)/shard_map/ppermute | solution.py:397
  11.5 1.9 %collective-permute-start.3 = (bf16[4,16,8,128]{3,2,1,0:T(8,128)(2,1)S(1)}, bf16[4,16,8,128]{3,2,1,0:T(8,128)(2,1)S(1)}, u32[]{:S(2)}, u32[]{:S(2)}) collective-permute-start(bf16[4,16,8,128]{3,2,1,0:T(8,128)(2,1)S(1)} %pad_maximum_fusion.lane_ref.refs_2_), channel_id=1, source_target_pairs={{0,1},{1,0},{2,3},{3,2},{4,5},{5,4},{6,7},{7,6},{8,9},{9,8},{10,11... | collective-permute-start | bytes 393224 | tf_op jit(solution)/shard_map/ppermute | solution.py:397
  11.6 5.9 %collective-permute-start.2 = (bf16[4,16,8,128]{3,2,1,0:T(8,128)(2,1)S(1)}, bf16[4,16,8,128]{3,2,1,0:T(8,128)(2,1)S(1)}, u32[]{:S(2)}, u32[]{:S(2)}) collective-permute-start(bf16[4,16,8,128]{3,2,1,0:T(8,128)(2,1)S(1)} %pad_maximum_fusion.lane_ref.refs_2_), channel_id=1, source_target_pairs={{0,2},{1,3},{2,0},{3,1},{4,6},{5,7},{6,4},{7,5},{8,10},{9,11},{10,... | collective-permute-start | bytes 393224 | tf_op jit(solution)/shard_map/ppermute | solution.py:397
  13.4 6.6 %copy-start.1 = (s32[2]{0:T(128)S(1)}, s32[2]{0:T(128)}, u32[]{:S(2)}) copy-start(s32[2]{0:T(128)} %refs_1_.3) | copy-start | bytes 28
  13.4 6.6 %copy-start.2 = (s32[16]{0:T(128)S(1)}, s32[16]{0:T(128)}, u32[]{:S(2)}) copy-start(s32[16]{0:T(128)} %refs_2_.1) | copy-start | bytes 196
  13.4 6.6 %copy-start.3 = (s32[16]{0:T(128)S(1)}, s32[16]{0:T(128)}, u32[]{:S(2)}) copy-start(s32[16]{0:T(128)} %refs_3_.1) | copy-start | bytes 196
  17.5 2.5 %collective-permute-start.4 = (bf16[4,16,8,128]{3,2,1,0:T(8,128)(2,1)S(1)}, bf16[4,16,8,128]{3,2,1,0:T(8,128)(2,1)S(1)}, u32[]{:S(2)}, u32[]{:S(2)}) collective-permute-start(bf16[4,16,8,128]{3,2,1,0:T(8,128)(2,1)S(1)} %collective-permute-done.2.lane_ref), channel_id=1, source_target_pairs={{0,1},{1,0},{2,3},{3,2},{4,5},{5,4},{6,7},{7,6},{8,9},{9,8},{10,11... | collective-permute-start | bytes 393224 | tf_op jit(solution)/shard_map/ppermute | solution.py:397
  22.9 1.9 %collective-permute-start.5 = (bf16[720,128]{1,0:T(8,128)(2,1)S(1)}, bf16[720,128]{1,0:T(8,128)(2,1)S(1)}, u32[]{:S(2)}, u32[]{:S(2)}) collective-permute-start(bf16[720,128]{1,0:T(8,128)(2,1)S(1)} %get-tuple-element.40), channel_id=1, source_target_pairs={{0,1},{1,0},{2,3},{3,2},{4,5},{5,4},{6,7},{7,6},{8,9},{9,8},{10,11... | collective-permute-start | bytes 552968 | tf_op jit(solution)/shard_map/ppermute | solution.py:397
  25.8 14.2 %all-to-all-start = ((bf16[8,96,128]{2,1,0:T(8,128)(2,1)}), bf16[8,96,128]{2,1,0:T(8,128)(2,1)S(1)}, u32[]{:S(2)}, u32[]{:S(2)}) async-start(bf16[8,96,128]{2,1,0:T(8,128)(2,1)} %join.1), calls=%async_computation | async-start | bytes 393216 | tf_op jit(solution)/shard_map/all_to_all | solution.py:426

commit v6 on v2

v6 whole, which is shorter than its diff:
```python
import functools
import math

import jax
import jax.numpy as jnp
from jax import lax
from jax.experimental import pallas as pl
from jax.experimental.pallas import tpu as pltpu
from jax.sharding import PartitionSpec as P

QUERY_HEADS = 128
KEY_HEADS = 8
HEAD_WIDTH = 128
ROPE_BASE = 500000.0
NEG_FILL = -1e30
SCALE = 1.0 / math.sqrt(HEAD_WIDTH)
GROUPED = KEY_HEADS // 2
CHUNKS = GROUPED // 2
MIX_ROWS = GROUPED * 64
STAT_ROWS = 16
MIB = 2**20


def dot(a, b, dims):
    return lax.dot_general(a, b, (dims, ((), ())), preferred_element_type=jnp.float32)


def round_bf16(x):
    return x.astype(jnp.bfloat16).astype(jnp.float32)


def lane_of(index_ref, devices):
    here = index_ref[0]
    chip = here // 2
    per_head = devices // 2 // KEY_HEADS
    return here, chip, per_head, (chip // per_head) % 2


def head_columns(head):
    return pl.ds(pl.multiple_of(head * HEAD_WIDTH, HEAD_WIDTH), HEAD_WIDTH)


def cache_copies(key_ref, value_ref, out_ref, parity, sems):
    copies = []
    for i, ref in enumerate((key_ref, value_ref)):
        for g in range(GROUPED):
            place = out_ref.at[i, :, g * HEAD_WIDTH : (g + 1) * HEAD_WIDTH]
            source = ref.at[:, head_columns(2 * g + parity)]
            copies.append(pltpu.make_async_copy(source, place, sems.at[i * GROUPED + g]))
    return copies


def pack_kernel(sizes, index_ref, query_ref, hidden_ref, key_ref, value_ref, *refs):
    own_query_ref, own_hidden_ref, cache_ref, query_buf, hidden_buf, sems = refs
    requests, tokens, devices = sizes
    _, _, _, parity = lane_of(index_ref, devices)
    loads = [
        pltpu.make_async_copy(query_ref, query_buf, sems.at[2 * GROUPED]),
        pltpu.make_async_copy(hidden_ref, hidden_buf, sems.at[2 * GROUPED + 1]),
    ]
    caches = cache_copies(key_ref, value_ref, cache_ref, 1 - parity, sems)
    for load in loads + caches:
        load.start()
    for load, ref, out_ref in zip(
        loads, (query_buf, hidden_buf), (own_query_ref, own_hidden_ref)
    ):
        load.wait()
        rows = jnp.concatenate([ref[b].astype(jnp.float32) for b in range(requests)], axis=0)
        for c in range(rows.shape[1] // HEAD_WIDTH):
            tile = rows[:, c * HEAD_WIDTH : (c + 1) * HEAD_WIDTH]
            out_ref[c] = tile.astype(jnp.bfloat16)
    for load in caches:
        load.wait()


def base_kernel(sizes, index_ref, own_ref, weight_ref, key_ref, value_ref, *refs):
    up_ref, base_ref, cache_ref, held_up_ref, buffer, sems = refs
    requests, tokens, devices = sizes
    _, _, _, parity = lane_of(index_ref, devices)
    parts, depth = buffer.shape[:2]
    loads = [
        pltpu.make_async_copy(
            weight_ref.at[pl.ds(p * depth, depth)], buffer.at[p], sems.at[2 * GROUPED + p]
        )
        for p in range(parts)
    ]
    others = cache_copies(key_ref, value_ref, cache_ref, parity, sems)
    others.append(pltpu.make_async_copy(up_ref, held_up_ref, sems.at[2 * GROUPED + parts]))
    for load in loads + others:
        load.start()
    tiles = depth // HEAD_WIDTH
    total = jnp.zeros(base_ref.shape, jnp.float32)
    for p in range(parts):
        hidden = jnp.concatenate([own_ref[p * tiles + c] for c in range(tiles)], axis=1)
        loads[p].wait()
        total += dot(hidden, buffer[p], ((1,), (0,)))
    base_ref[...] = total
    for load in others:
        load.wait()


def lower(sizes, masks, index_ref, lane_refs, down_ref, buffer, sems):
    requests, tokens, devices = sizes
    here, _, per_head, _ = lane_of(index_ref, devices)
    heads = QUERY_HEADS // devices
    depth = buffer.shape[1]
    chunks = depth // HEAD_WIDTH
    work = []
    for side, ref in enumerate(lane_refs):
        for i, mask in enumerate(masks):
            for hop in range(2):
                source = here ^ (2 * (mask ^ hop * per_head) + side)
                rows = pl.ds(pl.multiple_of(source * depth, depth), depth)
                at = len(work)
                copy = pltpu.make_async_copy(down_ref.at[rows], buffer.at[at], sems.at[at])
                copy.start()
                work.append((copy, ref, i, heads + hop * chunks))
    total = None
    for at, (copy, ref, i, first) in enumerate(work):
        hidden = jnp.concatenate([ref[i, first + c] for c in range(chunks)], axis=1)
        copy.wait()
        term = dot(hidden, buffer[at], ((1,), (0,)))
        total = term if total is None else total + term
    return total


def early_kernel(sizes, masks, index_ref, lane_ref, other_ref, down_ref, out_ref, buffer, sems):
    out_ref[...] = lower(sizes, masks, index_ref, (lane_ref, other_ref), down_ref, buffer, sems)


def project_kernel(sizes, masks, *refs):
    (index_ref, adapter_ref, rank_ref, pool_ref) = refs[:4]
    (lane_ref, other_ref, early_ref, base_ref, down_ref, up_ref) = refs[4:10]
    (own_ref, own_parts_ref, parts_ref, all_ref, buffer, sems) = refs[10:]
    requests, tokens, devices = sizes
    rows = requests * tokens
    here, _, _, parity = lane_of(index_ref, devices)
    lowered = early_ref[...]
    lowered += lower(sizes, masks, index_ref, (lane_ref, other_ref), down_ref, buffer, sems)
    row_request = lax.broadcasted_iota(jnp.int32, (rows, 1), 0) // tokens
    ranks = jnp.zeros((rows, 1), jnp.int32)
    owners = jnp.zeros((rows, 1), jnp.int32)
    for b in range(requests):
        adapter = adapter_ref[b]
        ranks = jnp.where(row_request == b, rank_ref[adapter], ranks)
        owners = jnp.where(row_request == b, pool_ref[adapter], owners)
    column = lax.broadcasted_iota(jnp.int32, lowered.shape, 1)
    lowered = jnp.where(column < ranks, lowered, 0.0).astype(jnp.bfloat16)
    lifted = dot(lowered, up_ref[...], ((1,), (0,)))
    all_ref[...] = base_ref[...] + jnp.where(owners == here, lifted, 0.0)
    step = GROUPED * rows
    for which, out_ref in ((parity, own_parts_ref), (1 - parity, parts_ref)):
        keys = [all_ref[:, head_columns(2 * g + which)] for g in range(GROUPED)]
        values = [all_ref[:, head_columns(KEY_HEADS + 2 * g + which)] for g in range(GROUPED)]
        keys = jnp.concatenate(keys, axis=0)
        values = jnp.concatenate(values, axis=0)
        if out_ref is own_parts_ref:
            own_ref[0] = keys
            own_ref[1] = values
        high = keys.astype(jnp.bfloat16)
        out_ref[:step] = high
        out_ref[step : 2 * step] = (keys - high.astype(jnp.float32)).astype(jnp.bfloat16)
        out_ref[2 * step :] = values.astype(jnp.bfloat16)


def chunks_of(masks, slots):
    order = sorted(masks)
    return [order[at : at + slots] for at in range(0, len(order), slots)]


def attend(sizes, masks, index_ref, length_ref, first_ref, second_ref, cache_ref, far_ref, put):
    requests, tokens, devices = sizes
    here, chip, per_head, _ = lane_of(index_ref, devices)
    heads = QUERY_HEADS // devices
    slot_rows = heads * requests * tokens
    positions = cache_ref.shape[1] // requests
    half = len(masks) // 2
    place = lax.broadcasted_iota(jnp.int32, (requests * positions, HEAD_WIDTH), 0)
    column = lax.broadcasted_iota(jnp.int32, (requests * positions, HEAD_WIDTH), 1)
    place_request = place // positions
    limit = jnp.zeros_like(place)
    for b in range(requests):
        limit = jnp.where(place_request == b, length_ref[b], limit)
    same = place_request == (column // tokens) % requests
    caches = (cache_ref, far_ref)
    allowed = [
        (device * positions + place % positions < limit) & same
        for device in (here, here ^ (2 * per_head))
    ]
    peaks, totals = [], []
    for number, chunk in enumerate(chunks_of(masks, HEAD_WIDTH // slot_rows)):
        query = jnp.concatenate(
            [
                (first_ref if masks.index(mask) < half else second_ref)[masks.index(mask) % half, h]
                for mask in chunk
                for h in range(heads)
            ],
            axis=0,
        )
        key_heads = sorted({mask // per_head for mask in chunk})
        spots = [head_columns(((chip // per_head) ^ head) // 2) for head in key_heads]
        share = HEAD_WIDTH // len(key_heads)
        scores = []
        for ref, valid in zip(caches, allowed):
            score = None
            for i, spot in enumerate(spots):
                part = dot(ref[0, :, spot], query, ((1,), (1,)))
                score = part if score is None else jnp.where(column < i * share, score, part)
            scores.append(jnp.where(valid, score * SCALE, NEG_FILL))
        peak = jnp.maximum(
            jnp.max(scores[0], axis=0, keepdims=True), jnp.max(scores[1], axis=0, keepdims=True)
        )
        peak = round_bf16(peak)
        total, weights = jnp.zeros_like(peak), []
        for score, valid in zip(scores, allowed):
            weight = jnp.where(valid, jnp.exp(score - peak), 0.0)
            total += jnp.sum(weight, axis=0, keepdims=True)
            weights.append(jnp.transpose(weight.astype(jnp.bfloat16)))
        peaks.append(peak)
        totals.append(total)
        for i, spot in enumerate(spots):
            own = slice(i * share, (i + 1) * share)
            mix = dot(weights[0][own], cache_ref[1, :, spot], ((1,), (0,)))
            mix += dot(weights[1][own], far_ref[1, :, spot], ((1,), (0,)))
            put(number, i * share, mix)
    return peaks, totals


def rows_of(items, count):
    row = lax.broadcasted_iota(jnp.int32, (count, HEAD_WIDTH), 0)
    out = jnp.zeros((count, HEAD_WIDTH), jnp.float32)
    for i, item in enumerate(items):
        out = jnp.where(row == i, item, out)
    return out


def other_kernel(sizes, masks, *refs):
    (index_ref, length_ref, first_ref, second_ref, cache_ref, far_ref, parts_ref, send_ref) = refs
    proj_rows = parts_ref.shape[0]

    def put(chunk, row, mix):
        at = chunk * 128 + row
        send_ref[at : at + mix.shape[0]] = mix.astype(jnp.bfloat16)

    peaks, totals = attend(
        sizes, masks, index_ref, length_ref, first_ref, second_ref, cache_ref, far_ref, put
    )
    highs = [round_bf16(total) for total in totals]
    lows = [total - high for total, high in zip(totals, highs)]
    send_ref[MIX_ROWS : MIX_ROWS + proj_rows] = parts_ref[...]
    send_ref[MIX_ROWS + proj_rows :] = rows_of(peaks + highs + lows, STAT_ROWS).astype(jnp.bfloat16)


def own_kernel(sizes, masks, *refs):
    (index_ref, length_ref, first_ref, second_ref, cache_ref, far_ref, mix_ref, stat_ref) = refs

    def put(chunk, row, mix):
        at = chunk * 128 + row
        mix_ref[at : at + mix.shape[0]] = mix

    peaks, totals = attend(
        sizes, masks, index_ref, length_ref, first_ref, second_ref, cache_ref, far_ref, put
    )
    stat_ref[...] = rows_of(peaks + totals, 8)


def join_kernel(sizes, masks, index_ref, mix_ref, stat_ref, proj_ref, far_ref, got_ref, got_far_ref, *refs):
    packet_refs, tail_ref = refs[:-1], refs[-1]
    requests, tokens, devices = sizes
    _, chip, per_head, _ = lane_of(index_ref, devices)
    rows = requests * tokens
    heads = QUERY_HEADS // devices
    slot_rows = heads * rows
    step = GROUPED * rows
    got = got_ref[MIX_ROWS + 3 * step :].astype(jnp.float32)
    own = stat_ref[...]
    own_peak, got_peak = own[:CHUNKS], got[:CHUNKS]
    peak = jnp.maximum(own_peak, got_peak)
    own_factor = jnp.exp(own_peak - peak)
    got_factor = jnp.exp(got_peak - peak)
    total = own_factor * own[CHUNKS : 2 * CHUNKS] + got_factor * (
        got[CHUNKS : 2 * CHUNKS] + got[2 * CHUNKS : 3 * CHUNKS]
    )
    high = round_bf16(total)
    low = total - high
    filler = jnp.zeros((128 - 2 * CHUNKS, 128), jnp.float32)
    table = jnp.transpose(jnp.concatenate([own_factor, got_factor, filler], axis=0))
    keys, values = proj_ref[0], proj_ref[1]
    for ref, at in ((far_ref, 0), (got_ref, MIX_ROWS), (got_far_ref, 0)):
        keys += ref[at : at + step].astype(jnp.float32)
        keys += ref[at + step : at + 2 * step].astype(jnp.float32)
        values += ref[at + 2 * step : at + 3 * step].astype(jnp.float32)
    keys_high = round_bf16(keys)
    for g in range(GROUPED):
        part = slice(g * rows, (g + 1) * rows)
        tail_ref[g, :rows] = keys_high[part]
        tail_ref[g, rows : 2 * rows] = (keys - keys_high)[part]
        tail_ref[g, 2 * rows :] = values[part]
    stat_row = lax.broadcasted_iota(jnp.int32, (rows, HEAD_WIDTH), 0)
    for c, chunk in enumerate(chunks_of(masks, HEAD_WIDTH // slot_rows)):
        span = slice(c * 128, c * 128 + 128)
        mix = mix_ref[span] * table[:, c : c + 1]
        mix += got_ref[span].astype(jnp.float32) * table[:, CHUNKS + c : CHUNKS + c + 1]
        stats = jnp.where(
            stat_row == 0,
            peak[c : c + 1],
            jnp.where(
                stat_row == 1, high[c : c + 1], jnp.where(stat_row == 2, low[c : c + 1], 0.0)
            ),
        )
        for t, mask in enumerate(chunk):
            packet_ref = packet_refs[masks.index(mask)]
            shifted = stats if t == 0 else pltpu.roll(stats, HEAD_WIDTH - t * slot_rows, 1)
            group = ((chip // per_head) ^ (mask // per_head)) // 2
            tail = jnp.concatenate([tail_ref[group], shifted], axis=0)
            packet_ref[:slot_rows] = mix[t * slot_rows : (t + 1) * slot_rows].astype(jnp.bfloat16)
            packet_ref[slot_rows:] = tail.astype(jnp.bfloat16)


def merge_kernel(devices, requests, tokens, own_ref, cos_ref, sin_ref, *refs):
    got_refs, out_ref = refs[:-1], refs[-1]
    rows = requests * tokens
    heads = QUERY_HEADS // devices
    mix_rows = heads * rows
    sources = len(got_refs)
    tails = [ref[mix_rows:].astype(jnp.float32) for ref in got_refs]
    sums = functools.reduce(jnp.add, [tail[: 3 * rows] for tail in tails])
    keys = sums[:rows] + sums[rows : 2 * rows]
    values = sums[2 * rows :].astype(jnp.bfloat16)
    turned = pltpu.roll(keys, HEAD_WIDTH // 2, 1)
    keys = (keys * cos_ref[...] + turned * sin_ref[...]).astype(jnp.bfloat16)
    query = jnp.concatenate([own_ref[h] for h in range(heads)], axis=0)
    if mix_rows < 128:
        query = jnp.concatenate(
            [query, jnp.zeros((128 - mix_rows, HEAD_WIDTH), jnp.bfloat16)], axis=0
        )
    fresh = dot(keys, query, ((1,), (1,))) * SCALE
    source = lax.broadcasted_iota(jnp.int32, fresh.shape, 0)
    column = lax.broadcasted_iota(jnp.int32, fresh.shape, 1) % rows
    allowed = (source // tokens == column // tokens) & (source % tokens <= column % tokens)
    fresh_peak = jnp.max(jnp.where(allowed, fresh, NEG_FILL), axis=0, keepdims=True)
    stats = [tail[3 * rows :] for tail in tails]
    peak = functools.reduce(jnp.maximum, [stat[0:1] for stat in stats], fresh_peak)
    weights = jnp.where(allowed, jnp.exp(fresh - peak), 0.0)
    factors = [jnp.exp(stat[0:1] - peak) for stat in stats]
    total = functools.reduce(
        jnp.add,
        [factor * (stat[1:2] + stat[2:3]) for factor, stat in zip(factors, stats)],
        jnp.sum(weights, axis=0, keepdims=True),
    )
    inverse = 1.0 / total
    filler = jnp.zeros((128 - sources - 1, 128), jnp.float32)
    table = jnp.concatenate([factor * inverse for factor in factors] + [inverse, filler], axis=0)
    table = jnp.transpose(table)[:mix_rows]
    weights = jnp.transpose(
        jnp.concatenate([weights, jnp.zeros((128 - rows, 128), jnp.float32)], axis=0)
    )[:mix_rows].astype(jnp.bfloat16)
    values = jnp.concatenate(
        [values, jnp.zeros((128 - rows, HEAD_WIDTH), jnp.bfloat16)], axis=0
    )
    mix = dot(weights, values, ((1,), (0,))) * table[:, sources : sources + 1]
    for s, ref in enumerate(got_refs):
        mix += ref[:mix_rows].astype(jnp.float32) * table[:, s : s + 1]
    for h in range(heads):
        tile = mix[h * rows : (h + 1) * rows]
        for b in range(requests):
            out_ref[b, :, h * HEAD_WIDTH : (h + 1) * HEAD_WIDTH] = tile[
                b * tokens : (b + 1) * tokens
            ].astype(jnp.bfloat16)


def rotation(lengths, tokens):
    half = HEAD_WIDTH // 2
    places = (lengths[:, None] + jnp.arange(tokens, dtype=jnp.int32)[None, :]).astype(jnp.float32)
    inverse_freq = jnp.exp(
        jnp.arange(half, dtype=jnp.float32) * (-2.0 * math.log(ROPE_BASE) / HEAD_WIDTH)
    )
    angles = places.reshape(-1, 1) * inverse_freq[None, :]
    cosine, sine = jnp.cos(angles), jnp.sin(angles)
    return jnp.concatenate([cosine, cosine], axis=1), jnp.concatenate([-sine, sine], axis=1)


def vmem():
    return pl.BlockSpec(memory_space=pltpu.VMEM)


def smem():
    return pl.BlockSpec(memory_space=pltpu.SMEM)


def hbm():
    return pl.BlockSpec(memory_space=pltpu.HBM)


def pinned(x):
    return pltpu.with_memory_space_constraint(x, pltpu.HBM)


def cost(flops, moved):
    return pl.CostEstimate(flops=int(flops), bytes_accessed=int(moved), transcendentals=0)


def swap(x, devices, bit):
    return lax.ppermute(x, "tensor", [(d, d ^ bit) for d in range(devices)])


def per_device(
    hidden,
    queries,
    key_value_weight,
    adapter_down_weight,
    adapter_up_weight,
    cached_key_rows,
    cached_value_rows,
    request_adapter,
    adapter_rank_list,
    adapter_pool_row,
    lengths,
):
    requests, tokens, width = hidden.shape
    rows = requests * tokens
    devices = lax.axis_size("tensor")
    sizes = (requests, tokens, devices)
    heads = QUERY_HEADS // devices
    chunks = width // HEAD_WIDTH
    lanes = devices // 2
    partner = lanes // KEY_HEADS
    slot_rows = heads * rows
    index = lax.axis_index("tensor").reshape(1).astype(jnp.int32)
    flat = requests * cached_key_rows.shape[1]
    cached_keys = pinned(cached_key_rows.reshape(flat, -1))
    cached_values = pinned(cached_value_rows.reshape(flat, -1))
    cache = pltpu.VMEM((2, flat, GROUPED * HEAD_WIDTH), jnp.bfloat16)
    cache_sems = 2 * GROUPED

    def call(kernel, operands, in_specs, out_shape, scratch, name):
        return pl.pallas_call(
            kernel,
            out_shape=tuple(out_shape),
            in_specs=in_specs,
            out_specs=(vmem(),) * len(out_shape),
            scratch_shapes=scratch,
            compiler_params=pltpu.CompilerParams(vmem_limit_bytes=12 * MIB),
            cost_estimate=cost(10**9 if name == "base" else 10**6, 0),
            name=name,
        )(*operands)

    own_queries, own_hidden, far_send = call(
        functools.partial(pack_kernel, sizes),
        (index, pinned(queries), pinned(hidden), cached_keys, cached_values),
        [smem()] + [hbm()] * 4,
        [
            pltpu.VMEM((heads, rows, HEAD_WIDTH), jnp.bfloat16),
            pltpu.VMEM((chunks, rows, HEAD_WIDTH), jnp.bfloat16),
            cache,
        ],
        [
            pltpu.VMEM(queries.shape, jnp.bfloat16),
            pltpu.VMEM(hidden.shape, jnp.bfloat16),
            pltpu.SemaphoreType.DMA((cache_sems + 2,)),
        ],
        "pack",
    )
    far_hidden = swap(own_hidden, devices, 2 * partner)
    far_cache = swap(far_send, devices, 2 * partner)

    out_width = key_value_weight.shape[1]
    parts = 4 if width % (4 * HEAD_WIDTH) == 0 else 1
    up = adapter_up_weight[0]
    base, own_cache, up = call(
        functools.partial(base_kernel, sizes),
        (index, own_hidden, pinned(key_value_weight), cached_keys, cached_values, pinned(up)),
        [smem(), vmem()] + [hbm()] * 4,
        [
            pltpu.VMEM((rows, out_width), jnp.float32),
            cache,
            pltpu.VMEM(up.shape, up.dtype),
        ],
        [
            pltpu.VMEM((parts, width // parts, out_width), jnp.bfloat16),
            pltpu.SemaphoreType.DMA((cache_sems + parts + 1,)),
        ],
        "base",
    )
    far_hidden, base = lax.optimization_barrier((far_hidden, base))

    masks, lane = [0], jnp.concatenate([own_queries, own_hidden, far_hidden], axis=0)[None]
    bits = [1 << i for i in reversed(range(lanes.bit_length() - 1)) if 1 << i != partner]
    for bit in bits[:-1]:
        masks += [mask ^ bit for mask in masks]
        lane = jnp.concatenate([lane, swap(lane, devices, 2 * bit)], axis=0)
    other = swap(lane, devices, 1)
    late_lane = swap(lane, devices, 2 * bits[-1])
    late_masks = [mask ^ bits[-1] for mask in masks]

    down = pinned(adapter_down_weight[0])
    rank = down.shape[1]
    sources = 4 * len(masks)
    streamed = [
        pltpu.VMEM((sources, width, rank), jnp.bfloat16),
        pltpu.SemaphoreType.DMA((sources,)),
    ]
    (early,) = call(
        functools.partial(early_kernel, sizes, masks),
        (index, lane, other, down),
        [smem()] + [vmem()] * 2 + [hbm()],
        [pltpu.VMEM((rows, rank), jnp.float32)],
        streamed,
        "lora_first",
    )
    late_lane, early = lax.optimization_barrier((late_lane, early))
    late_other = swap(late_lane, devices, 1)
    late_other, far_cache = lax.optimization_barrier((late_other, far_cache))
    step = GROUPED * rows
    proj, own_parts, parts = call(
        functools.partial(project_kernel, sizes, late_masks),
        (
            index,
            request_adapter,
            adapter_rank_list,
            adapter_pool_row,
            late_lane,
            late_other,
            early,
            base,
            down,
            up,
        ),
        [smem()] * 4 + [vmem()] * 4 + [hbm(), vmem()],
        [
            pltpu.VMEM((2, step, HEAD_WIDTH), jnp.float32),
            pltpu.VMEM((3 * step, HEAD_WIDTH), jnp.bfloat16),
            pltpu.VMEM((3 * step, HEAD_WIDTH), jnp.bfloat16),
        ],
        [pltpu.VMEM((rows, out_width), jnp.float32)] + streamed,
        "project",
    )
    far_parts = swap(parts, devices, 2 * partner)
    all_masks = masks + late_masks
    (send,) = call(
        functools.partial(other_kernel, sizes, all_masks),
        (index, lengths, other, late_other, own_cache, far_cache, own_parts),
        [smem()] * 2 + [vmem()] * 5,
        [pltpu.VMEM((MIX_ROWS + 3 * step + STAT_ROWS, HEAD_WIDTH), jnp.bfloat16)],
        [],
        "other_lane",
    )
    got = swap(send, devices, 1)
    got_far_parts = swap(far_parts, devices, 1)
    mix, stats = call(
        functools.partial(own_kernel, sizes, all_masks),
        (index, lengths, lane, late_lane, own_cache, far_cache),
        [smem()] * 2 + [vmem()] * 4,
        [
            pltpu.VMEM((MIX_ROWS, HEAD_WIDTH), jnp.float32),
            pltpu.VMEM((8, HEAD_WIDTH), jnp.float32),
        ],
        [],
        "own_lane",
    )
    packet = pltpu.VMEM((slot_rows + 4 * rows, HEAD_WIDTH), jnp.bfloat16)
    packets = call(
        functools.partial(join_kernel, sizes, all_masks),
        (index, mix, stats, proj, far_parts, got, got_far_parts),
        [smem()] + [vmem()] * 6,
        [packet] * len(all_masks),
        [pltpu.VMEM((GROUPED, 3 * rows, HEAD_WIDTH), jnp.float32)],
        "join",
    )
    packets = [
        x if mask == 0 else swap(x, devices, 2 * mask) for x, mask in zip(packets, all_masks)
    ]
    cosine, sine = rotation(lengths, tokens)
    return pl.pallas_call(
        functools.partial(merge_kernel, devices, requests, tokens),
        out_shape=jax.ShapeDtypeStruct((requests, tokens, heads * HEAD_WIDTH), jnp.bfloat16),
        in_specs=[vmem()] * (3 + len(packets)),
        out_specs=vmem(),
        compiler_params=pltpu.CompilerParams(vmem_limit_bytes=8 * MIB),
        name="merge_states",
    )(own_queries, cosine, sine, *packets)


def solution(mesh):
    in_specs = (
        P("groups", None, "tensor"),
        P("groups", None, "tensor"),
        P("tensor", None),
        P("tensor", None, None),
        P("tensor", None, None),
        P("groups", "tensor", None),
        P("groups", "tensor", None),
        P("groups"),
        P(),
        P(),
        P("groups"),
    )
    out_specs = P("groups", None, "tensor")
    return jax.shard_map(
        per_device, mesh=mesh, in_specs=in_specs, out_specs=out_specs, check_vma=False
    )
```

time: 55.7 us -> 39.4 us (0.71)
  local copies, waits for them, and re-layouts: 9.3 us -> 0.1 us
  starting transfers between devices: 23.9 us -> 14.7 us
  Pallas kernels: 9.98 us -> 13.3 us
  other arithmetic: 0.85 us -> 0.28 us
    ppermute x16 -> x12, starting transfers between devices: 23.9 us -> 14.7 us  [swap(): return lax.ppermute(x, 'tensor', [(d, d ^ bit) for d in range(devices)])]
    unnamed x49 -> x8, local copies, waits for them, and re-layouts: 9.2 us -> 0.01 us
    pallas_call x4 -> x7, Pallas kernels: 7.99 us -> 12.2 us  [call(): pl.pallas_call(kernel, out_shape=tuple(out_shape), in_specs=in_specs, out...]
    pallas_call x1, Pallas kernels: 2 us -> 1.05 us  [per_device(): pl.pallas_call(functools.partial(merge_kernel, devices, requests, tokens)...]
    concatenate x1, other arithmetic: 0.66 us -> 0.07 us  [rotation(): jnp.concatenate([cosine, cosine], axis=1)]
    ppermute x16 -> x12, waiting for transfers between devices: 11 us -> 10.7 us  [swap(): return lax.ppermute(x, 'tensor', [(d, d ^ bit) for d in range(devices)])]
  transfers between devices with their start and end apart: 16 -> 12, of which waited for: 6 -> 7; matrix products, arithmetic and copies ran while one was open for 3% -> 1% of each run, Pallas kernels for 1% -> 20%
where the time goes in v6:
time: 39.4 us; the launch traced here: 39.2 us
  starting transfers between devices  14.7 us (37%)
  Pallas kernels  13.3 us (34%)
  waiting for transfers between devices  10.7 us (27%)
    ppermute x12, starting transfers between devices, swap(): return lax.ppermute(x, 'tensor', [(d, d ^ bit) for d in range(devices)])  14.7 us
    pallas_call x7, Pallas kernels, call(): pl.pallas_call(kernel, out_shape=tuple(out_shape), in_specs=in_specs, out...  12.2 us
    ppermute x12, waiting for transfers between devices, swap(): return lax.ppermute(x, 'tensor', [(d, d ^ bit) for d in range(devices)])  10.7 us
    pallas_call x1, Pallas kernels, per_device(): pl.pallas_call(functools.partial(merge_kernel, devices, requests, tokens)...  1.05 us
  transfers between devices with their start and end apart: 12, of which 7 were waited for; matrix products, arithmetic and copies ran while one was open for 1% of the time, Pallas kernels for 20%

profile of v6, /device:TPU:0, one launch (start us, length us, event | category | flops | bytes accessed | tf_op | source)
XLA Modules:
  0.0 39.2 jit_solution(16501207735202892796)
XLA Ops:
  0.0 1.2 %pack.1 = (bf16[8,8,128]{2,1,0:T(8,128)(2,1)S(1)}, bf16[8,8,128]{2,1,0:T(8,128)(2,1)S(1)}, bf16[2,256,512]{2,1,0:T(8,128)(2,1)S(1)}) custom-call(s32[1]{0:T(128)} %bitcast.index_ref.refs_0_, bf16[2,4,1024]{2,1,0:T(4,128)(2,1)} %query_ref.1, bf16[2,4,1024]{2,1,0:T(4,128)(2,1)} %hidden_ref.1, bf16[256,1024]{1,0:T(8,128)(2,1)} %bitcast.9, ...), custom_call_target="tpu_custom_call" | custom-call | flops 1000000 | tf_op jit(solution)/shard_map/pack/pallas_call | solution.py:437
  1.2 3.0 %collective-permute-start = (bf16[8,8,128]{2,1,0:T(8,128)(2,1)S(1)}, bf16[8,8,128]{2,1,0:T(8,128)(2,1)S(1)}, u32[]{:S(2)}, u32[]{:S(2)}) collective-permute-start(bf16[8,8,128]{2,1,0:T(8,128)(2,1)S(1)} %get-tuple-element.27.own_ref), channel_id=1, source_target_pairs={{0,2},{1,3},{2,0},{3,1},{4,6},{5,7},{6,4},{7,5},{8,10},{9,11},{10,... | collective-permute-start | bytes 49160 | tf_op jit(solution)/shard_map/ppermute | solution.py:404
  4.2 0.1 collective-permute-start.5
  4.3 2.6 %base.1 = (f32[8,2048]{1,0:T(8,128)S(1)}, bf16[2,256,512]{2,1,0:T(8,128)(2,1)S(1)}, bf16[128,2048]{1,0:T(8,128)(2,1)S(1)}) custom-call(s32[1]{0:T(128)} %bitcast.index_ref.refs_0_, bf16[8,8,128]{2,1,0:T(8,128)(2,1)S(1)} %get-tuple-element.27.own_ref, bf16[1024,2048]{1,0:T(8,128)(2,1)} %weight_ref.1, bf16[256,1024]{1,0:T(8,128)(2,1)} %bitcast.10, ...), custom_call_target="tpu_custom_call" | custom-call | flops 1000000000 | tf_op jit(solution)/shard_map/base/pallas_call | solution.py:437
  7.0 3.1 %collective-permute-start.1 = (bf16[1,24,8,128]{3,2,1,0:T(8,128)(2,1)S(1)}, bf16[1,24,8,128]{3,2,1,0:T(8,128)(2,1)S(1)}, u32[]{:S(2)}, u32[]{:S(2)}) collective-permute-start(bf16[1,24,8,128]{3,2,1,0:T(8,128)(2,1)S(1)} %maximum_bitcast_fusion), channel_id=1, source_target_pairs={{0,8},{1,9},{2,10},{3,11},{4,12},{5,13},{6,14},{7,15},{8,0},{9,1},... | collective-permute-start | bytes 147464 | tf_op jit(solution)/shard_map/ppermute | solution.py:404
  10.1 2.2 %collective-permute-done.1 = bf16[1,24,8,128]{3,2,1,0:T(8,128)(2,1)S(1)} collective-permute-done((bf16[1,24,8,128]{3,2,1,0:T(8,128)(2,1)S(1)}, bf16[1,24,8,128]{3,2,1,0:T(8,128)(2,1)S(1)}, u32[]{:S(2)}, u32[]{:S(2)}) %collective-permute-start.1) | collective-permute-done | bytes 49184 | tf_op jit(solution)/shard_map/ppermute | solution.py:404
  12.3 0.1 collective-permute-start.3
  12.4 1.8 %collective-permute-start.2 = (bf16[2,24,8,128]{3,2,1,0:T(8,128)(2,1)S(1)}, bf16[2,24,8,128]{3,2,1,0:T(8,128)(2,1)S(1)}, u32[]{:S(2)}, u32[]{:S(2)}) collective-permute-start(bf16[2,24,8,128]{3,2,1,0:T(8,128)(2,1)S(1)} %pad_maximum_fusion.lane_ref.refs_2_), channel_id=1, source_target_pairs={{0,4},{1,5},{2,6},{3,7},{4,0},{5,1},{6,2},{7,3},{8,12},{9,13},{10,... | collective-permute-start | bytes 294920 | tf_op jit(solution)/shard_map/ppermute | solution.py:404
  14.2 0.0 collective-permute-done.3.other_ref.refs_2_
  14.2 2.2 %lora_first.1.refs_6_ = f32[8,128]{1,0:T(8,128)S(1)} custom-call(s32[1]{0:T(128)} %bitcast.index_ref.refs_0_, bf16[2,24,8,128]{3,2,1,0:T(8,128)(2,1)S(1)} %pad_maximum_fusion.lane_ref.refs_2_, bf16[2,24,8,128]{3,2,1,0:T(8,128)(2,1)S(1)} %collective-permute-done.3.other_ref.refs_2_, bf16[16384,128]{1,0:T(8,128)(2,1)} %bitcast.7), custom_call_target="tpu_custom_call" | custom-call | flops 1000000 | tf_op jit(solution)/shard_map/lora_first/pallas_call | solution.py:437
  16.4 1.2 %collective-permute-done.2.refs_3_.refs_4_ = bf16[2,24,8,128]{3,2,1,0:T(8,128)(2,1)S(1)} collective-permute-done((bf16[2,24,8,128]{3,2,1,0:T(8,128)(2,1)S(1)}, bf16[2,24,8,128]{3,2,1,0:T(8,128)(2,1)S(1)}, u32[]{:S(2)}, u32[]{:S(2)}) %collective-permute-start.2) | collective-permute-done | bytes 98336 | tf_op jit(solution)/shard_map/ppermute | solution.py:404
  17.6 0.0 collective-permute-start.4
  17.6 0.1 add_convert_fusion
  17.7 1.2 %collective-permute-done.4.refs_5_.refs_3_ = bf16[2,24,8,128]{3,2,1,0:T(8,128)(2,1)S(1)} collective-permute-done((bf16[2,24,8,128]{3,2,1,0:T(8,128)(2,1)S(1)}, bf16[2,24,8,128]{3,2,1,0:T(8,128)(2,1)S(1)}, u32[]{:S(2)}, u32[]{:S(2)}) %collective-permute-start.4) | collective-permute-done | bytes 98336 | tf_op jit(solution)/shard_map/ppermute | solution.py:404
  19.0 3.0 %project.1 = (f32[2,32,128]{2,1,0:T(8,128)S(1)}, bf16[96,128]{1,0:T(8,128)(2,1)S(1)}, bf16[96,128]{1,0:T(8,128)(2,1)S(1)}) custom-call(s32[1]{0:T(128)} %bitcast.index_ref.refs_0_, s32[2]{0:T(128)S(1)} %copy-done.1, s32[16]{0:T(128)S(1)} %copy-done.2, s32[16]{0:T(128)S(1)} %copy-done.3, bf16[2,24,8,128]{3,2,1,0:T(8,128)(2,1)S(1)} %collective-permute-done.2.refs_3_.refs_4_, ...), custom_call_target="tpu_custom_call" | custom-call | flops 1000000 | tf_op jit(solution)/shard_map/project/pallas_call | solution.py:437
  21.9 1.7 %collective-permute-start.6 = (bf16[96,128]{1,0:T(8,128)(2,1)S(1)}, bf16[96,128]{1,0:T(8,128)(2,1)S(1)}, u32[]{:S(2)}, u32[]{:S(2)}) collective-permute-start(bf16[96,128]{1,0:T(8,128)(2,1)S(1)} %get-tuple-element.41), channel_id=1, source_target_pairs={{0,2},{1,3},{2,0},{3,1},{4,6},{5,7},{6,4},{7,5},{8,10},{9,11},{10,... | collective-permute-start | bytes 73736 | tf_op jit(solution)/shard_map/ppermute | solution.py:404
  23.7 0.1 convert_element_type.11
  23.8 1.5 %other_lane.1 = bf16[368,128]{1,0:T(8,128)(2,1)S(1)} custom-call(s32[1]{0:T(128)} %bitcast.index_ref.refs_0_, s32[2]{0:T(128)S(1)} %copy-done, bf16[2,24,8,128]{3,2,1,0:T(8,128)(2,1)S(1)} %collective-permute-done.3.other_ref.refs_2_, bf16[2,24,8,128]{3,2,1,0:T(8,128)(2,1)S(1)} %collective-permute-done.4.refs_5_.refs_3_, ...), custom_call_target="tpu_custom_call" | custom-call | flops 1000000 | tf_op jit(solution)/shard_map/other_lane/pallas_call | solution.py:437
  25.2 0.1 collective-permute-start.7
  25.3 0.5 %collective-permute-done.6.far_ref = bf16[96,128]{1,0:T(8,128)(2,1)S(1)} collective-permute-done((bf16[96,128]{1,0:T(8,128)(2,1)S(1)}, bf16[96,128]{1,0:T(8,128)(2,1)S(1)}, u32[]{:S(2)}, u32[]{:S(2)}) %collective-permute-start.6) | collective-permute-done | bytes 24608 | tf_op jit(solution)/shard_map/ppermute | solution.py:404
  25.8 0.0 collective-permute-start.8
  25.8 0.1 fusion
  25.9 1.5 %own_lane.1 = (f32[256,128]{1,0:T(8,128)S(1)}, f32[8,128]{1,0:T(8,128)S(1)}) custom-call(s32[1]{0:T(128)} %bitcast.index_ref.refs_0_, s32[2]{0:T(128)S(1)} %copy-done, bf16[2,24,8,128]{3,2,1,0:T(8,128)(2,1)S(1)} %pad_maximum_fusion.lane_ref.refs_2_, bf16[2,24,8,128]{3,2,1,0:T(8,128)(2,1)S(1)} %collective-permute-done.2.refs_3_.refs_4_, ...), custom_call_target="tpu_custom_call" | custom-call | flops 1000000 | tf_op jit(solution)/shard_map/own_lane/pallas_call | solution.py:437
  27.4 0.0 collective-permute-done.7.got_ref
  27.4 0.3 join.1
  27.7 3.0 %collective-permute-start.9 = (bf16[96,128]{1,0:T(8,128)(2,1)S(1)}, bf16[96,128]{1,0:T(8,128)(2,1)S(1)}, u32[]{:S(2)}, u32[]{:S(2)}) collective-permute-start(bf16[96,128]{1,0:T(8,128)(2,1)S(1)} %get-tuple-element.44), channel_id=1, source_target_pairs={{0,8},{1,9},{2,10},{3,11},{4,12},{5,13},{6,14},{7,15},{8,0},{9,1},... | collective-permute-start | bytes 73736 | tf_op jit(solution)/shard_map/ppermute | solution.py:404
  30.8 1.8 %collective-permute-start.10 = (bf16[96,128]{1,0:T(8,128)(2,1)S(1)}, bf16[96,128]{1,0:T(8,128)(2,1)S(1)}, u32[]{:S(2)}, u32[]{:S(2)}) collective-permute-start(bf16[96,128]{1,0:T(8,128)(2,1)S(1)} %get-tuple-element.45), channel_id=1, source_target_pairs={{0,4},{1,5},{2,6},{3,7},{4,0},{5,1},{6,2},{7,3},{8,12},{9,13},{10,... | collective-permute-start | bytes 73736 | tf_op jit(solution)/shard_map/ppermute | solution.py:404
  32.5 0.1 pad_maximum_fusion.1
  32.6 0.1 collective-permute-done.9.refs_1_
  32.6 1.9 %collective-permute-done.10.refs_2_ = bf16[96,128]{1,0:T(8,128)(2,1)S(1)} collective-permute-done((bf16[96,128]{1,0:T(8,128)(2,1)S(1)}, bf16[96,128]{1,0:T(8,128)(2,1)S(1)}, u32[]{:S(2)}, u32[]{:S(2)}) %collective-permute-start.10) | collective-permute-done | bytes 24608 | tf_op jit(solution)/shard_map/ppermute | solution.py:404
  34.6 3.6 %collective-permute-done.11.refs_3_ = bf16[96,128]{1,0:T(8,128)(2,1)S(1)} collective-permute-done((bf16[96,128]{1,0:T(8,128)(2,1)S(1)}, bf16[96,128]{1,0:T(8,128)(2,1)S(1)}, u32[]{:S(2)}, u32[]{:S(2)}) %collective-permute-start.11) | collective-permute-done | bytes 24608 | tf_op jit(solution)/shard_map/ppermute | solution.py:404
  38.1 1.0 %merge_states.1 = bf16[2,4,1024]{2,1,0:T(4,128)(2,1)} custom-call(bf16[8,8,128]{2,1,0:T(8,128)(2,1)S(1)} %get-tuple-element.26.own_ref, f32[8,128]{1,0:T(8,128)S(1)} %get-tuple-element.50.cos_ref, f32[8,128]{1,0:T(8,128)S(1)} %get-tuple-element.51.sin_ref, bf16[96,128]{1,0:T(8,128)(2,1)S(1)} %get-tuple-element.43.refs_0_, ...), custom_call_target="tpu_custom_call" | custom-call | tf_op jit(solution)/shard_map/merge_states/pallas_call | solution.py:574
  (15 shorter events, 0.1 us)
Async XLA Ops:
  1.2 5.8 %collective-permute-start = (bf16[8,8,128]{2,1,0:T(8,128)(2,1)S(1)}, bf16[8,8,128]{2,1,0:T(8,128)(2,1)S(1)}, u32[]{:S(2)}, u32[]{:S(2)}) collective-permute-start(bf16[8,8,128]{2,1,0:T(8,128)(2,1)S(1)} %get-tuple-element.27.own_ref), channel_id=1, source_target_pairs={{0,2},{1,3},{2,0},{3,1},{4,6},{5,7},{6,4},{7,5},{8,10},{9,11},{10,... | collective-permute-start | bytes 49160 | tf_op jit(solution)/shard_map/ppermute | solution.py:404
  4.2 14.7 %collective-permute-start.5 = (bf16[2,256,512]{2,1,0:T(8,128)(2,1)S(1)}, bf16[2,256,512]{2,1,0:T(8,128)(2,1)S(1)}, u32[]{:S(2)}, u32[]{:S(2)}) collective-permute-start(bf16[2,256,512]{2,1,0:T(8,128)(2,1)S(1)} %get-tuple-element.32), channel_id=1, source_target_pairs={{0,2},{1,3},{2,0},{3,1},{4,6},{5,7},{6,4},{7,5},{8,10},{9,11},{10,... | collective-permute-start | bytes 1572872 | tf_op jit(solution)/shard_map/ppermute | solution.py:404
  4.3 13.3 %copy-start = (s32[2]{0:T(128)S(1)}, s32[2]{0:T(128)}, u32[]{:S(2)}) copy-start(s32[2]{0:T(128)} %refs_1_.5) | copy-start | bytes 28
  4.3 14.6 %copy-start.1 = (s32[2]{0:T(128)S(1)}, s32[2]{0:T(128)}, u32[]{:S(2)}) copy-start(s32[2]{0:T(128)} %refs_1_.4) | copy-start | bytes 28
  4.3 14.6 %copy-start.2 = (s32[16]{0:T(128)S(1)}, s32[16]{0:T(128)}, u32[]{:S(2)}) copy-start(s32[16]{0:T(128)} %refs_2_.1) | copy-start | bytes 196
  4.3 14.6 %copy-start.3 = (s32[16]{0:T(128)S(1)}, s32[16]{0:T(128)}, u32[]{:S(2)}) copy-start(s32[16]{0:T(128)} %refs_3_.1) | copy-start | bytes 196
  7.0 5.3 %collective-permute-start.1 = (bf16[1,24,8,128]{3,2,1,0:T(8,128)(2,1)S(1)}, bf16[1,24,8,128]{3,2,1,0:T(8,128)(2,1)S(1)}, u32[]{:S(2)}, u32[]{:S(2)}) collective-permute-start(bf16[1,24,8,128]{3,2,1,0:T(8,128)(2,1)S(1)} %maximum_bitcast_fusion), channel_id=1, source_target_pairs={{0,8},{1,9},{2,10},{3,11},{4,12},{5,13},{6,14},{7,15},{8,0},{9,1},... | collective-permute-start | bytes 147464 | tf_op jit(solution)/shard_map/ppermute | solution.py:404
  12.3 1.9 %collective-permute-start.3 = (bf16[2,24,8,128]{3,2,1,0:T(8,128)(2,1)S(1)}, bf16[2,24,8,128]{3,2,1,0:T(8,128)(2,1)S(1)}, u32[]{:S(2)}, u32[]{:S(2)}) collective-permute-start(bf16[2,24,8,128]{3,2,1,0:T(8,128)(2,1)S(1)} %pad_maximum_fusion.lane_ref.refs_2_), channel_id=1, source_target_pairs={{0,1},{1,0},{2,3},{3,2},{4,5},{5,4},{6,7},{7,6},{8,9},{9,8},{10,11... | collective-permute-start | bytes 294920 | tf_op jit(solution)/shard_map/ppermute | solution.py:404
  12.4 5.2 %collective-permute-start.2 = (bf16[2,24,8,128]{3,2,1,0:T(8,128)(2,1)S(1)}, bf16[2,24,8,128]{3,2,1,0:T(8,128)(2,1)S(1)}, u32[]{:S(2)}, u32[]{:S(2)}) collective-permute-start(bf16[2,24,8,128]{3,2,1,0:T(8,128)(2,1)S(1)} %pad_maximum_fusion.lane_ref.refs_2_), channel_id=1, source_target_pairs={{0,4},{1,5},{2,6},{3,7},{4,0},{5,1},{6,2},{7,3},{8,12},{9,13},{10,... | collective-permute-start | bytes 294920 | tf_op jit(solution)/shard_map/ppermute | solution.py:404
  17.6 1.3 %collective-permute-start.4 = (bf16[2,24,8,128]{3,2,1,0:T(8,128)(2,1)S(1)}, bf16[2,24,8,128]{3,2,1,0:T(8,128)(2,1)S(1)}, u32[]{:S(2)}, u32[]{:S(2)}) collective-permute-start(bf16[2,24,8,128]{3,2,1,0:T(8,128)(2,1)S(1)} %collective-permute-done.2.refs_3_.refs_4_), channel_id=1, source_target_pairs={{0,1},{1,0},{2,3},{3,2},{4,5},{5,4},{6,7},{7,6},{8,9},{9,8},{10,11... | collective-permute-start | bytes 294920 | tf_op jit(solution)/shard_map/ppermute | solution.py:404
  21.9 3.9 %collective-permute-start.6 = (bf16[96,128]{1,0:T(8,128)(2,1)S(1)}, bf16[96,128]{1,0:T(8,128)(2,1)S(1)}, u32[]{:S(2)}, u32[]{:S(2)}) collective-permute-start(bf16[96,128]{1,0:T(8,128)(2,1)S(1)} %get-tuple-element.41), channel_id=1, source_target_pairs={{0,2},{1,3},{2,0},{3,1},{4,6},{5,7},{6,4},{7,5},{8,10},{9,11},{10,... | collective-permute-start | bytes 73736 | tf_op jit(solution)/shard_map/ppermute | solution.py:404
  25.2 2.2 %collective-permute-start.7 = (bf16[368,128]{1,0:T(8,128)(2,1)S(1)}, bf16[368,128]{1,0:T(8,128)(2,1)S(1)}, u32[]{:S(2)}, u32[]{:S(2)}) collective-permute-start(bf16[368,128]{1,0:T(8,128)(2,1)S(1)} %other_lane.1), channel_id=1, source_target_pairs={{0,1},{1,0},{2,3},{3,2},{4,5},{5,4},{6,7},{7,6},{8,9},{9,8},{10,11... | collective-permute-start | bytes 282632 | tf_op jit(solution)/shard_map/ppermute | solution.py:404
  25.8 1.6 %collective-permute-start.8 = (bf16[96,128]{1,0:T(8,128)(2,1)S(1)}, bf16[96,128]{1,0:T(8,128)(2,1)S(1)}, u32[]{:S(2)}, u32[]{:S(2)}) collective-permute-start(bf16[96,128]{1,0:T(8,128)(2,1)S(1)} %collective-permute-done.6.far_ref), channel_id=1, source_target_pairs={{0,1},{1,0},{2,3},{3,2},{4,5},{5,4},{6,7},{7,6},{8,9},{9,8},{10,11... | collective-permute-start | bytes 73736 | tf_op jit(solution)/shard_map/ppermute | solution.py:404
  27.7 4.9 %collective-permute-start.9 = (bf16[96,128]{1,0:T(8,128)(2,1)S(1)}, bf16[96,128]{1,0:T(8,128)(2,1)S(1)}, u32[]{:S(2)}, u32[]{:S(2)}) collective-permute-start(bf16[96,128]{1,0:T(8,128)(2,1)S(1)} %get-tuple-element.44), channel_id=1, source_target_pairs={{0,8},{1,9},{2,10},{3,11},{4,12},{5,13},{6,14},{7,15},{8,0},{9,1},... | collective-permute-start | bytes 73736 | tf_op jit(solution)/shard_map/ppermute | solution.py:404
  30.8 3.8 %collective-permute-start.10 = (bf16[96,128]{1,0:T(8,128)(2,1)S(1)}, bf16[96,128]{1,0:T(8,128)(2,1)S(1)}, u32[]{:S(2)}, u32[]{:S(2)}) collective-permute-start(bf16[96,128]{1,0:T(8,128)(2,1)S(1)} %get-tuple-element.45), channel_id=1, source_target_pairs={{0,4},{1,5},{2,6},{3,7},{4,0},{5,1},{6,2},{7,3},{8,12},{9,13},{10,... | collective-permute-start | bytes 73736 | tf_op jit(solution)/shard_map/ppermute | solution.py:404
  32.5 5.6 %collective-permute-start.11 = (bf16[96,128]{1,0:T(8,128)(2,1)S(1)}, bf16[96,128]{1,0:T(8,128)(2,1)S(1)}, u32[]{:S(2)}, u32[]{:S(2)}) collective-permute-start(bf16[96,128]{1,0:T(8,128)(2,1)S(1)} %get-tuple-element.46), channel_id=1, source_target_pairs={{0,12},{1,13},{2,14},{3,15},{4,8},{5,9},{6,10},{7,11},{8,4},{9,5},... | collective-permute-start | bytes 73736 | tf_op jit(solution)/shard_map/ppermute | solution.py:404

commit v7 on v6

--- a/solution.py
+++ b/solution.py
@@ -99,44 +99,59 @@
         load.wait()
 
 
-def lower(sizes, masks, index_ref, lane_refs, down_ref, buffer, sems):
+def places_of(sizes, masks, chunks):
     requests, tokens, devices = sizes
-    here, _, per_head, _ = lane_of(index_ref, devices)
     heads = QUERY_HEADS // devices
+    per_head = devices // 2 // KEY_HEADS
+    return [
+        (side, i, heads + hop * chunks, 2 * (mask ^ hop * per_head) + side)
+        for side in range(2)
+        for i, mask in enumerate(masks)
+        for hop in range(2)
+    ]
+
+
+def streams(sizes, masks, index_ref, down_ref, buffer, sems):
     depth = buffer.shape[1]
-    chunks = depth // HEAD_WIDTH
-    work = []
-    for side, ref in enumerate(lane_refs):
-        for i, mask in enumerate(masks):
-            for hop in range(2):
-                source = here ^ (2 * (mask ^ hop * per_head) + side)
-                rows = pl.ds(pl.multiple_of(source * depth, depth), depth)
-                at = len(work)
-                copy = pltpu.make_async_copy(down_ref.at[rows], buffer.at[at], sems.at[at])
-                copy.start()
-                work.append((copy, ref, i, heads + hop * chunks))
+    copies = []
+    for at, (_, _, _, mask) in enumerate(places_of(sizes, masks, depth // HEAD_WIDTH)):
+        rows = pl.ds(pl.multiple_of((index_ref[0] ^ mask) * depth, depth), depth)
+        copies.append(pltpu.make_async_copy(down_ref.at[rows], buffer.at[at], sems.at[at]))
+    return copies
+
+
+def lower(sizes, masks, lane_refs, buffer, copies):
     total = None
-    for at, (copy, ref, i, first) in enumerate(work):
-        hidden = jnp.concatenate([ref[i, first + c] for c in range(chunks)], axis=1)
-        copy.wait()
+    chunks = buffer.shape[1] // HEAD_WIDTH
+    for at, (side, i, first, _) in enumerate(places_of(sizes, masks, chunks)):
+        tiles = range(first, first + chunks)
+        hidden = jnp.concatenate([lane_refs[side][i, c] for c in tiles], axis=1)
+        if copies:
+            copies[at].wait()
         term = dot(hidden, buffer[at], ((1,), (0,)))
         total = term if total is None else total + term
     return total
 
 
-def early_kernel(sizes, masks, index_ref, lane_ref, other_ref, down_ref, out_ref, buffer, sems):
-    out_ref[...] = lower(sizes, masks, index_ref, (lane_ref, other_ref), down_ref, buffer, sems)
+def early_kernel(sizes, masks, late_masks, *refs):
+    (index_ref, lane_ref, other_ref, down_ref, out_ref, held_ref, buffer, sems, late_sems) = refs
+    copies = streams(sizes, masks, index_ref, down_ref, buffer, sems)
+    late = streams(sizes, late_masks, index_ref, down_ref, held_ref, late_sems)
+    for copy in copies + late:
+        copy.start()
+    out_ref[...] = lower(sizes, masks, (lane_ref, other_ref), buffer, copies)
+    for copy in late:
+        copy.wait()
 
 
 def project_kernel(sizes, masks, *refs):
     (index_ref, adapter_ref, rank_ref, pool_ref) = refs[:4]
     (lane_ref, other_ref, early_ref, base_ref, down_ref, up_ref) = refs[4:10]
-    (own_ref, own_parts_ref, parts_ref, all_ref, buffer, sems) = refs[10:]
+    (own_ref, own_parts_ref, parts_ref, all_ref) = refs[10:]
     requests, tokens, devices = sizes
     rows = requests * tokens
     here, _, _, parity = lane_of(index_ref, devices)
-    lowered = early_ref[...]
-    lowered += lower(sizes, masks, index_ref, (lane_ref, other_ref), down_ref, buffer, sems)
+    lowered = early_ref[...] + lower(sizes, masks, (lane_ref, other_ref), down_ref, [])
     row_request = lax.broadcasted_iota(jnp.int32, (rows, 1), 0) // tokens
     ranks = jnp.zeros((rows, 1), jnp.int32)
     owners = jnp.zeros((rows, 1), jnp.int32)
@@ -461,8 +476,12 @@
         ],
         "pack",
     )
+    far_cache = swap(far_send, devices, 2 * partner)
+    bits = [1 << i for i in reversed(range(lanes.bit_length() - 1)) if 1 << i != partner]
+    own_slot = jnp.concatenate([own_queries, own_hidden], axis=0)
+    first_slot = swap(own_slot, devices, 2 * bits[0])
     far_hidden = swap(own_hidden, devices, 2 * partner)
-    far_cache = swap(far_send, devices, 2 * partner)
+    first_far_hidden = swap(own_hidden, devices, 2 * (partner ^ bits[0]))
 
     out_width = key_value_weight.shape[1]
     parts = 4 if width % (4 * HEAD_WIDTH) == 0 else 1
@@ -482,11 +501,12 @@
         ],
         "base",
     )
-    far_hidden, base = lax.optimization_barrier((far_hidden, base))
-
-    masks, lane = [0], jnp.concatenate([own_queries, own_hidden, far_hidden], axis=0)[None]
-    bits = [1 << i for i in reversed(range(lanes.bit_length() - 1)) if 1 << i != partner]
-    for bit in bits[:-1]:
+    first_far_hidden, base = lax.optimization_barrier((first_far_hidden, base))
+
+    masks = [0, bits[0]]
+    slots = [own_slot, far_hidden, first_slot, first_far_hidden]
+    lane = jnp.concatenate(slots, axis=0).reshape(2, -1, rows, HEAD_WIDTH)
+    for bit in bits[1:-1]:
         masks += [mask ^ bit for mask in masks]
         lane = jnp.concatenate([lane, swap(lane, devices, 2 * bit)], axis=0)
     other = swap(lane, devices, 1)
@@ -496,16 +516,13 @@
     down = pinned(adapter_down_weight[0])
     rank = down.shape[1]
     sources = 4 * len(masks)
-    streamed = [
-        pltpu.VMEM((sources, width, rank), jnp.bfloat16),
-        pltpu.SemaphoreType.DMA((sources,)),
-    ]
-    (early,) = call(
-        functools.partial(early_kernel, sizes, masks),
+    half = pltpu.VMEM((sources, width, rank), jnp.bfloat16)
+    (early, late_down) = call(
+        functools.partial(early_kernel, sizes, masks, late_masks),
         (index, lane, other, down),
         [smem()] + [vmem()] * 2 + [hbm()],
-        [pltpu.VMEM((rows, rank), jnp.float32)],
-        streamed,
+        [pltpu.VMEM((rows, rank), jnp.float32), half],
+        [half, pltpu.SemaphoreType.DMA((sources,)), pltpu.SemaphoreType.DMA((sources,))],
         "lora_first",
     )
     late_lane, early = lax.optimization_barrier((late_lane, early))
@@ -523,16 +540,16 @@
             late_other,
             early,
             base,
-            down,
+            late_down,
             up,
         ),
-        [smem()] * 4 + [vmem()] * 4 + [hbm(), vmem()],
+        [smem()] * 4 + [vmem()] * 6,
         [
             pltpu.VMEM((2, step, HEAD_WIDTH), jnp.float32),
             pltpu.VMEM((3 * step, HEAD_WIDTH), jnp.bfloat16),
             pltpu.VMEM((3 * step, HEAD_WIDTH), jnp.bfloat16),
         ],
-        [pltpu.VMEM((rows, out_width), jnp.float32)] + streamed,
+        [pltpu.VMEM((rows, out_width), jnp.float32)],
         "project",
     )
     far_parts = swap(parts, devices, 2 * partner)
@@ -567,9 +584,9 @@
         [pltpu.VMEM((GROUPED, 3 * rows, HEAD_WIDTH), jnp.float32)],
         "join",
     )
-    packets = [
-        x if mask == 0 else swap(x, devices, 2 * mask) for x, mask in zip(packets, all_masks)
-    ]
+    order = sorted(range(len(all_masks)), key=lambda i: -all_masks[i])
+    order = [i for i in order if all_masks[i] not in (0, bits[0])] + [1]
+    packets = [packets[0]] + [swap(packets[i], devices, 2 * all_masks[i]) for i in order]
     cosine, sine = rotation(lengths, tokens)
     return pl.pallas_call(
         functools.partial(merge_kernel, devices, requests, tokens),

time: 39.4 us -> 36.6 us (0.929)
  Pallas kernels: 13.3 us -> 11.6 us
  waiting for transfers between devices: 10.7 us -> 9.05 us
  starting transfers between devices: 14.7 us -> 15.2 us
    pallas_call x7, Pallas kernels: 12.2 us -> 10.6 us  [call(): pl.pallas_call(kernel, out_shape=tuple(out_shape), in_specs=in_specs, out...]
    ppermute x12 -> x13, waiting for transfers between devices: 10.7 us -> 9.05 us  [swap(): return lax.ppermute(x, 'tensor', [(d, d ^ bit) for d in range(devices)])]
    ppermute x12 -> x13, starting transfers between devices: 14.7 us -> 15.2 us  [swap(): return lax.ppermute(x, 'tensor', [(d, d ^ bit) for d in range(devices)])]
  transfers between devices with their start and end apart: 12 -> 13, of which waited for: 7 -> 8; matrix products, arithmetic and copies ran while one was open for 1% -> 1% of each run, Pallas kernels for 20% -> 22%
where the time goes in v7:
time: 36.6 us; the launch traced here: 36.4 us
  starting transfers between devices  15.2 us (42%)
  Pallas kernels  11.6 us (32%)
  waiting for transfers between devices  9.05 us (25%)
    ppermute x13, starting transfers between devices, swap(): return lax.ppermute(x, 'tensor', [(d, d ^ bit) for d in range(devices)])  15.2 us
    pallas_call x7, Pallas kernels, call(): pl.pallas_call(kernel, out_shape=tuple(out_shape), in_specs=in_specs, out...  10.6 us
    ppermute x13, waiting for transfers between devices, swap(): return lax.ppermute(x, 'tensor', [(d, d ^ bit) for d in range(devices)])  9.05 us
    pallas_call x1, Pallas kernels, per_device(): pl.pallas_call(functools.partial(merge_kernel, devices, requests, tokens)...  1.05 us
  transfers between devices with their start and end apart: 13, of which 8 were waited for; matrix products, arithmetic and copies ran while one was open for 1% of the time, Pallas kernels for 22%

profile of v7, /device:TPU:0, one launch (start us, length us, event | category | flops | bytes accessed | tf_op | source)
XLA Modules:
  0.0 36.4 jit_solution(16577026173608166396)
XLA Ops:
  0.0 1.2 %pack.1 = (bf16[8,8,128]{2,1,0:T(8,128)(2,1)S(1)}, bf16[8,8,128]{2,1,0:T(8,128)(2,1)S(1)}, bf16[2,256,512]{2,1,0:T(8,128)(2,1)S(1)}) custom-call(s32[1]{0:T(128)} %bitcast.index_ref.refs_0_, bf16[2,4,1024]{2,1,0:T(4,128)(2,1)} %query_ref.1, bf16[2,4,1024]{2,1,0:T(4,128)(2,1)} %hidden_ref.1, bf16[256,1024]{1,0:T(8,128)(2,1)} %bitcast.11, ...), custom_call_target="tpu_custom_call" | custom-call | flops 1000000 | tf_op jit(solution)/shard_map/pack/pallas_call | solution.py:452
  1.2 5.1 %collective-permute-start.2 = (bf16[8,8,128]{2,1,0:T(8,128)(2,1)S(1)}, bf16[8,8,128]{2,1,0:T(8,128)(2,1)S(1)}, u32[]{:S(2)}, u32[]{:S(2)}) collective-permute-start(bf16[8,8,128]{2,1,0:T(8,128)(2,1)S(1)} %get-tuple-element.29.own_ref), channel_id=1, source_target_pairs={{0,10},{1,11},{2,8},{3,9},{4,14},{5,15},{6,12},{7,13},{8,2},{9,3},... | collective-permute-start | bytes 49160 | tf_op jit(solution)/shard_map/ppermute | solution.py:419
  6.3 0.5 %collective-permute-start = (bf16[8,8,128]{2,1,0:T(8,128)(2,1)S(1)}, bf16[8,8,128]{2,1,0:T(8,128)(2,1)S(1)}, u32[]{:S(2)}, u32[]{:S(2)}) collective-permute-start(bf16[8,8,128]{2,1,0:T(8,128)(2,1)S(1)} %get-tuple-element.29.own_ref), channel_id=1, source_target_pairs={{0,2},{1,3},{2,0},{3,1},{4,6},{5,7},{6,4},{7,5},{8,10},{9,11},{10,... | collective-permute-start | bytes 49160 | tf_op jit(solution)/shard_map/ppermute | solution.py:419
  6.8 0.1 collective-permute-start.1
  6.9 1.7 %collective-permute-start.6 = (bf16[2,256,512]{2,1,0:T(8,128)(2,1)S(1)}, bf16[2,256,512]{2,1,0:T(8,128)(2,1)S(1)}, u32[]{:S(2)}, u32[]{:S(2)}) collective-permute-start(bf16[2,256,512]{2,1,0:T(8,128)(2,1)S(1)} %get-tuple-element.35), channel_id=1, source_target_pairs={{0,2},{1,3},{2,0},{3,1},{4,6},{5,7},{6,4},{7,5},{8,10},{9,11},{10,... | collective-permute-start | bytes 1572872 | tf_op jit(solution)/shard_map/ppermute | solution.py:419
  8.7 0.0 copy-start.2
  8.7 0.0 copy-start.3
  8.7 2.6 %base.1 = (f32[8,2048]{1,0:T(8,128)S(1)}, bf16[2,256,512]{2,1,0:T(8,128)(2,1)S(1)}, bf16[128,2048]{1,0:T(8,128)(2,1)S(1)}) custom-call(s32[1]{0:T(128)} %bitcast.index_ref.refs_0_, bf16[8,8,128]{2,1,0:T(8,128)(2,1)S(1)} %get-tuple-element.29.own_ref, bf16[1024,2048]{1,0:T(8,128)(2,1)} %weight_ref.1, bf16[256,1024]{1,0:T(8,128)(2,1)} %bitcast.12, ...), custom_call_target="tpu_custom_call" | custom-call | flops 1000000000 | tf_op jit(solution)/shard_map/base/pallas_call | solution.py:452
  11.3 0.3 collective-permute-done.1
  11.6 0.1 collective-permute-start.4
  11.7 1.6 %collective-permute-start.3 = (bf16[2,24,8,128]{3,2,1,0:T(8,128)(2,1)S(1)}, bf16[2,24,8,128]{3,2,1,0:T(8,128)(2,1)S(1)}, u32[]{:S(2)}, u32[]{:S(2)}) collective-permute-start(bf16[2,24,8,128]{3,2,1,0:T(8,128)(2,1)S(1)} %bitcast.7), channel_id=1, source_target_pairs={{0,4},{1,5},{2,6},{3,7},{4,0},{5,1},{6,2},{7,3},{8,12},{9,13},{10,... | collective-permute-start | bytes 294920 | tf_op jit(solution)/shard_map/ppermute | solution.py:419
  13.3 2.4 %lora_first.1 = (f32[8,128]{1,0:T(8,128)S(1)}, bf16[8,1024,128]{2,1,0:T(8,128)(2,1)S(1)}) custom-call(s32[1]{0:T(128)} %bitcast.index_ref.refs_0_, bf16[2,24,8,128]{3,2,1,0:T(8,128)(2,1)S(1)} %bitcast.8, bf16[2,24,8,128]{3,2,1,0:T(8,128)(2,1)S(1)} %collective-permute-done.4.refs_2_, bf16[16384,128]{1,0:T(8,128)(2,1)} %bitcast.10), custom_call_target="tpu_custom_call" | custom-call | flops 1000000 | tf_op jit(solution)/shard_map/lora_first/pallas_call | solution.py:452
  15.7 1.2 %collective-permute-done.3.refs_3_.refs_4_ = bf16[2,24,8,128]{3,2,1,0:T(8,128)(2,1)S(1)} collective-permute-done((bf16[2,24,8,128]{3,2,1,0:T(8,128)(2,1)S(1)}, bf16[2,24,8,128]{3,2,1,0:T(8,128)(2,1)S(1)}, u32[]{:S(2)}, u32[]{:S(2)}) %collective-permute-start.3) | collective-permute-done | bytes 98336 | tf_op jit(solution)/shard_map/ppermute | solution.py:419
  16.9 0.1 add_convert_fusion
  17.0 1.2 %collective-permute-done.5.refs_5_.refs_3_ = bf16[2,24,8,128]{3,2,1,0:T(8,128)(2,1)S(1)} collective-permute-done((bf16[2,24,8,128]{3,2,1,0:T(8,128)(2,1)S(1)}, bf16[2,24,8,128]{3,2,1,0:T(8,128)(2,1)S(1)}, u32[]{:S(2)}, u32[]{:S(2)}) %collective-permute-start.5) | collective-permute-done | bytes 98336 | tf_op jit(solution)/shard_map/ppermute | solution.py:419
  18.2 2.0 %collective-permute-done.6.refs_5_ = bf16[2,256,512]{2,1,0:T(8,128)(2,1)S(1)} collective-permute-done((bf16[2,256,512]{2,1,0:T(8,128)(2,1)S(1)}, bf16[2,256,512]{2,1,0:T(8,128)(2,1)S(1)}, u32[]{:S(2)}, u32[]{:S(2)}) %collective-permute-start.6) | collective-permute-done | bytes 524320 | tf_op jit(solution)/shard_map/ppermute | solution.py:419
  20.2 1.1 %project.1 = (f32[2,32,128]{2,1,0:T(8,128)S(1)}, bf16[96,128]{1,0:T(8,128)(2,1)S(1)}, bf16[96,128]{1,0:T(8,128)(2,1)S(1)}) custom-call(s32[1]{0:T(128)} %bitcast.index_ref.refs_0_, s32[2]{0:T(128)S(1)} %copy-done.1, s32[16]{0:T(128)S(1)} %copy-done.2, s32[16]{0:T(128)S(1)} %copy-done.3, bf16[2,24,8,128]{3,2,1,0:T(8,128)(2,1)S(1)} %collective-permute-done.3.refs_3_.refs_4_, ...), custom_call_target="tpu_custom_call" | custom-call | flops 1000000 | tf_op jit(solution)/shard_map/project/pallas_call | solution.py:452
  21.3 1.5 %collective-permute-start.7 = (bf16[96,128]{1,0:T(8,128)(2,1)S(1)}, bf16[96,128]{1,0:T(8,128)(2,1)S(1)}, u32[]{:S(2)}, u32[]{:S(2)}) collective-permute-start(bf16[96,128]{1,0:T(8,128)(2,1)S(1)} %get-tuple-element.45), channel_id=1, source_target_pairs={{0,2},{1,3},{2,0},{3,1},{4,6},{5,7},{6,4},{7,5},{8,10},{9,11},{10,... | collective-permute-start | bytes 73736 | tf_op jit(solution)/shard_map/ppermute | solution.py:419
  22.9 0.1 convert_element_type.11
  22.9 1.5 %other_lane.1 = bf16[368,128]{1,0:T(8,128)(2,1)S(1)} custom-call(s32[1]{0:T(128)} %bitcast.index_ref.refs_0_, s32[2]{0:T(128)S(1)} %copy-done, bf16[2,24,8,128]{3,2,1,0:T(8,128)(2,1)S(1)} %collective-permute-done.4.refs_2_, bf16[2,24,8,128]{3,2,1,0:T(8,128)(2,1)S(1)} %collective-permute-done.5.refs_5_.refs_3_, ...), custom_call_target="tpu_custom_call" | custom-call | flops 1000000 | tf_op jit(solution)/shard_map/other_lane/pallas_call | solution.py:452
  24.4 0.1 collective-permute-start.8
  24.5 0.7 %collective-permute-done.7.far_ref = bf16[96,128]{1,0:T(8,128)(2,1)S(1)} collective-permute-done((bf16[96,128]{1,0:T(8,128)(2,1)S(1)}, bf16[96,128]{1,0:T(8,128)(2,1)S(1)}, u32[]{:S(2)}, u32[]{:S(2)}) %collective-permute-start.7) | collective-permute-done | bytes 24608 | tf_op jit(solution)/shard_map/ppermute | solution.py:419
  25.2 0.1 fusion
  25.3 1.5 %own_lane.1 = (f32[256,128]{1,0:T(8,128)S(1)}, f32[8,128]{1,0:T(8,128)S(1)}) custom-call(s32[1]{0:T(128)} %bitcast.index_ref.refs_0_, s32[2]{0:T(128)S(1)} %copy-done, bf16[2,24,8,128]{3,2,1,0:T(8,128)(2,1)S(1)} %bitcast.9, bf16[2,24,8,128]{3,2,1,0:T(8,128)(2,1)S(1)} %collective-permute-done.3.refs_3_.refs_4_, ...), custom_call_target="tpu_custom_call" | custom-call | flops 1000000 | tf_op jit(solution)/shard_map/own_lane/pallas_call | solution.py:452
  26.8 0.3 join.1
  27.1 3.5 %collective-permute-start.10 = (bf16[96,128]{1,0:T(8,128)(2,1)S(1)}, bf16[96,128]{1,0:T(8,128)(2,1)S(1)}, u32[]{:S(2)}, u32[]{:S(2)}) collective-permute-start(bf16[96,128]{1,0:T(8,128)(2,1)S(1)} %get-tuple-element.48), channel_id=1, source_target_pairs={{0,12},{1,13},{2,14},{3,15},{4,8},{5,9},{6,10},{7,11},{8,4},{9,5},... | collective-permute-start | bytes 73736 | tf_op jit(solution)/shard_map/ppermute | solution.py:419
  30.6 1.0 %collective-permute-start.12 = (bf16[96,128]{1,0:T(8,128)(2,1)S(1)}, bf16[96,128]{1,0:T(8,128)(2,1)S(1)}, u32[]{:S(2)}, u32[]{:S(2)}) collective-permute-start(bf16[96,128]{1,0:T(8,128)(2,1)S(1)} %get-tuple-element.50), channel_id=1, source_target_pairs={{0,8},{1,9},{2,10},{3,11},{4,12},{5,13},{6,14},{7,15},{8,0},{9,1},... | collective-permute-start | bytes 73736 | tf_op jit(solution)/shard_map/ppermute | solution.py:419
  31.6 0.1 pad_maximum_fusion.1
  31.7 1.4 %collective-permute-done.10.refs_1_ = bf16[96,128]{1,0:T(8,128)(2,1)S(1)} collective-permute-done((bf16[96,128]{1,0:T(8,128)(2,1)S(1)}, bf16[96,128]{1,0:T(8,128)(2,1)S(1)}, u32[]{:S(2)}, u32[]{:S(2)}) %collective-permute-start.10) | collective-permute-done | bytes 24608 | tf_op jit(solution)/shard_map/ppermute | solution.py:419
  33.0 1.7 %collective-permute-done.11.refs_2_ = bf16[96,128]{1,0:T(8,128)(2,1)S(1)} collective-permute-done((bf16[96,128]{1,0:T(8,128)(2,1)S(1)}, bf16[96,128]{1,0:T(8,128)(2,1)S(1)}, u32[]{:S(2)}, u32[]{:S(2)}) %collective-permute-start.11) | collective-permute-done | bytes 24608 | tf_op jit(solution)/shard_map/ppermute | solution.py:419
  34.7 0.6 %collective-permute-done.12.refs_3_ = bf16[96,128]{1,0:T(8,128)(2,1)S(1)} collective-permute-done((bf16[96,128]{1,0:T(8,128)(2,1)S(1)}, bf16[96,128]{1,0:T(8,128)(2,1)S(1)}, u32[]{:S(2)}, u32[]{:S(2)}) %collective-permute-start.12) | collective-permute-done | bytes 24608 | tf_op jit(solution)/shard_map/ppermute | solution.py:419
  35.3 1.0 %merge_states.1 = bf16[2,4,1024]{2,1,0:T(4,128)(2,1)} custom-call(bf16[8,8,128]{2,1,0:T(8,128)(2,1)S(1)} %get-tuple-element.28.own_ref, f32[8,128]{1,0:T(8,128)S(1)} %get-tuple-element.54.cos_ref, f32[8,128]{1,0:T(8,128)S(1)} %get-tuple-element.55.sin_ref, bf16[96,128]{1,0:T(8,128)(2,1)S(1)} %get-tuple-element.47.refs_0_, ...), custom_call_target="tpu_custom_call" | custom-call | tf_op jit(solution)/shard_map/merge_states/pallas_call | solution.py:591
  (21 shorter events, 0.1 us)
Async XLA Ops:
  1.2 10.1 %collective-permute-start.2 = (bf16[8,8,128]{2,1,0:T(8,128)(2,1)S(1)}, bf16[8,8,128]{2,1,0:T(8,128)(2,1)S(1)}, u32[]{:S(2)}, u32[]{:S(2)}) collective-permute-start(bf16[8,8,128]{2,1,0:T(8,128)(2,1)S(1)} %get-tuple-element.29.own_ref), channel_id=1, source_target_pairs={{0,10},{1,11},{2,8},{3,9},{4,14},{5,15},{6,12},{7,13},{8,2},{9,3},... | collective-permute-start | bytes 49160 | tf_op jit(solution)/shard_map/ppermute | solution.py:419
  6.3 5.0 %collective-permute-start = (bf16[8,8,128]{2,1,0:T(8,128)(2,1)S(1)}, bf16[8,8,128]{2,1,0:T(8,128)(2,1)S(1)}, u32[]{:S(2)}, u32[]{:S(2)}) collective-permute-start(bf16[8,8,128]{2,1,0:T(8,128)(2,1)S(1)} %get-tuple-element.29.own_ref), channel_id=1, source_target_pairs={{0,2},{1,3},{2,0},{3,1},{4,6},{5,7},{6,4},{7,5},{8,10},{9,11},{10,... | collective-permute-start | bytes 49160 | tf_op jit(solution)/shard_map/ppermute | solution.py:419
  6.8 4.8 %collective-permute-start.1 = (bf16[16,8,128]{2,1,0:T(8,128)(2,1)S(1)}, bf16[16,8,128]{2,1,0:T(8,128)(2,1)S(1)}, u32[]{:S(2)}, u32[]{:S(2)}) collective-permute-start(bf16[16,8,128]{2,1,0:T(8,128)(2,1)S(1)} %pad_maximum_fusion), channel_id=1, source_target_pairs={{0,8},{1,9},{2,10},{3,11},{4,12},{5,13},{6,14},{7,15},{8,0},{9,1},... | collective-permute-start | bytes 98312 | tf_op jit(solution)/shard_map/ppermute | solution.py:419
  6.9 13.3 %collective-permute-start.6 = (bf16[2,256,512]{2,1,0:T(8,128)(2,1)S(1)}, bf16[2,256,512]{2,1,0:T(8,128)(2,1)S(1)}, u32[]{:S(2)}, u32[]{:S(2)}) collective-permute-start(bf16[2,256,512]{2,1,0:T(8,128)(2,1)S(1)} %get-tuple-element.35), channel_id=1, source_target_pairs={{0,2},{1,3},{2,0},{3,1},{4,6},{5,7},{6,4},{7,5},{8,10},{9,11},{10,... | collective-permute-start | bytes 1572872 | tf_op jit(solution)/shard_map/ppermute | solution.py:419
  8.6 8.3 %copy-start = (s32[2]{0:T(128)S(1)}, s32[2]{0:T(128)}, u32[]{:S(2)}) copy-start(s32[2]{0:T(128)} %refs_1_.5) | copy-start | bytes 28
  8.6 11.5 %copy-start.1 = (s32[2]{0:T(128)S(1)}, s32[2]{0:T(128)}, u32[]{:S(2)}) copy-start(s32[2]{0:T(128)} %refs_1_.4) | copy-start | bytes 28
  8.7 11.5 %copy-start.2 = (s32[16]{0:T(128)S(1)}, s32[16]{0:T(128)}, u32[]{:S(2)}) copy-start(s32[16]{0:T(128)} %refs_2_.1) | copy-start | bytes 196
  8.7 11.5 %copy-start.3 = (s32[16]{0:T(128)S(1)}, s32[16]{0:T(128)}, u32[]{:S(2)}) copy-start(s32[16]{0:T(128)} %refs_3_.1) | copy-start | bytes 196
  11.6 1.7 %collective-permute-start.4 = (bf16[2,24,8,128]{3,2,1,0:T(8,128)(2,1)S(1)}, bf16[2,24,8,128]{3,2,1,0:T(8,128)(2,1)S(1)}, u32[]{:S(2)}, u32[]{:S(2)}) collective-permute-start(bf16[2,24,8,128]{3,2,1,0:T(8,128)(2,1)S(1)} %bitcast.6), channel_id=1, source_target_pairs={{0,1},{1,0},{2,3},{3,2},{4,5},{5,4},{6,7},{7,6},{8,9},{9,8},{10,11... | collective-permute-start | bytes 294920 | tf_op jit(solution)/shard_map/ppermute | solution.py:419
  11.7 5.2 %collective-permute-start.3 = (bf16[2,24,8,128]{3,2,1,0:T(8,128)(2,1)S(1)}, bf16[2,24,8,128]{3,2,1,0:T(8,128)(2,1)S(1)}, u32[]{:S(2)}, u32[]{:S(2)}) collective-permute-start(bf16[2,24,8,128]{3,2,1,0:T(8,128)(2,1)S(1)} %bitcast.7), channel_id=1, source_target_pairs={{0,4},{1,5},{2,6},{3,7},{4,0},{5,1},{6,2},{7,3},{8,12},{9,13},{10,... | collective-permute-start | bytes 294920 | tf_op jit(solution)/shard_map/ppermute | solution.py:419
  16.9 1.3 %collective-permute-start.5 = (bf16[2,24,8,128]{3,2,1,0:T(8,128)(2,1)S(1)}, bf16[2,24,8,128]{3,2,1,0:T(8,128)(2,1)S(1)}, u32[]{:S(2)}, u32[]{:S(2)}) collective-permute-start(bf16[2,24,8,128]{3,2,1,0:T(8,128)(2,1)S(1)} %collective-permute-done.3.refs_3_.refs_4_), channel_id=1, source_target_pairs={{0,1},{1,0},{2,3},{3,2},{4,5},{5,4},{6,7},{7,6},{8,9},{9,8},{10,11... | collective-permute-start | bytes 294920 | tf_op jit(solution)/shard_map/ppermute | solution.py:419
  21.3 3.9 %collective-permute-start.7 = (bf16[96,128]{1,0:T(8,128)(2,1)S(1)}, bf16[96,128]{1,0:T(8,128)(2,1)S(1)}, u32[]{:S(2)}, u32[]{:S(2)}) collective-permute-start(bf16[96,128]{1,0:T(8,128)(2,1)S(1)} %get-tuple-element.45), channel_id=1, source_target_pairs={{0,2},{1,3},{2,0},{3,1},{4,6},{5,7},{6,4},{7,5},{8,10},{9,11},{10,... | collective-permute-start | bytes 73736 | tf_op jit(solution)/shard_map/ppermute | solution.py:419
  24.4 2.4 %collective-permute-start.8 = (bf16[368,128]{1,0:T(8,128)(2,1)S(1)}, bf16[368,128]{1,0:T(8,128)(2,1)S(1)}, u32[]{:S(2)}, u32[]{:S(2)}) collective-permute-start(bf16[368,128]{1,0:T(8,128)(2,1)S(1)} %other_lane.1), channel_id=1, source_target_pairs={{0,1},{1,0},{2,3},{3,2},{4,5},{5,4},{6,7},{7,6},{8,9},{9,8},{10,11... | collective-permute-start | bytes 282632 | tf_op jit(solution)/shard_map/ppermute | solution.py:419
  25.2 1.6 %collective-permute-start.9 = (bf16[96,128]{1,0:T(8,128)(2,1)S(1)}, bf16[96,128]{1,0:T(8,128)(2,1)S(1)}, u32[]{:S(2)}, u32[]{:S(2)}) collective-permute-start(bf16[96,128]{1,0:T(8,128)(2,1)S(1)} %collective-permute-done.7.far_ref), channel_id=1, source_target_pairs={{0,1},{1,0},{2,3},{3,2},{4,5},{5,4},{6,7},{7,6},{8,9},{9,8},{10,11... | collective-permute-start | bytes 73736 | tf_op jit(solution)/shard_map/ppermute | solution.py:419
  27.1 5.9 %collective-permute-start.10 = (bf16[96,128]{1,0:T(8,128)(2,1)S(1)}, bf16[96,128]{1,0:T(8,128)(2,1)S(1)}, u32[]{:S(2)}, u32[]{:S(2)}) collective-permute-start(bf16[96,128]{1,0:T(8,128)(2,1)S(1)} %get-tuple-element.48), channel_id=1, source_target_pairs={{0,12},{1,13},{2,14},{3,15},{4,8},{5,9},{6,10},{7,11},{8,4},{9,5},... | collective-permute-start | bytes 73736 | tf_op jit(solution)/shard_map/ppermute | solution.py:419
  30.6 4.1 %collective-permute-start.11 = (bf16[96,128]{1,0:T(8,128)(2,1)S(1)}, bf16[96,128]{1,0:T(8,128)(2,1)S(1)}, u32[]{:S(2)}, u32[]{:S(2)}) collective-permute-start(bf16[96,128]{1,0:T(8,128)(2,1)S(1)} %get-tuple-element.49), channel_id=1, source_target_pairs={{0,4},{1,5},{2,6},{3,7},{4,0},{5,1},{6,2},{7,3},{8,12},{9,13},{10,... | collective-permute-start | bytes 73736 | tf_op jit(solution)/shard_map/ppermute | solution.py:419
  30.6 4.7 %collective-permute-start.12 = (bf16[96,128]{1,0:T(8,128)(2,1)S(1)}, bf16[96,128]{1,0:T(8,128)(2,1)S(1)}, u32[]{:S(2)}, u32[]{:S(2)}) collective-permute-start(bf16[96,128]{1,0:T(8,128)(2,1)S(1)} %get-tuple-element.50), channel_id=1, source_target_pairs={{0,8},{1,9},{2,10},{3,11},{4,12},{5,13},{6,14},{7,15},{8,0},{9,1},... | collective-permute-start | bytes 73736 | tf_op jit(solution)/shard_map/ppermute | solution.py:419

commit v8 on v6

--- a/solution.py
+++ b/solution.py
@@ -29,6 +29,100 @@
     return x.astype(jnp.bfloat16).astype(jnp.float32)
 
 
+class Plan:
+    def __init__(self, devices, width):
+        lanes = devices // 2
+        per_head = lanes // KEY_HEADS
+        self.devices, self.per_head, self.partner = devices, per_head, per_head
+        self.heads, self.chunks = QUERY_HEADS // devices, width // HEAD_WIDTH
+        near = [m for m in range(1, lanes) if not m & self.partner]
+        far = [m for m in range(lanes) if m & self.partner]
+        if per_head > 1:
+            self.single = 1
+            self.near_pairs = [(m, m ^ 1) for m in near if m % 2 == 0]
+        else:
+            self.single = near[-1]
+            self.near_pairs = list(zip(near[:-1:2], near[1:-1:2]))
+        self.far_pairs = list(zip(far[::2], far[1::2]))
+        size = self.heads + self.chunks
+        slots = [((0, 0), ((0, 0), (1, 0))), ((self.single,) * 2, ((2, 0), (3, 0)))]
+        for k, (a, b) in enumerate(self.near_pairs):
+            at = size + 2 * size * k
+            slots.append(((a, b), ((2, at), (2, at + size))))
+            slots.append(((b, a), ((3, at + size), (3, at))))
+        self.slots = sorted(slots, key=self.head_masks)
+        self.far_slots = []
+        for k, (a, b) in enumerate(self.far_pairs):
+            at = 2 * self.chunks * k
+            self.far_slots.append(((a, b), ((0, at), (0, at + self.chunks))))
+            self.far_slots.append(((b, a), ((1, at + self.chunks), (1, at))))
+
+    def head_masks(self, slot):
+        return tuple(mask // self.per_head for mask in slot[0])
+
+    def attention_chunks(self, slot_rows, side=0):
+        count = HEAD_WIDTH // slot_rows
+        by_masks = {slot[0]: slot for slot in self.slots}
+        slots = [by_masks[slot[0][::-1]] if side else slot for slot in self.slots]
+        chunks = []
+        for at in range(0, len(slots), count):
+            runs = []
+            for slot in slots[at : at + count]:
+                if runs and self.head_masks(runs[-1][0]) == self.head_masks(slot):
+                    runs[-1].append(slot)
+                else:
+                    runs.append([slot])
+            chunks.append(runs)
+        return chunks
+
+
+def here_mask(masks, here):
+    return masks[0] if masks[0] == masks[1] else jnp.where(here % 2 == 0, masks[0], masks[1])
+
+
+def sources_of(slots, skip):
+    return [
+        (array, tile + skip, masks, side)
+        for masks, places in slots
+        for side, (array, tile) in enumerate(places)
+    ]
+
+
+def streams(sources, index_ref, down_ref, buffer, sems):
+    depth = buffer.shape[1]
+    here = index_ref[0]
+    copies = []
+    for at, (_, _, masks, side) in enumerate(sources):
+        source = here ^ (2 * here_mask(masks, here) + side)
+        rows = pl.ds(pl.multiple_of(source * depth, depth), depth)
+        copies.append(pltpu.make_async_copy(down_ref.at[rows], buffer.at[at], sems.at[at]))
+    return copies
+
+
+def lower(sources, arrays, buffer, copies):
+    total = None
+    chunks = buffer.shape[1] // HEAD_WIDTH
+    for at, (array, first, _, _) in enumerate(sources):
+        hidden = jnp.concatenate([arrays[array][first + c] for c in range(chunks)], axis=1)
+        if copies:
+            copies[at].wait()
+        term = dot(hidden, buffer[at], ((1,), (0,)))
+        total = term if total is None else total + term
+    return total
+
+
+def early_kernel(plan, *refs):
+    (index_ref, *arrays, down_ref, out_ref, held_ref, buffer, sems, late_sems) = refs
+    sources = sources_of(plan.slots, plan.heads)
+    copies = streams(sources, index_ref, down_ref, buffer, sems)
+    late = streams(sources_of(plan.far_slots, 0), index_ref, down_ref, held_ref, late_sems)
+    for copy in copies + late:
+        copy.start()
+    out_ref[...] = lower(sources, arrays, buffer, copies)
+    for copy in late:
+        copy.wait()
+
+
 def lane_of(index_ref, devices):
     here = index_ref[0]
     chip = here // 2
@@ -51,7 +145,7 @@
 
 
 def pack_kernel(sizes, index_ref, query_ref, hidden_ref, key_ref, value_ref, *refs):
-    own_query_ref, own_hidden_ref, cache_ref, query_buf, hidden_buf, sems = refs
+    own_ref, cache_ref, query_buf, hidden_buf, sems = refs
     requests, tokens, devices = sizes
     _, _, _, parity = lane_of(index_ref, devices)
     loads = [
@@ -61,14 +155,14 @@
     caches = cache_copies(key_ref, value_ref, cache_ref, 1 - parity, sems)
     for load in loads + caches:
         load.start()
-    for load, ref, out_ref in zip(
-        loads, (query_buf, hidden_buf), (own_query_ref, own_hidden_ref)
-    ):
+    at = 0
+    for load, ref in zip(loads, (query_buf, hidden_buf)):
         load.wait()
         rows = jnp.concatenate([ref[b].astype(jnp.float32) for b in range(requests)], axis=0)
         for c in range(rows.shape[1] // HEAD_WIDTH):
             tile = rows[:, c * HEAD_WIDTH : (c + 1) * HEAD_WIDTH]
-            out_ref[c] = tile.astype(jnp.bfloat16)
+            own_ref[at] = tile.astype(jnp.bfloat16)
+            at += 1
     for load in caches:
         load.wait()
 
@@ -89,9 +183,10 @@
     for load in loads + others:
         load.start()
     tiles = depth // HEAD_WIDTH
+    first = QUERY_HEADS // devices
     total = jnp.zeros(base_ref.shape, jnp.float32)
     for p in range(parts):
-        hidden = jnp.concatenate([own_ref[p * tiles + c] for c in range(tiles)], axis=1)
+        hidden = jnp.concatenate([own_ref[first + p * tiles + c] for c in range(tiles)], axis=1)
         loads[p].wait()
         total += dot(hidden, buffer[p], ((1,), (0,)))
     base_ref[...] = total
@@ -99,44 +194,15 @@
         load.wait()
 
 
-def lower(sizes, masks, index_ref, lane_refs, down_ref, buffer, sems):
-    requests, tokens, devices = sizes
-    here, _, per_head, _ = lane_of(index_ref, devices)
-    heads = QUERY_HEADS // devices
-    depth = buffer.shape[1]
-    chunks = depth // HEAD_WIDTH
-    work = []
-    for side, ref in enumerate(lane_refs):
-        for i, mask in enumerate(masks):
-            for hop in range(2):
-                source = here ^ (2 * (mask ^ hop * per_head) + side)
-                rows = pl.ds(pl.multiple_of(source * depth, depth), depth)
-                at = len(work)
-                copy = pltpu.make_async_copy(down_ref.at[rows], buffer.at[at], sems.at[at])
-                copy.start()
-                work.append((copy, ref, i, heads + hop * chunks))
-    total = None
-    for at, (copy, ref, i, first) in enumerate(work):
-        hidden = jnp.concatenate([ref[i, first + c] for c in range(chunks)], axis=1)
-        copy.wait()
-        term = dot(hidden, buffer[at], ((1,), (0,)))
-        total = term if total is None else total + term
-    return total
-
-
-def early_kernel(sizes, masks, index_ref, lane_ref, other_ref, down_ref, out_ref, buffer, sems):
-    out_ref[...] = lower(sizes, masks, index_ref, (lane_ref, other_ref), down_ref, buffer, sems)
-
-
-def project_kernel(sizes, masks, *refs):
+def project_kernel(sizes, plan, *refs):
     (index_ref, adapter_ref, rank_ref, pool_ref) = refs[:4]
-    (lane_ref, other_ref, early_ref, base_ref, down_ref, up_ref) = refs[4:10]
-    (own_ref, own_parts_ref, parts_ref, all_ref, buffer, sems) = refs[10:]
+    (far_ref, other_far_ref, early_ref, base_ref, down_ref, up_ref) = refs[4:10]
+    (own_ref, own_parts_ref, parts_ref, all_ref) = refs[10:]
     requests, tokens, devices = sizes
     rows = requests * tokens
     here, _, _, parity = lane_of(index_ref, devices)
-    lowered = early_ref[...]
-    lowered += lower(sizes, masks, index_ref, (lane_ref, other_ref), down_ref, buffer, sems)
+    sources = sources_of(plan.far_slots, 0)
+    lowered = early_ref[...] + lower(sources, (far_ref, other_far_ref), down_ref, [])
     row_request = lax.broadcasted_iota(jnp.int32, (rows, 1), 0) // tokens
     ranks = jnp.zeros((rows, 1), jnp.int32)
     owners = jnp.zeros((rows, 1), jnp.int32)
@@ -163,18 +229,12 @@
         out_ref[2 * step :] = values.astype(jnp.bfloat16)
 
 
-def chunks_of(masks, slots):
-    order = sorted(masks)
-    return [order[at : at + slots] for at in range(0, len(order), slots)]
-
-
-def attend(sizes, masks, index_ref, length_ref, first_ref, second_ref, cache_ref, far_ref, put):
+def attend(sizes, plan, side, index_ref, length_ref, arrays, cache_ref, far_ref, put):
     requests, tokens, devices = sizes
     here, chip, per_head, _ = lane_of(index_ref, devices)
-    heads = QUERY_HEADS // devices
+    heads = plan.heads
     slot_rows = heads * requests * tokens
     positions = cache_ref.shape[1] // requests
-    half = len(masks) // 2
     place = lax.broadcasted_iota(jnp.int32, (requests * positions, HEAD_WIDTH), 0)
     column = lax.broadcasted_iota(jnp.int32, (requests * positions, HEAD_WIDTH), 1)
     place_request = place // positions
@@ -188,18 +248,16 @@
         for device in (here, here ^ (2 * per_head))
     ]
     peaks, totals = [], []
-    for number, chunk in enumerate(chunks_of(masks, HEAD_WIDTH // slot_rows)):
+    for number, runs in enumerate(plan.attention_chunks(slot_rows, side)):
+        places = [places[side] for run in runs for _, places in run]
         query = jnp.concatenate(
-            [
-                (first_ref if masks.index(mask) < half else second_ref)[masks.index(mask) % half, h]
-                for mask in chunk
-                for h in range(heads)
-            ],
-            axis=0,
+            [arrays[array][tile + h] for array, tile in places for h in range(heads)], axis=0
         )
-        key_heads = sorted({mask // per_head for mask in chunk})
-        spots = [head_columns(((chip // per_head) ^ head) // 2) for head in key_heads]
-        share = HEAD_WIDTH // len(key_heads)
+        spots = [
+            head_columns(((chip // per_head) ^ (here_mask(run[0][0], here) // per_head)) // 2)
+            for run in runs
+        ]
+        share = HEAD_WIDTH // len(runs)
         scores = []
         for ref, valid in zip(caches, allowed):
             score = None
@@ -234,8 +292,8 @@
     return out
 
 
-def other_kernel(sizes, masks, *refs):
-    (index_ref, length_ref, first_ref, second_ref, cache_ref, far_ref, parts_ref, send_ref) = refs
+def other_kernel(sizes, plan, *refs):
+    (index_ref, length_ref, *arrays, cache_ref, far_ref, parts_ref, send_ref) = refs
     proj_rows = parts_ref.shape[0]
 
     def put(chunk, row, mix):
@@ -243,7 +301,7 @@
         send_ref[at : at + mix.shape[0]] = mix.astype(jnp.bfloat16)
 
     peaks, totals = attend(
-        sizes, masks, index_ref, length_ref, first_ref, second_ref, cache_ref, far_ref, put
+        sizes, plan, 1, index_ref, length_ref, arrays, cache_ref, far_ref, put
     )
     highs = [round_bf16(total) for total in totals]
     lows = [total - high for total, high in zip(totals, highs)]
@@ -251,23 +309,23 @@
     send_ref[MIX_ROWS + proj_rows :] = rows_of(peaks + highs + lows, STAT_ROWS).astype(jnp.bfloat16)
 
 
-def own_kernel(sizes, masks, *refs):
-    (index_ref, length_ref, first_ref, second_ref, cache_ref, far_ref, mix_ref, stat_ref) = refs
+def own_kernel(sizes, plan, *refs):
+    (index_ref, length_ref, *arrays, cache_ref, far_ref, mix_ref, stat_ref) = refs
 
     def put(chunk, row, mix):
         at = chunk * 128 + row
         mix_ref[at : at + mix.shape[0]] = mix
 
     peaks, totals = attend(
-        sizes, masks, index_ref, length_ref, first_ref, second_ref, cache_ref, far_ref, put
+        sizes, plan, 0, index_ref, length_ref, arrays, cache_ref, far_ref, put
     )
     stat_ref[...] = rows_of(peaks + totals, 8)
 
 
-def join_kernel(sizes, masks, index_ref, mix_ref, stat_ref, proj_ref, far_ref, got_ref, got_far_ref, *refs):
+def join_kernel(sizes, plan, index_ref, mix_ref, stat_ref, proj_ref, far_ref, got_ref, got_far_ref, *refs):
     packet_refs, tail_ref = refs[:-1], refs[-1]
     requests, tokens, devices = sizes
-    _, chip, per_head, _ = lane_of(index_ref, devices)
+    here, chip, per_head, _ = lane_of(index_ref, devices)
     rows = requests * tokens
     heads = QUERY_HEADS // devices
     slot_rows = heads * rows
@@ -297,7 +355,7 @@
         tail_ref[g, rows : 2 * rows] = (keys - keys_high)[part]
         tail_ref[g, 2 * rows :] = values[part]
     stat_row = lax.broadcasted_iota(jnp.int32, (rows, HEAD_WIDTH), 0)
-    for c, chunk in enumerate(chunks_of(masks, HEAD_WIDTH // slot_rows)):
+    for c, runs in enumerate(plan.attention_chunks(slot_rows)):
         span = slice(c * 128, c * 128 + 128)
         mix = mix_ref[span] * table[:, c : c + 1]
         mix += got_ref[span].astype(jnp.float32) * table[:, CHUNKS + c : CHUNKS + c + 1]
@@ -308,10 +366,11 @@
                 stat_row == 1, high[c : c + 1], jnp.where(stat_row == 2, low[c : c + 1], 0.0)
             ),
         )
-        for t, mask in enumerate(chunk):
-            packet_ref = packet_refs[masks.index(mask)]
+        chunk = [masks for run in runs for masks, _ in run]
+        for t, masks in enumerate(chunk):
+            packet_ref = packet_refs[c * len(chunk) + t]
             shifted = stats if t == 0 else pltpu.roll(stats, HEAD_WIDTH - t * slot_rows, 1)
-            group = ((chip // per_head) ^ (mask // per_head)) // 2
+            group = ((chip // per_head) ^ (here_mask(masks, here) // per_head)) // 2
             tail = jnp.concatenate([tail_ref[group], shifted], axis=0)
             packet_ref[:slot_rows] = mix[t * slot_rows : (t + 1) * slot_rows].astype(jnp.bfloat16)
             packet_ref[slot_rows:] = tail.astype(jnp.bfloat16)
@@ -400,8 +459,9 @@
     return pl.CostEstimate(flops=int(flops), bytes_accessed=int(moved), transcendentals=0)
 
 
-def swap(x, devices, bit):
-    return lax.ppermute(x, "tensor", [(d, d ^ bit) for d in range(devices)])
+def trade(x, devices, even, odd, core=0):
+    pairs = [(d, d ^ (2 * (odd if d % 2 else even) + core)) for d in range(devices)]
+    return lax.ppermute(x, "tensor", pairs)
 
 
 def per_device(
@@ -421,10 +481,8 @@
     rows = requests * tokens
     devices = lax.axis_size("tensor")
     sizes = (requests, tokens, devices)
-    heads = QUERY_HEADS // devices
-    chunks = width // HEAD_WIDTH
-    lanes = devices // 2
-    partner = lanes // KEY_HEADS
+    plan = Plan(devices, width)
+    heads, chunks, partner = plan.heads, plan.chunks, plan.partner
     slot_rows = heads * rows
     index = lax.axis_index("tensor").reshape(1).astype(jnp.int32)
     flat = requests * cached_key_rows.shape[1]
@@ -445,15 +503,14 @@
             name=name,
         )(*operands)
 
-    own_queries, own_hidden, far_send = call(
+    def core_swap(x):
+        return trade(x, devices, 0, 0, core=1)
+
+    own, far_send = call(
         functools.partial(pack_kernel, sizes),
         (index, pinned(queries), pinned(hidden), cached_keys, cached_values),
         [smem()] + [hbm()] * 4,
-        [
-            pltpu.VMEM((heads, rows, HEAD_WIDTH), jnp.bfloat16),
-            pltpu.VMEM((chunks, rows, HEAD_WIDTH), jnp.bfloat16),
-            cache,
-        ],
+        [pltpu.VMEM((heads + chunks, rows, HEAD_WIDTH), jnp.bfloat16), cache],
         [
             pltpu.VMEM(queries.shape, jnp.bfloat16),
             pltpu.VMEM(hidden.shape, jnp.bfloat16),
@@ -461,15 +518,20 @@
         ],
         "pack",
     )
-    far_hidden = swap(own_hidden, devices, 2 * partner)
-    far_cache = swap(far_send, devices, 2 * partner)
+    far_cache = trade(far_send, devices, partner, partner)
+    own, other = lax.optimization_barrier((own, core_swap(own)))
+    near = [trade(own, devices, plan.single, plan.single)]
+    both = jnp.concatenate([own, other], axis=0)
+    both_hidden = jnp.concatenate([own[heads:], other[heads:]], axis=0)
+    near += [trade(both, devices, a, b) for a, b in plan.near_pairs]
+    far = [trade(both_hidden, devices, a, b) for a, b in plan.far_pairs]
 
     out_width = key_value_weight.shape[1]
     parts = 4 if width % (4 * HEAD_WIDTH) == 0 else 1
     up = adapter_up_weight[0]
     base, own_cache, up = call(
         functools.partial(base_kernel, sizes),
-        (index, own_hidden, pinned(key_value_weight), cached_keys, cached_values, pinned(up)),
+        (index, own, pinned(key_value_weight), cached_keys, cached_values, pinned(up)),
         [smem(), vmem()] + [hbm()] * 4,
         [
             pltpu.VMEM((rows, out_width), jnp.float32),
@@ -482,75 +544,64 @@
         ],
         "base",
     )
-    far_hidden, base = lax.optimization_barrier((far_hidden, base))
-
-    masks, lane = [0], jnp.concatenate([own_queries, own_hidden, far_hidden], axis=0)[None]
-    bits = [1 << i for i in reversed(range(lanes.bit_length() - 1)) if 1 << i != partner]
-    for bit in bits[:-1]:
-        masks += [mask ^ bit for mask in masks]
-        lane = jnp.concatenate([lane, swap(lane, devices, 2 * bit)], axis=0)
-    other = swap(lane, devices, 1)
-    late_lane = swap(lane, devices, 2 * bits[-1])
-    late_masks = [mask ^ bits[-1] for mask in masks]
+    near = jnp.concatenate(near, axis=0)
+    other_near = core_swap(near)
+    far = jnp.concatenate(far, axis=0)
+    far, base = lax.optimization_barrier((far, base))
+    other_far, far_cache = lax.optimization_barrier((core_swap(far), far_cache))
 
     down = pinned(adapter_down_weight[0])
     rank = down.shape[1]
-    sources = 4 * len(masks)
-    streamed = [
-        pltpu.VMEM((sources, width, rank), jnp.bfloat16),
-        pltpu.SemaphoreType.DMA((sources,)),
-    ]
-    (early,) = call(
-        functools.partial(early_kernel, sizes, masks),
-        (index, lane, other, down),
-        [smem()] + [vmem()] * 2 + [hbm()],
-        [pltpu.VMEM((rows, rank), jnp.float32)],
-        streamed,
-        "lora_first",
-    )
-    late_lane, early = lax.optimization_barrier((late_lane, early))
-    late_other = swap(late_lane, devices, 1)
-    late_other, far_cache = lax.optimization_barrier((late_other, far_cache))
+    half = pltpu.VMEM((devices // 2, width, rank), jnp.bfloat16)
+    half_sems = pltpu.SemaphoreType.DMA((devices // 2,))
+    arrays = (own, other, near, other_near)
+    (early, far_down) = call(
+        functools.partial(early_kernel, plan),
+        (index,) + arrays + (down,),
+        [smem()] + [vmem()] * 4 + [hbm()],
+        [pltpu.VMEM((rows, rank), jnp.float32), half],
+        [half, half_sems, half_sems],
+        "lora_near",
+    )
     step = GROUPED * rows
     proj, own_parts, parts = call(
-        functools.partial(project_kernel, sizes, late_masks),
+        functools.partial(project_kernel, sizes, plan),
         (
             index,
             request_adapter,
             adapter_rank_list,
             adapter_pool_row,
-            late_lane,
-            late_other,
+            far,
+            other_far,
             early,
             base,
-            down,
+            far_down,
             up,
         ),
-        [smem()] * 4 + [vmem()] * 4 + [hbm(), vmem()],
+        [smem()] * 4 + [vmem()] * 6,
         [
             pltpu.VMEM((2, step, HEAD_WIDTH), jnp.float32),
             pltpu.VMEM((3 * step, HEAD_WIDTH), jnp.bfloat16),
             pltpu.VMEM((3 * step, HEAD_WIDTH), jnp.bfloat16),
         ],
-        [pltpu.VMEM((rows, out_width), jnp.float32)] + streamed,
+        [pltpu.VMEM((rows, out_width), jnp.float32)],
         "project",
     )
-    far_parts = swap(parts, devices, 2 * partner)
-    all_masks = masks + late_masks
+    far_parts = trade(parts, devices, partner, partner)
     (send,) = call(
-        functools.partial(other_kernel, sizes, all_masks),
-        (index, lengths, other, late_other, own_cache, far_cache, own_parts),
-        [smem()] * 2 + [vmem()] * 5,
+        functools.partial(other_kernel, sizes, plan),
+        (index, lengths) + arrays + (own_cache, far_cache, own_parts),
+        [smem()] * 2 + [vmem()] * 7,
         [pltpu.VMEM((MIX_ROWS + 3 * step + STAT_ROWS, HEAD_WIDTH), jnp.bfloat16)],
         [],
         "other_lane",
     )
-    got = swap(send, devices, 1)
-    got_far_parts = swap(far_parts, devices, 1)
+    got = core_swap(send)
+    got_far_parts = core_swap(far_parts)
     mix, stats = call(
-        functools.partial(own_kernel, sizes, all_masks),
-        (index, lengths, lane, late_lane, own_cache, far_cache),
-        [smem()] * 2 + [vmem()] * 4,
+        functools.partial(own_kernel, sizes, plan),
+        (index, lengths) + arrays + (own_cache, far_cache),
+        [smem()] * 2 + [vmem()] * 6,
         [
             pltpu.VMEM((MIX_ROWS, HEAD_WIDTH), jnp.float32),
             pltpu.VMEM((8, HEAD_WIDTH), jnp.float32),
@@ -560,15 +611,16 @@
     )
     packet = pltpu.VMEM((slot_rows + 4 * rows, HEAD_WIDTH), jnp.bfloat16)
     packets = call(
-        functools.partial(join_kernel, sizes, all_masks),
+        functools.partial(join_kernel, sizes, plan),
         (index, mix, stats, proj, far_parts, got, got_far_parts),
         [smem()] + [vmem()] * 6,
-        [packet] * len(all_masks),
+        [packet] * len(plan.slots),
         [pltpu.VMEM((GROUPED, 3 * rows, HEAD_WIDTH), jnp.float32)],
         "join",
     )
     packets = [
-        x if mask == 0 else swap(x, devices, 2 * mask) for x, mask in zip(packets, all_masks)
+        trade(x, devices, *masks) if masks != (0, 0) else x
+        for x, (masks, _) in zip(packets, plan.slots)
     ]
     cosine, sine = rotation(lengths, tokens)
     return pl.pallas_call(
@@ -578,7 +630,7 @@
         out_specs=vmem(),
         compiler_params=pltpu.CompilerParams(vmem_limit_bytes=8 * MIB),
         name="merge_states",
-    )(own_queries, cosine, sine, *packets)
+    )(own, cosine, sine, *packets)
 
 
 def solution(mesh):

time: 39.4 us -> 40.6 us (1.030)
  Pallas kernels: 13.3 us -> 11.6 us
  waiting for transfers between devices: 10.7 us -> 12.2 us
  starting transfers between devices: 14.7 us -> 16 us
    pallas_call x7, Pallas kernels: 12.2 us -> 10.6 us  [call(): pl.pallas_call(kernel, out_shape=tuple(out_shape), in_specs=in_specs, out...]
    ppermute x12 -> x14, waiting for transfers between devices: 10.7 us -> 12.2 us  [trade(): return lax.ppermute(x, 'tensor', pairs)]
    ppermute x12 -> x14, starting transfers between devices: 14.7 us -> 16 us  [trade(): return lax.ppermute(x, 'tensor', pairs)]
  transfers between devices with their start and end apart: 12 -> 14, of which waited for: 7 -> 5; matrix products, arithmetic and copies ran while one was open for 1% -> 1% of each run, Pallas kernels for 20% -> 20%
where the time goes in v8:
time: 40.6 us; the launch traced here: 40.4 us
  starting transfers between devices  16 us (39%)
  waiting for transfers between devices  12.2 us (30%)
  Pallas kernels  11.6 us (29%)
    ppermute x14, starting transfers between devices, trade(): return lax.ppermute(x, 'tensor', pairs)  16 us
    ppermute x14, waiting for transfers between devices, trade(): return lax.ppermute(x, 'tensor', pairs)  12.2 us
    pallas_call x7, Pallas kernels, call(): pl.pallas_call(kernel, out_shape=tuple(out_shape), in_specs=in_specs, out...  10.6 us
    pallas_call x1, Pallas kernels, per_device(): pl.pallas_call(functools.partial(merge_kernel, devices, requests, tokens)...  1.05 us
  transfers between devices with their start and end apart: 14, of which 5 were waited for; matrix products, arithmetic and copies ran while one was open for 1% of the time, Pallas kernels for 20%

profile of v8, /device:TPU:0, one launch (start us, length us, event | category | flops | bytes accessed | tf_op | source)
XLA Modules:
  0.0 40.4 jit_solution(1642548523089110496)
XLA Ops:
  0.0 1.2 %pack.1 = (bf16[16,8,128]{2,1,0:T(8,128)(2,1)S(1)}, bf16[2,256,512]{2,1,0:T(8,128)(2,1)S(1)}) custom-call(s32[1]{0:T(128)} %bitcast.index_ref.refs_0_, bf16[2,4,1024]{2,1,0:T(4,128)(2,1)} %query_ref.1, bf16[2,4,1024]{2,1,0:T(4,128)(2,1)} %hidden_ref.1, bf16[256,1024]{1,0:T(8,128)(2,1)} %bitcast.6, bf16[256,1024]{1,0:T(8,128)(2,1)} %bitcast.8), custom_call_target="tpu_custom_call" | custom-call | flops 1000000 | tf_op jit(solution)/shard_map/pack/pallas_call | solution.py:495
  1.2 0.5 %collective-permute-start = (bf16[16,8,128]{2,1,0:T(8,128)(2,1)S(1)}, bf16[16,8,128]{2,1,0:T(8,128)(2,1)S(1)}, u32[]{:S(2)}, u32[]{:S(2)}) collective-permute-start(bf16[16,8,128]{2,1,0:T(8,128)(2,1)S(1)} %get-tuple-element.28.own_ref.refs_2_.refs_1_), channel_id=1, source_target_pairs={{0,1},{1,0},{2,3},{3,2},{4,5},{5,4},{6,7},{7,6},{8,9},{9,8},{10,11... | collective-permute-start | bytes 98312 | tf_op jit(solution)/shard_map/ppermute | solution.py:464
  1.7 2.6 %collective-permute-start.7 = (bf16[2,256,512]{2,1,0:T(8,128)(2,1)S(1)}, bf16[2,256,512]{2,1,0:T(8,128)(2,1)S(1)}, u32[]{:S(2)}, u32[]{:S(2)}) collective-permute-start(bf16[2,256,512]{2,1,0:T(8,128)(2,1)S(1)} %get-tuple-element.33), channel_id=1, source_target_pairs={{0,2},{1,3},{2,0},{3,1},{4,6},{5,7},{6,4},{7,5},{8,10},{9,11},{10,... | collective-permute-start | bytes 1572872 | tf_op jit(solution)/shard_map/ppermute | solution.py:464
  4.3 0.0 collective-permute-done.refs_3_.refs_2_
  4.4 3.2 %collective-permute-start.5 = (bf16[16,8,128]{2,1,0:T(8,128)(2,1)S(1)}, bf16[16,8,128]{2,1,0:T(8,128)(2,1)S(1)}, u32[]{:S(2)}, u32[]{:S(2)}) collective-permute-start(bf16[16,8,128]{2,1,0:T(8,128)(2,1)S(1)} %pad_maximum_fusion.2), channel_id=1, source_target_pairs={{0,10},{1,15},{2,8},{3,13},{4,14},{5,11},{6,12},{7,9},{8,2},{9,7},... | collective-permute-start | bytes 98312 | tf_op jit(solution)/shard_map/ppermute | solution.py:464
  7.6 0.9 %collective-permute-start.4 = (bf16[16,8,128]{2,1,0:T(8,128)(2,1)S(1)}, bf16[16,8,128]{2,1,0:T(8,128)(2,1)S(1)}, u32[]{:S(2)}, u32[]{:S(2)}) collective-permute-start(bf16[16,8,128]{2,1,0:T(8,128)(2,1)S(1)} %pad_maximum_fusion.2), channel_id=1, source_target_pairs={{0,2},{1,7},{2,0},{3,5},{4,6},{5,3},{6,4},{7,1},{8,10},{9,15},{10,... | collective-permute-start | bytes 98312 | tf_op jit(solution)/shard_map/ppermute | solution.py:464
  8.5 1.3 %collective-permute-start.1 = (bf16[16,8,128]{2,1,0:T(8,128)(2,1)S(1)}, bf16[16,8,128]{2,1,0:T(8,128)(2,1)S(1)}, u32[]{:S(2)}, u32[]{:S(2)}) collective-permute-start(bf16[16,8,128]{2,1,0:T(8,128)(2,1)S(1)} %get-tuple-element.28.own_ref.refs_2_.refs_1_), channel_id=1, source_target_pairs={{0,12},{1,13},{2,14},{3,15},{4,8},{5,9},{6,10},{7,11},{8,4},{9,5},... | collective-permute-start | bytes 98312 | tf_op jit(solution)/shard_map/ppermute | solution.py:464
  9.8 0.3 collective-permute-start.2
  10.1 2.6 %base.1 = (f32[8,2048]{1,0:T(8,128)S(1)}, bf16[2,256,512]{2,1,0:T(8,128)(2,1)S(1)}, bf16[128,2048]{1,0:T(8,128)(2,1)S(1)}) custom-call(s32[1]{0:T(128)} %bitcast.index_ref.refs_0_, bf16[16,8,128]{2,1,0:T(8,128)(2,1)S(1)} %get-tuple-element.28.own_ref.refs_2_.refs_1_, bf16[1024,2048]{1,0:T(8,128)(2,1)} %weight_ref.1, bf16[256,1024]{1,0:T(8,128)(2,1)} %bitcast.7, ...), custom_call_target="tpu_custom_call" | custom-call | flops 1000000000 | tf_op jit(solution)/shard_map/base/pallas_call | solution.py:495
  12.8 5.5 %collective-permute-done.4 = bf16[16,8,128]{2,1,0:T(8,128)(2,1)S(1)} collective-permute-done((bf16[16,8,128]{2,1,0:T(8,128)(2,1)S(1)}, bf16[16,8,128]{2,1,0:T(8,128)(2,1)S(1)}, u32[]{:S(2)}, u32[]{:S(2)}) %collective-permute-start.4) | collective-permute-done | bytes 32800 | tf_op jit(solution)/shard_map/ppermute | solution.py:464
  18.3 0.1 collective-permute-start.6
  18.4 0.5 %collective-permute-start.3 = (bf16[48,8,128]{2,1,0:T(8,128)(2,1)S(1)}, bf16[48,8,128]{2,1,0:T(8,128)(2,1)S(1)}, u32[]{:S(2)}, u32[]{:S(2)}) collective-permute-start(bf16[48,8,128]{2,1,0:T(8,128)(2,1)S(1)} %constant_dynamic-update-slice_fusion.refs_4_.refs_3_), channel_id=1, source_target_pairs={{0,1},{1,0},{2,3},{3,2},{4,5},{5,4},{6,7},{7,6},{8,9},{9,8},{10,11... | collective-permute-start | bytes 294920 | tf_op jit(solution)/shard_map/ppermute | solution.py:464
  18.9 0.1 add_convert_fusion
  19.0 0.9 %collective-permute-done.3.refs_5_.refs_4_ = bf16[48,8,128]{2,1,0:T(8,128)(2,1)S(1)} collective-permute-done((bf16[48,8,128]{2,1,0:T(8,128)(2,1)S(1)}, bf16[48,8,128]{2,1,0:T(8,128)(2,1)S(1)}, u32[]{:S(2)}, u32[]{:S(2)}) %collective-permute-start.3) | collective-permute-done | bytes 98336 | tf_op jit(solution)/shard_map/ppermute | solution.py:464
  19.9 2.4 %lora_near.1 = (f32[8,128]{1,0:T(8,128)S(1)}, bf16[8,1024,128]{2,1,0:T(8,128)(2,1)S(1)}) custom-call(s32[1]{0:T(128)} %bitcast.index_ref.refs_0_, bf16[16,8,128]{2,1,0:T(8,128)(2,1)S(1)} %get-tuple-element.28.own_ref.refs_2_.refs_1_, bf16[16,8,128]{2,1,0:T(8,128)(2,1)S(1)} %collective-permute-done.refs_3_.refs_2_, ...), custom_call_target="tpu_custom_call" | custom-call | flops 1000000 | tf_op jit(solution)/shard_map/lora_near/pallas_call | solution.py:495
  22.3 1.1 %project.1 = (f32[2,32,128]{2,1,0:T(8,128)S(1)}, bf16[96,128]{1,0:T(8,128)(2,1)S(1)}, bf16[96,128]{1,0:T(8,128)(2,1)S(1)}) custom-call(s32[1]{0:T(128)} %bitcast.index_ref.refs_0_, s32[2]{0:T(128)S(1)} %copy-done.1, s32[16]{0:T(128)S(1)} %copy-done.2, s32[16]{0:T(128)S(1)} %copy-done.3, bf16[32,8,128]{2,1,0:T(8,128)(2,1)S(1)} %pad_maximum_fusion.1.refs_4_, ...), custom_call_target="tpu_custom_call" | custom-call | flops 1000000 | tf_op jit(solution)/shard_map/project/pallas_call | solution.py:495
  23.4 1.8 %collective-permute-start.8 = (bf16[96,128]{1,0:T(8,128)(2,1)S(1)}, bf16[96,128]{1,0:T(8,128)(2,1)S(1)}, u32[]{:S(2)}, u32[]{:S(2)}) collective-permute-start(bf16[96,128]{1,0:T(8,128)(2,1)S(1)} %get-tuple-element.43), channel_id=1, source_target_pairs={{0,2},{1,3},{2,0},{3,1},{4,6},{5,7},{6,4},{7,5},{8,10},{9,11},{10,... | collective-permute-start | bytes 73736 | tf_op jit(solution)/shard_map/ppermute | solution.py:464
  25.3 0.1 convert_element_type.11
  25.4 1.5 %other_lane.1 = bf16[368,128]{1,0:T(8,128)(2,1)S(1)} custom-call(s32[1]{0:T(128)} %bitcast.index_ref.refs_0_, s32[2]{0:T(128)S(1)} %copy-done, bf16[16,8,128]{2,1,0:T(8,128)(2,1)S(1)} %get-tuple-element.28.own_ref.refs_2_.refs_1_, bf16[16,8,128]{2,1,0:T(8,128)(2,1)S(1)} %collective-permute-done.refs_3_.refs_2_, ...), custom_call_target="tpu_custom_call" | custom-call | flops 1000000 | tf_op jit(solution)/shard_map/other_lane/pallas_call | solution.py:495
  26.8 0.1 collective-permute-start.9
  27.0 0.3 collective-permute-done.8.far_ref
  27.3 0.1 collective-permute-start.10
  27.4 0.1 fusion
  27.5 1.5 %own_lane.1 = (f32[256,128]{1,0:T(8,128)S(1)}, f32[8,128]{1,0:T(8,128)S(1)}) custom-call(s32[1]{0:T(128)} %bitcast.index_ref.refs_0_, s32[2]{0:T(128)S(1)} %copy-done, bf16[16,8,128]{2,1,0:T(8,128)(2,1)S(1)} %get-tuple-element.28.own_ref.refs_2_.refs_1_, bf16[16,8,128]{2,1,0:T(8,128)(2,1)S(1)} %collective-permute-done.refs_3_.refs_2_, ...), custom_call_target="tpu_custom_call" | custom-call | flops 1000000 | tf_op jit(solution)/shard_map/own_lane/pallas_call | solution.py:495
  29.0 0.3 join.1
  29.3 1.8 %collective-permute-start.11 = (bf16[96,128]{1,0:T(8,128)(2,1)S(1)}, bf16[96,128]{1,0:T(8,128)(2,1)S(1)}, u32[]{:S(2)}, u32[]{:S(2)}) collective-permute-start(bf16[96,128]{1,0:T(8,128)(2,1)S(1)} %get-tuple-element.46), channel_id=1, source_target_pairs={{0,4},{1,9},{2,6},{3,11},{4,0},{5,13},{6,2},{7,15},{8,12},{9,1},{1... | collective-permute-start | bytes 73736 | tf_op jit(solution)/shard_map/ppermute | solution.py:464
  31.1 2.6 %collective-permute-start.12 = (bf16[96,128]{1,0:T(8,128)(2,1)S(1)}, bf16[96,128]{1,0:T(8,128)(2,1)S(1)}, u32[]{:S(2)}, u32[]{:S(2)}) collective-permute-start(bf16[96,128]{1,0:T(8,128)(2,1)S(1)} %get-tuple-element.47), channel_id=1, source_target_pairs={{0,8},{1,5},{2,10},{3,7},{4,12},{5,1},{6,14},{7,3},{8,0},{9,13},{1... | collective-permute-start | bytes 73736 | tf_op jit(solution)/shard_map/ppermute | solution.py:464
  33.7 0.1 collective-permute-start.13
  33.8 0.1 pad_maximum_fusion.3
  33.9 2.1 %collective-permute-done.12.refs_2_ = bf16[96,128]{1,0:T(8,128)(2,1)S(1)} collective-permute-done((bf16[96,128]{1,0:T(8,128)(2,1)S(1)}, bf16[96,128]{1,0:T(8,128)(2,1)S(1)}, u32[]{:S(2)}, u32[]{:S(2)}) %collective-permute-start.12) | collective-permute-done | bytes 24608 | tf_op jit(solution)/shard_map/ppermute | solution.py:464
  35.9 3.4 %collective-permute-done.13.refs_3_ = bf16[96,128]{1,0:T(8,128)(2,1)S(1)} collective-permute-done((bf16[96,128]{1,0:T(8,128)(2,1)S(1)}, bf16[96,128]{1,0:T(8,128)(2,1)S(1)}, u32[]{:S(2)}, u32[]{:S(2)}) %collective-permute-start.13) | collective-permute-done | bytes 24608 | tf_op jit(solution)/shard_map/ppermute | solution.py:464
  39.3 1.0 %merge_states.1 = bf16[2,4,1024]{2,1,0:T(4,128)(2,1)} custom-call(bf16[16,8,128]{2,1,0:T(8,128)(2,1)S(1)} %get-tuple-element.28.own_ref.refs_2_.refs_1_, f32[8,128]{1,0:T(8,128)S(1)} %get-tuple-element.52.cos_ref, f32[8,128]{1,0:T(8,128)S(1)} %get-tuple-element.53.sin_ref, bf16[96,128]{1,0:T(8,128)(2,1)S(1)} %get-tuple-element.45.refs_0_, ...), custom_call_target="tpu_custom_call" | custom-call | tf_op jit(solution)/shard_map/merge_states/pallas_call | solution.py:626
  (24 shorter events, 0.1 us)
Async XLA Ops:
  0.0 18.9 %copy-start = (s32[2]{0:T(128)S(1)}, s32[2]{0:T(128)}, u32[]{:S(2)}) copy-start(s32[2]{0:T(128)} %refs_1_.5) | copy-start | bytes 28
  1.2 3.1 %collective-permute-start = (bf16[16,8,128]{2,1,0:T(8,128)(2,1)S(1)}, bf16[16,8,128]{2,1,0:T(8,128)(2,1)S(1)}, u32[]{:S(2)}, u32[]{:S(2)}) collective-permute-start(bf16[16,8,128]{2,1,0:T(8,128)(2,1)S(1)} %get-tuple-element.28.own_ref.refs_2_.refs_1_), channel_id=1, source_target_pairs={{0,1},{1,0},{2,3},{3,2},{4,5},{5,4},{6,7},{7,6},{8,9},{9,8},{10,11... | collective-permute-start | bytes 98312 | tf_op jit(solution)/shard_map/ppermute | solution.py:464
  1.7 20.5 %collective-permute-start.7 = (bf16[2,256,512]{2,1,0:T(8,128)(2,1)S(1)}, bf16[2,256,512]{2,1,0:T(8,128)(2,1)S(1)}, u32[]{:S(2)}, u32[]{:S(2)}) collective-permute-start(bf16[2,256,512]{2,1,0:T(8,128)(2,1)S(1)} %get-tuple-element.33), channel_id=1, source_target_pairs={{0,2},{1,3},{2,0},{3,1},{4,6},{5,7},{6,4},{7,5},{8,10},{9,11},{10,... | collective-permute-start | bytes 1572872 | tf_op jit(solution)/shard_map/ppermute | solution.py:464
  4.4 8.4 %collective-permute-start.5 = (bf16[16,8,128]{2,1,0:T(8,128)(2,1)S(1)}, bf16[16,8,128]{2,1,0:T(8,128)(2,1)S(1)}, u32[]{:S(2)}, u32[]{:S(2)}) collective-permute-start(bf16[16,8,128]{2,1,0:T(8,128)(2,1)S(1)} %pad_maximum_fusion.2), channel_id=1, source_target_pairs={{0,10},{1,15},{2,8},{3,13},{4,14},{5,11},{6,12},{7,9},{8,2},{9,7},... | collective-permute-start | bytes 98312 | tf_op jit(solution)/shard_map/ppermute | solution.py:464
  7.6 10.7 %collective-permute-start.4 = (bf16[16,8,128]{2,1,0:T(8,128)(2,1)S(1)}, bf16[16,8,128]{2,1,0:T(8,128)(2,1)S(1)}, u32[]{:S(2)}, u32[]{:S(2)}) collective-permute-start(bf16[16,8,128]{2,1,0:T(8,128)(2,1)S(1)} %pad_maximum_fusion.2), channel_id=1, source_target_pairs={{0,2},{1,7},{2,0},{3,5},{4,6},{5,3},{6,4},{7,1},{8,10},{9,15},{10,... | collective-permute-start | bytes 98312 | tf_op jit(solution)/shard_map/ppermute | solution.py:464
  8.5 9.9 %collective-permute-start.1 = (bf16[16,8,128]{2,1,0:T(8,128)(2,1)S(1)}, bf16[16,8,128]{2,1,0:T(8,128)(2,1)S(1)}, u32[]{:S(2)}, u32[]{:S(2)}) collective-permute-start(bf16[16,8,128]{2,1,0:T(8,128)(2,1)S(1)} %get-tuple-element.28.own_ref.refs_2_.refs_1_), channel_id=1, source_target_pairs={{0,12},{1,13},{2,14},{3,15},{4,8},{5,9},{6,10},{7,11},{8,4},{9,5},... | collective-permute-start | bytes 98312 | tf_op jit(solution)/shard_map/ppermute | solution.py:464
  9.8 8.5 %collective-permute-start.2 = (bf16[32,8,128]{2,1,0:T(8,128)(2,1)S(1)}, bf16[32,8,128]{2,1,0:T(8,128)(2,1)S(1)}, u32[]{:S(2)}, u32[]{:S(2)}) collective-permute-start(bf16[32,8,128]{2,1,0:T(8,128)(2,1)S(1)} %pad_maximum_fusion), channel_id=1, source_target_pairs={{0,4},{1,9},{2,6},{3,11},{4,0},{5,13},{6,2},{7,15},{8,12},{9,1},{1... | collective-permute-start | bytes 196616 | tf_op jit(solution)/shard_map/ppermute | solution.py:464
  10.1 12.1 %copy-start.1 = (s32[2]{0:T(128)S(1)}, s32[2]{0:T(128)}, u32[]{:S(2)}) copy-start(s32[2]{0:T(128)} %refs_1_.4) | copy-start | bytes 28
  10.1 12.1 %copy-start.2 = (s32[16]{0:T(128)S(1)}, s32[16]{0:T(128)}, u32[]{:S(2)}) copy-start(s32[16]{0:T(128)} %refs_2_.1) | copy-start | bytes 196
  10.1 12.2 %copy-start.3 = (s32[16]{0:T(128)S(1)}, s32[16]{0:T(128)}, u32[]{:S(2)}) copy-start(s32[16]{0:T(128)} %refs_3_.1) | copy-start | bytes 196
  18.3 4.0 %collective-permute-start.6 = (bf16[32,8,128]{2,1,0:T(8,128)(2,1)S(1)}, bf16[32,8,128]{2,1,0:T(8,128)(2,1)S(1)}, u32[]{:S(2)}, u32[]{:S(2)}) collective-permute-start(bf16[32,8,128]{2,1,0:T(8,128)(2,1)S(1)} %pad_maximum_fusion.1.refs_4_), channel_id=1, source_target_pairs={{0,1},{1,0},{2,3},{3,2},{4,5},{5,4},{6,7},{7,6},{8,9},{9,8},{10,11... | collective-permute-start | bytes 196616 | tf_op jit(solution)/shard_map/ppermute | solution.py:464
  18.4 1.5 %collective-permute-start.3 = (bf16[48,8,128]{2,1,0:T(8,128)(2,1)S(1)}, bf16[48,8,128]{2,1,0:T(8,128)(2,1)S(1)}, u32[]{:S(2)}, u32[]{:S(2)}) collective-permute-start(bf16[48,8,128]{2,1,0:T(8,128)(2,1)S(1)} %constant_dynamic-update-slice_fusion.refs_4_.refs_3_), channel_id=1, source_target_pairs={{0,1},{1,0},{2,3},{3,2},{4,5},{5,4},{6,7},{7,6},{8,9},{9,8},{10,11... | collective-permute-start | bytes 294920 | tf_op jit(solution)/shard_map/ppermute | solution.py:464
  23.4 3.9 %collective-permute-start.8 = (bf16[96,128]{1,0:T(8,128)(2,1)S(1)}, bf16[96,128]{1,0:T(8,128)(2,1)S(1)}, u32[]{:S(2)}, u32[]{:S(2)}) collective-permute-start(bf16[96,128]{1,0:T(8,128)(2,1)S(1)} %get-tuple-element.43), channel_id=1, source_target_pairs={{0,2},{1,3},{2,0},{3,1},{4,6},{5,7},{6,4},{7,5},{8,10},{9,11},{10,... | collective-permute-start | bytes 73736 | tf_op jit(solution)/shard_map/ppermute | solution.py:464
  26.8 2.2 %collective-permute-start.9 = (bf16[368,128]{1,0:T(8,128)(2,1)S(1)}, bf16[368,128]{1,0:T(8,128)(2,1)S(1)}, u32[]{:S(2)}, u32[]{:S(2)}) collective-permute-start(bf16[368,128]{1,0:T(8,128)(2,1)S(1)} %other_lane.1), channel_id=1, source_target_pairs={{0,1},{1,0},{2,3},{3,2},{4,5},{5,4},{6,7},{7,6},{8,9},{9,8},{10,11... | collective-permute-start | bytes 282632 | tf_op jit(solution)/shard_map/ppermute | solution.py:464
  27.3 1.7 %collective-permute-start.10 = (bf16[96,128]{1,0:T(8,128)(2,1)S(1)}, bf16[96,128]{1,0:T(8,128)(2,1)S(1)}, u32[]{:S(2)}, u32[]{:S(2)}) collective-permute-start(bf16[96,128]{1,0:T(8,128)(2,1)S(1)} %collective-permute-done.8.far_ref), channel_id=1, source_target_pairs={{0,1},{1,0},{2,3},{3,2},{4,5},{5,4},{6,7},{7,6},{8,9},{9,8},{10,11... | collective-permute-start | bytes 73736 | tf_op jit(solution)/shard_map/ppermute | solution.py:464
  29.3 4.5 %collective-permute-start.11 = (bf16[96,128]{1,0:T(8,128)(2,1)S(1)}, bf16[96,128]{1,0:T(8,128)(2,1)S(1)}, u32[]{:S(2)}, u32[]{:S(2)}) collective-permute-start(bf16[96,128]{1,0:T(8,128)(2,1)S(1)} %get-tuple-element.46), channel_id=1, source_target_pairs={{0,4},{1,9},{2,6},{3,11},{4,0},{5,13},{6,2},{7,15},{8,12},{9,1},{1... | collective-permute-start | bytes 73736 | tf_op jit(solution)/shard_map/ppermute | solution.py:464
  31.1 4.8 %collective-permute-start.12 = (bf16[96,128]{1,0:T(8,128)(2,1)S(1)}, bf16[96,128]{1,0:T(8,128)(2,1)S(1)}, u32[]{:S(2)}, u32[]{:S(2)}) collective-permute-start(bf16[96,128]{1,0:T(8,128)(2,1)S(1)} %get-tuple-element.47), channel_id=1, source_target_pairs={{0,8},{1,5},{2,10},{3,7},{4,12},{5,1},{6,14},{7,3},{8,0},{9,13},{1... | collective-permute-start | bytes 73736 | tf_op jit(solution)/shard_map/ppermute | solution.py:464
  33.7 5.6 %collective-permute-start.13 = (bf16[96,128]{1,0:T(8,128)(2,1)S(1)}, bf16[96,128]{1,0:T(8,128)(2,1)S(1)}, u32[]{:S(2)}, u32[]{:S(2)}) collective-permute-start(bf16[96,128]{1,0:T(8,128)(2,1)S(1)} %get-tuple-element.48), channel_id=1, source_target_pairs={{0,12},{1,13},{2,14},{3,15},{4,8},{5,9},{6,10},{7,11},{8,4},{9,5},... | collective-permute-start | bytes 73736 | tf_op jit(solution)/shard_map/ppermute | solution.py:464

commit v9 on v8

--- a/solution.py
+++ b/solution.py
@@ -36,26 +36,21 @@
         self.devices, self.per_head, self.partner = devices, per_head, per_head
         self.heads, self.chunks = QUERY_HEADS // devices, width // HEAD_WIDTH
         near = [m for m in range(1, lanes) if not m & self.partner]
-        far = [m for m in range(lanes) if m & self.partner]
         if per_head > 1:
             self.single = 1
             self.near_pairs = [(m, m ^ 1) for m in near if m % 2 == 0]
         else:
             self.single = near[-1]
             self.near_pairs = list(zip(near[:-1:2], near[1:-1:2]))
-        self.far_pairs = list(zip(far[::2], far[1::2]))
-        size = self.heads + self.chunks
-        slots = [((0, 0), ((0, 0), (1, 0))), ((self.single,) * 2, ((2, 0), (3, 0)))]
+        size = self.heads + 2 * self.chunks
+        slots = [((self.single,) * 2, ((0, 0), (1, 0)))]
         for k, (a, b) in enumerate(self.near_pairs):
             at = size + 2 * size * k
-            slots.append(((a, b), ((2, at), (2, at + size))))
-            slots.append(((b, a), ((3, at + size), (3, at))))
-        self.slots = sorted(slots, key=self.head_masks)
-        self.far_slots = []
-        for k, (a, b) in enumerate(self.far_pairs):
-            at = 2 * self.chunks * k
-            self.far_slots.append(((a, b), ((0, at), (0, at + self.chunks))))
-            self.far_slots.append(((b, a), ((1, at + self.chunks), (1, at))))
+            slots.append(((a, b), ((0, at), (0, at + size))))
+            slots.append(((b, a), ((1, at + size), (1, at))))
+        self.near_slots = slots
+        shifted = [(masks, tuple((i + 2, at) for i, at in places)) for masks, places in slots]
+        self.slots = sorted([((0, 0), ((0, 0), (1, 0)))] + shifted, key=self.head_masks)
 
     def head_masks(self, slot):
         return tuple(mask // self.per_head for mask in slot[0])
@@ -80,11 +75,12 @@
     return masks[0] if masks[0] == masks[1] else jnp.where(here % 2 == 0, masks[0], masks[1])
 
 
-def sources_of(slots, skip):
+def sources_of(plan, slots):
     return [
-        (array, tile + skip, masks, side)
+        (array, tile + plan.heads + hop * plan.chunks, tuple(m ^ hop * plan.partner for m in masks), side)
         for masks, places in slots
         for side, (array, tile) in enumerate(places)
+        for hop in range(2)
     ]
 
 
@@ -113,9 +109,9 @@
 
 def early_kernel(plan, *refs):
     (index_ref, *arrays, down_ref, out_ref, held_ref, buffer, sems, late_sems) = refs
-    sources = sources_of(plan.slots, plan.heads)
+    sources = sources_of(plan, [((0, 0), ((0, 0), (1, 0)))])
     copies = streams(sources, index_ref, down_ref, buffer, sems)
-    late = streams(sources_of(plan.far_slots, 0), index_ref, down_ref, held_ref, late_sems)
+    late = streams(sources_of(plan, plan.near_slots), index_ref, down_ref, held_ref, late_sems)
     for copy in copies + late:
         copy.start()
     out_ref[...] = lower(sources, arrays, buffer, copies)
@@ -145,7 +141,7 @@
 
 
 def pack_kernel(sizes, index_ref, query_ref, hidden_ref, key_ref, value_ref, *refs):
-    own_ref, cache_ref, query_buf, hidden_buf, sems = refs
+    own_query_ref, own_hidden_ref, cache_ref, query_buf, hidden_buf, sems = refs
     requests, tokens, devices = sizes
     _, _, _, parity = lane_of(index_ref, devices)
     loads = [
@@ -155,14 +151,12 @@
     caches = cache_copies(key_ref, value_ref, cache_ref, 1 - parity, sems)
     for load in loads + caches:
         load.start()
-    at = 0
-    for load, ref in zip(loads, (query_buf, hidden_buf)):
+    for load, ref, out_ref in zip(loads, (query_buf, hidden_buf), (own_query_ref, own_hidden_ref)):
         load.wait()
         rows = jnp.concatenate([ref[b].astype(jnp.float32) for b in range(requests)], axis=0)
         for c in range(rows.shape[1] // HEAD_WIDTH):
             tile = rows[:, c * HEAD_WIDTH : (c + 1) * HEAD_WIDTH]
-            own_ref[at] = tile.astype(jnp.bfloat16)
-            at += 1
+            out_ref[c] = tile.astype(jnp.bfloat16)
     for load in caches:
         load.wait()
 
@@ -183,10 +177,9 @@
     for load in loads + others:
         load.start()
     tiles = depth // HEAD_WIDTH
-    first = QUERY_HEADS // devices
     total = jnp.zeros(base_ref.shape, jnp.float32)
     for p in range(parts):
-        hidden = jnp.concatenate([own_ref[first + p * tiles + c] for c in range(tiles)], axis=1)
+        hidden = jnp.concatenate([own_ref[p * tiles + c] for c in range(tiles)], axis=1)
         loads[p].wait()
         total += dot(hidden, buffer[p], ((1,), (0,)))
     base_ref[...] = total
@@ -196,13 +189,13 @@
 
 def project_kernel(sizes, plan, *refs):
     (index_ref, adapter_ref, rank_ref, pool_ref) = refs[:4]
-    (far_ref, other_far_ref, early_ref, base_ref, down_ref, up_ref) = refs[4:10]
+    (near_ref, other_near_ref, early_ref, base_ref, down_ref, up_ref) = refs[4:10]
     (own_ref, own_parts_ref, parts_ref, all_ref) = refs[10:]
     requests, tokens, devices = sizes
     rows = requests * tokens
     here, _, _, parity = lane_of(index_ref, devices)
-    sources = sources_of(plan.far_slots, 0)
-    lowered = early_ref[...] + lower(sources, (far_ref, other_far_ref), down_ref, [])
+    sources = sources_of(plan, plan.near_slots)
+    lowered = early_ref[...] + lower(sources, (near_ref, other_near_ref), down_ref, [])
     row_request = lax.broadcasted_iota(jnp.int32, (rows, 1), 0) // tokens
     ranks = jnp.zeros((rows, 1), jnp.int32)
     owners = jnp.zeros((rows, 1), jnp.int32)
@@ -499,18 +492,22 @@
             out_specs=(vmem(),) * len(out_shape),
             scratch_shapes=scratch,
             compiler_params=pltpu.CompilerParams(vmem_limit_bytes=12 * MIB),
-            cost_estimate=cost(10**9 if name == "base" else 10**6, 0),
+            cost_estimate=cost(10**6, 0),
             name=name,
         )(*operands)
 
     def core_swap(x):
         return trade(x, devices, 0, 0, core=1)
 
-    own, far_send = call(
+    own_queries, own_hidden, far_send = call(
         functools.partial(pack_kernel, sizes),
         (index, pinned(queries), pinned(hidden), cached_keys, cached_values),
         [smem()] + [hbm()] * 4,
-        [pltpu.VMEM((heads + chunks, rows, HEAD_WIDTH), jnp.bfloat16), cache],
+        [
+            pltpu.VMEM((heads, rows, HEAD_WIDTH), jnp.bfloat16),
+            pltpu.VMEM((chunks, rows, HEAD_WIDTH), jnp.bfloat16),
+            cache,
+        ],
         [
             pltpu.VMEM(queries.shape, jnp.bfloat16),
             pltpu.VMEM(hidden.shape, jnp.bfloat16),
@@ -518,20 +515,14 @@
         ],
         "pack",
     )
+    far_hidden = trade(own_hidden, devices, partner, partner)
     far_cache = trade(far_send, devices, partner, partner)
-    own, other = lax.optimization_barrier((own, core_swap(own)))
-    near = [trade(own, devices, plan.single, plan.single)]
-    both = jnp.concatenate([own, other], axis=0)
-    both_hidden = jnp.concatenate([own[heads:], other[heads:]], axis=0)
-    near += [trade(both, devices, a, b) for a, b in plan.near_pairs]
-    far = [trade(both_hidden, devices, a, b) for a, b in plan.far_pairs]
-
     out_width = key_value_weight.shape[1]
     parts = 4 if width % (4 * HEAD_WIDTH) == 0 else 1
     up = adapter_up_weight[0]
     base, own_cache, up = call(
         functools.partial(base_kernel, sizes),
-        (index, own, pinned(key_value_weight), cached_keys, cached_values, pinned(up)),
+        (index, own_hidden, pinned(key_value_weight), cached_keys, cached_values, pinned(up)),
         [smem(), vmem()] + [hbm()] * 4,
         [
             pltpu.VMEM((rows, out_width), jnp.float32),
@@ -544,25 +535,34 @@
         ],
         "base",
     )
+    far_hidden, base = lax.optimization_barrier((far_hidden, base))
+    own = jnp.concatenate([own_queries, own_hidden, far_hidden], axis=0)
+    other = core_swap(own)
+    both = jnp.concatenate([own, other], axis=0)
+    near = [trade(own, devices, plan.single, plan.single)]
+    near += [trade(both, devices, a, b) for a, b in plan.near_pairs]
     near = jnp.concatenate(near, axis=0)
-    other_near = core_swap(near)
-    far = jnp.concatenate(far, axis=0)
-    far, base = lax.optimization_barrier((far, base))
-    other_far, far_cache = lax.optimization_barrier((core_swap(far), far_cache))
 
     down = pinned(adapter_down_weight[0])
     rank = down.shape[1]
-    half = pltpu.VMEM((devices // 2, width, rank), jnp.bfloat16)
-    half_sems = pltpu.SemaphoreType.DMA((devices // 2,))
+    (early, near_down) = call(
+        functools.partial(early_kernel, plan),
+        (index, own, other, down),
+        [smem()] + [vmem()] * 2 + [hbm()],
+        [
+            pltpu.VMEM((rows, rank), jnp.float32),
+            pltpu.VMEM((devices - 4, width, rank), jnp.bfloat16),
+        ],
+        [
+            pltpu.VMEM((4, width, rank), jnp.bfloat16),
+            pltpu.SemaphoreType.DMA((4,)),
+            pltpu.SemaphoreType.DMA((devices - 4,)),
+        ],
+        "lora_own",
+    )
+    near, early, far_cache = lax.optimization_barrier((near, early, far_cache))
+    other_near = core_swap(near)
     arrays = (own, other, near, other_near)
-    (early, far_down) = call(
-        functools.partial(early_kernel, plan),
-        (index,) + arrays + (down,),
-        [smem()] + [vmem()] * 4 + [hbm()],
-        [pltpu.VMEM((rows, rank), jnp.float32), half],
-        [half, half_sems, half_sems],
-        "lora_near",
-    )
     step = GROUPED * rows
     proj, own_parts, parts = call(
         functools.partial(project_kernel, sizes, plan),
@@ -571,11 +571,11 @@
             request_adapter,
             adapter_rank_list,
             adapter_pool_row,
-            far,
-            other_far,
+            near,
+            other_near,
             early,
             base,
-            far_down,
+            near_down,
             up,
         ),
         [smem()] * 4 + [vmem()] * 6,
@@ -630,7 +630,7 @@
         out_specs=vmem(),
         compiler_params=pltpu.CompilerParams(vmem_limit_bytes=8 * MIB),
         name="merge_states",
-    )(own, cosine, sine, *packets)
+    )(own_queries, cosine, sine, *packets)
 
 
 def solution(mesh):

time: 40.6 us -> 37.3 us (0.919)
  starting transfers between devices: 16 us -> 13.1 us
  waiting for transfers between devices: 12.2 us -> 11.7 us
    ppermute x14 -> x12, starting transfers between devices: 16 us -> 13.1 us  [trade(): return lax.ppermute(x, 'tensor', pairs)]
    ppermute x14 -> x12, waiting for transfers between devices: 12.2 us -> 11.7 us  [trade(): return lax.ppermute(x, 'tensor', pairs)]
  transfers between devices with their start and end apart: 14 -> 12, of which waited for: 5 -> 7; matrix products, arithmetic and copies ran while one was open for 1% -> 1% of each run, Pallas kernels for 20% -> 22%
where the time goes in v9:
time: 37.3 us; the launch traced here: 37 us
  starting transfers between devices  13.1 us (35%)
  Pallas kernels  11.8 us (32%)
  waiting for transfers between devices  11.7 us (31%)
    ppermute x12, starting transfers between devices, trade(): return lax.ppermute(x, 'tensor', pairs)  13.1 us
    ppermute x12, waiting for transfers between devices, trade(): return lax.ppermute(x, 'tensor', pairs)  11.7 us
    pallas_call x7, Pallas kernels, call(): pl.pallas_call(kernel, out_shape=tuple(out_shape), in_specs=in_specs, out...  10.7 us
    pallas_call x1, Pallas kernels, per_device(): pl.pallas_call(functools.partial(merge_kernel, devices, requests, tokens)...  1.05 us
  transfers between devices with their start and end apart: 12, of which 7 were waited for; matrix products, arithmetic and copies ran while one was open for 1% of the time, Pallas kernels for 22%

profile of v9, /device:TPU:0, one launch (start us, length us, event | category | flops | bytes accessed | tf_op | source)
XLA Modules:
  0.0 37.0 jit_solution(5124312849022128001)
XLA Ops:
  0.0 1.2 %pack.1 = (bf16[8,8,128]{2,1,0:T(8,128)(2,1)S(1)}, bf16[8,8,128]{2,1,0:T(8,128)(2,1)S(1)}, bf16[2,256,512]{2,1,0:T(8,128)(2,1)S(1)}) custom-call(s32[1]{0:T(128)} %bitcast.index_ref.refs_0_, bf16[2,4,1024]{2,1,0:T(4,128)(2,1)} %query_ref.1, bf16[2,4,1024]{2,1,0:T(4,128)(2,1)} %hidden_ref.1, bf16[256,1024]{1,0:T(8,128)(2,1)} %bitcast.6, bf16[256,1024]{1,0:T(8,128)(2,1)} %bitcast.8), custom_call_target="tpu_custom_call" | custom-call | flops 1000000 | tf_op jit(solution)/shard_map/pack/pallas_call | solution.py:488
  1.2 3.0 %collective-permute-start = (bf16[8,8,128]{2,1,0:T(8,128)(2,1)S(1)}, bf16[8,8,128]{2,1,0:T(8,128)(2,1)S(1)}, u32[]{:S(2)}, u32[]{:S(2)}) collective-permute-start(bf16[8,8,128]{2,1,0:T(8,128)(2,1)S(1)} %get-tuple-element.28.own_ref), channel_id=1, source_target_pairs={{0,2},{1,3},{2,0},{3,1},{4,6},{5,7},{6,4},{7,5},{8,10},{9,11},{10,... | collective-permute-start | bytes 49160 | tf_op jit(solution)/shard_map/ppermute | solution.py:457
  4.2 0.1 collective-permute-start.4
  4.3 0.0 copy-start.1
  4.3 0.0 copy-start.2
  4.3 0.0 copy-start.3
  4.4 2.6 %base.1 = (f32[8,2048]{1,0:T(8,128)S(1)}, bf16[2,256,512]{2,1,0:T(8,128)(2,1)S(1)}, bf16[128,2048]{1,0:T(8,128)(2,1)S(1)}) custom-call(s32[1]{0:T(128)} %bitcast.index_ref.refs_0_, bf16[8,8,128]{2,1,0:T(8,128)(2,1)S(1)} %get-tuple-element.28.own_ref, bf16[1024,2048]{1,0:T(8,128)(2,1)} %weight_ref.1, bf16[256,1024]{1,0:T(8,128)(2,1)} %bitcast.7, ...), custom_call_target="tpu_custom_call" | custom-call | flops 1000000 | tf_op jit(solution)/shard_map/base/pallas_call | solution.py:488
  7.0 0.1 collective-permute-start.1
  7.1 1.2 %collective-permute-done.1.refs_2_.refs_3_ = bf16[24,8,128]{2,1,0:T(8,128)(2,1)S(1)} collective-permute-done((bf16[24,8,128]{2,1,0:T(8,128)(2,1)S(1)}, bf16[24,8,128]{2,1,0:T(8,128)(2,1)S(1)}, u32[]{:S(2)}, u32[]{:S(2)}) %collective-permute-start.1) | collective-permute-done | bytes 49184 | tf_op jit(solution)/shard_map/ppermute | solution.py:457
  8.3 2.1 %collective-permute-start.3 = (bf16[48,8,128]{2,1,0:T(8,128)(2,1)S(1)}, bf16[48,8,128]{2,1,0:T(8,128)(2,1)S(1)}, u32[]{:S(2)}, u32[]{:S(2)}) collective-permute-start(bf16[48,8,128]{2,1,0:T(8,128)(2,1)S(1)} %pad_maximum_fusion.1), channel_id=1, source_target_pairs={{0,4},{1,9},{2,6},{3,11},{4,0},{5,13},{6,2},{7,15},{8,12},{9,1},{1... | collective-permute-start | bytes 294920 | tf_op jit(solution)/shard_map/ppermute | solution.py:457
  10.4 2.5 %collective-permute-start.2 = (bf16[24,8,128]{2,1,0:T(8,128)(2,1)S(1)}, bf16[24,8,128]{2,1,0:T(8,128)(2,1)S(1)}, u32[]{:S(2)}, u32[]{:S(2)}) collective-permute-start(bf16[24,8,128]{2,1,0:T(8,128)(2,1)S(1)} %constant_dynamic-update-slice_fusion.refs_1_.refs_2_), channel_id=1, source_target_pairs={{0,12},{1,13},{2,14},{3,15},{4,8},{5,9},{6,10},{7,11},{8,4},{9,5},... | collective-permute-start | bytes 147464 | tf_op jit(solution)/shard_map/ppermute | solution.py:457
  12.9 2.4 %lora_own.1 = (f32[8,128]{1,0:T(8,128)S(1)}, bf16[12,1024,128]{2,1,0:T(8,128)(2,1)S(1)}) custom-call(s32[1]{0:T(128)} %bitcast.index_ref.refs_0_, bf16[24,8,128]{2,1,0:T(8,128)(2,1)S(1)} %constant_dynamic-update-slice_fusion.refs_1_.refs_2_, bf16[24,8,128]{2,1,0:T(8,128)(2,1)S(1)} %collective-permute-done.1.refs_2_.refs_3_, bf16[16384,128]{1,0:T(8,128)(2,1)} %bitcast.5), custom_call_target="tpu_custom_call" | custom-call | flops 1000000 | tf_op jit(solution)/shard_map/lora_own/pallas_call | solution.py:488
  15.3 1.5 %collective-permute-done.2 = bf16[24,8,128]{2,1,0:T(8,128)(2,1)S(1)} collective-permute-done((bf16[24,8,128]{2,1,0:T(8,128)(2,1)S(1)}, bf16[24,8,128]{2,1,0:T(8,128)(2,1)S(1)}, u32[]{:S(2)}, u32[]{:S(2)}) %collective-permute-start.2) | collective-permute-done | bytes 49184 | tf_op jit(solution)/shard_map/ppermute | solution.py:457
  16.8 0.9 %collective-permute-done.4.refs_7_ = bf16[2,256,512]{2,1,0:T(8,128)(2,1)S(1)} collective-permute-done((bf16[2,256,512]{2,1,0:T(8,128)(2,1)S(1)}, bf16[2,256,512]{2,1,0:T(8,128)(2,1)S(1)}, u32[]{:S(2)}, u32[]{:S(2)}) %collective-permute-start.4) | collective-permute-done | bytes 524320 | tf_op jit(solution)/shard_map/ppermute | solution.py:457
  17.6 0.1 add_convert_fusion
  17.7 1.3 %collective-permute-done.5.refs_5_ = bf16[72,8,128]{2,1,0:T(8,128)(2,1)S(1)} collective-permute-done((bf16[72,8,128]{2,1,0:T(8,128)(2,1)S(1)}, bf16[72,8,128]{2,1,0:T(8,128)(2,1)S(1)}, u32[]{:S(2)}, u32[]{:S(2)}) %collective-permute-start.5) | collective-permute-done | bytes 147488 | tf_op jit(solution)/shard_map/ppermute | solution.py:457
  19.0 1.3 %project.1 = (f32[2,32,128]{2,1,0:T(8,128)S(1)}, bf16[96,128]{1,0:T(8,128)(2,1)S(1)}, bf16[96,128]{1,0:T(8,128)(2,1)S(1)}) custom-call(s32[1]{0:T(128)} %bitcast.index_ref.refs_0_, s32[2]{0:T(128)S(1)} %copy-done.1, s32[16]{0:T(128)S(1)} %copy-done.2, s32[16]{0:T(128)S(1)} %copy-done.3, bf16[72,8,128]{2,1,0:T(8,128)(2,1)S(1)} %pad_maximum_fusion.refs_4_, ...), custom_call_target="tpu_custom_call" | custom-call | flops 1000000 | tf_op jit(solution)/shard_map/project/pallas_call | solution.py:488
  20.3 0.8 %collective-permute-start.6 = (bf16[96,128]{1,0:T(8,128)(2,1)S(1)}, bf16[96,128]{1,0:T(8,128)(2,1)S(1)}, u32[]{:S(2)}, u32[]{:S(2)}) collective-permute-start(bf16[96,128]{1,0:T(8,128)(2,1)S(1)} %get-tuple-element.43), channel_id=1, source_target_pairs={{0,2},{1,3},{2,0},{3,1},{4,6},{5,7},{6,4},{7,5},{8,10},{9,11},{10,... | collective-permute-start | bytes 73736 | tf_op jit(solution)/shard_map/ppermute | solution.py:457
  21.1 0.1 convert_element_type.11
  21.2 1.5 %other_lane.1 = bf16[368,128]{1,0:T(8,128)(2,1)S(1)} custom-call(s32[1]{0:T(128)} %bitcast.index_ref.refs_0_, s32[2]{0:T(128)S(1)} %copy-done, bf16[24,8,128]{2,1,0:T(8,128)(2,1)S(1)} %constant_dynamic-update-slice_fusion.refs_1_.refs_2_, bf16[24,8,128]{2,1,0:T(8,128)(2,1)S(1)} %collective-permute-done.1.refs_2_.refs_3_, ...), custom_call_target="tpu_custom_call" | custom-call | flops 1000000 | tf_op jit(solution)/shard_map/other_lane/pallas_call | solution.py:488
  22.7 0.1 collective-permute-start.7
  22.7 1.4 %collective-permute-done.6.far_ref = bf16[96,128]{1,0:T(8,128)(2,1)S(1)} collective-permute-done((bf16[96,128]{1,0:T(8,128)(2,1)S(1)}, bf16[96,128]{1,0:T(8,128)(2,1)S(1)}, u32[]{:S(2)}, u32[]{:S(2)}) %collective-permute-start.6) | collective-permute-done | bytes 24608 | tf_op jit(solution)/shard_map/ppermute | solution.py:457
  24.2 0.1 fusion
  24.3 1.5 %own_lane.1 = (f32[256,128]{1,0:T(8,128)S(1)}, f32[8,128]{1,0:T(8,128)S(1)}) custom-call(s32[1]{0:T(128)} %bitcast.index_ref.refs_0_, s32[2]{0:T(128)S(1)} %copy-done, bf16[24,8,128]{2,1,0:T(8,128)(2,1)S(1)} %constant_dynamic-update-slice_fusion.refs_1_.refs_2_, bf16[24,8,128]{2,1,0:T(8,128)(2,1)S(1)} %collective-permute-done.1.refs_2_.refs_3_, ...), custom_call_target="tpu_custom_call" | custom-call | flops 1000000 | tf_op jit(solution)/shard_map/own_lane/pallas_call | solution.py:488
  25.8 0.3 join.1
  26.1 1.7 %collective-permute-start.9 = (bf16[96,128]{1,0:T(8,128)(2,1)S(1)}, bf16[96,128]{1,0:T(8,128)(2,1)S(1)}, u32[]{:S(2)}, u32[]{:S(2)}) collective-permute-start(bf16[96,128]{1,0:T(8,128)(2,1)S(1)} %get-tuple-element.46), channel_id=1, source_target_pairs={{0,4},{1,9},{2,6},{3,11},{4,0},{5,13},{6,2},{7,15},{8,12},{9,1},{1... | collective-permute-start | bytes 73736 | tf_op jit(solution)/shard_map/ppermute | solution.py:457
  27.8 2.6 %collective-permute-start.10 = (bf16[96,128]{1,0:T(8,128)(2,1)S(1)}, bf16[96,128]{1,0:T(8,128)(2,1)S(1)}, u32[]{:S(2)}, u32[]{:S(2)}) collective-permute-start(bf16[96,128]{1,0:T(8,128)(2,1)S(1)} %get-tuple-element.47), channel_id=1, source_target_pairs={{0,8},{1,5},{2,10},{3,7},{4,12},{5,1},{6,14},{7,3},{8,0},{9,13},{1... | collective-permute-start | bytes 73736 | tf_op jit(solution)/shard_map/ppermute | solution.py:457
  30.4 0.2 collective-permute-start.11
  30.5 0.1 pad_maximum_fusion.2
  30.6 2.0 %collective-permute-done.10.refs_2_ = bf16[96,128]{1,0:T(8,128)(2,1)S(1)} collective-permute-done((bf16[96,128]{1,0:T(8,128)(2,1)S(1)}, bf16[96,128]{1,0:T(8,128)(2,1)S(1)}, u32[]{:S(2)}, u32[]{:S(2)}) %collective-permute-start.10) | collective-permute-done | bytes 24608 | tf_op jit(solution)/shard_map/ppermute | solution.py:457
  32.6 3.4 %collective-permute-done.11.refs_3_ = bf16[96,128]{1,0:T(8,128)(2,1)S(1)} collective-permute-done((bf16[96,128]{1,0:T(8,128)(2,1)S(1)}, bf16[96,128]{1,0:T(8,128)(2,1)S(1)}, u32[]{:S(2)}, u32[]{:S(2)}) %collective-permute-start.11) | collective-permute-done | bytes 24608 | tf_op jit(solution)/shard_map/ppermute | solution.py:457
  36.0 1.0 %merge_states.1 = bf16[2,4,1024]{2,1,0:T(4,128)(2,1)} custom-call(bf16[8,8,128]{2,1,0:T(8,128)(2,1)S(1)} %get-tuple-element.27.own_ref, f32[8,128]{1,0:T(8,128)S(1)} %get-tuple-element.52.cos_ref, f32[8,128]{1,0:T(8,128)S(1)} %get-tuple-element.53.sin_ref, bf16[96,128]{1,0:T(8,128)(2,1)S(1)} %get-tuple-element.45.refs_0_, ...), custom_call_target="tpu_custom_call" | custom-call | tf_op jit(solution)/shard_map/merge_states/pallas_call | solution.py:626
  (18 shorter events, 0.1 us)
Async XLA Ops:
  1.2 5.8 %collective-permute-start = (bf16[8,8,128]{2,1,0:T(8,128)(2,1)S(1)}, bf16[8,8,128]{2,1,0:T(8,128)(2,1)S(1)}, u32[]{:S(2)}, u32[]{:S(2)}) collective-permute-start(bf16[8,8,128]{2,1,0:T(8,128)(2,1)S(1)} %get-tuple-element.28.own_ref), channel_id=1, source_target_pairs={{0,2},{1,3},{2,0},{3,1},{4,6},{5,7},{6,4},{7,5},{8,10},{9,11},{10,... | collective-permute-start | bytes 49160 | tf_op jit(solution)/shard_map/ppermute | solution.py:457
  4.2 13.4 %collective-permute-start.4 = (bf16[2,256,512]{2,1,0:T(8,128)(2,1)S(1)}, bf16[2,256,512]{2,1,0:T(8,128)(2,1)S(1)}, u32[]{:S(2)}, u32[]{:S(2)}) collective-permute-start(bf16[2,256,512]{2,1,0:T(8,128)(2,1)S(1)} %get-tuple-element.32), channel_id=1, source_target_pairs={{0,2},{1,3},{2,0},{3,1},{4,6},{5,7},{6,4},{7,5},{8,10},{9,11},{10,... | collective-permute-start | bytes 1572872 | tf_op jit(solution)/shard_map/ppermute | solution.py:457
  4.3 13.3 %copy-start = (s32[2]{0:T(128)S(1)}, s32[2]{0:T(128)}, u32[]{:S(2)}) copy-start(s32[2]{0:T(128)} %refs_1_.5) | copy-start | bytes 28
  4.3 14.7 %copy-start.1 = (s32[2]{0:T(128)S(1)}, s32[2]{0:T(128)}, u32[]{:S(2)}) copy-start(s32[2]{0:T(128)} %refs_1_.4) | copy-start | bytes 28
  4.3 14.7 %copy-start.2 = (s32[16]{0:T(128)S(1)}, s32[16]{0:T(128)}, u32[]{:S(2)}) copy-start(s32[16]{0:T(128)} %refs_2_.1) | copy-start | bytes 196
  4.3 14.6 %copy-start.3 = (s32[16]{0:T(128)S(1)}, s32[16]{0:T(128)}, u32[]{:S(2)}) copy-start(s32[16]{0:T(128)} %refs_3_.1) | copy-start | bytes 196
  7.0 1.3 %collective-permute-start.1 = (bf16[24,8,128]{2,1,0:T(8,128)(2,1)S(1)}, bf16[24,8,128]{2,1,0:T(8,128)(2,1)S(1)}, u32[]{:S(2)}, u32[]{:S(2)}) collective-permute-start(bf16[24,8,128]{2,1,0:T(8,128)(2,1)S(1)} %constant_dynamic-update-slice_fusion.refs_1_.refs_2_), channel_id=1, source_target_pairs={{0,1},{1,0},{2,3},{3,2},{4,5},{5,4},{6,7},{7,6},{8,9},{9,8},{10,11... | collective-permute-start | bytes 147464 | tf_op jit(solution)/shard_map/ppermute | solution.py:457
  8.3 8.4 %collective-permute-start.3 = (bf16[48,8,128]{2,1,0:T(8,128)(2,1)S(1)}, bf16[48,8,128]{2,1,0:T(8,128)(2,1)S(1)}, u32[]{:S(2)}, u32[]{:S(2)}) collective-permute-start(bf16[48,8,128]{2,1,0:T(8,128)(2,1)S(1)} %pad_maximum_fusion.1), channel_id=1, source_target_pairs={{0,4},{1,9},{2,6},{3,11},{4,0},{5,13},{6,2},{7,15},{8,12},{9,1},{1... | collective-permute-start | bytes 294920 | tf_op jit(solution)/shard_map/ppermute | solution.py:457
  10.4 6.3 %collective-permute-start.2 = (bf16[24,8,128]{2,1,0:T(8,128)(2,1)S(1)}, bf16[24,8,128]{2,1,0:T(8,128)(2,1)S(1)}, u32[]{:S(2)}, u32[]{:S(2)}) collective-permute-start(bf16[24,8,128]{2,1,0:T(8,128)(2,1)S(1)} %constant_dynamic-update-slice_fusion.refs_1_.refs_2_), channel_id=1, source_target_pairs={{0,12},{1,13},{2,14},{3,15},{4,8},{5,9},{6,10},{7,11},{8,4},{9,5},... | collective-permute-start | bytes 147464 | tf_op jit(solution)/shard_map/ppermute | solution.py:457
  17.6 1.4 %collective-permute-start.5 = (bf16[72,8,128]{2,1,0:T(8,128)(2,1)S(1)}, bf16[72,8,128]{2,1,0:T(8,128)(2,1)S(1)}, u32[]{:S(2)}, u32[]{:S(2)}) collective-permute-start(bf16[72,8,128]{2,1,0:T(8,128)(2,1)S(1)} %pad_maximum_fusion.refs_4_), channel_id=1, source_target_pairs={{0,1},{1,0},{2,3},{3,2},{4,5},{5,4},{6,7},{7,6},{8,9},{9,8},{10,11... | collective-permute-start | bytes 442376 | tf_op jit(solution)/shard_map/ppermute | solution.py:457
  20.3 3.9 %collective-permute-start.6 = (bf16[96,128]{1,0:T(8,128)(2,1)S(1)}, bf16[96,128]{1,0:T(8,128)(2,1)S(1)}, u32[]{:S(2)}, u32[]{:S(2)}) collective-permute-start(bf16[96,128]{1,0:T(8,128)(2,1)S(1)} %get-tuple-element.43), channel_id=1, source_target_pairs={{0,2},{1,3},{2,0},{3,1},{4,6},{5,7},{6,4},{7,5},{8,10},{9,11},{10,... | collective-permute-start | bytes 73736 | tf_op jit(solution)/shard_map/ppermute | solution.py:457
  22.7 3.1 %collective-permute-start.7 = (bf16[368,128]{1,0:T(8,128)(2,1)S(1)}, bf16[368,128]{1,0:T(8,128)(2,1)S(1)}, u32[]{:S(2)}, u32[]{:S(2)}) collective-permute-start(bf16[368,128]{1,0:T(8,128)(2,1)S(1)} %other_lane.1), channel_id=1, source_target_pairs={{0,1},{1,0},{2,3},{3,2},{4,5},{5,4},{6,7},{7,6},{8,9},{9,8},{10,11... | collective-permute-start | bytes 282632 | tf_op jit(solution)/shard_map/ppermute | solution.py:457
  24.2 1.6 %collective-permute-start.8 = (bf16[96,128]{1,0:T(8,128)(2,1)S(1)}, bf16[96,128]{1,0:T(8,128)(2,1)S(1)}, u32[]{:S(2)}, u32[]{:S(2)}) collective-permute-start(bf16[96,128]{1,0:T(8,128)(2,1)S(1)} %collective-permute-done.6.far_ref), channel_id=1, source_target_pairs={{0,1},{1,0},{2,3},{3,2},{4,5},{5,4},{6,7},{7,6},{8,9},{9,8},{10,11... | collective-permute-start | bytes 73736 | tf_op jit(solution)/shard_map/ppermute | solution.py:457
  26.1 4.5 %collective-permute-start.9 = (bf16[96,128]{1,0:T(8,128)(2,1)S(1)}, bf16[96,128]{1,0:T(8,128)(2,1)S(1)}, u32[]{:S(2)}, u32[]{:S(2)}) collective-permute-start(bf16[96,128]{1,0:T(8,128)(2,1)S(1)} %get-tuple-element.46), channel_id=1, source_target_pairs={{0,4},{1,9},{2,6},{3,11},{4,0},{5,13},{6,2},{7,15},{8,12},{9,1},{1... | collective-permute-start | bytes 73736 | tf_op jit(solution)/shard_map/ppermute | solution.py:457
  27.8 4.8 %collective-permute-start.10 = (bf16[96,128]{1,0:T(8,128)(2,1)S(1)}, bf16[96,128]{1,0:T(8,128)(2,1)S(1)}, u32[]{:S(2)}, u32[]{:S(2)}) collective-permute-start(bf16[96,128]{1,0:T(8,128)(2,1)S(1)} %get-tuple-element.47), channel_id=1, source_target_pairs={{0,8},{1,5},{2,10},{3,7},{4,12},{5,1},{6,14},{7,3},{8,0},{9,13},{1... | collective-permute-start | bytes 73736 | tf_op jit(solution)/shard_map/ppermute | solution.py:457
  30.4 5.6 %collective-permute-start.11 = (bf16[96,128]{1,0:T(8,128)(2,1)S(1)}, bf16[96,128]{1,0:T(8,128)(2,1)S(1)}, u32[]{:S(2)}, u32[]{:S(2)}) collective-permute-start(bf16[96,128]{1,0:T(8,128)(2,1)S(1)} %get-tuple-element.48), channel_id=1, source_target_pairs={{0,12},{1,13},{2,14},{3,15},{4,8},{5,9},{6,10},{7,11},{8,4},{9,5},... | collective-permute-start | bytes 73736 | tf_op jit(solution)/shard_map/ppermute | solution.py:457

commit v10 on v8

v10 whole, which is shorter than its diff:
```python
import functools
import math

import jax
import jax.numpy as jnp
from jax import lax
from jax.experimental import pallas as pl
from jax.experimental.pallas import tpu as pltpu
from jax.sharding import PartitionSpec as P

QUERY_HEADS = 128
KEY_HEADS = 8
HEAD_WIDTH = 128
ROPE_BASE = 500000.0
NEG_FILL = -1e30
SCALE = 1.0 / math.sqrt(HEAD_WIDTH)
CHUNKS = KEY_HEADS // 2
MIX_ROWS = CHUNKS * 128
STAT_ROWS = 16
MIB = 2**20


def dot(a, b, dims):
    return lax.dot_general(a, b, (dims, ((), ())), preferred_element_type=jnp.float32)


def round_bf16(x):
    return x.astype(jnp.bfloat16).astype(jnp.float32)


class Plan:
    def __init__(self, devices, width):
        lanes = devices // 2
        self.per_head = per_head = lanes // KEY_HEADS
        self.heads, self.chunks = QUERY_HEADS // devices, width // HEAD_WIDTH
        if per_head > 1:
            self.single = 1
            self.pairs = [(m, m ^ 1) for m in range(lanes - 2, 0, -2)]
        else:
            self.single = lanes - 1
            self.pairs = [(m, m + 1) for m in range(lanes - 3, 0, -2)]
        size = self.heads + self.chunks
        self.own = ((0, 0), ((0, 0), (1, 0)))
        self.one = ((self.single,) * 2, ((2, 0), (3, 0)))
        self.mine, self.theirs = [], []
        for k, (a, b) in enumerate(self.pairs):
            self.mine.append(((a, b), ((4 + 2 * k, 0), (4 + 2 * k, size))))
            self.theirs.append(((b, a), ((5 + 2 * k, size), (5 + 2 * k, 0))))

    def head_masks(self, unit):
        return tuple(mask // self.per_head for mask in unit[0][0])

    def units(self, keep):
        if keep:
            units = [(self.own, 0), (self.one, 0)]
            units += [(slot, side) for slot in self.mine for side in (0, 1)]
        else:
            units = [(self.own, 1), (self.one, 1)]
            units += [(slot, side) for slot in self.theirs for side in (1, 0)]
        if self.per_head > 1:
            units.sort(key=self.head_masks)
        return units

    def attention_chunks(self, slot_rows, keep):
        units = self.units(keep)
        count = HEAD_WIDTH // slot_rows
        chunks = []
        for at in range(0, len(units), count):
            runs = []
            for unit in units[at : at + count]:
                if runs and self.head_masks(runs[-1][0]) == self.head_masks(unit):
                    runs[-1].append(unit)
                else:
                    runs.append([unit])
            chunks.append(runs)
        return chunks

    def slots(self):
        return [self.own, self.one] + self.mine + self.theirs


def here_mask(masks, here):
    return masks[0] if masks[0] == masks[1] else jnp.where(here % 2 == 0, masks[0], masks[1])


def head_columns(head):
    return pl.ds(pl.multiple_of(head * HEAD_WIDTH, HEAD_WIDTH), HEAD_WIDTH)


def sources_of(plan):
    return [
        (array, tile + plan.heads, masks, side)
        for masks, places in plan.slots()
        for side, (array, tile) in enumerate(places)
    ]


def streams(sources, index_ref, down_ref, halves, sems):
    count, depth = halves[0].shape[:2]
    here = index_ref[0]
    copies = []
    for at, (_, _, masks, side) in enumerate(sources):
        source = here ^ (2 * here_mask(masks, here) + side)
        rows = pl.ds(pl.multiple_of(source * depth, depth), depth)
        place = halves[at // count].at[at % count]
        copies.append(pltpu.make_async_copy(down_ref.at[rows], place, sems.at[at]))
    return copies


def lower(sources, arrays, halves):
    total = None
    count, depth = halves[0].shape[:2]
    for at, (array, first, _, _) in enumerate(sources):
        tiles = range(first, first + depth // HEAD_WIDTH)
        hidden = jnp.concatenate([arrays[array][c] for c in tiles], axis=1)
        term = dot(hidden, halves[at // count][at % count], ((1,), (0,)))
        total = term if total is None else total + term
    return total


def pack_kernel(requests, query_ref, hidden_ref, own_ref, query_buf, hidden_buf, sems):
    loads = [
        pltpu.make_async_copy(query_ref, query_buf, sems.at[0]),
        pltpu.make_async_copy(hidden_ref, hidden_buf, sems.at[1]),
    ]
    for load in loads:
        load.start()
    at = 0
    for load, ref in zip(loads, (query_buf, hidden_buf)):
        load.wait()
        rows = jnp.concatenate([ref[b].astype(jnp.float32) for b in range(requests)], axis=0)
        for c in range(rows.shape[1] // HEAD_WIDTH):
            tile = rows[:, c * HEAD_WIDTH : (c + 1) * HEAD_WIDTH]
            own_ref[at] = tile.astype(jnp.bfloat16)
            at += 1


def base_kernel(plan, index_ref, own_ref, weight_ref, *refs):
    down_ref, *sources = refs[:4]
    base_ref, *held = refs[4:8]
    halves, (buffer, sems, down_sems) = refs[8:10], refs[10:]
    parts, depth = buffer.shape[:2]
    loads = [
        pltpu.make_async_copy(weight_ref.at[pl.ds(p * depth, depth)], buffer.at[p], sems.at[p])
        for p in range(parts)
    ]
    others = [
        pltpu.make_async_copy(source, place, sems.at[parts + i])
        for i, (source, place) in enumerate(zip(sources, held))
    ]
    others += streams(sources_of(plan), index_ref, down_ref, halves, down_sems)
    for load in loads + others:
        load.start()
    tiles = depth // HEAD_WIDTH
    total = jnp.zeros(base_ref.shape, jnp.float32)
    for p in range(parts):
        first = plan.heads + p * tiles
        hidden = jnp.concatenate([own_ref[first + c] for c in range(tiles)], axis=1)
        loads[p].wait()
        total += dot(hidden, buffer[p], ((1,), (0,)))
    base_ref[...] = total
    for load in others:
        load.wait()


def project_kernel(sizes, plan, *refs):
    (index_ref, adapter_ref, rank_ref, pool_ref, *arrays) = refs[:-6]
    (base_ref, up_ref, *halves, own_ref, parts_ref) = refs[-6:]
    requests, tokens, devices = sizes
    rows = requests * tokens
    lowered = lower(sources_of(plan), arrays, halves)
    row_request = lax.broadcasted_iota(jnp.int32, (rows, 1), 0) // tokens
    ranks = jnp.zeros((rows, 1), jnp.int32)
    owners = jnp.zeros((rows, 1), jnp.int32)
    for b in range(requests):
        adapter = adapter_ref[b]
        ranks = jnp.where(row_request == b, rank_ref[adapter], ranks)
        owners = jnp.where(row_request == b, pool_ref[adapter], owners)
    column = lax.broadcasted_iota(jnp.int32, lowered.shape, 1)
    lowered = jnp.where(column < ranks, lowered, 0.0).astype(jnp.bfloat16)
    lifted = dot(lowered, up_ref[...], ((1,), (0,)))
    projected = base_ref[...] + jnp.where(owners == index_ref[0], lifted, 0.0)
    split = KEY_HEADS * HEAD_WIDTH
    step = KEY_HEADS * rows
    keys, values = [
        jnp.concatenate(
            [projected[:, at + j * HEAD_WIDTH : at + (j + 1) * HEAD_WIDTH] for j in range(KEY_HEADS)],
            axis=0,
        )
        for at in (0, split)
    ]
    own_ref[0] = keys
    own_ref[1] = values
    high = keys.astype(jnp.bfloat16)
    parts_ref[:step] = high
    parts_ref[step : 2 * step] = (keys - high.astype(jnp.float32)).astype(jnp.bfloat16)
    parts_ref[2 * step :] = values.astype(jnp.bfloat16)


def attend(sizes, plan, keep, index_ref, length_ref, arrays, key_ref, value_ref, put):
    requests, tokens, devices = sizes
    here = index_ref[0]
    chip = here // 2
    per_head = plan.per_head
    slot_rows = plan.heads * requests * tokens
    positions = key_ref.shape[0] // requests
    place = lax.broadcasted_iota(jnp.int32, (requests * positions, HEAD_WIDTH), 0)
    column = lax.broadcasted_iota(jnp.int32, (requests * positions, HEAD_WIDTH), 1)
    place_request = place // positions
    limit = jnp.zeros_like(place)
    for b in range(requests):
        limit = jnp.where(place_request == b, length_ref[b], limit)
    allowed = (here * positions + place % positions < limit) & (
        place_request == (column // tokens) % requests
    )
    peaks, totals = [], []
    for number, runs in enumerate(plan.attention_chunks(slot_rows, keep)):
        places = [slot[1][side] for run in runs for slot, side in run]
        query = jnp.concatenate(
            [arrays[array][tile + h] for array, tile in places for h in range(plan.heads)], axis=0
        )
        spots = [
            head_columns((chip // per_head) ^ (here_mask(run[0][0][0], here) // per_head))
            for run in runs
        ]
        share = HEAD_WIDTH // len(runs)
        scores = None
        for i, spot in enumerate(spots):
            part = dot(key_ref[:, spot], query, ((1,), (1,)))
            scores = part if scores is None else jnp.where(column < i * share, scores, part)
        scores = scores * SCALE
        peak = jnp.max(jnp.where(allowed, scores, NEG_FILL), axis=0, keepdims=True)
        peak = round_bf16(peak)
        weights = jnp.where(allowed, jnp.exp(scores - peak), 0.0)
        peaks.append(peak)
        totals.append(jnp.sum(weights, axis=0, keepdims=True))
        weights = jnp.transpose(weights.astype(jnp.bfloat16))
        for i, spot in enumerate(spots):
            own = slice(i * share, (i + 1) * share)
            put(number, i * share, dot(weights[own], value_ref[:, spot], ((1,), (0,))))
    return peaks, totals


def rows_of(items, count):
    row = lax.broadcasted_iota(jnp.int32, (count, HEAD_WIDTH), 0)
    out = jnp.zeros((count, HEAD_WIDTH), jnp.float32)
    for i, item in enumerate(items):
        out = jnp.where(row == i, item, out)
    return out


def send_kernel(sizes, plan, *refs):
    (index_ref, length_ref, *arrays, key_ref, value_ref, send_ref) = refs

    def put(chunk, row, mix):
        at = chunk * 128 + row
        send_ref[at : at + mix.shape[0]] = mix.astype(jnp.bfloat16)

    peaks, totals = attend(
        sizes, plan, False, index_ref, length_ref, arrays, key_ref, value_ref, put
    )
    highs = [round_bf16(total) for total in totals]
    lows = [total - high for total, high in zip(totals, highs)]
    send_ref[MIX_ROWS:] = rows_of(peaks + highs + lows, STAT_ROWS).astype(jnp.bfloat16)


def keep_kernel(sizes, plan, *refs):
    (index_ref, length_ref, *arrays, key_ref, value_ref, mix_ref, stat_ref) = refs

    def put(chunk, row, mix):
        at = chunk * 128 + row
        mix_ref[at : at + mix.shape[0]] = mix

    peaks, totals = attend(
        sizes, plan, True, index_ref, length_ref, arrays, key_ref, value_ref, put
    )
    stat_ref[...] = rows_of(peaks + totals, 8)


def join_kernel(sizes, plan, index_ref, mix_ref, stat_ref, proj_ref, got_parts_ref, got_ref, *refs):
    packet_refs, tail_ref = refs[:-1], refs[-1]
    requests, tokens, devices = sizes
    here = index_ref[0]
    chip = here // 2
    per_head = plan.per_head
    rows = requests * tokens
    slot_rows = plan.heads * rows
    step = KEY_HEADS * rows
    got = got_ref[MIX_ROWS:].astype(jnp.float32)
    own = stat_ref[...]
    own_peak, got_peak = own[:CHUNKS], got[:CHUNKS]
    peak = jnp.maximum(own_peak, got_peak)
    own_factor = jnp.exp(own_peak - peak)
    got_factor = jnp.exp(got_peak - peak)
    total = own_factor * own[CHUNKS : 2 * CHUNKS] + got_factor * (
        got[CHUNKS : 2 * CHUNKS] + got[2 * CHUNKS : 3 * CHUNKS]
    )
    high = round_bf16(total)
    low = total - high
    filler = jnp.zeros((128 - 2 * CHUNKS, 128), jnp.float32)
    table = jnp.transpose(jnp.concatenate([own_factor, got_factor, filler], axis=0))
    keys = proj_ref[0] + got_parts_ref[:step].astype(jnp.float32)
    keys += got_parts_ref[step : 2 * step].astype(jnp.float32)
    values = proj_ref[1] + got_parts_ref[2 * step :].astype(jnp.float32)
    keys_high = round_bf16(keys)
    for j in range(KEY_HEADS):
        part = slice(j * rows, (j + 1) * rows)
        tail_ref[j, :rows] = keys_high[part]
        tail_ref[j, rows : 2 * rows] = (keys - keys_high)[part]
        tail_ref[j, 2 * rows :] = values[part]
    stat_row = lax.broadcasted_iota(jnp.int32, (rows, HEAD_WIDTH), 0)
    packet = {id(slot): ref for slot, ref in zip([plan.own, plan.one] + plan.mine, packet_refs)}
    for c, runs in enumerate(plan.attention_chunks(slot_rows, True)):
        span = slice(c * 128, c * 128 + 128)
        mix = mix_ref[span] * table[:, c : c + 1]
        mix += got_ref[span].astype(jnp.float32) * table[:, CHUNKS + c : CHUNKS + c + 1]
        stats = jnp.where(
            stat_row == 0,
            peak[c : c + 1],
            jnp.where(
                stat_row == 1, high[c : c + 1], jnp.where(stat_row == 2, low[c : c + 1], 0.0)
            ),
        )
        for t, (slot, side) in enumerate(unit for run in runs for unit in run):
            packet_ref = packet[id(slot)]
            at = side * slot_rows
            packet_ref[at : at + slot_rows] = mix[t * slot_rows : (t + 1) * slot_rows].astype(
                jnp.bfloat16
            )
            if side == 0:
                shifted = stats if t == 0 else pltpu.roll(stats, HEAD_WIDTH - t * slot_rows, 1)
                head = (chip // per_head) ^ (here_mask(slot[0], here) // per_head)
                tail = jnp.concatenate([tail_ref[head], shifted], axis=0)
                packet_ref[packet_ref.shape[0] - 4 * rows :] = tail.astype(jnp.bfloat16)


def merge_kernel(devices, requests, tokens, swapped, own_ref, cos_ref, sin_ref, *refs):
    got_refs, out_ref = refs[:-1], refs[-1]
    rows = requests * tokens
    heads = QUERY_HEADS // devices
    mix_rows = heads * rows
    sources = len(got_refs)
    tails = [ref[ref.shape[0] - 4 * rows :].astype(jnp.float32) for ref in got_refs]
    sums = functools.reduce(jnp.add, [tail[: 3 * rows] for tail in tails])
    keys = sums[:rows] + sums[rows : 2 * rows]
    values = sums[2 * rows :].astype(jnp.bfloat16)
    turned = pltpu.roll(keys, HEAD_WIDTH // 2, 1)
    keys = (keys * cos_ref[...] + turned * sin_ref[...]).astype(jnp.bfloat16)
    query = jnp.concatenate([own_ref[h] for h in range(heads)], axis=0)
    if mix_rows < 128:
        query = jnp.concatenate(
            [query, jnp.zeros((128 - mix_rows, HEAD_WIDTH), jnp.bfloat16)], axis=0
        )
    fresh = dot(keys, query, ((1,), (1,))) * SCALE
    source = lax.broadcasted_iota(jnp.int32, fresh.shape, 0)
    column = lax.broadcasted_iota(jnp.int32, fresh.shape, 1) % rows
    allowed = (source // tokens == column // tokens) & (source % tokens <= column % tokens)
    fresh_peak = jnp.max(jnp.where(allowed, fresh, NEG_FILL), axis=0, keepdims=True)
    stats = [tail[3 * rows :] for tail in tails]
    for s in range(swapped, sources):
        stats[s] = pltpu.roll(stats[s], HEAD_WIDTH - mix_rows, 1)
    peak = functools.reduce(jnp.maximum, [stat[0:1] for stat in stats], fresh_peak)
    weights = jnp.where(allowed, jnp.exp(fresh - peak), 0.0)
    factors = [jnp.exp(stat[0:1] - peak) for stat in stats]
    total = functools.reduce(
        jnp.add,
        [factor * (stat[1:2] + stat[2:3]) for factor, stat in zip(factors, stats)],
        jnp.sum(weights, axis=0, keepdims=True),
    )
    inverse = 1.0 / total
    filler = jnp.zeros((128 - sources - 1, 128), jnp.float32)
    table = jnp.concatenate([factor * inverse for factor in factors] + [inverse, filler], axis=0)
    table = jnp.transpose(table)[:mix_rows]
    weights = jnp.transpose(
        jnp.concatenate([weights, jnp.zeros((128 - rows, 128), jnp.float32)], axis=0)
    )[:mix_rows].astype(jnp.bfloat16)
    values = jnp.concatenate(
        [values, jnp.zeros((128 - rows, HEAD_WIDTH), jnp.bfloat16)], axis=0
    )
    mix = dot(weights, values, ((1,), (0,))) * table[:, sources : sources + 1]
    for s, ref in enumerate(got_refs):
        mix += ref[:mix_rows].astype(jnp.float32) * table[:, s : s + 1]
    for h in range(heads):
        tile = mix[h * rows : (h + 1) * rows]
        for b in range(requests):
            out_ref[b, :, h * HEAD_WIDTH : (h + 1) * HEAD_WIDTH] = tile[
                b * tokens : (b + 1) * tokens
            ].astype(jnp.bfloat16)


def rotation(lengths, tokens):
    half = HEAD_WIDTH // 2
    places = (lengths[:, None] + jnp.arange(tokens, dtype=jnp.int32)[None, :]).astype(jnp.float32)
    inverse_freq = jnp.exp(
        jnp.arange(half, dtype=jnp.float32) * (-2.0 * math.log(ROPE_BASE) / HEAD_WIDTH)
    )
    angles = places.reshape(-1, 1) * inverse_freq[None, :]
    cosine, sine = jnp.cos(angles), jnp.sin(angles)
    return jnp.concatenate([cosine, cosine], axis=1), jnp.concatenate([-sine, sine], axis=1)


def vmem():
    return pl.BlockSpec(memory_space=pltpu.VMEM)


def smem():
    return pl.BlockSpec(memory_space=pltpu.SMEM)


def hbm():
    return pl.BlockSpec(memory_space=pltpu.HBM)


def pinned(x):
    return pltpu.with_memory_space_constraint(x, pltpu.HBM)


def cost(flops, moved):
    return pl.CostEstimate(flops=int(flops), bytes_accessed=int(moved), transcendentals=0)


def trade(x, devices, even, odd, core=0):
    pairs = [(d, d ^ (2 * (odd if d % 2 else even) + core)) for d in range(devices)]
    return lax.ppermute(x, "tensor", pairs)


def per_device(
    hidden,
    queries,
    key_value_weight,
    adapter_down_weight,
    adapter_up_weight,
    cached_key_rows,
    cached_value_rows,
    request_adapter,
    adapter_rank_list,
    adapter_pool_row,
    lengths,
):
    requests, tokens, width = hidden.shape
    rows = requests * tokens
    devices = lax.axis_size("tensor")
    sizes = (requests, tokens, devices)
    plan = Plan(devices, width)
    heads, chunks = plan.heads, plan.chunks
    slot_rows = heads * rows
    index = lax.axis_index("tensor").reshape(1).astype(jnp.int32)

    def call(kernel, operands, in_specs, out_shape, scratch, name):
        return pl.pallas_call(
            kernel,
            out_shape=tuple(out_shape),
            in_specs=in_specs,
            out_specs=(vmem(),) * len(out_shape),
            scratch_shapes=scratch,
            compiler_params=pltpu.CompilerParams(vmem_limit_bytes=12 * MIB),
            cost_estimate=cost(10**6, 0),
            name=name,
        )(*operands)

    def core_swap(x):
        return trade(x, devices, 0, 0, core=1)

    (own,) = call(
        functools.partial(pack_kernel, requests),
        (pinned(queries), pinned(hidden)),
        [hbm()] * 2,
        [pltpu.VMEM((heads + chunks, rows, HEAD_WIDTH), jnp.bfloat16)],
        [
            pltpu.VMEM(queries.shape, jnp.bfloat16),
            pltpu.VMEM(hidden.shape, jnp.bfloat16),
            pltpu.SemaphoreType.DMA((2,)),
        ],
        "pack",
    )
    other = core_swap(own)
    one = trade(own, devices, plan.single, plan.single)
    both = jnp.concatenate([own, other], axis=0)
    mine = [trade(both, devices, a, b) for a, b in plan.pairs]

    flat = requests * cached_key_rows.shape[1]
    big = (
        cached_key_rows.reshape(flat, -1),
        cached_value_rows.reshape(flat, -1),
        adapter_up_weight[0],
    )
    out_width = key_value_weight.shape[1]
    parts = 4 if width % (4 * HEAD_WIDTH) == 0 else 1
    down = adapter_down_weight[0]
    half = pltpu.VMEM((devices // 2, width, down.shape[1]), jnp.bfloat16)
    base, keys, values, up, *halves = call(
        functools.partial(base_kernel, plan),
        (index, own, pinned(key_value_weight), pinned(down)) + tuple(pinned(x) for x in big),
        [smem(), vmem()] + [hbm()] * 5,
        [pltpu.VMEM((rows, out_width), jnp.float32)]
        + [pltpu.VMEM(x.shape, x.dtype) for x in big]
        + [half, half],
        [
            pltpu.VMEM((parts, width // parts, out_width), jnp.bfloat16),
            pltpu.SemaphoreType.DMA((parts + 3,)),
            pltpu.SemaphoreType.DMA((devices,)),
        ],
        "base",
    )
    one, mine[0], base = lax.optimization_barrier((one, mine[0], base))
    arrays = [own, other, one, core_swap(one)]
    for x in mine:
        arrays += [x, core_swap(x)]
    arrays = tuple(arrays)
    step = KEY_HEADS * rows
    proj, proj_parts = call(
        functools.partial(project_kernel, sizes, plan),
        (index, request_adapter, adapter_rank_list, adapter_pool_row)
        + arrays
        + (base, up, *halves),
        [smem()] * 4 + [vmem()] * (len(arrays) + 4),
        [
            pltpu.VMEM((2, step, HEAD_WIDTH), jnp.float32),
            pltpu.VMEM((3 * step, HEAD_WIDTH), jnp.bfloat16),
        ],
        [],
        "project",
    )
    got_parts = core_swap(proj_parts)
    (send,) = call(
        functools.partial(send_kernel, sizes, plan),
        (index, lengths) + arrays + (keys, values),
        [smem()] * 2 + [vmem()] * (len(arrays) + 2),
        [pltpu.VMEM((MIX_ROWS + STAT_ROWS, HEAD_WIDTH), jnp.bfloat16)],
        [],
        "send_states",
    )
    got = core_swap(send)
    mix, stats = call(
        functools.partial(keep_kernel, sizes, plan),
        (index, lengths) + arrays + (keys, values),
        [smem()] * 2 + [vmem()] * (len(arrays) + 2),
        [
            pltpu.VMEM((MIX_ROWS, HEAD_WIDTH), jnp.float32),
            pltpu.VMEM((8, HEAD_WIDTH), jnp.float32),
        ],
        [],
        "keep_states",
    )
    packets = call(
        functools.partial(join_kernel, sizes, plan),
        (index, mix, stats, proj, got_parts, got),
        [smem()] + [vmem()] * 5,
        [pltpu.VMEM((slot_rows + 4 * rows, HEAD_WIDTH), jnp.bfloat16)] * 2
        + [pltpu.VMEM((2 * slot_rows + 4 * rows, HEAD_WIDTH), jnp.bfloat16)] * len(plan.pairs),
        [pltpu.VMEM((KEY_HEADS, 3 * rows, HEAD_WIDTH), jnp.float32)],
        "join",
    )
    heard = [packets[0], trade(packets[1], devices, plan.single, plan.single)]
    heard += [trade(x, devices, a, b) for x, (a, b) in zip(packets[2:], plan.pairs)]
    heard[1], heard[2] = lax.optimization_barrier((heard[1], heard[2]))
    heard += [core_swap(x[slot_rows:]) for x in heard[2:]]
    cosine, sine = rotation(lengths, tokens)
    return pl.pallas_call(
        functools.partial(merge_kernel, devices, requests, tokens, 2 + len(plan.pairs)),
        out_shape=jax.ShapeDtypeStruct((requests, tokens, heads * HEAD_WIDTH), jnp.bfloat16),
        in_specs=[vmem()] * (3 + len(heard)),
        out_specs=vmem(),
        compiler_params=pltpu.CompilerParams(vmem_limit_bytes=8 * MIB),
        name="merge_states",
    )(own, cosine, sine, *heard)


def solution(mesh):
    in_specs = (
        P("groups", None, "tensor"),
        P("groups", None, "tensor"),
        P("tensor", None),
        P("tensor", None, None),
        P("tensor", None, None),
        P("groups", "tensor", None),
        P("groups", "tensor", None),
        P("groups"),
        P(),
        P(),
        P("groups"),
    )
    out_specs = P("groups", None, "tensor")
    return jax.shard_map(
        per_device, mesh=mesh, in_specs=in_specs, out_specs=out_specs, check_vma=False
    )
```

time: 40.6 us -> 36.3 us (0.89)
  waiting for transfers between devices: 12.2 us -> 7.23 us
  starting transfers between devices: 16 us -> 17.5 us
  Pallas kernels: 11.6 us -> 10.8 us
    ppermute x14 -> x18, waiting for transfers between devices: 12.2 us -> 7.23 us  [trade(): return lax.ppermute(x, 'tensor', pairs)]
    ppermute x14 -> x18, starting transfers between devices: 16 us -> 17.5 us  [trade(): return lax.ppermute(x, 'tensor', pairs)]
    pallas_call x7 -> x6, Pallas kernels: 10.6 us -> 9.69 us  [call(): pl.pallas_call(kernel, out_shape=tuple(out_shape), in_specs=in_specs, out...]
  transfers between devices with their start and end apart: 14 -> 18, of which waited for: 5 -> 8; matrix products, arithmetic and copies ran while one was open for 1% -> 1% of each run, Pallas kernels for 20% -> 20%
where the time goes in v10:
time: 36.3 us; the launch traced here: 36 us
  starting transfers between devices  17.5 us (48%)
  Pallas kernels  10.8 us (30%)
  waiting for transfers between devices  7.23 us (20%)
    ppermute x18, starting transfers between devices, trade(): return lax.ppermute(x, 'tensor', pairs)  17.5 us
    pallas_call x6, Pallas kernels, call(): pl.pallas_call(kernel, out_shape=tuple(out_shape), in_specs=in_specs, out...  9.69 us
    ppermute x18, waiting for transfers between devices, trade(): return lax.ppermute(x, 'tensor', pairs)  7.23 us
    pallas_call x1, Pallas kernels, per_device(): pl.pallas_call(functools.partial(merge_kernel, devices, requests, tokens,...  1.11 us
  transfers between devices with their start and end apart: 18, of which 8 were waited for; matrix products, arithmetic and copies ran while one was open for 1% of the time, Pallas kernels for 20%

profile of v10, /device:TPU:0, one launch (start us, length us, event | category | flops | bytes accessed | tf_op | source)
XLA Modules:
  0.0 36.0 jit_solution(12694713908923559669)
XLA Ops:
  0.0 0.8 %pack.1.own_ref.refs_2_.refs_4_ = bf16[16,8,128]{2,1,0:T(8,128)(2,1)S(1)} custom-call(bf16[2,4,1024]{2,1,0:T(4,128)(2,1)} %query_ref.1, bf16[2,4,1024]{2,1,0:T(4,128)(2,1)} %hidden_ref.1), custom_call_target="tpu_custom_call" | custom-call | flops 1000000 | tf_op jit(solution)/shard_map/pack/pallas_call | solution.py:450
  0.8 0.5 %collective-permute-start = (bf16[16,8,128]{2,1,0:T(8,128)(2,1)S(1)}, bf16[16,8,128]{2,1,0:T(8,128)(2,1)S(1)}, u32[]{:S(2)}, u32[]{:S(2)}) collective-permute-start(bf16[16,8,128]{2,1,0:T(8,128)(2,1)S(1)} %pack.1.own_ref.refs_2_.refs_4_), channel_id=1, source_target_pairs={{0,1},{1,0},{2,3},{3,2},{4,5},{5,4},{6,7},{7,6},{8,9},{9,8},{10,11... | collective-permute-start | bytes 98312 | tf_op jit(solution)/shard_map/ppermute | solution.py:424
  1.3 0.9 %collective-permute-done.refs_3_.refs_5_ = bf16[16,8,128]{2,1,0:T(8,128)(2,1)S(1)} collective-permute-done((bf16[16,8,128]{2,1,0:T(8,128)(2,1)S(1)}, bf16[16,8,128]{2,1,0:T(8,128)(2,1)S(1)}, u32[]{:S(2)}, u32[]{:S(2)}) %collective-permute-start) | collective-permute-done | bytes 32800 | tf_op jit(solution)/shard_map/ppermute | solution.py:424
  2.2 5.0 %collective-permute-start.2 = (bf16[32,8,128]{2,1,0:T(8,128)(2,1)S(1)}, bf16[32,8,128]{2,1,0:T(8,128)(2,1)S(1)}, u32[]{:S(2)}, u32[]{:S(2)}) collective-permute-start(bf16[32,8,128]{2,1,0:T(8,128)(2,1)S(1)} %pad_maximum_fusion), channel_id=1, source_target_pairs={{0,10},{1,13},{2,8},{3,15},{4,14},{5,9},{6,12},{7,11},{8,2},{9,5},... | collective-permute-start | bytes 196616 | tf_op jit(solution)/shard_map/ppermute | solution.py:424
  7.1 0.5 %collective-permute-start.7 = (bf16[32,8,128]{2,1,0:T(8,128)(2,1)S(1)}, bf16[32,8,128]{2,1,0:T(8,128)(2,1)S(1)}, u32[]{:S(2)}, u32[]{:S(2)}) collective-permute-start(bf16[32,8,128]{2,1,0:T(8,128)(2,1)S(1)} %pad_maximum_fusion), channel_id=1, source_target_pairs={{0,2},{1,5},{2,0},{3,7},{4,6},{5,1},{6,4},{7,3},{8,10},{9,13},{10,... | collective-permute-start | bytes 196616 | tf_op jit(solution)/shard_map/ppermute | solution.py:424
  7.6 2.5 %collective-permute-start.5 = (bf16[32,8,128]{2,1,0:T(8,128)(2,1)S(1)}, bf16[32,8,128]{2,1,0:T(8,128)(2,1)S(1)}, u32[]{:S(2)}, u32[]{:S(2)}) collective-permute-start(bf16[32,8,128]{2,1,0:T(8,128)(2,1)S(1)} %pad_maximum_fusion), channel_id=1, source_target_pairs={{0,6},{1,9},{2,4},{3,11},{4,2},{5,13},{6,0},{7,15},{8,14},{9,1},{1... | collective-permute-start | bytes 196616 | tf_op jit(solution)/shard_map/ppermute | solution.py:424
  10.2 4.0 %base.1 = (f32[8,2048]{1,0:T(8,128)S(1)}, bf16[256,1024]{1,0:T(8,128)(2,1)S(1)}, bf16[256,1024]{1,0:T(8,128)(2,1)S(1)}, bf16[128,2048]{1,0:T(8,128)(2,1)S(1)}, b...) custom-call(s32[1]{0:T(128)} %bitcast.index_ref.refs_0_, ...), custom_call_target="tpu_custom_call" | custom-call | flops 1000000 | tf_op jit(solution)/shard_map/base/pallas_call | solution.py:450
  14.2 2.5 %collective-permute-done.1.refs_4_.refs_6_ = bf16[16,8,128]{2,1,0:T(8,128)(2,1)S(1)} collective-permute-done((bf16[16,8,128]{2,1,0:T(8,128)(2,1)S(1)}, bf16[16,8,128]{2,1,0:T(8,128)(2,1)S(1)}, u32[]{:S(2)}, u32[]{:S(2)}) %collective-permute-start.1) | collective-permute-done | bytes 32800 | tf_op jit(solution)/shard_map/ppermute | solution.py:424
  16.8 0.5 %collective-permute-start.6 = (bf16[32,8,128]{2,1,0:T(8,128)(2,1)S(1)}, bf16[32,8,128]{2,1,0:T(8,128)(2,1)S(1)}, u32[]{:S(2)}, u32[]{:S(2)}) collective-permute-start(bf16[32,8,128]{2,1,0:T(8,128)(2,1)S(1)} %collective-permute-done.5.refs_8_.refs_10_), channel_id=1, source_target_pairs={{0,1},{1,0},{2,3},{3,2},{4,5},{5,4},{6,7},{7,6},{8,9},{9,8},{10,11... | collective-permute-start | bytes 196616 | tf_op jit(solution)/shard_map/ppermute | solution.py:424
  17.3 0.1 collective-permute-start.4
  17.4 0.4 %collective-permute-start.3 = (bf16[16,8,128]{2,1,0:T(8,128)(2,1)S(1)}, bf16[16,8,128]{2,1,0:T(8,128)(2,1)S(1)}, u32[]{:S(2)}, u32[]{:S(2)}) collective-permute-start(bf16[16,8,128]{2,1,0:T(8,128)(2,1)S(1)} %collective-permute-done.1.refs_4_.refs_6_), channel_id=1, source_target_pairs={{0,1},{1,0},{2,3},{3,2},{4,5},{5,4},{6,7},{7,6},{8,9},{9,8},{10,11... | collective-permute-start | bytes 98312 | tf_op jit(solution)/shard_map/ppermute | solution.py:424
  17.8 0.9 %collective-permute-done.3.refs_5_.refs_7_ = bf16[16,8,128]{2,1,0:T(8,128)(2,1)S(1)} collective-permute-done((bf16[16,8,128]{2,1,0:T(8,128)(2,1)S(1)}, bf16[16,8,128]{2,1,0:T(8,128)(2,1)S(1)}, u32[]{:S(2)}, u32[]{:S(2)}) %collective-permute-start.3) | collective-permute-done | bytes 32800 | tf_op jit(solution)/shard_map/ppermute | solution.py:424
  18.7 1.6 %send_states.1 = bf16[528,128]{1,0:T(8,128)(2,1)S(1)} custom-call(s32[1]{0:T(128)} %bitcast.index_ref.refs_0_, s32[2]{0:T(128)S(1)} %copy-done, bf16[16,8,128]{2,1,0:T(8,128)(2,1)S(1)} %pack.1.own_ref.refs_2_.refs_4_, bf16[16,8,128]{2,1,0:T(8,128)(2,1)S(1)} %collective-permute-done.refs_3_.refs_5_, ...), custom_call_target="tpu_custom_call" | custom-call | flops 1000000 | tf_op jit(solution)/shard_map/send_states/pallas_call | solution.py:450
  20.3 0.4 %collective-permute-start.10 = (bf16[528,128]{1,0:T(8,128)(2,1)S(1)}, bf16[528,128]{1,0:T(8,128)(2,1)S(1)}, u32[]{:S(2)}, u32[]{:S(2)}) collective-permute-start(bf16[528,128]{1,0:T(8,128)(2,1)S(1)} %send_states.1), channel_id=1, source_target_pairs={{0,1},{1,0},{2,3},{3,2},{4,5},{5,4},{6,7},{7,6},{8,9},{9,8},{10,11... | collective-permute-start | bytes 405512 | tf_op jit(solution)/shard_map/ppermute | solution.py:424
  20.7 0.1 add_convert_fusion
  20.7 1.4 %project.1 = (f32[2,64,128]{2,1,0:T(8,128)S(1)}, bf16[192,128]{1,0:T(8,128)(2,1)S(1)}) custom-call(s32[1]{0:T(128)} %bitcast.index_ref.refs_0_, s32[2]{0:T(128)S(1)} %copy-done.1, s32[16]{0:T(128)S(1)} %copy-done.2, s32[16]{0:T(128)S(1)} %copy-done.3, bf16[16,8,128]{2,1,0:T(8,128)(2,1)S(1)} %pack.1.own_ref.refs_2_.refs_4_, ...), custom_call_target="tpu_custom_call" | custom-call | flops 1000000 | tf_op jit(solution)/shard_map/project/pallas_call | solution.py:450
  22.1 0.2 collective-permute-start.9
  22.4 0.1 convert_element_type.11
  22.5 1.6 %keep_states.1 = (f32[512,128]{1,0:T(8,128)S(1)}, f32[8,128]{1,0:T(8,128)S(1)}) custom-call(s32[1]{0:T(128)} %bitcast.index_ref.refs_0_, s32[2]{0:T(128)S(1)} %copy-done, bf16[16,8,128]{2,1,0:T(8,128)(2,1)S(1)} %pack.1.own_ref.refs_2_.refs_4_, bf16[16,8,128]{2,1,0:T(8,128)(2,1)S(1)} %collective-permute-done.refs_3_.refs_5_, ...), custom_call_target="tpu_custom_call" | custom-call | flops 1000000 | tf_op jit(solution)/shard_map/keep_states/pallas_call | solution.py:450
  24.1 0.3 join.1
  24.4 2.3 %collective-permute-start.11 = (bf16[96,128]{1,0:T(8,128)(2,1)S(1)}, bf16[96,128]{1,0:T(8,128)(2,1)S(1)}, u32[]{:S(2)}, u32[]{:S(2)}) collective-permute-start(bf16[96,128]{1,0:T(8,128)(2,1)S(1)} %get-tuple-element.39), channel_id=1, source_target_pairs={{0,14},{1,15},{2,12},{3,13},{4,10},{5,11},{6,8},{7,9},{8,6},{9,7},... | collective-permute-start | bytes 73736 | tf_op jit(solution)/shard_map/ppermute | solution.py:424
  26.7 3.0 %collective-permute-start.13 = (bf16[160,128]{1,0:T(8,128)(2,1)S(1)}, bf16[160,128]{1,0:T(8,128)(2,1)S(1)}, u32[]{:S(2)}, u32[]{:S(2)}) collective-permute-start(bf16[160,128]{1,0:T(8,128)(2,1)S(1)} %get-tuple-element.43), channel_id=1, source_target_pairs={{0,6},{1,9},{2,4},{3,11},{4,2},{5,13},{6,0},{7,15},{8,14},{9,1},{1... | collective-permute-start | bytes 122888 | tf_op jit(solution)/shard_map/ppermute | solution.py:424
  29.7 1.5 %collective-permute-start.14 = (bf16[160,128]{1,0:T(8,128)(2,1)S(1)}, bf16[160,128]{1,0:T(8,128)(2,1)S(1)}, u32[]{:S(2)}, u32[]{:S(2)}) collective-permute-start(bf16[160,128]{1,0:T(8,128)(2,1)S(1)} %get-tuple-element.44), channel_id=1, source_target_pairs={{0,2},{1,5},{2,0},{3,7},{4,6},{5,1},{6,4},{7,3},{8,10},{9,13},{10,... | collective-permute-start | bytes 122888 | tf_op jit(solution)/shard_map/ppermute | solution.py:424
  31.2 0.1 fusion
  31.3 1.7 %collective-permute-done.12.refs_2_ = bf16[160,128]{1,0:T(8,128)(2,1)S(1)} collective-permute-done((bf16[160,128]{1,0:T(8,128)(2,1)S(1)}, bf16[160,128]{1,0:T(8,128)(2,1)S(1)}, u32[]{:S(2)}, u32[]{:S(2)}) %collective-permute-start.12) | collective-permute-done | bytes 40992 | tf_op jit(solution)/shard_map/ppermute | solution.py:424
  33.1 0.5 %collective-permute-start.16 = (bf16[96,128]{1,0:T(8,128)(2,1)S(1)}, bf16[96,128]{1,0:T(8,128)(2,1)S(1)}, u32[]{:S(2)}, u32[]{:S(2)}) collective-permute-start(bf16[96,128]{1,0:T(8,128)(2,1)S(1)} %slice.12), channel_id=1, source_target_pairs={{0,1},{1,0},{2,3},{3,2},{4,5},{5,4},{6,7},{7,6},{8,9},{9,8},{10,11... | collective-permute-start | bytes 73736 | tf_op jit(solution)/shard_map/ppermute | solution.py:424
  33.6 0.1 collective-permute-done.14.refs_4_
  33.7 0.1 pad_maximum_fusion.1
  33.8 0.5 %collective-permute-done.15.refs_5_ = bf16[96,128]{1,0:T(8,128)(2,1)S(1)} collective-permute-done((bf16[96,128]{1,0:T(8,128)(2,1)S(1)}, bf16[96,128]{1,0:T(8,128)(2,1)S(1)}, u32[]{:S(2)}, u32[]{:S(2)}) %collective-permute-start.15) | collective-permute-done | bytes 24608 | tf_op jit(solution)/shard_map/ppermute | solution.py:424
  34.3 0.2 collective-permute-done.16.refs_6_
  34.5 0.5 %collective-permute-done.17.refs_7_ = bf16[96,128]{1,0:T(8,128)(2,1)S(1)} collective-permute-done((bf16[96,128]{1,0:T(8,128)(2,1)S(1)}, bf16[96,128]{1,0:T(8,128)(2,1)S(1)}, u32[]{:S(2)}, u32[]{:S(2)}) %collective-permute-start.17) | collective-permute-done | bytes 24608 | tf_op jit(solution)/shard_map/ppermute | solution.py:424
  34.9 1.1 %merge_states.1 = bf16[2,4,1024]{2,1,0:T(4,128)(2,1)} custom-call(bf16[16,8,128]{2,1,0:T(8,128)(2,1)S(1)} %pack.1.own_ref.refs_2_.refs_4_, f32[8,128]{1,0:T(8,128)S(1)} %get-tuple-element.48.cos_ref, f32[8,128]{1,0:T(8,128)S(1)} %get-tuple-element.49.sin_ref, bf16[96,128]{1,0:T(8,128)(2,1)S(1)} %get-tuple-element.38.refs_0_, ...), custom_call_target="tpu_custom_call" | custom-call | tf_op jit(solution)/shard_map/merge_states/pallas_call | solution.py:559
  (28 shorter events, 0.1 us)
Async XLA Ops:
  0.8 1.4 %collective-permute-start = (bf16[16,8,128]{2,1,0:T(8,128)(2,1)S(1)}, bf16[16,8,128]{2,1,0:T(8,128)(2,1)S(1)}, u32[]{:S(2)}, u32[]{:S(2)}) collective-permute-start(bf16[16,8,128]{2,1,0:T(8,128)(2,1)S(1)} %pack.1.own_ref.refs_2_.refs_4_), channel_id=1, source_target_pairs={{0,1},{1,0},{2,3},{3,2},{4,5},{5,4},{6,7},{7,6},{8,9},{9,8},{10,11... | collective-permute-start | bytes 98312 | tf_op jit(solution)/shard_map/ppermute | solution.py:424
  2.2 14.6 %collective-permute-start.2 = (bf16[32,8,128]{2,1,0:T(8,128)(2,1)S(1)}, bf16[32,8,128]{2,1,0:T(8,128)(2,1)S(1)}, u32[]{:S(2)}, u32[]{:S(2)}) collective-permute-start(bf16[32,8,128]{2,1,0:T(8,128)(2,1)S(1)} %pad_maximum_fusion), channel_id=1, source_target_pairs={{0,10},{1,13},{2,8},{3,15},{4,14},{5,9},{6,12},{7,11},{8,2},{9,5},... | collective-permute-start | bytes 196616 | tf_op jit(solution)/shard_map/ppermute | solution.py:424
  7.1 9.7 %collective-permute-start.7 = (bf16[32,8,128]{2,1,0:T(8,128)(2,1)S(1)}, bf16[32,8,128]{2,1,0:T(8,128)(2,1)S(1)}, u32[]{:S(2)}, u32[]{:S(2)}) collective-permute-start(bf16[32,8,128]{2,1,0:T(8,128)(2,1)S(1)} %pad_maximum_fusion), channel_id=1, source_target_pairs={{0,2},{1,5},{2,0},{3,7},{4,6},{5,1},{6,4},{7,3},{8,10},{9,13},{10,... | collective-permute-start | bytes 196616 | tf_op jit(solution)/shard_map/ppermute | solution.py:424
  7.6 9.2 %collective-permute-start.5 = (bf16[32,8,128]{2,1,0:T(8,128)(2,1)S(1)}, bf16[32,8,128]{2,1,0:T(8,128)(2,1)S(1)}, u32[]{:S(2)}, u32[]{:S(2)}) collective-permute-start(bf16[32,8,128]{2,1,0:T(8,128)(2,1)S(1)} %pad_maximum_fusion), channel_id=1, source_target_pairs={{0,6},{1,9},{2,4},{3,11},{4,2},{5,13},{6,0},{7,15},{8,14},{9,1},{1... | collective-permute-start | bytes 196616 | tf_op jit(solution)/shard_map/ppermute | solution.py:424
  10.1 6.6 %collective-permute-start.1 = (bf16[16,8,128]{2,1,0:T(8,128)(2,1)S(1)}, bf16[16,8,128]{2,1,0:T(8,128)(2,1)S(1)}, u32[]{:S(2)}, u32[]{:S(2)}) collective-permute-start(bf16[16,8,128]{2,1,0:T(8,128)(2,1)S(1)} %pack.1.own_ref.refs_2_.refs_4_), channel_id=1, source_target_pairs={{0,14},{1,15},{2,12},{3,13},{4,10},{5,11},{6,8},{7,9},{8,6},{9,7},... | collective-permute-start | bytes 98312 | tf_op jit(solution)/shard_map/ppermute | solution.py:424
  10.1 8.5 %copy-start = (s32[2]{0:T(128)S(1)}, s32[2]{0:T(128)}, u32[]{:S(2)}) copy-start(s32[2]{0:T(128)} %refs_1_.5) | copy-start | bytes 28
  10.2 10.6 %copy-start.1 = (s32[2]{0:T(128)S(1)}, s32[2]{0:T(128)}, u32[]{:S(2)}) copy-start(s32[2]{0:T(128)} %refs_1_.4) | copy-start | bytes 28
  10.2 10.6 %copy-start.2 = (s32[16]{0:T(128)S(1)}, s32[16]{0:T(128)}, u32[]{:S(2)}) copy-start(s32[16]{0:T(128)} %refs_2_.1) | copy-start | bytes 196
  10.2 10.6 %copy-start.3 = (s32[16]{0:T(128)S(1)}, s32[16]{0:T(128)}, u32[]{:S(2)}) copy-start(s32[16]{0:T(128)} %refs_3_.1) | copy-start | bytes 196
  16.8 1.9 %collective-permute-start.8 = (bf16[32,8,128]{2,1,0:T(8,128)(2,1)S(1)}, bf16[32,8,128]{2,1,0:T(8,128)(2,1)S(1)}, u32[]{:S(2)}, u32[]{:S(2)}) collective-permute-start(bf16[32,8,128]{2,1,0:T(8,128)(2,1)S(1)} %collective-permute-done.7.refs_10_.refs_12_), channel_id=1, source_target_pairs={{0,1},{1,0},{2,3},{3,2},{4,5},{5,4},{6,7},{7,6},{8,9},{9,8},{10,11... | collective-permute-start | bytes 196616 | tf_op jit(solution)/shard_map/ppermute | solution.py:424
  16.8 1.9 %collective-permute-start.6 = (bf16[32,8,128]{2,1,0:T(8,128)(2,1)S(1)}, bf16[32,8,128]{2,1,0:T(8,128)(2,1)S(1)}, u32[]{:S(2)}, u32[]{:S(2)}) collective-permute-start(bf16[32,8,128]{2,1,0:T(8,128)(2,1)S(1)} %collective-permute-done.5.refs_8_.refs_10_), channel_id=1, source_target_pairs={{0,1},{1,0},{2,3},{3,2},{4,5},{5,4},{6,7},{7,6},{8,9},{9,8},{10,11... | collective-permute-start | bytes 196616 | tf_op jit(solution)/shard_map/ppermute | solution.py:424
  17.3 1.4 %collective-permute-start.4 = (bf16[32,8,128]{2,1,0:T(8,128)(2,1)S(1)}, bf16[32,8,128]{2,1,0:T(8,128)(2,1)S(1)}, u32[]{:S(2)}, u32[]{:S(2)}) collective-permute-start(bf16[32,8,128]{2,1,0:T(8,128)(2,1)S(1)} %collective-permute-done.2.refs_6_.refs_8_), channel_id=1, source_target_pairs={{0,1},{1,0},{2,3},{3,2},{4,5},{5,4},{6,7},{7,6},{8,9},{9,8},{10,11... | collective-permute-start | bytes 196616 | tf_op jit(solution)/shard_map/ppermute | solution.py:424
  17.4 1.3 %collective-permute-start.3 = (bf16[16,8,128]{2,1,0:T(8,128)(2,1)S(1)}, bf16[16,8,128]{2,1,0:T(8,128)(2,1)S(1)}, u32[]{:S(2)}, u32[]{:S(2)}) collective-permute-start(bf16[16,8,128]{2,1,0:T(8,128)(2,1)S(1)} %collective-permute-done.1.refs_4_.refs_6_), channel_id=1, source_target_pairs={{0,1},{1,0},{2,3},{3,2},{4,5},{5,4},{6,7},{7,6},{8,9},{9,8},{10,11... | collective-permute-start | bytes 98312 | tf_op jit(solution)/shard_map/ppermute | solution.py:424
  20.3 3.8 %collective-permute-start.10 = (bf16[528,128]{1,0:T(8,128)(2,1)S(1)}, bf16[528,128]{1,0:T(8,128)(2,1)S(1)}, u32[]{:S(2)}, u32[]{:S(2)}) collective-permute-start(bf16[528,128]{1,0:T(8,128)(2,1)S(1)} %send_states.1), channel_id=1, source_target_pairs={{0,1},{1,0},{2,3},{3,2},{4,5},{5,4},{6,7},{7,6},{8,9},{9,8},{10,11... | collective-permute-start | bytes 405512 | tf_op jit(solution)/shard_map/ppermute | solution.py:424
  22.1 1.9 %collective-permute-start.9 = (bf16[192,128]{1,0:T(8,128)(2,1)S(1)}, bf16[192,128]{1,0:T(8,128)(2,1)S(1)}, u32[]{:S(2)}, u32[]{:S(2)}) collective-permute-start(bf16[192,128]{1,0:T(8,128)(2,1)S(1)} %get-tuple-element.37), channel_id=1, source_target_pairs={{0,1},{1,0},{2,3},{3,2},{4,5},{5,4},{6,7},{7,6},{8,9},{9,8},{10,11... | collective-permute-start | bytes 147464 | tf_op jit(solution)/shard_map/ppermute | solution.py:424
  24.4 6.9 %collective-permute-start.11 = (bf16[96,128]{1,0:T(8,128)(2,1)S(1)}, bf16[96,128]{1,0:T(8,128)(2,1)S(1)}, u32[]{:S(2)}, u32[]{:S(2)}) collective-permute-start(bf16[96,128]{1,0:T(8,128)(2,1)S(1)} %get-tuple-element.39), channel_id=1, source_target_pairs={{0,14},{1,15},{2,12},{3,13},{4,10},{5,11},{6,8},{7,9},{8,6},{9,7},... | collective-permute-start | bytes 73736 | tf_op jit(solution)/shard_map/ppermute | solution.py:424
  26.7 6.3 %collective-permute-start.12 = (bf16[160,128]{1,0:T(8,128)(2,1)S(1)}, bf16[160,128]{1,0:T(8,128)(2,1)S(1)}, u32[]{:S(2)}, u32[]{:S(2)}) collective-permute-start(bf16[160,128]{1,0:T(8,128)(2,1)S(1)} %get-tuple-element.40), channel_id=1, source_target_pairs={{0,10},{1,13},{2,8},{3,15},{4,14},{5,9},{6,12},{7,11},{8,2},{9,5},... | collective-permute-start | bytes 122888 | tf_op jit(solution)/shard_map/ppermute | solution.py:424
  26.7 6.3 %collective-permute-start.13 = (bf16[160,128]{1,0:T(8,128)(2,1)S(1)}, bf16[160,128]{1,0:T(8,128)(2,1)S(1)}, u32[]{:S(2)}, u32[]{:S(2)}) collective-permute-start(bf16[160,128]{1,0:T(8,128)(2,1)S(1)} %get-tuple-element.43), channel_id=1, source_target_pairs={{0,6},{1,9},{2,4},{3,11},{4,2},{5,13},{6,0},{7,15},{8,14},{9,1},{1... | collective-permute-start | bytes 122888 | tf_op jit(solution)/shard_map/ppermute | solution.py:424
  29.7 4.0 %collective-permute-start.14 = (bf16[160,128]{1,0:T(8,128)(2,1)S(1)}, bf16[160,128]{1,0:T(8,128)(2,1)S(1)}, u32[]{:S(2)}, u32[]{:S(2)}) collective-permute-start(bf16[160,128]{1,0:T(8,128)(2,1)S(1)} %get-tuple-element.44), channel_id=1, source_target_pairs={{0,2},{1,5},{2,0},{3,7},{4,6},{5,1},{6,4},{7,3},{8,10},{9,13},{10,... | collective-permute-start | bytes 122888 | tf_op jit(solution)/shard_map/ppermute | solution.py:424
  33.1 1.2 %collective-permute-start.15 = (bf16[96,128]{1,0:T(8,128)(2,1)S(1)}, bf16[96,128]{1,0:T(8,128)(2,1)S(1)}, u32[]{:S(2)}, u32[]{:S(2)}) collective-permute-start(bf16[96,128]{1,0:T(8,128)(2,1)S(1)} %slice.9), channel_id=1, source_target_pairs={{0,1},{1,0},{2,3},{3,2},{4,5},{5,4},{6,7},{7,6},{8,9},{9,8},{10,11... | collective-permute-start | bytes 73736 | tf_op jit(solution)/shard_map/ppermute | solution.py:424
  33.1 1.3 %collective-permute-start.16 = (bf16[96,128]{1,0:T(8,128)(2,1)S(1)}, bf16[96,128]{1,0:T(8,128)(2,1)S(1)}, u32[]{:S(2)}, u32[]{:S(2)}) collective-permute-start(bf16[96,128]{1,0:T(8,128)(2,1)S(1)} %slice.12), channel_id=1, source_target_pairs={{0,1},{1,0},{2,3},{3,2},{4,5},{5,4},{6,7},{7,6},{8,9},{9,8},{10,11... | collective-permute-start | bytes 73736 | tf_op jit(solution)/shard_map/ppermute | solution.py:424
  33.7 1.2 %collective-permute-start.17 = (bf16[96,128]{1,0:T(8,128)(2,1)S(1)}, bf16[96,128]{1,0:T(8,128)(2,1)S(1)}, u32[]{:S(2)}, u32[]{:S(2)}) collective-permute-start(bf16[96,128]{1,0:T(8,128)(2,1)S(1)} %slice.13), channel_id=1, source_target_pairs={{0,1},{1,0},{2,3},{3,2},{4,5},{5,4},{6,7},{7,6},{8,9},{9,8},{10,11... | collective-permute-start | bytes 73736 | tf_op jit(solution)/shard_map/ppermute | solution.py:424

commit v11 on v10

--- a/solution.py
+++ b/solution.py
@@ -33,19 +33,16 @@
         lanes = devices // 2
         self.per_head = per_head = lanes // KEY_HEADS
         self.heads, self.chunks = QUERY_HEADS // devices, width // HEAD_WIDTH
-        if per_head > 1:
-            self.single = 1
-            self.pairs = [(m, m ^ 1) for m in range(lanes - 2, 0, -2)]
-        else:
-            self.single = lanes - 1
-            self.pairs = [(m, m + 1) for m in range(lanes - 3, 0, -2)]
+        self.single = 1
+        self.pairs = [(m, m + 1) for m in range(lanes - 2, 0, -2)]
         size = self.heads + self.chunks
         self.own = ((0, 0), ((0, 0), (1, 0)))
         self.one = ((self.single,) * 2, ((2, 0), (3, 0)))
         self.mine, self.theirs = [], []
         for k, (a, b) in enumerate(self.pairs):
-            self.mine.append(((a, b), ((4 + 2 * k, 0), (4 + 2 * k, size))))
-            self.theirs.append(((b, a), ((5 + 2 * k, size), (5 + 2 * k, 0))))
+            at = 2 * size * k
+            self.mine.append(((a, b), ((4, at), (4, at + size))))
+            self.theirs.append(((b, a), ((5, at + size), (5, at))))
 
     def head_masks(self, unit):
         return tuple(mask // self.per_head for mask in unit[0][0])
@@ -95,15 +92,14 @@
     ]
 
 
-def streams(sources, index_ref, down_ref, halves, sems):
-    count, depth = halves[0].shape[:2]
+def streams(sources, index_ref, down_ref, half_ref, sems):
+    depth = half_ref.shape[1]
     here = index_ref[0]
     copies = []
     for at, (_, _, masks, side) in enumerate(sources):
         source = here ^ (2 * here_mask(masks, here) + side)
         rows = pl.ds(pl.multiple_of(source * depth, depth), depth)
-        place = halves[at // count].at[at % count]
-        copies.append(pltpu.make_async_copy(down_ref.at[rows], place, sems.at[at]))
+        copies.append(pltpu.make_async_copy(down_ref.at[rows], half_ref.at[at], sems.at[at]))
     return copies
 
 
@@ -135,10 +131,9 @@
             at += 1
 
 
-def base_kernel(plan, index_ref, own_ref, weight_ref, *refs):
-    down_ref, *sources = refs[:4]
-    base_ref, *held = refs[4:8]
-    halves, (buffer, sems, down_sems) = refs[8:10], refs[10:]
+def base_kernel(heads, own_ref, weight_ref, *refs):
+    sources, base_ref, held = refs[:3], refs[3], refs[4:7]
+    buffer, sems = refs[7:]
     parts, depth = buffer.shape[:2]
     loads = [
         pltpu.make_async_copy(weight_ref.at[pl.ds(p * depth, depth)], buffer.at[p], sems.at[p])
@@ -148,14 +143,12 @@
         pltpu.make_async_copy(source, place, sems.at[parts + i])
         for i, (source, place) in enumerate(zip(sources, held))
     ]
-    others += streams(sources_of(plan), index_ref, down_ref, halves, down_sems)
     for load in loads + others:
         load.start()
     tiles = depth // HEAD_WIDTH
     total = jnp.zeros(base_ref.shape, jnp.float32)
     for p in range(parts):
-        first = plan.heads + p * tiles
-        hidden = jnp.concatenate([own_ref[first + c] for c in range(tiles)], axis=1)
+        hidden = jnp.concatenate([own_ref[heads + p * tiles + c] for c in range(tiles)], axis=1)
         loads[p].wait()
         total += dot(hidden, buffer[p], ((1,), (0,)))
     base_ref[...] = total
@@ -163,10 +156,82 @@
         load.wait()
 
 
-def project_kernel(sizes, plan, *refs):
-    (index_ref, adapter_ref, rank_ref, pool_ref, *arrays) = refs[:-6]
-    (base_ref, up_ref, *halves, own_ref, parts_ref) = refs[-6:]
+def fetch_kernel(sources, index_ref, down_ref, half_ref, sems):
+    copies = streams(sources, index_ref, down_ref, half_ref, sems)
+    for copy in copies:
+        copy.start()
+    for copy in copies:
+        copy.wait()
+
+
+def attend(sizes, plan, keep, index_ref, length_ref, arrays, key_ref, value_ref, put):
     requests, tokens, devices = sizes
+    here = index_ref[0]
+    chip = here // 2
+    per_head = plan.per_head
+    slot_rows = plan.heads * requests * tokens
+    positions = key_ref.shape[0] // requests
+    place = lax.broadcasted_iota(jnp.int32, (requests * positions, HEAD_WIDTH), 0)
+    column = lax.broadcasted_iota(jnp.int32, (requests * positions, HEAD_WIDTH), 1)
+    place_request = place // positions
+    limit = jnp.zeros_like(place)
+    for b in range(requests):
+        limit = jnp.where(place_request == b, length_ref[b], limit)
+    allowed = (here * positions + place % positions < limit) & (
+        place_request == (column // tokens) % requests
+    )
+    peaks, totals = [], []
+    for number, runs in enumerate(plan.attention_chunks(slot_rows, keep)):
+        places = [slot[1][side] for run in runs for slot, side in run]
+        query = jnp.concatenate(
+            [arrays[array][tile + h] for array, tile in places for h in range(plan.heads)], axis=0
+        )
+        spots = [
+            head_columns((chip // per_head) ^ (here_mask(run[0][0][0], here) // per_head))
+            for run in runs
+        ]
+        share = HEAD_WIDTH // len(runs)
+        scores = None
+        for i, spot in enumerate(spots):
+            part = dot(key_ref[:, spot], query, ((1,), (1,)))
+            scores = part if scores is None else jnp.where(column < i * share, scores, part)
+        scores = scores * SCALE
+        peak = jnp.max(jnp.where(allowed, scores, NEG_FILL), axis=0, keepdims=True)
+        peak = round_bf16(peak)
+        weights = jnp.where(allowed, jnp.exp(scores - peak), 0.0)
+        peaks.append(peak)
+        totals.append(jnp.sum(weights, axis=0, keepdims=True))
+        weights = jnp.transpose(weights.astype(jnp.bfloat16))
+        for i, spot in enumerate(spots):
+            own = slice(i * share, (i + 1) * share)
+            put(number, i * share, dot(weights[own], value_ref[:, spot], ((1,), (0,))))
+    return peaks, totals
+
+
+def rows_of(items, count):
+    row = lax.broadcasted_iota(jnp.int32, (count, HEAD_WIDTH), 0)
+    out = jnp.zeros((count, HEAD_WIDTH), jnp.float32)
+    for i, item in enumerate(items):
+        out = jnp.where(row == i, item, out)
+    return out
+
+
+def send_kernel(sizes, plan, *refs):
+    (index_ref, length_ref, adapter_ref, rank_ref, pool_ref, *arrays) = refs[:-9]
+    (key_ref, value_ref, base_ref, up_ref, *halves, send_ref, own_ref, parts_ref) = refs[-9:]
+    requests, tokens, devices = sizes
+
+    def put(chunk, row, mix):
+        at = chunk * 128 + row
+        send_ref[at : at + mix.shape[0]] = mix.astype(jnp.bfloat16)
+
+    peaks, totals = attend(
+        sizes, plan, False, index_ref, length_ref, arrays, key_ref, value_ref, put
+    )
+    highs = [round_bf16(total) for total in totals]
+    lows = [total - high for total, high in zip(totals, highs)]
+    send_ref[MIX_ROWS:] = rows_of(peaks + highs + lows, STAT_ROWS).astype(jnp.bfloat16)
+
     rows = requests * tokens
     lowered = lower(sources_of(plan), arrays, halves)
     row_request = lax.broadcasted_iota(jnp.int32, (rows, 1), 0) // tokens
@@ -195,73 +260,6 @@
     parts_ref[:step] = high
     parts_ref[step : 2 * step] = (keys - high.astype(jnp.float32)).astype(jnp.bfloat16)
     parts_ref[2 * step :] = values.astype(jnp.bfloat16)
-
-
-def attend(sizes, plan, keep, index_ref, length_ref, arrays, key_ref, value_ref, put):
-    requests, tokens, devices = sizes
-    here = index_ref[0]
-    chip = here // 2
-    per_head = plan.per_head
-    slot_rows = plan.heads * requests * tokens
-    positions = key_ref.shape[0] // requests
-    place = lax.broadcasted_iota(jnp.int32, (requests * positions, HEAD_WIDTH), 0)
-    column = lax.broadcasted_iota(jnp.int32, (requests * positions, HEAD_WIDTH), 1)
-    place_request = place // positions
-    limit = jnp.zeros_like(place)
-    for b in range(requests):
-        limit = jnp.where(place_request == b, length_ref[b], limit)
-    allowed = (here * positions + place % positions < limit) & (
-        place_request == (column // tokens) % requests
-    )
-    peaks, totals = [], []
-    for number, runs in enumerate(plan.attention_chunks(slot_rows, keep)):
-        places = [slot[1][side] for run in runs for slot, side in run]
-        query = jnp.concatenate(
-            [arrays[array][tile + h] for array, tile in places for h in range(plan.heads)], axis=0
-        )
-        spots = [
-            head_columns((chip // per_head) ^ (here_mask(run[0][0][0], here) // per_head))
-            for run in runs
-        ]
-        share = HEAD_WIDTH // len(runs)
-        scores = None
-        for i, spot in enumerate(spots):
-            part = dot(key_ref[:, spot], query, ((1,), (1,)))
-            scores = part if scores is None else jnp.where(column < i * share, scores, part)
-        scores = scores * SCALE
-        peak = jnp.max(jnp.where(allowed, scores, NEG_FILL), axis=0, keepdims=True)
-        peak = round_bf16(peak)
-        weights = jnp.where(allowed, jnp.exp(scores - peak), 0.0)
-        peaks.append(peak)
-        totals.append(jnp.sum(weights, axis=0, keepdims=True))
-        weights = jnp.transpose(weights.astype(jnp.bfloat16))
-        for i, spot in enumerate(spots):
-            own = slice(i * share, (i + 1) * share)
-            put(number, i * share, dot(weights[own], value_ref[:, spot], ((1,), (0,))))
-    return peaks, totals
-
-
-def rows_of(items, count):
-    row = lax.broadcasted_iota(jnp.int32, (count, HEAD_WIDTH), 0)
-    out = jnp.zeros((count, HEAD_WIDTH), jnp.float32)
-    for i, item in enumerate(items):
-        out = jnp.where(row == i, item, out)
-    return out
-
-
-def send_kernel(sizes, plan, *refs):
-    (index_ref, length_ref, *arrays, key_ref, value_ref, send_ref) = refs
-
-    def put(chunk, row, mix):
-        at = chunk * 128 + row
-        send_ref[at : at + mix.shape[0]] = mix.astype(jnp.bfloat16)
-
-    peaks, totals = attend(
-        sizes, plan, False, index_ref, length_ref, arrays, key_ref, value_ref, put
-    )
-    highs = [round_bf16(total) for total in totals]
-    lows = [total - high for total, high in zip(totals, highs)]
-    send_ref[MIX_ROWS:] = rows_of(peaks + highs + lows, STAT_ROWS).astype(jnp.bfloat16)
 
 
 def keep_kernel(sizes, plan, *refs):
@@ -486,50 +484,53 @@
     )
     out_width = key_value_weight.shape[1]
     parts = 4 if width % (4 * HEAD_WIDTH) == 0 else 1
-    down = adapter_down_weight[0]
-    half = pltpu.VMEM((devices // 2, width, down.shape[1]), jnp.bfloat16)
-    base, keys, values, up, *halves = call(
-        functools.partial(base_kernel, plan),
-        (index, own, pinned(key_value_weight), pinned(down)) + tuple(pinned(x) for x in big),
-        [smem(), vmem()] + [hbm()] * 5,
-        [pltpu.VMEM((rows, out_width), jnp.float32)]
-        + [pltpu.VMEM(x.shape, x.dtype) for x in big]
-        + [half, half],
+    base, keys, values, up = call(
+        functools.partial(base_kernel, heads),
+        (own, pinned(key_value_weight)) + tuple(pinned(x) for x in big),
+        [vmem()] + [hbm()] * 4,
+        [pltpu.VMEM((rows, out_width), jnp.float32)] + [pltpu.VMEM(x.shape, x.dtype) for x in big],
         [
             pltpu.VMEM((parts, width // parts, out_width), jnp.bfloat16),
             pltpu.SemaphoreType.DMA((parts + 3,)),
-            pltpu.SemaphoreType.DMA((devices,)),
         ],
         "base",
     )
-    one, mine[0], base = lax.optimization_barrier((one, mine[0], base))
-    arrays = [own, other, one, core_swap(one)]
-    for x in mine:
-        arrays += [x, core_swap(x)]
-    arrays = tuple(arrays)
+    down = adapter_down_weight[0]
+    count = devices // 2
+    first, second = [
+        call(
+            functools.partial(fetch_kernel, sources_of(plan)[at : at + count]),
+            (index, pinned(down)),
+            [smem(), hbm()],
+            [pltpu.VMEM((count, width, down.shape[1]), jnp.bfloat16)],
+            [pltpu.SemaphoreType.DMA((count,))],
+            "fetch",
+        )[0]
+        for at in (0, count)
+    ]
+    one, base, first = lax.optimization_barrier((one, base, first))
+    other_one = core_swap(one)
+    mine = jnp.concatenate(mine, axis=0)
+    mine, other_one = lax.optimization_barrier((mine, other_one))
+    other_mine, second = lax.optimization_barrier((core_swap(mine), second))
+    arrays = (own, other, one, other_one, mine, other_mine)
+    halves = (first, second)
     step = KEY_HEADS * rows
-    proj, proj_parts = call(
-        functools.partial(project_kernel, sizes, plan),
-        (index, request_adapter, adapter_rank_list, adapter_pool_row)
+    send, proj, proj_parts = call(
+        functools.partial(send_kernel, sizes, plan),
+        (index, lengths, request_adapter, adapter_rank_list, adapter_pool_row)
         + arrays
-        + (base, up, *halves),
-        [smem()] * 4 + [vmem()] * (len(arrays) + 4),
+        + (keys, values, base, up, *halves),
+        [smem()] * 5 + [vmem()] * (len(arrays) + 6),
         [
+            pltpu.VMEM((MIX_ROWS + STAT_ROWS, HEAD_WIDTH), jnp.bfloat16),
             pltpu.VMEM((2, step, HEAD_WIDTH), jnp.float32),
             pltpu.VMEM((3 * step, HEAD_WIDTH), jnp.bfloat16),
         ],
         [],
-        "project",
+        "send_states",
     )
     got_parts = core_swap(proj_parts)
-    (send,) = call(
-        functools.partial(send_kernel, sizes, plan),
-        (index, lengths) + arrays + (keys, values),
-        [smem()] * 2 + [vmem()] * (len(arrays) + 2),
-        [pltpu.VMEM((MIX_ROWS + STAT_ROWS, HEAD_WIDTH), jnp.bfloat16)],
-        [],
-        "send_states",
-    )
     got = core_swap(send)
     mix, stats = call(
         functools.partial(keep_kernel, sizes, plan),
@@ -553,7 +554,6 @@
     )
     heard = [packets[0], trade(packets[1], devices, plan.single, plan.single)]
     heard += [trade(x, devices, a, b) for x, (a, b) in zip(packets[2:], plan.pairs)]
-    heard[1], heard[2] = lax.optimization_barrier((heard[1], heard[2]))
     heard += [core_swap(x[slot_rows:]) for x in heard[2:]]
     cosine, sine = rotation(lengths, tokens)
     return pl.pallas_call(

time: 36.3 us -> 33.7 us (0.928)
  starting transfers between devices: 17.5 us -> 15 us
  waiting for transfers between devices: 7.23 us -> 5.83 us
  Pallas kernels: 10.8 us -> 11.9 us
    ppermute x18 -> x16, starting transfers between devices: 17.5 us -> 15 us  [trade(): return lax.ppermute(x, 'tensor', pairs)]
    ppermute x18 -> x16, waiting for transfers between devices: 7.23 us -> 5.83 us  [trade(): return lax.ppermute(x, 'tensor', pairs)]
    pallas_call x6 -> x7, Pallas kernels: 9.69 us -> 10.8 us  [call(): pl.pallas_call(kernel, out_shape=tuple(out_shape), in_specs=in_specs, out...]
  transfers between devices with their start and end apart: 18 -> 16, of which waited for: 8 -> 6; matrix products, arithmetic and copies ran while one was open for 1% -> 1% of each run, Pallas kernels for 20% -> 22%
where the time goes in v11:
time: 33.7 us; the launch traced here: 33.3 us
  starting transfers between devices  15 us (45%)
  Pallas kernels  11.9 us (35%)
  waiting for transfers between devices  5.83 us (17%)
    ppermute x16, starting transfers between devices, trade(): return lax.ppermute(x, 'tensor', pairs)  15 us
    pallas_call x7, Pallas kernels, call(): pl.pallas_call(kernel, out_shape=tuple(out_shape), in_specs=in_specs, out...  10.8 us
    ppermute x16, waiting for transfers between devices, trade(): return lax.ppermute(x, 'tensor', pairs)  5.83 us
    pallas_call x1, Pallas kernels, per_device(): pl.pallas_call(functools.partial(merge_kernel, devices, requests, tokens,...  1.11 us
  transfers between devices with their start and end apart: 16, of which 6 were waited for; matrix products, arithmetic and copies ran while one was open for 1% of the time, Pallas kernels for 22%

profile of v11, /device:TPU:0, one launch (start us, length us, event | category | flops | bytes accessed | tf_op | source)
XLA Modules:
  0.0 33.3 jit_solution(17017941644575252815)
XLA Ops:
  0.0 0.8 %pack.1.own_ref.refs_2_.refs_5_ = bf16[16,8,128]{2,1,0:T(8,128)(2,1)S(1)} custom-call(bf16[2,4,1024]{2,1,0:T(4,128)(2,1)} %query_ref.1, bf16[2,4,1024]{2,1,0:T(4,128)(2,1)} %hidden_ref.1), custom_call_target="tpu_custom_call" | custom-call | flops 1000000 | tf_op jit(solution)/shard_map/pack/pallas_call | solution.py:448
  0.8 0.5 %collective-permute-start = (bf16[16,8,128]{2,1,0:T(8,128)(2,1)S(1)}, bf16[16,8,128]{2,1,0:T(8,128)(2,1)S(1)}, u32[]{:S(2)}, u32[]{:S(2)}) collective-permute-start(bf16[16,8,128]{2,1,0:T(8,128)(2,1)S(1)} %pack.1.own_ref.refs_2_.refs_5_), channel_id=1, source_target_pairs={{0,1},{1,0},{2,3},{3,2},{4,5},{5,4},{6,7},{7,6},{8,9},{9,8},{10,11... | collective-permute-start | bytes 98312 | tf_op jit(solution)/shard_map/ppermute | solution.py:422
  1.3 0.9 %collective-permute-done.refs_3_.refs_6_ = bf16[16,8,128]{2,1,0:T(8,128)(2,1)S(1)} collective-permute-done((bf16[16,8,128]{2,1,0:T(8,128)(2,1)S(1)}, bf16[16,8,128]{2,1,0:T(8,128)(2,1)S(1)}, u32[]{:S(2)}, u32[]{:S(2)}) %collective-permute-start) | collective-permute-done | bytes 32800 | tf_op jit(solution)/shard_map/ppermute | solution.py:422
  2.2 5.0 %collective-permute-start.2 = (bf16[32,8,128]{2,1,0:T(8,128)(2,1)S(1)}, bf16[32,8,128]{2,1,0:T(8,128)(2,1)S(1)}, u32[]{:S(2)}, u32[]{:S(2)}) collective-permute-start(bf16[32,8,128]{2,1,0:T(8,128)(2,1)S(1)} %pad_maximum_fusion.1), channel_id=1, source_target_pairs={{0,12},{1,15},{2,14},{3,13},{4,8},{5,11},{6,10},{7,9},{8,4},{9,7},... | collective-permute-start | bytes 196616 | tf_op jit(solution)/shard_map/ppermute | solution.py:422
  7.2 0.6 %collective-permute-start.4 = (bf16[32,8,128]{2,1,0:T(8,128)(2,1)S(1)}, bf16[32,8,128]{2,1,0:T(8,128)(2,1)S(1)}, u32[]{:S(2)}, u32[]{:S(2)}) collective-permute-start(bf16[32,8,128]{2,1,0:T(8,128)(2,1)S(1)} %pad_maximum_fusion.1), channel_id=1, source_target_pairs={{0,4},{1,7},{2,6},{3,5},{4,0},{5,3},{6,2},{7,1},{8,12},{9,15},{10,... | collective-permute-start | bytes 196616 | tf_op jit(solution)/shard_map/ppermute | solution.py:422
  7.8 1.7 %collective-permute-start.1 = (bf16[16,8,128]{2,1,0:T(8,128)(2,1)S(1)}, bf16[16,8,128]{2,1,0:T(8,128)(2,1)S(1)}, u32[]{:S(2)}, u32[]{:S(2)}) collective-permute-start(bf16[16,8,128]{2,1,0:T(8,128)(2,1)S(1)} %pack.1.own_ref.refs_2_.refs_5_), channel_id=1, source_target_pairs={{0,2},{1,3},{2,0},{3,1},{4,6},{5,7},{6,4},{7,5},{8,10},{9,11},{10,... | collective-permute-start | bytes 98312 | tf_op jit(solution)/shard_map/ppermute | solution.py:422
  9.5 1.6 %fetch.2.refs_15_ = bf16[8,1024,128]{2,1,0:T(8,128)(2,1)S(1)} custom-call(s32[1]{0:T(128)} %bitcast.index_ref.refs_0_, bf16[16384,128]{1,0:T(8,128)(2,1)} %bitcast.5), custom_call_target="tpu_custom_call" | custom-call | flops 1000000 | tf_op jit(solution)/shard_map/fetch/pallas_call | solution.py:448
  11.0 2.7 %base.1 = (f32[8,2048]{1,0:T(8,128)S(1)}, bf16[256,1024]{1,0:T(8,128)(2,1)S(1)}, bf16[256,1024]{1,0:T(8,128)(2,1)S(1)}, bf16[128,2048]{1,0:T(8,128)(2,1)S(1)}) custom-call(bf16[16,8,128]{2,1,0:T(8,128)(2,1)S(1)} %pack.1.own_ref.refs_2_.refs_5_, bf16[1024,2048]{1,0:T(8,128)(2,1)} %weight_ref.1, bf16[256,1024]{1,0:T(8,128)(2,1)} %bitcast.7, ...), custom_call_target="tpu_custom_call" | custom-call | flops 1000000 | tf_op jit(solution)/shard_map/base/pallas_call | solution.py:448
  13.8 0.1 collective-permute-start.5
  14.0 1.1 %collective-permute-done.5.refs_5_.refs_8_ = bf16[16,8,128]{2,1,0:T(8,128)(2,1)S(1)} collective-permute-done((bf16[16,8,128]{2,1,0:T(8,128)(2,1)S(1)}, bf16[16,8,128]{2,1,0:T(8,128)(2,1)S(1)}, u32[]{:S(2)}, u32[]{:S(2)}) %collective-permute-start.5) | collective-permute-done | bytes 32800 | tf_op jit(solution)/shard_map/ppermute | solution.py:422
  15.1 0.2 collective-permute-start.6
  15.2 1.6 %fetch.3.refs_16_ = bf16[8,1024,128]{2,1,0:T(8,128)(2,1)S(1)} custom-call(s32[1]{0:T(128)} %bitcast.index_ref.refs_0_, bf16[16384,128]{1,0:T(8,128)(2,1)} %bitcast.6), custom_call_target="tpu_custom_call" | custom-call | flops 1000000 | tf_op jit(solution)/shard_map/fetch/pallas_call | solution.py:448
  16.9 2.3 %send_states.1 = (bf16[528,128]{1,0:T(8,128)(2,1)S(1)}, f32[2,64,128]{2,1,0:T(8,128)S(1)}, bf16[192,128]{1,0:T(8,128)(2,1)S(1)}) custom-call(s32[1]{0:T(128)} %bitcast.index_ref.refs_0_, s32[2]{0:T(128)S(1)} %copy-done, s32[2]{0:T(128)S(1)} %copy-done.1, s32[16]{0:T(128)S(1)} %copy-done.2, s32[16]{0:T(128)S(1)} %copy-done.3, ...), custom_call_target="tpu_custom_call" | custom-call | flops 1000000 | tf_op jit(solution)/shard_map/send_states/pallas_call | solution.py:448
  19.2 0.4 %collective-permute-start.8 = (bf16[528,128]{1,0:T(8,128)(2,1)S(1)}, bf16[528,128]{1,0:T(8,128)(2,1)S(1)}, u32[]{:S(2)}, u32[]{:S(2)}) collective-permute-start(bf16[528,128]{1,0:T(8,128)(2,1)S(1)} %get-tuple-element.41), channel_id=1, source_target_pairs={{0,1},{1,0},{2,3},{3,2},{4,5},{5,4},{6,7},{7,6},{8,9},{9,8},{10,11... | collective-permute-start | bytes 405512 | tf_op jit(solution)/shard_map/ppermute | solution.py:422
  19.6 0.1 add_convert_fusion
  19.7 0.2 collective-permute-start.7
  19.8 0.1 convert_element_type.11
  19.9 1.6 %keep_states.1 = (f32[512,128]{1,0:T(8,128)S(1)}, f32[8,128]{1,0:T(8,128)S(1)}) custom-call(s32[1]{0:T(128)} %bitcast.index_ref.refs_0_, s32[2]{0:T(128)S(1)} %copy-done, bf16[16,8,128]{2,1,0:T(8,128)(2,1)S(1)} %pack.1.own_ref.refs_2_.refs_5_, bf16[16,8,128]{2,1,0:T(8,128)(2,1)S(1)} %collective-permute-done.refs_3_.refs_6_, ...), custom_call_target="tpu_custom_call" | custom-call | flops 1000000 | tf_op jit(solution)/shard_map/keep_states/pallas_call | solution.py:448
  21.5 0.3 %join.1 = (bf16[96,128]{1,0:T(8,128)(2,1)S(1)}, bf16[96,128]{1,0:T(8,128)(2,1)S(1)}, bf16[160,128]{1,0:T(8,128)(2,1)S(1)}, bf16[160,128]{1,0:T(8,128)(2,1)S(1)}, bf16[160,128]{1,0:T(8,128)(2,1)S(1)}) custom-call(s32[1]{0:T(128)} %bitcast.index_ref.refs_0_, f32[512,128]{1,0:T(8,128)S(1)} %get-tuple-element.33.mix_ref, ...), custom_call_target="tpu_custom_call" | custom-call | flops 1000000 | tf_op jit(solution)/shard_map/join/pallas_call | solution.py:448
  21.9 3.7 %collective-permute-start.10 = (bf16[160,128]{1,0:T(8,128)(2,1)S(1)}, bf16[160,128]{1,0:T(8,128)(2,1)S(1)}, u32[]{:S(2)}, u32[]{:S(2)}) collective-permute-start(bf16[160,128]{1,0:T(8,128)(2,1)S(1)} %get-tuple-element.44), channel_id=1, source_target_pairs={{0,12},{1,15},{2,14},{3,13},{4,8},{5,11},{6,10},{7,9},{8,4},{9,7},... | collective-permute-start | bytes 122888 | tf_op jit(solution)/shard_map/ppermute | solution.py:422
  25.5 0.8 %collective-permute-start.12 = (bf16[160,128]{1,0:T(8,128)(2,1)S(1)}, bf16[160,128]{1,0:T(8,128)(2,1)S(1)}, u32[]{:S(2)}, u32[]{:S(2)}) collective-permute-start(bf16[160,128]{1,0:T(8,128)(2,1)S(1)} %get-tuple-element.46), channel_id=1, source_target_pairs={{0,4},{1,7},{2,6},{3,5},{4,0},{5,3},{6,2},{7,1},{8,12},{9,15},{10,... | collective-permute-start | bytes 122888 | tf_op jit(solution)/shard_map/ppermute | solution.py:422
  26.3 0.1 fusion
  26.4 1.3 %collective-permute-start.9 = (bf16[96,128]{1,0:T(8,128)(2,1)S(1)}, bf16[96,128]{1,0:T(8,128)(2,1)S(1)}, u32[]{:S(2)}, u32[]{:S(2)}) collective-permute-start(bf16[96,128]{1,0:T(8,128)(2,1)S(1)} %get-tuple-element.43), channel_id=1, source_target_pairs={{0,2},{1,3},{2,0},{3,1},{4,6},{5,7},{6,4},{7,5},{8,10},{9,11},{10,... | collective-permute-start | bytes 73736 | tf_op jit(solution)/shard_map/ppermute | solution.py:422
  27.7 0.3 collective-permute-done.10.refs_2_
  28.0 0.1 collective-permute-start.13
  28.1 2.8 %collective-permute-done.11.refs_3_ = bf16[160,128]{1,0:T(8,128)(2,1)S(1)} collective-permute-done((bf16[160,128]{1,0:T(8,128)(2,1)S(1)}, bf16[160,128]{1,0:T(8,128)(2,1)S(1)}, u32[]{:S(2)}, u32[]{:S(2)}) %collective-permute-start.11) | collective-permute-done | bytes 40992 | tf_op jit(solution)/shard_map/ppermute | solution.py:422
  30.9 0.1 collective-permute-start.14
  31.0 0.4 %collective-permute-start.15 = (bf16[96,128]{1,0:T(8,128)(2,1)S(1)}, bf16[96,128]{1,0:T(8,128)(2,1)S(1)}, u32[]{:S(2)}, u32[]{:S(2)}) collective-permute-start(bf16[96,128]{1,0:T(8,128)(2,1)S(1)} %slice.14), channel_id=1, source_target_pairs={{0,1},{1,0},{2,3},{3,2},{4,5},{5,4},{6,7},{7,6},{8,9},{9,8},{10,11... | collective-permute-start | bytes 73736 | tf_op jit(solution)/shard_map/ppermute | solution.py:422
  31.4 0.1 pad_maximum_fusion.2
  31.5 0.6 %collective-permute-done.14.refs_6_ = bf16[96,128]{1,0:T(8,128)(2,1)S(1)} collective-permute-done((bf16[96,128]{1,0:T(8,128)(2,1)S(1)}, bf16[96,128]{1,0:T(8,128)(2,1)S(1)}, u32[]{:S(2)}, u32[]{:S(2)}) %collective-permute-start.14) | collective-permute-done | bytes 24608 | tf_op jit(solution)/shard_map/ppermute | solution.py:422
  32.1 0.2 collective-permute-done.15.refs_7_
  32.2 1.1 %merge_states.1 = bf16[2,4,1024]{2,1,0:T(4,128)(2,1)} custom-call(bf16[16,8,128]{2,1,0:T(8,128)(2,1)S(1)} %pack.1.own_ref.refs_2_.refs_5_, f32[8,128]{1,0:T(8,128)S(1)} %get-tuple-element.50.cos_ref, f32[8,128]{1,0:T(8,128)S(1)} %get-tuple-element.51.sin_ref, bf16[96,128]{1,0:T(8,128)(2,1)S(1)} %get-tuple-element.42.refs_0_, ...), custom_call_target="tpu_custom_call" | custom-call | tf_op jit(solution)/shard_map/merge_states/pallas_call | solution.py:559
  (26 shorter events, 0.1 us)
Async XLA Ops:
  0.8 1.4 %collective-permute-start = (bf16[16,8,128]{2,1,0:T(8,128)(2,1)S(1)}, bf16[16,8,128]{2,1,0:T(8,128)(2,1)S(1)}, u32[]{:S(2)}, u32[]{:S(2)}) collective-permute-start(bf16[16,8,128]{2,1,0:T(8,128)(2,1)S(1)} %pack.1.own_ref.refs_2_.refs_5_), channel_id=1, source_target_pairs={{0,1},{1,0},{2,3},{3,2},{4,5},{5,4},{6,7},{7,6},{8,9},{9,8},{10,11... | collective-permute-start | bytes 98312 | tf_op jit(solution)/shard_map/ppermute | solution.py:422
  2.2 11.8 %collective-permute-start.2 = (bf16[32,8,128]{2,1,0:T(8,128)(2,1)S(1)}, bf16[32,8,128]{2,1,0:T(8,128)(2,1)S(1)}, u32[]{:S(2)}, u32[]{:S(2)}) collective-permute-start(bf16[32,8,128]{2,1,0:T(8,128)(2,1)S(1)} %pad_maximum_fusion.1), channel_id=1, source_target_pairs={{0,12},{1,15},{2,14},{3,13},{4,8},{5,11},{6,10},{7,9},{8,4},{9,7},... | collective-permute-start | bytes 196616 | tf_op jit(solution)/shard_map/ppermute | solution.py:422
  7.2 6.8 %collective-permute-start.3 = (bf16[32,8,128]{2,1,0:T(8,128)(2,1)S(1)}, bf16[32,8,128]{2,1,0:T(8,128)(2,1)S(1)}, u32[]{:S(2)}, u32[]{:S(2)}) collective-permute-start(bf16[32,8,128]{2,1,0:T(8,128)(2,1)S(1)} %pad_maximum_fusion.1), channel_id=1, source_target_pairs={{0,8},{1,11},{2,10},{3,9},{4,12},{5,15},{6,14},{7,13},{8,0},{9,3},... | collective-permute-start | bytes 196616 | tf_op jit(solution)/shard_map/ppermute | solution.py:422
  7.2 6.8 %collective-permute-start.4 = (bf16[32,8,128]{2,1,0:T(8,128)(2,1)S(1)}, bf16[32,8,128]{2,1,0:T(8,128)(2,1)S(1)}, u32[]{:S(2)}, u32[]{:S(2)}) collective-permute-start(bf16[32,8,128]{2,1,0:T(8,128)(2,1)S(1)} %pad_maximum_fusion.1), channel_id=1, source_target_pairs={{0,4},{1,7},{2,6},{3,5},{4,0},{5,3},{6,2},{7,1},{8,12},{9,15},{10,... | collective-permute-start | bytes 196616 | tf_op jit(solution)/shard_map/ppermute | solution.py:422
  7.8 6.0 %collective-permute-start.1 = (bf16[16,8,128]{2,1,0:T(8,128)(2,1)S(1)}, bf16[16,8,128]{2,1,0:T(8,128)(2,1)S(1)}, u32[]{:S(2)}, u32[]{:S(2)}) collective-permute-start(bf16[16,8,128]{2,1,0:T(8,128)(2,1)S(1)} %pack.1.own_ref.refs_2_.refs_5_), channel_id=1, source_target_pairs={{0,2},{1,3},{2,0},{3,1},{4,6},{5,7},{6,4},{7,5},{8,10},{9,11},{10,... | collective-permute-start | bytes 98312 | tf_op jit(solution)/shard_map/ppermute | solution.py:422
  13.7 3.1 %copy-start = (s32[2]{0:T(128)S(1)}, s32[2]{0:T(128)}, u32[]{:S(2)}) copy-start(s32[2]{0:T(128)} %refs_1_.3) | copy-start | bytes 28
  13.8 3.1 %copy-start.1 = (s32[2]{0:T(128)S(1)}, s32[2]{0:T(128)}, u32[]{:S(2)}) copy-start(s32[2]{0:T(128)} %refs_2_.1) | copy-start | bytes 28
  13.8 3.1 %copy-start.2 = (s32[16]{0:T(128)S(1)}, s32[16]{0:T(128)}, u32[]{:S(2)}) copy-start(s32[16]{0:T(128)} %refs_3_.1) | copy-start | bytes 196
  13.8 3.1 %copy-start.3 = (s32[16]{0:T(128)S(1)}, s32[16]{0:T(128)}, u32[]{:S(2)}) copy-start(s32[16]{0:T(128)} %refs_4_.1) | copy-start | bytes 196
  13.8 1.3 %collective-permute-start.5 = (bf16[16,8,128]{2,1,0:T(8,128)(2,1)S(1)}, bf16[16,8,128]{2,1,0:T(8,128)(2,1)S(1)}, u32[]{:S(2)}, u32[]{:S(2)}) collective-permute-start(bf16[16,8,128]{2,1,0:T(8,128)(2,1)S(1)} %collective-permute-done.1.refs_4_.refs_7_), channel_id=1, source_target_pairs={{0,1},{1,0},{2,3},{3,2},{4,5},{5,4},{6,7},{7,6},{8,9},{9,8},{10,11... | collective-permute-start | bytes 98312 | tf_op jit(solution)/shard_map/ppermute | solution.py:422
  15.1 1.7 %collective-permute-start.6 = (bf16[96,8,128]{2,1,0:T(8,128)(2,1)S(1)}, bf16[96,8,128]{2,1,0:T(8,128)(2,1)S(1)}, u32[]{:S(2)}, u32[]{:S(2)}) collective-permute-start(bf16[96,8,128]{2,1,0:T(8,128)(2,1)S(1)} %pad_maximum_fusion.refs_6_.refs_9_), channel_id=1, source_target_pairs={{0,1},{1,0},{2,3},{3,2},{4,5},{5,4},{6,7},{7,6},{8,9},{9,8},{10,11... | collective-permute-start | bytes 589832 | tf_op jit(solution)/shard_map/ppermute | solution.py:422
  19.2 2.3 %collective-permute-start.8 = (bf16[528,128]{1,0:T(8,128)(2,1)S(1)}, bf16[528,128]{1,0:T(8,128)(2,1)S(1)}, u32[]{:S(2)}, u32[]{:S(2)}) collective-permute-start(bf16[528,128]{1,0:T(8,128)(2,1)S(1)} %get-tuple-element.41), channel_id=1, source_target_pairs={{0,1},{1,0},{2,3},{3,2},{4,5},{5,4},{6,7},{7,6},{8,9},{9,8},{10,11... | collective-permute-start | bytes 405512 | tf_op jit(solution)/shard_map/ppermute | solution.py:422
  19.7 1.8 %collective-permute-start.7 = (bf16[192,128]{1,0:T(8,128)(2,1)S(1)}, bf16[192,128]{1,0:T(8,128)(2,1)S(1)}, u32[]{:S(2)}, u32[]{:S(2)}) collective-permute-start(bf16[192,128]{1,0:T(8,128)(2,1)S(1)} %get-tuple-element.40), channel_id=1, source_target_pairs={{0,1},{1,0},{2,3},{3,2},{4,5},{5,4},{6,7},{7,6},{8,9},{9,8},{10,11... | collective-permute-start | bytes 147464 | tf_op jit(solution)/shard_map/ppermute | solution.py:422
  21.9 6.2 %collective-permute-start.10 = (bf16[160,128]{1,0:T(8,128)(2,1)S(1)}, bf16[160,128]{1,0:T(8,128)(2,1)S(1)}, u32[]{:S(2)}, u32[]{:S(2)}) collective-permute-start(bf16[160,128]{1,0:T(8,128)(2,1)S(1)} %get-tuple-element.44), channel_id=1, source_target_pairs={{0,12},{1,15},{2,14},{3,13},{4,8},{5,11},{6,10},{7,9},{8,4},{9,7},... | collective-permute-start | bytes 122888 | tf_op jit(solution)/shard_map/ppermute | solution.py:422
  25.5 5.3 %collective-permute-start.11 = (bf16[160,128]{1,0:T(8,128)(2,1)S(1)}, bf16[160,128]{1,0:T(8,128)(2,1)S(1)}, u32[]{:S(2)}, u32[]{:S(2)}) collective-permute-start(bf16[160,128]{1,0:T(8,128)(2,1)S(1)} %get-tuple-element.45), channel_id=1, source_target_pairs={{0,8},{1,11},{2,10},{3,9},{4,12},{5,15},{6,14},{7,13},{8,0},{9,3},... | collective-permute-start | bytes 122888 | tf_op jit(solution)/shard_map/ppermute | solution.py:422
  25.5 5.5 %collective-permute-start.12 = (bf16[160,128]{1,0:T(8,128)(2,1)S(1)}, bf16[160,128]{1,0:T(8,128)(2,1)S(1)}, u32[]{:S(2)}, u32[]{:S(2)}) collective-permute-start(bf16[160,128]{1,0:T(8,128)(2,1)S(1)} %get-tuple-element.46), channel_id=1, source_target_pairs={{0,4},{1,7},{2,6},{3,5},{4,0},{5,3},{6,2},{7,1},{8,12},{9,15},{10,... | collective-permute-start | bytes 122888 | tf_op jit(solution)/shard_map/ppermute | solution.py:422
  26.4 5.0 %collective-permute-start.9 = (bf16[96,128]{1,0:T(8,128)(2,1)S(1)}, bf16[96,128]{1,0:T(8,128)(2,1)S(1)}, u32[]{:S(2)}, u32[]{:S(2)}) collective-permute-start(bf16[96,128]{1,0:T(8,128)(2,1)S(1)} %get-tuple-element.43), channel_id=1, source_target_pairs={{0,2},{1,3},{2,0},{3,1},{4,6},{5,7},{6,4},{7,5},{8,10},{9,11},{10,... | collective-permute-start | bytes 73736 | tf_op jit(solution)/shard_map/ppermute | solution.py:422
  28.0 3.4 %collective-permute-start.13 = (bf16[96,128]{1,0:T(8,128)(2,1)S(1)}, bf16[96,128]{1,0:T(8,128)(2,1)S(1)}, u32[]{:S(2)}, u32[]{:S(2)}) collective-permute-start(bf16[96,128]{1,0:T(8,128)(2,1)S(1)} %slice.12), channel_id=1, source_target_pairs={{0,1},{1,0},{2,3},{3,2},{4,5},{5,4},{6,7},{7,6},{8,9},{9,8},{10,11... | collective-permute-start | bytes 73736 | tf_op jit(solution)/shard_map/ppermute | solution.py:422
  30.9 1.2 %collective-permute-start.14 = (bf16[96,128]{1,0:T(8,128)(2,1)S(1)}, bf16[96,128]{1,0:T(8,128)(2,1)S(1)}, u32[]{:S(2)}, u32[]{:S(2)}) collective-permute-start(bf16[96,128]{1,0:T(8,128)(2,1)S(1)} %slice.13), channel_id=1, source_target_pairs={{0,1},{1,0},{2,3},{3,2},{4,5},{5,4},{6,7},{7,6},{8,9},{9,8},{10,11... | collective-permute-start | bytes 73736 | tf_op jit(solution)/shard_map/ppermute | solution.py:422
  31.0 1.2 %collective-permute-start.15 = (bf16[96,128]{1,0:T(8,128)(2,1)S(1)}, bf16[96,128]{1,0:T(8,128)(2,1)S(1)}, u32[]{:S(2)}, u32[]{:S(2)}) collective-permute-start(bf16[96,128]{1,0:T(8,128)(2,1)S(1)} %slice.14), channel_id=1, source_target_pairs={{0,1},{1,0},{2,3},{3,2},{4,5},{5,4},{6,7},{7,6},{8,9},{9,8},{10,11... | collective-permute-start | bytes 73736 | tf_op jit(solution)/shard_map/ppermute | solution.py:422

commit v12 on v11

--- a/solution.py
+++ b/solution.py
@@ -35,6 +35,7 @@
         self.heads, self.chunks = QUERY_HEADS // devices, width // HEAD_WIDTH
         self.single = 1
         self.pairs = [(m, m + 1) for m in range(lanes - 2, 0, -2)]
+        self.pairs[:2] = self.pairs[1::-1]
         size = self.heads + self.chunks
         self.own = ((0, 0), ((0, 0), (1, 0)))
         self.one = ((self.single,) * 2, ((2, 0), (3, 0)))
@@ -92,24 +93,25 @@
     ]
 
 
-def streams(sources, index_ref, down_ref, half_ref, sems):
-    depth = half_ref.shape[1]
+def streams(sources, index_ref, down_ref, rows_ref, sems):
+    depth = rows_ref.shape[1]
     here = index_ref[0]
     copies = []
     for at, (_, _, masks, side) in enumerate(sources):
         source = here ^ (2 * here_mask(masks, here) + side)
         rows = pl.ds(pl.multiple_of(source * depth, depth), depth)
-        copies.append(pltpu.make_async_copy(down_ref.at[rows], half_ref.at[at], sems.at[at]))
+        copies.append(pltpu.make_async_copy(down_ref.at[rows], rows_ref.at[at], sems.at[at]))
     return copies
 
 
-def lower(sources, arrays, halves):
+def lower(sources, arrays, factors):
     total = None
-    count, depth = halves[0].shape[:2]
+    count, depth = factors[0].shape[:2]
     for at, (array, first, _, _) in enumerate(sources):
         tiles = range(first, first + depth // HEAD_WIDTH)
         hidden = jnp.concatenate([arrays[array][c] for c in tiles], axis=1)
-        term = dot(hidden, halves[at // count][at % count], ((1,), (0,)))
+        factor = factors[0][at] if at < count else factors[1][at - count]
+        term = dot(hidden, factor, ((1,), (0,)))
         total = term if total is None else total + term
     return total
 
@@ -131,18 +133,26 @@
             at += 1
 
 
-def base_kernel(heads, own_ref, weight_ref, *refs):
-    sources, base_ref, held = refs[:3], refs[3], refs[4:7]
-    buffer, sems = refs[7:]
+def load_kernel(*refs):
+    count = len(refs) // 2
+    sems = refs[-1]
+    copies = [
+        pltpu.make_async_copy(refs[i], refs[count + i], sems.at[i]) for i in range(count)
+    ]
+    for copy in copies:
+        copy.start()
+    for copy in copies:
+        copy.wait()
+
+
+def base_kernel(heads, sources, index_ref, own_ref, weight_ref, down_ref, base_ref, rows_ref, *scratch):
+    buffer, sems, row_sems = scratch
     parts, depth = buffer.shape[:2]
     loads = [
         pltpu.make_async_copy(weight_ref.at[pl.ds(p * depth, depth)], buffer.at[p], sems.at[p])
         for p in range(parts)
     ]
-    others = [
-        pltpu.make_async_copy(source, place, sems.at[parts + i])
-        for i, (source, place) in enumerate(zip(sources, held))
-    ]
+    others = streams(sources, index_ref, down_ref, rows_ref, row_sems)
     for load in loads + others:
         load.start()
     tiles = depth // HEAD_WIDTH
@@ -156,8 +166,8 @@
         load.wait()
 
 
-def fetch_kernel(sources, index_ref, down_ref, half_ref, sems):
-    copies = streams(sources, index_ref, down_ref, half_ref, sems)
+def fetch_kernel(sources, index_ref, down_ref, rows_ref, sems):
+    copies = streams(sources, index_ref, down_ref, rows_ref, sems)
     for copy in copies:
         copy.start()
     for copy in copies:
@@ -218,7 +228,7 @@
 
 def send_kernel(sizes, plan, *refs):
     (index_ref, length_ref, adapter_ref, rank_ref, pool_ref, *arrays) = refs[:-9]
-    (key_ref, value_ref, base_ref, up_ref, *halves, send_ref, own_ref, parts_ref) = refs[-9:]
+    (key_ref, value_ref, base_ref, up_ref, *factors, send_ref, own_ref, parts_ref) = refs[-9:]
     requests, tokens, devices = sizes
 
     def put(chunk, row, mix):
@@ -233,7 +243,7 @@
     send_ref[MIX_ROWS:] = rows_of(peaks + highs + lows, STAT_ROWS).astype(jnp.bfloat16)
 
     rows = requests * tokens
-    lowered = lower(sources_of(plan), arrays, halves)
+    lowered = lower(sources_of(plan), arrays, factors)
     row_request = lax.broadcasted_iota(jnp.int32, (rows, 1), 0) // tokens
     ranks = jnp.zeros((rows, 1), jnp.int32)
     owners = jnp.zeros((rows, 1), jnp.int32)
@@ -471,56 +481,64 @@
         ],
         "pack",
     )
-    other = core_swap(own)
-    one = trade(own, devices, plan.single, plan.single)
-    both = jnp.concatenate([own, other], axis=0)
-    mine = [trade(both, devices, a, b) for a, b in plan.pairs]
-
     flat = requests * cached_key_rows.shape[1]
     big = (
         cached_key_rows.reshape(flat, -1),
         cached_value_rows.reshape(flat, -1),
         adapter_up_weight[0],
     )
+    keys, values, up = call(
+        load_kernel,
+        tuple(pinned(x) for x in big),
+        [hbm()] * 3,
+        [pltpu.VMEM(x.shape, x.dtype) for x in big],
+        [pltpu.SemaphoreType.DMA((3,))],
+        "load",
+    )
+    other, keys = lax.optimization_barrier((core_swap(own), keys))
+    one = trade(own, devices, plan.single, plan.single)
+    both = jnp.concatenate([own, other], axis=0)
+    mine = [trade(both, devices, a, b) for a, b in plan.pairs]
+
     out_width = key_value_weight.shape[1]
     parts = 4 if width % (4 * HEAD_WIDTH) == 0 else 1
-    base, keys, values, up = call(
-        functools.partial(base_kernel, heads),
-        (own, pinned(key_value_weight)) + tuple(pinned(x) for x in big),
-        [vmem()] + [hbm()] * 4,
-        [pltpu.VMEM((rows, out_width), jnp.float32)] + [pltpu.VMEM(x.shape, x.dtype) for x in big],
+    down = pinned(adapter_down_weight[0])
+    rank = down.shape[1]
+    sources = sources_of(plan)
+    count = 5 * devices // 8
+    base, first = call(
+        functools.partial(base_kernel, heads, sources[:count]),
+        (index, own, pinned(key_value_weight), down),
+        [smem(), vmem()] + [hbm()] * 2,
+        [
+            pltpu.VMEM((rows, out_width), jnp.float32),
+            pltpu.VMEM((count, width, rank), jnp.bfloat16),
+        ],
         [
             pltpu.VMEM((parts, width // parts, out_width), jnp.bfloat16),
-            pltpu.SemaphoreType.DMA((parts + 3,)),
+            pltpu.SemaphoreType.DMA((parts,)),
+            pltpu.SemaphoreType.DMA((count,)),
         ],
         "base",
     )
-    down = adapter_down_weight[0]
-    count = devices // 2
-    first, second = [
-        call(
-            functools.partial(fetch_kernel, sources_of(plan)[at : at + count]),
-            (index, pinned(down)),
-            [smem(), hbm()],
-            [pltpu.VMEM((count, width, down.shape[1]), jnp.bfloat16)],
-            [pltpu.SemaphoreType.DMA((count,))],
-            "fetch",
-        )[0]
-        for at in (0, count)
-    ]
-    one, base, first = lax.optimization_barrier((one, base, first))
-    other_one = core_swap(one)
-    mine = jnp.concatenate(mine, axis=0)
-    mine, other_one = lax.optimization_barrier((mine, other_one))
-    other_mine, second = lax.optimization_barrier((core_swap(mine), second))
+    mine, one, base = lax.optimization_barrier((jnp.concatenate(mine, axis=0), one, base))
+    other_one, other_mine = core_swap(one), core_swap(mine)
+    (second,) = call(
+        functools.partial(fetch_kernel, sources[count:]),
+        (index, down),
+        [smem(), hbm()],
+        [pltpu.VMEM((devices - count, width, rank), jnp.bfloat16)],
+        [pltpu.SemaphoreType.DMA((devices - count,))],
+        "fetch",
+    )
+    other_mine, second = lax.optimization_barrier((other_mine, second))
     arrays = (own, other, one, other_one, mine, other_mine)
-    halves = (first, second)
     step = KEY_HEADS * rows
     send, proj, proj_parts = call(
         functools.partial(send_kernel, sizes, plan),
         (index, lengths, request_adapter, adapter_rank_list, adapter_pool_row)
         + arrays
-        + (keys, values, base, up, *halves),
+        + (keys, values, base, up, first, second),
         [smem()] * 5 + [vmem()] * (len(arrays) + 6),
         [
             pltpu.VMEM((MIX_ROWS + STAT_ROWS, HEAD_WIDTH), jnp.bfloat16),

time: 33.7 us -> 32.7 us (0.970)
  waiting for transfers between devices: 5.83 us -> 4.85 us
    ppermute x16, waiting for transfers between devices: 5.83 us -> 4.85 us  [trade(): return lax.ppermute(x, 'tensor', pairs)]
  transfers between devices with their start and end apart: 16 -> 16, of which waited for: 6 -> 6; matrix products, arithmetic and copies ran while one was open for 1% -> 1% of each run, Pallas kernels for 22% -> 24%
where the time goes in v12:
time: 32.7 us; the launch traced here: 32.3 us
  starting transfers between devices  14.7 us (45%)
  Pallas kernels  12.1 us (37%)
  waiting for transfers between devices  4.85 us (15%)
    ppermute x16, starting transfers between devices, trade(): return lax.ppermute(x, 'tensor', pairs)  14.7 us
    pallas_call x7, Pallas kernels, call(): pl.pallas_call(kernel, out_shape=tuple(out_shape), in_specs=in_specs, out...  11 us
    ppermute x16, waiting for transfers between devices, trade(): return lax.ppermute(x, 'tensor', pairs)  4.85 us
    pallas_call x1, Pallas kernels, per_device(): pl.pallas_call(functools.partial(merge_kernel, devices, requests, tokens,...  1.11 us
  transfers between devices with their start and end apart: 16, of which 6 were waited for; matrix products, arithmetic and copies ran while one was open for 1% of the time, Pallas kernels for 24%

profile of v12, /device:TPU:0, one launch (start us, length us, event | category | flops | bytes accessed | tf_op | source)
XLA Modules:
  0.0 32.3 jit_solution(14725194250822698267)
XLA Ops:
  0.0 0.8 %pack.1.own_ref.refs_2_.refs_5_ = bf16[16,8,128]{2,1,0:T(8,128)(2,1)S(1)} custom-call(bf16[2,4,1024]{2,1,0:T(4,128)(2,1)} %query_ref.1, bf16[2,4,1024]{2,1,0:T(4,128)(2,1)} %hidden_ref.1), custom_call_target="tpu_custom_call" | custom-call | flops 1000000 | tf_op jit(solution)/shard_map/pack/pallas_call | solution.py:458
  0.8 0.5 %collective-permute-start = (bf16[16,8,128]{2,1,0:T(8,128)(2,1)S(1)}, bf16[16,8,128]{2,1,0:T(8,128)(2,1)S(1)}, u32[]{:S(2)}, u32[]{:S(2)}) collective-permute-start(bf16[16,8,128]{2,1,0:T(8,128)(2,1)S(1)} %pack.1.own_ref.refs_2_.refs_5_), channel_id=1, source_target_pairs={{0,1},{1,0},{2,3},{3,2},{4,5},{5,4},{6,7},{7,6},{8,9},{9,8},{10,11... | collective-permute-start | bytes 98312 | tf_op jit(solution)/shard_map/ppermute | solution.py:432
  1.3 1.4 %load.1 = (bf16[256,1024]{1,0:T(8,128)(2,1)S(1)}, bf16[256,1024]{1,0:T(8,128)(2,1)S(1)}, bf16[128,2048]{1,0:T(8,128)(2,1)S(1)}) custom-call(bf16[256,1024]{1,0:T(8,128)(2,1)} %bitcast.7, bf16[256,1024]{1,0:T(8,128)(2,1)} %bitcast.8, bf16[128,2048]{1,0:T(8,128)(2,1)} %bitcast.9), custom_call_target="tpu_custom_call" | custom-call | flops 1000000 | tf_op jit(solution)/shard_map/load/pallas_call | solution.py:458
  2.7 3.7 %collective-permute-start.1 = (bf16[32,8,128]{2,1,0:T(8,128)(2,1)S(1)}, bf16[32,8,128]{2,1,0:T(8,128)(2,1)S(1)}, u32[]{:S(2)}, u32[]{:S(2)}) collective-permute-start(bf16[32,8,128]{2,1,0:T(8,128)(2,1)S(1)} %pad_maximum_fusion.1), channel_id=1, source_target_pairs={{0,8},{1,11},{2,10},{3,9},{4,12},{5,15},{6,14},{7,13},{8,0},{9,3},... | collective-permute-start | bytes 196616 | tf_op jit(solution)/shard_map/ppermute | solution.py:432
  6.4 1.3 %collective-permute-start.2 = (bf16[32,8,128]{2,1,0:T(8,128)(2,1)S(1)}, bf16[32,8,128]{2,1,0:T(8,128)(2,1)S(1)}, u32[]{:S(2)}, u32[]{:S(2)}) collective-permute-start(bf16[32,8,128]{2,1,0:T(8,128)(2,1)S(1)} %pad_maximum_fusion.1), channel_id=1, source_target_pairs={{0,12},{1,15},{2,14},{3,13},{4,8},{5,11},{6,10},{7,9},{8,4},{9,7},... | collective-permute-start | bytes 196616 | tf_op jit(solution)/shard_map/ppermute | solution.py:432
  7.7 0.2 collective-permute-start.3
  7.9 1.5 %collective-permute-start.4 = (bf16[16,8,128]{2,1,0:T(8,128)(2,1)S(1)}, bf16[16,8,128]{2,1,0:T(8,128)(2,1)S(1)}, u32[]{:S(2)}, u32[]{:S(2)}) collective-permute-start(bf16[16,8,128]{2,1,0:T(8,128)(2,1)S(1)} %pack.1.own_ref.refs_2_.refs_5_), channel_id=1, source_target_pairs={{0,2},{1,3},{2,0},{3,1},{4,6},{5,7},{6,4},{7,5},{8,10},{9,11},{10,... | collective-permute-start | bytes 98312 | tf_op jit(solution)/shard_map/ppermute | solution.py:432
  9.5 3.3 %base.1 = (f32[8,2048]{1,0:T(8,128)S(1)}, bf16[10,1024,128]{2,1,0:T(8,128)(2,1)S(1)}) custom-call(s32[1]{0:T(128)} %bitcast.index_ref.refs_0_, bf16[16,8,128]{2,1,0:T(8,128)(2,1)S(1)} %pack.1.own_ref.refs_2_.refs_5_, bf16[1024,2048]{1,0:T(8,128)(2,1)} %weight_ref.1, bf16[16384,128]{1,0:T(8,128)(2,1)} %bitcast.5), custom_call_target="tpu_custom_call" | custom-call | flops 1000000 | tf_op jit(solution)/shard_map/base/pallas_call | solution.py:458
  12.8 0.3 collective-permute-done.2
  13.1 0.4 %collective-permute-done.3 = bf16[32,8,128]{2,1,0:T(8,128)(2,1)S(1)} collective-permute-done((bf16[32,8,128]{2,1,0:T(8,128)(2,1)S(1)}, bf16[32,8,128]{2,1,0:T(8,128)(2,1)S(1)}, u32[]{:S(2)}, u32[]{:S(2)}) %collective-permute-start.3) | collective-permute-done | bytes 65568 | tf_op jit(solution)/shard_map/ppermute | solution.py:432
  13.6 1.2 %collective-permute-start.6 = (bf16[96,8,128]{2,1,0:T(8,128)(2,1)S(1)}, bf16[96,8,128]{2,1,0:T(8,128)(2,1)S(1)}, u32[]{:S(2)}, u32[]{:S(2)}) collective-permute-start(bf16[96,8,128]{2,1,0:T(8,128)(2,1)S(1)} %pad_maximum_fusion.refs_6_.refs_9_), channel_id=1, source_target_pairs={{0,1},{1,0},{2,3},{3,2},{4,5},{5,4},{6,7},{7,6},{8,9},{9,8},{10,11... | collective-permute-start | bytes 589832 | tf_op jit(solution)/shard_map/ppermute | solution.py:432
  14.7 0.1 collective-permute-start.5
  14.8 1.4 %fetch.1.refs_16_ = bf16[6,1024,128]{2,1,0:T(8,128)(2,1)S(1)} custom-call(s32[1]{0:T(128)} %bitcast.index_ref.refs_0_, bf16[16384,128]{1,0:T(8,128)(2,1)} %bitcast.6), custom_call_target="tpu_custom_call" | custom-call | flops 1000000 | tf_op jit(solution)/shard_map/fetch/pallas_call | solution.py:458
  16.3 2.3 %send_states.1 = (bf16[528,128]{1,0:T(8,128)(2,1)S(1)}, f32[2,64,128]{2,1,0:T(8,128)S(1)}, bf16[192,128]{1,0:T(8,128)(2,1)S(1)}) custom-call(s32[1]{0:T(128)} %bitcast.index_ref.refs_0_, s32[2]{0:T(128)S(1)} %copy-done, s32[2]{0:T(128)S(1)} %copy-done.1, s32[16]{0:T(128)S(1)} %copy-done.2, s32[16]{0:T(128)S(1)} %copy-done.3, ...), custom_call_target="tpu_custom_call" | custom-call | flops 1000000 | tf_op jit(solution)/shard_map/send_states/pallas_call | solution.py:458
  18.6 0.5 %collective-permute-start.8 = (bf16[528,128]{1,0:T(8,128)(2,1)S(1)}, bf16[528,128]{1,0:T(8,128)(2,1)S(1)}, u32[]{:S(2)}, u32[]{:S(2)}) collective-permute-start(bf16[528,128]{1,0:T(8,128)(2,1)S(1)} %get-tuple-element.43), channel_id=1, source_target_pairs={{0,1},{1,0},{2,3},{3,2},{4,5},{5,4},{6,7},{7,6},{8,9},{9,8},{10,11... | collective-permute-start | bytes 405512 | tf_op jit(solution)/shard_map/ppermute | solution.py:432
  19.2 0.1 collective-permute-start.7
  19.2 0.1 convert_element_type.11
  19.3 1.6 %keep_states.1 = (f32[512,128]{1,0:T(8,128)S(1)}, f32[8,128]{1,0:T(8,128)S(1)}) custom-call(s32[1]{0:T(128)} %bitcast.index_ref.refs_0_, s32[2]{0:T(128)S(1)} %copy-done, bf16[16,8,128]{2,1,0:T(8,128)(2,1)S(1)} %pack.1.own_ref.refs_2_.refs_5_, bf16[16,8,128]{2,1,0:T(8,128)(2,1)S(1)} %collective-permute-done.refs_3_.refs_6_, ...), custom_call_target="tpu_custom_call" | custom-call | flops 1000000 | tf_op jit(solution)/shard_map/keep_states/pallas_call | solution.py:458
  20.9 0.3 %join.1 = (bf16[96,128]{1,0:T(8,128)(2,1)S(1)}, bf16[96,128]{1,0:T(8,128)(2,1)S(1)}, bf16[160,128]{1,0:T(8,128)(2,1)S(1)}, bf16[160,128]{1,0:T(8,128)(2,1)S(1)}, bf16[160,128]{1,0:T(8,128)(2,1)S(1)}) custom-call(s32[1]{0:T(128)} %bitcast.index_ref.refs_0_, f32[512,128]{1,0:T(8,128)S(1)} %get-tuple-element.35.mix_ref, ...), custom_call_target="tpu_custom_call" | custom-call | flops 1000000 | tf_op jit(solution)/shard_map/join/pallas_call | solution.py:458
  21.3 2.3 %collective-permute-start.10 = (bf16[160,128]{1,0:T(8,128)(2,1)S(1)}, bf16[160,128]{1,0:T(8,128)(2,1)S(1)}, u32[]{:S(2)}, u32[]{:S(2)}) collective-permute-start(bf16[160,128]{1,0:T(8,128)(2,1)S(1)} %get-tuple-element.46), channel_id=1, source_target_pairs={{0,8},{1,11},{2,10},{3,9},{4,12},{5,15},{6,14},{7,13},{8,0},{9,3},... | collective-permute-start | bytes 122888 | tf_op jit(solution)/shard_map/ppermute | solution.py:432
  23.6 0.9 %collective-permute-start.11 = (bf16[160,128]{1,0:T(8,128)(2,1)S(1)}, bf16[160,128]{1,0:T(8,128)(2,1)S(1)}, u32[]{:S(2)}, u32[]{:S(2)}) collective-permute-start(bf16[160,128]{1,0:T(8,128)(2,1)S(1)} %get-tuple-element.47), channel_id=1, source_target_pairs={{0,12},{1,15},{2,14},{3,13},{4,8},{5,11},{6,10},{7,9},{8,4},{9,7},... | collective-permute-start | bytes 122888 | tf_op jit(solution)/shard_map/ppermute | solution.py:432
  24.5 0.5 %collective-permute-start.12 = (bf16[160,128]{1,0:T(8,128)(2,1)S(1)}, bf16[160,128]{1,0:T(8,128)(2,1)S(1)}, u32[]{:S(2)}, u32[]{:S(2)}) collective-permute-start(bf16[160,128]{1,0:T(8,128)(2,1)S(1)} %get-tuple-element.48), channel_id=1, source_target_pairs={{0,4},{1,7},{2,6},{3,5},{4,0},{5,3},{6,2},{7,1},{8,12},{9,15},{10,... | collective-permute-start | bytes 122888 | tf_op jit(solution)/shard_map/ppermute | solution.py:432
  25.0 0.1 fusion
  25.1 1.2 %collective-permute-start.9 = (bf16[96,128]{1,0:T(8,128)(2,1)S(1)}, bf16[96,128]{1,0:T(8,128)(2,1)S(1)}, u32[]{:S(2)}, u32[]{:S(2)}) collective-permute-start(bf16[96,128]{1,0:T(8,128)(2,1)S(1)} %get-tuple-element.45), channel_id=1, source_target_pairs={{0,2},{1,3},{2,0},{3,1},{4,6},{5,7},{6,4},{7,5},{8,10},{9,11},{10,... | collective-permute-start | bytes 73736 | tf_op jit(solution)/shard_map/ppermute | solution.py:432
  26.3 1.1 %collective-permute-done.10.refs_2_ = bf16[160,128]{1,0:T(8,128)(2,1)S(1)} collective-permute-done((bf16[160,128]{1,0:T(8,128)(2,1)S(1)}, bf16[160,128]{1,0:T(8,128)(2,1)S(1)}, u32[]{:S(2)}, u32[]{:S(2)}) %collective-permute-start.10) | collective-permute-done | bytes 40992 | tf_op jit(solution)/shard_map/ppermute | solution.py:432
  27.4 0.2 collective-permute-start.13
  27.6 2.2 %collective-permute-done.11.refs_3_ = bf16[160,128]{1,0:T(8,128)(2,1)S(1)} collective-permute-done((bf16[160,128]{1,0:T(8,128)(2,1)S(1)}, bf16[160,128]{1,0:T(8,128)(2,1)S(1)}, u32[]{:S(2)}, u32[]{:S(2)}) %collective-permute-start.11) | collective-permute-done | bytes 40992 | tf_op jit(solution)/shard_map/ppermute | solution.py:432
  29.8 0.2 collective-permute-start.14
  30.0 0.3 collective-permute-start.15
  30.4 0.6 %collective-permute-done.14.refs_6_ = bf16[96,128]{1,0:T(8,128)(2,1)S(1)} collective-permute-done((bf16[96,128]{1,0:T(8,128)(2,1)S(1)}, bf16[96,128]{1,0:T(8,128)(2,1)S(1)}, u32[]{:S(2)}, u32[]{:S(2)}) %collective-permute-start.14) | collective-permute-done | bytes 24608 | tf_op jit(solution)/shard_map/ppermute | solution.py:432
  31.0 0.2 collective-permute-done.15.refs_7_
  31.2 1.1 %merge_states.1 = bf16[2,4,1024]{2,1,0:T(4,128)(2,1)} custom-call(bf16[16,8,128]{2,1,0:T(8,128)(2,1)S(1)} %pack.1.own_ref.refs_2_.refs_5_, f32[8,128]{1,0:T(8,128)S(1)} %get-tuple-element.52.cos_ref, f32[8,128]{1,0:T(8,128)S(1)} %get-tuple-element.53.sin_ref, bf16[96,128]{1,0:T(8,128)(2,1)S(1)} %get-tuple-element.44.refs_0_, ...), custom_call_target="tpu_custom_call" | custom-call | tf_op jit(solution)/shard_map/merge_states/pallas_call | solution.py:577
  (26 shorter events, 0.2 us)
Async XLA Ops:
  0.8 1.9 %collective-permute-start = (bf16[16,8,128]{2,1,0:T(8,128)(2,1)S(1)}, bf16[16,8,128]{2,1,0:T(8,128)(2,1)S(1)}, u32[]{:S(2)}, u32[]{:S(2)}) collective-permute-start(bf16[16,8,128]{2,1,0:T(8,128)(2,1)S(1)} %pack.1.own_ref.refs_2_.refs_5_), channel_id=1, source_target_pairs={{0,1},{1,0},{2,3},{3,2},{4,5},{5,4},{6,7},{7,6},{8,9},{9,8},{10,11... | collective-permute-start | bytes 98312 | tf_op jit(solution)/shard_map/ppermute | solution.py:432
  2.7 10.1 %collective-permute-start.1 = (bf16[32,8,128]{2,1,0:T(8,128)(2,1)S(1)}, bf16[32,8,128]{2,1,0:T(8,128)(2,1)S(1)}, u32[]{:S(2)}, u32[]{:S(2)}) collective-permute-start(bf16[32,8,128]{2,1,0:T(8,128)(2,1)S(1)} %pad_maximum_fusion.1), channel_id=1, source_target_pairs={{0,8},{1,11},{2,10},{3,9},{4,12},{5,15},{6,14},{7,13},{8,0},{9,3},... | collective-permute-start | bytes 196616 | tf_op jit(solution)/shard_map/ppermute | solution.py:432
  6.4 6.8 %collective-permute-start.2 = (bf16[32,8,128]{2,1,0:T(8,128)(2,1)S(1)}, bf16[32,8,128]{2,1,0:T(8,128)(2,1)S(1)}, u32[]{:S(2)}, u32[]{:S(2)}) collective-permute-start(bf16[32,8,128]{2,1,0:T(8,128)(2,1)S(1)} %pad_maximum_fusion.1), channel_id=1, source_target_pairs={{0,12},{1,15},{2,14},{3,13},{4,8},{5,11},{6,10},{7,9},{8,4},{9,7},... | collective-permute-start | bytes 196616 | tf_op jit(solution)/shard_map/ppermute | solution.py:432
  7.7 5.8 %collective-permute-start.3 = (bf16[32,8,128]{2,1,0:T(8,128)(2,1)S(1)}, bf16[32,8,128]{2,1,0:T(8,128)(2,1)S(1)}, u32[]{:S(2)}, u32[]{:S(2)}) collective-permute-start(bf16[32,8,128]{2,1,0:T(8,128)(2,1)S(1)} %pad_maximum_fusion.1), channel_id=1, source_target_pairs={{0,4},{1,7},{2,6},{3,5},{4,0},{5,3},{6,2},{7,1},{8,12},{9,15},{10,... | collective-permute-start | bytes 196616 | tf_op jit(solution)/shard_map/ppermute | solution.py:432
  7.9 5.6 %collective-permute-start.4 = (bf16[16,8,128]{2,1,0:T(8,128)(2,1)S(1)}, bf16[16,8,128]{2,1,0:T(8,128)(2,1)S(1)}, u32[]{:S(2)}, u32[]{:S(2)}) collective-permute-start(bf16[16,8,128]{2,1,0:T(8,128)(2,1)S(1)} %pack.1.own_ref.refs_2_.refs_5_), channel_id=1, source_target_pairs={{0,2},{1,3},{2,0},{3,1},{4,6},{5,7},{6,4},{7,5},{8,10},{9,11},{10,... | collective-permute-start | bytes 98312 | tf_op jit(solution)/shard_map/ppermute | solution.py:432
  12.8 3.5 %copy-start = (s32[2]{0:T(128)S(1)}, s32[2]{0:T(128)}, u32[]{:S(2)}) copy-start(s32[2]{0:T(128)} %refs_1_.3) | copy-start | bytes 28
  12.8 3.5 %copy-start.1 = (s32[2]{0:T(128)S(1)}, s32[2]{0:T(128)}, u32[]{:S(2)}) copy-start(s32[2]{0:T(128)} %refs_2_.1) | copy-start | bytes 28
  12.8 3.5 %copy-start.2 = (s32[16]{0:T(128)S(1)}, s32[16]{0:T(128)}, u32[]{:S(2)}) copy-start(s32[16]{0:T(128)} %refs_3_.1) | copy-start | bytes 196
  12.8 3.5 %copy-start.3 = (s32[16]{0:T(128)S(1)}, s32[16]{0:T(128)}, u32[]{:S(2)}) copy-start(s32[16]{0:T(128)} %refs_4_.1) | copy-start | bytes 196
  13.6 2.6 %collective-permute-start.6 = (bf16[96,8,128]{2,1,0:T(8,128)(2,1)S(1)}, bf16[96,8,128]{2,1,0:T(8,128)(2,1)S(1)}, u32[]{:S(2)}, u32[]{:S(2)}) collective-permute-start(bf16[96,8,128]{2,1,0:T(8,128)(2,1)S(1)} %pad_maximum_fusion.refs_6_.refs_9_), channel_id=1, source_target_pairs={{0,1},{1,0},{2,3},{3,2},{4,5},{5,4},{6,7},{7,6},{8,9},{9,8},{10,11... | collective-permute-start | bytes 589832 | tf_op jit(solution)/shard_map/ppermute | solution.py:432
  14.7 1.5 %collective-permute-start.5 = (bf16[16,8,128]{2,1,0:T(8,128)(2,1)S(1)}, bf16[16,8,128]{2,1,0:T(8,128)(2,1)S(1)}, u32[]{:S(2)}, u32[]{:S(2)}) collective-permute-start(bf16[16,8,128]{2,1,0:T(8,128)(2,1)S(1)} %collective-permute-done.4.refs_4_.refs_7_), channel_id=1, source_target_pairs={{0,1},{1,0},{2,3},{3,2},{4,5},{5,4},{6,7},{7,6},{8,9},{9,8},{10,11... | collective-permute-start | bytes 98312 | tf_op jit(solution)/shard_map/ppermute | solution.py:432
  18.6 2.3 %collective-permute-start.8 = (bf16[528,128]{1,0:T(8,128)(2,1)S(1)}, bf16[528,128]{1,0:T(8,128)(2,1)S(1)}, u32[]{:S(2)}, u32[]{:S(2)}) collective-permute-start(bf16[528,128]{1,0:T(8,128)(2,1)S(1)} %get-tuple-element.43), channel_id=1, source_target_pairs={{0,1},{1,0},{2,3},{3,2},{4,5},{5,4},{6,7},{7,6},{8,9},{9,8},{10,11... | collective-permute-start | bytes 405512 | tf_op jit(solution)/shard_map/ppermute | solution.py:432
  19.2 1.8 %collective-permute-start.7 = (bf16[192,128]{1,0:T(8,128)(2,1)S(1)}, bf16[192,128]{1,0:T(8,128)(2,1)S(1)}, u32[]{:S(2)}, u32[]{:S(2)}) collective-permute-start(bf16[192,128]{1,0:T(8,128)(2,1)S(1)} %get-tuple-element.42), channel_id=1, source_target_pairs={{0,1},{1,0},{2,3},{3,2},{4,5},{5,4},{6,7},{7,6},{8,9},{9,8},{10,11... | collective-permute-start | bytes 147464 | tf_op jit(solution)/shard_map/ppermute | solution.py:432
  21.3 6.1 %collective-permute-start.10 = (bf16[160,128]{1,0:T(8,128)(2,1)S(1)}, bf16[160,128]{1,0:T(8,128)(2,1)S(1)}, u32[]{:S(2)}, u32[]{:S(2)}) collective-permute-start(bf16[160,128]{1,0:T(8,128)(2,1)S(1)} %get-tuple-element.46), channel_id=1, source_target_pairs={{0,8},{1,11},{2,10},{3,9},{4,12},{5,15},{6,14},{7,13},{8,0},{9,3},... | collective-permute-start | bytes 122888 | tf_op jit(solution)/shard_map/ppermute | solution.py:432
  23.6 6.2 %collective-permute-start.11 = (bf16[160,128]{1,0:T(8,128)(2,1)S(1)}, bf16[160,128]{1,0:T(8,128)(2,1)S(1)}, u32[]{:S(2)}, u32[]{:S(2)}) collective-permute-start(bf16[160,128]{1,0:T(8,128)(2,1)S(1)} %get-tuple-element.47), channel_id=1, source_target_pairs={{0,12},{1,15},{2,14},{3,13},{4,8},{5,11},{6,10},{7,9},{8,4},{9,7},... | collective-permute-start | bytes 122888 | tf_op jit(solution)/shard_map/ppermute | solution.py:432
  24.5 5.6 %collective-permute-start.12 = (bf16[160,128]{1,0:T(8,128)(2,1)S(1)}, bf16[160,128]{1,0:T(8,128)(2,1)S(1)}, u32[]{:S(2)}, u32[]{:S(2)}) collective-permute-start(bf16[160,128]{1,0:T(8,128)(2,1)S(1)} %get-tuple-element.48), channel_id=1, source_target_pairs={{0,4},{1,7},{2,6},{3,5},{4,0},{5,3},{6,2},{7,1},{8,12},{9,15},{10,... | collective-permute-start | bytes 122888 | tf_op jit(solution)/shard_map/ppermute | solution.py:432
  25.1 5.3 %collective-permute-start.9 = (bf16[96,128]{1,0:T(8,128)(2,1)S(1)}, bf16[96,128]{1,0:T(8,128)(2,1)S(1)}, u32[]{:S(2)}, u32[]{:S(2)}) collective-permute-start(bf16[96,128]{1,0:T(8,128)(2,1)S(1)} %get-tuple-element.45), channel_id=1, source_target_pairs={{0,2},{1,3},{2,0},{3,1},{4,6},{5,7},{6,4},{7,5},{8,10},{9,11},{10,... | collective-permute-start | bytes 73736 | tf_op jit(solution)/shard_map/ppermute | solution.py:432
  27.4 3.0 %collective-permute-start.13 = (bf16[96,128]{1,0:T(8,128)(2,1)S(1)}, bf16[96,128]{1,0:T(8,128)(2,1)S(1)}, u32[]{:S(2)}, u32[]{:S(2)}) collective-permute-start(bf16[96,128]{1,0:T(8,128)(2,1)S(1)} %slice.12), channel_id=1, source_target_pairs={{0,1},{1,0},{2,3},{3,2},{4,5},{5,4},{6,7},{7,6},{8,9},{9,8},{10,11... | collective-permute-start | bytes 73736 | tf_op jit(solution)/shard_map/ppermute | solution.py:432
  29.8 1.2 %collective-permute-start.14 = (bf16[96,128]{1,0:T(8,128)(2,1)S(1)}, bf16[96,128]{1,0:T(8,128)(2,1)S(1)}, u32[]{:S(2)}, u32[]{:S(2)}) collective-permute-start(bf16[96,128]{1,0:T(8,128)(2,1)S(1)} %slice.13), channel_id=1, source_target_pairs={{0,1},{1,0},{2,3},{3,2},{4,5},{5,4},{6,7},{7,6},{8,9},{9,8},{10,11... | collective-permute-start | bytes 73736 | tf_op jit(solution)/shard_map/ppermute | solution.py:432
  30.0 1.2 %collective-permute-start.15 = (bf16[96,128]{1,0:T(8,128)(2,1)S(1)}, bf16[96,128]{1,0:T(8,128)(2,1)S(1)}, u32[]{:S(2)}, u32[]{:S(2)}) collective-permute-start(bf16[96,128]{1,0:T(8,128)(2,1)S(1)} %slice.14), channel_id=1, source_target_pairs={{0,1},{1,0},{2,3},{3,2},{4,5},{5,4},{6,7},{7,6},{8,9},{9,8},{10,11... | collective-permute-start | bytes 73736 | tf_op jit(solution)/shard_map/ppermute | solution.py:432

commit v13 on v11

--- a/solution.py
+++ b/solution.py
@@ -12,7 +12,7 @@
 KEY_HEADS = 8
 HEAD_WIDTH = 128
 ROPE_BASE = 500000.0
-NEG_FILL = -1e30
+NEG_FILL = -(2.0**100)
 SCALE = 1.0 / math.sqrt(HEAD_WIDTH)
 CHUNKS = KEY_HEADS // 2
 MIX_ROWS = CHUNKS * 128
@@ -34,7 +34,8 @@
         self.per_head = per_head = lanes // KEY_HEADS
         self.heads, self.chunks = QUERY_HEADS // devices, width // HEAD_WIDTH
         self.single = 1
-        self.pairs = [(m, m + 1) for m in range(lanes - 2, 0, -2)]
+        self.pairs = [(m, m + 1) for m in range(2, lanes, 2)]
+        self.pairs[-2:] = self.pairs[:-3:-1]
         size = self.heads + self.chunks
         self.own = ((0, 0), ((0, 0), (1, 0)))
         self.one = ((self.single,) * 2, ((2, 0), (3, 0)))
@@ -92,14 +93,15 @@
     ]
 
 
-def streams(sources, index_ref, down_ref, half_ref, sems):
-    depth = half_ref.shape[1]
+def streams(sources, index_ref, down_ref, halves, sems):
+    count, depth = halves[0].shape[:2]
     here = index_ref[0]
     copies = []
     for at, (_, _, masks, side) in enumerate(sources):
         source = here ^ (2 * here_mask(masks, here) + side)
         rows = pl.ds(pl.multiple_of(source * depth, depth), depth)
-        copies.append(pltpu.make_async_copy(down_ref.at[rows], half_ref.at[at], sems.at[at]))
+        place = halves[at // count].at[at % count]
+        copies.append(pltpu.make_async_copy(down_ref.at[rows], place, sems.at[at]))
     return copies
 
 
@@ -131,9 +133,9 @@
             at += 1
 
 
-def base_kernel(heads, own_ref, weight_ref, *refs):
-    sources, base_ref, held = refs[:3], refs[3], refs[4:7]
-    buffer, sems = refs[7:]
+def base_kernel(heads, sources, index_ref, own_ref, weight_ref, down_ref, *refs):
+    others, (base_ref, *held) = refs[:3], refs[3:7]
+    *halves, buffer, sems, row_sems = refs[7:]
     parts, depth = buffer.shape[:2]
     loads = [
         pltpu.make_async_copy(weight_ref.at[pl.ds(p * depth, depth)], buffer.at[p], sems.at[p])
@@ -141,8 +143,9 @@
     ]
     others = [
         pltpu.make_async_copy(source, place, sems.at[parts + i])
-        for i, (source, place) in enumerate(zip(sources, held))
+        for i, (source, place) in enumerate(zip(others, held))
     ]
+    others += streams(sources, index_ref, down_ref, halves, row_sems)
     for load in loads + others:
         load.start()
     tiles = depth // HEAD_WIDTH
@@ -154,14 +157,6 @@
     base_ref[...] = total
     for load in others:
         load.wait()
-
-
-def fetch_kernel(sources, index_ref, down_ref, half_ref, sems):
-    copies = streams(sources, index_ref, down_ref, half_ref, sems)
-    for copy in copies:
-        copy.start()
-    for copy in copies:
-        copy.wait()
 
 
 def attend(sizes, plan, keep, index_ref, length_ref, arrays, key_ref, value_ref, put):
@@ -195,10 +190,9 @@
         for i, spot in enumerate(spots):
             part = dot(key_ref[:, spot], query, ((1,), (1,)))
             scores = part if scores is None else jnp.where(column < i * share, scores, part)
-        scores = scores * SCALE
-        peak = jnp.max(jnp.where(allowed, scores, NEG_FILL), axis=0, keepdims=True)
-        peak = round_bf16(peak)
-        weights = jnp.where(allowed, jnp.exp(scores - peak), 0.0)
+        scores = jnp.where(allowed, scores * SCALE, NEG_FILL)
+        peak = round_bf16(jnp.max(scores, axis=0, keepdims=True))
+        weights = jnp.exp(scores - peak)
         peaks.append(peak)
         totals.append(jnp.sum(weights, axis=0, keepdims=True))
         weights = jnp.transpose(weights.astype(jnp.bfloat16))
@@ -263,7 +257,9 @@
 
 
 def keep_kernel(sizes, plan, *refs):
-    (index_ref, length_ref, *arrays, key_ref, value_ref, mix_ref, stat_ref) = refs
+    (index_ref, length_ref, own_ref, one_ref, pairs_ref) = refs[:5]
+    (key_ref, value_ref, mix_ref, stat_ref) = refs[5:]
+    arrays = {0: own_ref, 2: one_ref, 4: pairs_ref}
 
     def put(chunk, row, mix):
         at = chunk * 128 + row
@@ -366,14 +362,23 @@
         jnp.sum(weights, axis=0, keepdims=True),
     )
     inverse = 1.0 / total
-    filler = jnp.zeros((128 - sources - 1, 128), jnp.float32)
-    table = jnp.concatenate([factor * inverse for factor in factors] + [inverse, filler], axis=0)
+    start = -(-(sources + 1) // rows) * rows
+    table = jnp.concatenate(
+        [factor * inverse for factor in factors]
+        + [inverse, jnp.zeros((start - sources - 1, 128), jnp.float32), weights]
+        + [jnp.zeros((128 - start - rows, 128), jnp.float32)],
+        axis=0,
+    )
     table = jnp.transpose(table)[:mix_rows]
-    weights = jnp.transpose(
-        jnp.concatenate([weights, jnp.zeros((128 - rows, 128), jnp.float32)], axis=0)
-    )[:mix_rows].astype(jnp.bfloat16)
+    lane = lax.broadcasted_iota(jnp.int32, table.shape, 1)
+    weights = jnp.where((lane >= start) & (lane < start + rows), table, 0.0).astype(jnp.bfloat16)
     values = jnp.concatenate(
-        [values, jnp.zeros((128 - rows, HEAD_WIDTH), jnp.bfloat16)], axis=0
+        [
+            jnp.zeros((start, HEAD_WIDTH), jnp.bfloat16),
+            values,
+            jnp.zeros((128 - start - rows, HEAD_WIDTH), jnp.bfloat16),
+        ],
+        axis=0,
     )
     mix = dot(weights, values, ((1,), (0,))) * table[:, sources : sources + 1]
     for s, ref in enumerate(got_refs):
@@ -471,50 +476,52 @@
         ],
         "pack",
     )
-    other = core_swap(own)
+    flat = requests * cached_key_rows.shape[1]
     one = trade(own, devices, plan.single, plan.single)
+    other, late_own, late_lengths = lax.optimization_barrier((core_swap(own), own, lengths))
     both = jnp.concatenate([own, other], axis=0)
     mine = [trade(both, devices, a, b) for a, b in plan.pairs]
 
-    flat = requests * cached_key_rows.shape[1]
+    out_width = key_value_weight.shape[1]
+    parts = 4 if width % (4 * HEAD_WIDTH) == 0 else 1
+    down = pinned(adapter_down_weight[0])
+    rank = down.shape[1]
     big = (
         cached_key_rows.reshape(flat, -1),
         cached_value_rows.reshape(flat, -1),
         adapter_up_weight[0],
     )
-    out_width = key_value_weight.shape[1]
-    parts = 4 if width % (4 * HEAD_WIDTH) == 0 else 1
-    base, keys, values, up = call(
-        functools.partial(base_kernel, heads),
-        (own, pinned(key_value_weight)) + tuple(pinned(x) for x in big),
-        [vmem()] + [hbm()] * 4,
-        [pltpu.VMEM((rows, out_width), jnp.float32)] + [pltpu.VMEM(x.shape, x.dtype) for x in big],
+    base, keys, values, up, *halves = call(
+        functools.partial(base_kernel, heads, sources_of(plan)),
+        (index, late_own, pinned(key_value_weight), down) + tuple(pinned(x) for x in big),
+        [smem(), vmem()] + [hbm()] * 5,
+        [pltpu.VMEM((rows, out_width), jnp.float32)]
+        + [pltpu.VMEM(x.shape, x.dtype) for x in big]
+        + [pltpu.VMEM((devices // 2, width, rank), jnp.bfloat16)] * 2,
         [
             pltpu.VMEM((parts, width // parts, out_width), jnp.bfloat16),
             pltpu.SemaphoreType.DMA((parts + 3,)),
+            pltpu.SemaphoreType.DMA((devices,)),
         ],
         "base",
     )
-    down = adapter_down_weight[0]
-    count = devices // 2
-    first, second = [
-        call(
-            functools.partial(fetch_kernel, sources_of(plan)[at : at + count]),
-            (index, pinned(down)),
-            [smem(), hbm()],
-            [pltpu.VMEM((count, width, down.shape[1]), jnp.bfloat16)],
-            [pltpu.SemaphoreType.DMA((count,))],
-            "fetch",
-        )[0]
-        for at in (0, count)
-    ]
-    one, base, first = lax.optimization_barrier((one, base, first))
-    other_one = core_swap(one)
+    cosine, sine = rotation(late_lengths, tokens)
     mine = jnp.concatenate(mine, axis=0)
-    mine, other_one = lax.optimization_barrier((mine, other_one))
-    other_mine, second = lax.optimization_barrier((core_swap(mine), second))
+    mine, one, base, cosine, sine = lax.optimization_barrier((mine, one, base, cosine, sine))
+    other_one, other_mine = core_swap(one), core_swap(mine)
+    mix, stats = call(
+        functools.partial(keep_kernel, sizes, plan),
+        (index, lengths, own, one, mine, keys, values),
+        [smem()] * 2 + [vmem()] * 5,
+        [
+            pltpu.VMEM((MIX_ROWS, HEAD_WIDTH), jnp.float32),
+            pltpu.VMEM((8, HEAD_WIDTH), jnp.float32),
+        ],
+        [],
+        "keep_states",
+    )
+    other_mine, mix = lax.optimization_barrier((other_mine, mix))
     arrays = (own, other, one, other_one, mine, other_mine)
-    halves = (first, second)
     step = KEY_HEADS * rows
     send, proj, proj_parts = call(
         functools.partial(send_kernel, sizes, plan),
@@ -532,17 +539,6 @@
     )
     got_parts = core_swap(proj_parts)
     got = core_swap(send)
-    mix, stats = call(
-        functools.partial(keep_kernel, sizes, plan),
-        (index, lengths) + arrays + (keys, values),
-        [smem()] * 2 + [vmem()] * (len(arrays) + 2),
-        [
-            pltpu.VMEM((MIX_ROWS, HEAD_WIDTH), jnp.float32),
-            pltpu.VMEM((8, HEAD_WIDTH), jnp.float32),
-        ],
-        [],
-        "keep_states",
-    )
     packets = call(
         functools.partial(join_kernel, sizes, plan),
         (index, mix, stats, proj, got_parts, got),
@@ -553,9 +549,8 @@
         "join",
     )
     heard = [packets[0], trade(packets[1], devices, plan.single, plan.single)]
-    heard += [trade(x, devices, a, b) for x, (a, b) in zip(packets[2:], plan.pairs)]
+    heard += [trade(x, devices, a, b) for x, (a, b) in zip(packets[:1:-1], plan.pairs[::-1])]
     heard += [core_swap(x[slot_rows:]) for x in heard[2:]]
-    cosine, sine = rotation(lengths, tokens)
     return pl.pallas_call(
         functools.partial(merge_kernel, devices, requests, tokens, 2 + len(plan.pairs)),
         out_shape=jax.ShapeDtypeStruct((requests, tokens, heads * HEAD_WIDTH), jnp.bfloat16),

time: 33.7 us -> 32.3 us (0.958)
  Pallas kernels: 11.9 us -> 10.1 us
  starting transfers between devices: 15 us -> 13.5 us
  waiting for transfers between devices: 5.83 us -> 7.13 us
  other arithmetic: 0.3 us -> 0.96 us
    pallas_call x7 -> x5, Pallas kernels: 10.8 us -> 8.98 us  [call(): pl.pallas_call(kernel, out_shape=tuple(out_shape), in_specs=in_specs, out...]
    ppermute x16, starting transfers between devices: 15 us -> 13.5 us  [trade(): return lax.ppermute(x, 'tensor', pairs)]
    ppermute x16, waiting for transfers between devices: 5.83 us -> 7.13 us  [trade(): return lax.ppermute(x, 'tensor', pairs)]
    convert_element_type x1, other arithmetic: 0.07 us -> 0.73 us  [rotation(): (lengths[:, None] + jnp.arange(tokens, dtype=jnp.int32)[None, :]).astype(...]
  transfers between devices with their start and end apart: 16 -> 16, of which waited for: 6 -> 8; matrix products, arithmetic and copies ran while one was open for 1% -> 3% of each run, Pallas kernels for 22% -> 17%
where the time goes in v13:
time: 32.3 us; the launch traced here: 32 us
  starting transfers between devices  13.5 us (42%)
  Pallas kernels  10.1 us (31%)
  waiting for transfers between devices  7.13 us (22%)
  other arithmetic  0.96 us (3%)
    ppermute x16, starting transfers between devices, trade(): return lax.ppermute(x, 'tensor', pairs)  13.5 us
    pallas_call x5, Pallas kernels, call(): pl.pallas_call(kernel, out_shape=tuple(out_shape), in_specs=in_specs, out...  8.98 us
    ppermute x16, waiting for transfers between devices, trade(): return lax.ppermute(x, 'tensor', pairs)  7.13 us
    pallas_call x1, Pallas kernels, per_device(): pl.pallas_call(functools.partial(merge_kernel, devices, requests, tokens,...  1.13 us
    convert_element_type x1, other arithmetic, rotation(): (lengths[:, None] + jnp.arange(tokens, dtype=jnp.int32)[None, :]).astype(...  0.73 us
  transfers between devices with their start and end apart: 16, of which 8 were waited for; matrix products, arithmetic and copies ran while one was open for 3% of the time, Pallas kernels for 17%

profile of v13, /device:TPU:0, one launch (start us, length us, event | category | flops | bytes accessed | tf_op | source)
XLA Modules:
  0.0 32.0 jit_solution(16234333219128309622)
XLA Ops:
  0.0 0.8 %pack.1.own_ref.refs_2_.refs_5_ = bf16[16,8,128]{2,1,0:T(8,128)(2,1)S(1)} custom-call(bf16[2,4,1024]{2,1,0:T(4,128)(2,1)} %query_ref.1, bf16[2,4,1024]{2,1,0:T(4,128)(2,1)} %hidden_ref.1), custom_call_target="tpu_custom_call" | custom-call | flops 1000000 | tf_op jit(solution)/shard_map/pack/pallas_call | solution.py:453
  0.8 0.5 %collective-permute-start = (bf16[16,8,128]{2,1,0:T(8,128)(2,1)S(1)}, bf16[16,8,128]{2,1,0:T(8,128)(2,1)S(1)}, u32[]{:S(2)}, u32[]{:S(2)}) collective-permute-start(bf16[16,8,128]{2,1,0:T(8,128)(2,1)S(1)} %pack.1.own_ref.refs_2_.refs_5_), channel_id=1, source_target_pairs={{0,1},{1,0},{2,3},{3,2},{4,5},{5,4},{6,7},{7,6},{8,9},{9,8},{10,11... | collective-permute-start | bytes 98312 | tf_op jit(solution)/shard_map/ppermute | solution.py:427
  1.3 2.6 %collective-permute-start.4 = (bf16[16,8,128]{2,1,0:T(8,128)(2,1)S(1)}, bf16[16,8,128]{2,1,0:T(8,128)(2,1)S(1)}, u32[]{:S(2)}, u32[]{:S(2)}) collective-permute-start(bf16[16,8,128]{2,1,0:T(8,128)(2,1)S(1)} %pack.1.own_ref.refs_2_.refs_5_), channel_id=1, source_target_pairs={{0,2},{1,3},{2,0},{3,1},{4,6},{5,7},{6,4},{7,5},{8,10},{9,11},{10,... | collective-permute-start | bytes 98312 | tf_op jit(solution)/shard_map/ppermute | solution.py:427
  3.9 2.7 %collective-permute-start.3 = (bf16[32,8,128]{2,1,0:T(8,128)(2,1)S(1)}, bf16[32,8,128]{2,1,0:T(8,128)(2,1)S(1)}, u32[]{:S(2)}, u32[]{:S(2)}) collective-permute-start(bf16[32,8,128]{2,1,0:T(8,128)(2,1)S(1)} %pad_maximum_fusion.1), channel_id=1, source_target_pairs={{0,8},{1,11},{2,10},{3,9},{4,12},{5,15},{6,14},{7,13},{8,0},{9,3},... | collective-permute-start | bytes 196616 | tf_op jit(solution)/shard_map/ppermute | solution.py:427
  6.6 1.3 %collective-permute-start.2 = (bf16[32,8,128]{2,1,0:T(8,128)(2,1)S(1)}, bf16[32,8,128]{2,1,0:T(8,128)(2,1)S(1)}, u32[]{:S(2)}, u32[]{:S(2)}) collective-permute-start(bf16[32,8,128]{2,1,0:T(8,128)(2,1)S(1)} %pad_maximum_fusion.1), channel_id=1, source_target_pairs={{0,12},{1,15},{2,14},{3,13},{4,8},{5,11},{6,10},{7,9},{8,4},{9,7},... | collective-permute-start | bytes 196616 | tf_op jit(solution)/shard_map/ppermute | solution.py:427
  7.9 0.2 collective-permute-start.1
  8.1 0.7 %add_convert_fusion = f32[2,4]{1,0:T(2,128)S(1)} fusion(s32[2]{0:T(128)} %refs_1_.3), kind=kLoop, calls=%fused_computation.6 | loop fusion | flops 16 | bytes 40 | tf_op jit(solution)/shard_map/convert_element_type | solution.py:396
  8.9 0.1 convert_element_type.11
  8.9 0.1 fusion
  9.1 0.0 copy-start.1
  9.1 4.1 %base.1 = (f32[8,2048]{1,0:T(8,128)S(1)}, bf16[256,1024]{1,0:T(8,128)(2,1)S(1)}, bf16[256,1024]{1,0:T(8,128)(2,1)S(1)}, bf16[128,2048]{1,0:T(8,128)(2,1)S(1)}, b...) custom-call(s32[1]{0:T(128)} %bitcast.index_ref.refs_0_, ...), custom_call_target="tpu_custom_call" | custom-call | flops 1000000 | tf_op jit(solution)/shard_map/base/pallas_call | solution.py:453
  13.2 0.1 pad_maximum_fusion.2
  13.2 0.1 collective-permute-done.2
  13.4 0.8 %collective-permute-done.1 = bf16[32,8,128]{2,1,0:T(8,128)(2,1)S(1)} collective-permute-done((bf16[32,8,128]{2,1,0:T(8,128)(2,1)S(1)}, bf16[32,8,128]{2,1,0:T(8,128)(2,1)S(1)}, u32[]{:S(2)}, u32[]{:S(2)}) %collective-permute-start.1) | collective-permute-done | bytes 65568 | tf_op jit(solution)/shard_map/ppermute | solution.py:427
  14.2 0.3 collective-permute-start.5
  14.5 0.3 collective-permute-start.6
  14.8 1.5 %keep_states.1 = (f32[512,128]{1,0:T(8,128)S(1)}, f32[8,128]{1,0:T(8,128)S(1)}) custom-call(s32[1]{0:T(128)} %bitcast.index_ref.refs_0_, s32[2]{0:T(128)S(1)} %copy-done, bf16[16,8,128]{2,1,0:T(8,128)(2,1)S(1)} %pack.1.own_ref.refs_2_.refs_5_, bf16[16,8,128]{2,1,0:T(8,128)(2,1)S(1)} %collective-permute-done.4.refs_3_.refs_7_, ...), custom_call_target="tpu_custom_call" | custom-call | flops 1000000 | tf_op jit(solution)/shard_map/keep_states/pallas_call | solution.py:453
  16.4 2.3 %send_states.1 = (bf16[528,128]{1,0:T(8,128)(2,1)S(1)}, f32[2,64,128]{2,1,0:T(8,128)S(1)}, bf16[192,128]{1,0:T(8,128)(2,1)S(1)}) custom-call(s32[1]{0:T(128)} %bitcast.index_ref.refs_0_, s32[2]{0:T(128)S(1)} %copy-done, s32[2]{0:T(128)S(1)} %copy-done.1, s32[16]{0:T(128)S(1)} %copy-done.2, s32[16]{0:T(128)S(1)} %copy-done.3, ...), custom_call_target="tpu_custom_call" | custom-call | flops 1000000 | tf_op jit(solution)/shard_map/send_states/pallas_call | solution.py:453
  18.7 0.3 collective-permute-start.8
  19.0 0.3 collective-permute-start.7
  19.3 0.9 %collective-permute-done.7.got_parts_ref = bf16[192,128]{1,0:T(8,128)(2,1)S(1)} collective-permute-done((bf16[192,128]{1,0:T(8,128)(2,1)S(1)}, bf16[192,128]{1,0:T(8,128)(2,1)S(1)}, u32[]{:S(2)}, u32[]{:S(2)}) %collective-permute-start.7) | collective-permute-done | bytes 49184 | tf_op jit(solution)/shard_map/ppermute | solution.py:427
  20.2 0.3 %join.1 = (bf16[96,128]{1,0:T(8,128)(2,1)S(1)}, bf16[96,128]{1,0:T(8,128)(2,1)S(1)}, bf16[160,128]{1,0:T(8,128)(2,1)S(1)}, bf16[160,128]{1,0:T(8,128)(2,1)S(1)}, bf16[160,128]{1,0:T(8,128)(2,1)S(1)}) custom-call(s32[1]{0:T(128)} %bitcast.index_ref.refs_0_, f32[512,128]{1,0:T(8,128)S(1)} %get-tuple-element.42.mix_ref, ...), custom_call_target="tpu_custom_call" | custom-call | flops 1000000 | tf_op jit(solution)/shard_map/join/pallas_call | solution.py:453
  20.6 2.5 %collective-permute-start.10 = (bf16[160,128]{1,0:T(8,128)(2,1)S(1)}, bf16[160,128]{1,0:T(8,128)(2,1)S(1)}, u32[]{:S(2)}, u32[]{:S(2)}) collective-permute-start(bf16[160,128]{1,0:T(8,128)(2,1)S(1)} %get-tuple-element.54), channel_id=1, source_target_pairs={{0,8},{1,11},{2,10},{3,9},{4,12},{5,15},{6,14},{7,13},{8,0},{9,3},... | collective-permute-start | bytes 122888 | tf_op jit(solution)/shard_map/ppermute | solution.py:427
  23.1 1.3 %collective-permute-start.11 = (bf16[160,128]{1,0:T(8,128)(2,1)S(1)}, bf16[160,128]{1,0:T(8,128)(2,1)S(1)}, u32[]{:S(2)}, u32[]{:S(2)}) collective-permute-start(bf16[160,128]{1,0:T(8,128)(2,1)S(1)} %get-tuple-element.55), channel_id=1, source_target_pairs={{0,12},{1,15},{2,14},{3,13},{4,8},{5,11},{6,10},{7,9},{8,4},{9,7},... | collective-permute-start | bytes 122888 | tf_op jit(solution)/shard_map/ppermute | solution.py:427
  24.4 0.9 %collective-permute-start.9 = (bf16[96,128]{1,0:T(8,128)(2,1)S(1)}, bf16[96,128]{1,0:T(8,128)(2,1)S(1)}, u32[]{:S(2)}, u32[]{:S(2)}) collective-permute-start(bf16[96,128]{1,0:T(8,128)(2,1)S(1)} %get-tuple-element.53), channel_id=1, source_target_pairs={{0,2},{1,3},{2,0},{3,1},{4,6},{5,7},{6,4},{7,5},{8,10},{9,11},{10,... | collective-permute-start | bytes 73736 | tf_op jit(solution)/shard_map/ppermute | solution.py:427
  25.3 1.4 %collective-permute-done.10.refs_2_ = bf16[160,128]{1,0:T(8,128)(2,1)S(1)} collective-permute-done((bf16[160,128]{1,0:T(8,128)(2,1)S(1)}, bf16[160,128]{1,0:T(8,128)(2,1)S(1)}, u32[]{:S(2)}, u32[]{:S(2)}) %collective-permute-start.10) | collective-permute-done | bytes 40992 | tf_op jit(solution)/shard_map/ppermute | solution.py:427
  26.7 2.6 %collective-permute-done.11.refs_3_ = bf16[160,128]{1,0:T(8,128)(2,1)S(1)} collective-permute-done((bf16[160,128]{1,0:T(8,128)(2,1)S(1)}, bf16[160,128]{1,0:T(8,128)(2,1)S(1)}, u32[]{:S(2)}, u32[]{:S(2)}) %collective-permute-start.11) | collective-permute-done | bytes 40992 | tf_op jit(solution)/shard_map/ppermute | solution.py:427
  29.3 0.3 %collective-permute-done.12.refs_4_ = bf16[160,128]{1,0:T(8,128)(2,1)S(1)} collective-permute-done((bf16[160,128]{1,0:T(8,128)(2,1)S(1)}, bf16[160,128]{1,0:T(8,128)(2,1)S(1)}, u32[]{:S(2)}, u32[]{:S(2)}) %collective-permute-start.12) | collective-permute-done | bytes 40992 | tf_op jit(solution)/shard_map/ppermute | solution.py:427
  29.6 0.3 collective-permute-start.15
  29.9 0.6 %collective-permute-done.14.refs_6_ = bf16[96,128]{1,0:T(8,128)(2,1)S(1)} collective-permute-done((bf16[96,128]{1,0:T(8,128)(2,1)S(1)}, bf16[96,128]{1,0:T(8,128)(2,1)S(1)}, u32[]{:S(2)}, u32[]{:S(2)}) %collective-permute-start.14) | collective-permute-done | bytes 24608 | tf_op jit(solution)/shard_map/ppermute | solution.py:427
  30.5 0.4 %collective-permute-done.15.refs_7_ = bf16[96,128]{1,0:T(8,128)(2,1)S(1)} collective-permute-done((bf16[96,128]{1,0:T(8,128)(2,1)S(1)}, bf16[96,128]{1,0:T(8,128)(2,1)S(1)}, u32[]{:S(2)}, u32[]{:S(2)}) %collective-permute-start.15) | collective-permute-done | bytes 24608 | tf_op jit(solution)/shard_map/ppermute | solution.py:427
  30.8 1.1 %merge_states.1 = bf16[2,4,1024]{2,1,0:T(4,128)(2,1)} custom-call(bf16[16,8,128]{2,1,0:T(8,128)(2,1)S(1)} %pack.1.own_ref.refs_2_.refs_5_, f32[8,128]{1,0:T(8,128)S(1)} %get-tuple-element.35.cos_ref, f32[8,128]{1,0:T(8,128)S(1)} %get-tuple-element.36.sin_ref, bf16[96,128]{1,0:T(8,128)(2,1)S(1)} %get-tuple-element.52.refs_0_, ...), custom_call_target="tpu_custom_call" | custom-call | tf_op jit(solution)/shard_map/merge_states/pallas_call | solution.py:554
  (24 shorter events, 0.1 us)
Async XLA Ops:
  0.8 3.1 %collective-permute-start = (bf16[16,8,128]{2,1,0:T(8,128)(2,1)S(1)}, bf16[16,8,128]{2,1,0:T(8,128)(2,1)S(1)}, u32[]{:S(2)}, u32[]{:S(2)}) collective-permute-start(bf16[16,8,128]{2,1,0:T(8,128)(2,1)S(1)} %pack.1.own_ref.refs_2_.refs_5_), channel_id=1, source_target_pairs={{0,1},{1,0},{2,3},{3,2},{4,5},{5,4},{6,7},{7,6},{8,9},{9,8},{10,11... | collective-permute-start | bytes 98312 | tf_op jit(solution)/shard_map/ppermute | solution.py:427
  1.3 13.0 %collective-permute-start.4 = (bf16[16,8,128]{2,1,0:T(8,128)(2,1)S(1)}, bf16[16,8,128]{2,1,0:T(8,128)(2,1)S(1)}, u32[]{:S(2)}, u32[]{:S(2)}) collective-permute-start(bf16[16,8,128]{2,1,0:T(8,128)(2,1)S(1)} %pack.1.own_ref.refs_2_.refs_5_), channel_id=1, source_target_pairs={{0,2},{1,3},{2,0},{3,1},{4,6},{5,7},{6,4},{7,5},{8,10},{9,11},{10,... | collective-permute-start | bytes 98312 | tf_op jit(solution)/shard_map/ppermute | solution.py:427
  3.9 9.3 %collective-permute-start.3 = (bf16[32,8,128]{2,1,0:T(8,128)(2,1)S(1)}, bf16[32,8,128]{2,1,0:T(8,128)(2,1)S(1)}, u32[]{:S(2)}, u32[]{:S(2)}) collective-permute-start(bf16[32,8,128]{2,1,0:T(8,128)(2,1)S(1)} %pad_maximum_fusion.1), channel_id=1, source_target_pairs={{0,8},{1,11},{2,10},{3,9},{4,12},{5,15},{6,14},{7,13},{8,0},{9,3},... | collective-permute-start | bytes 196616 | tf_op jit(solution)/shard_map/ppermute | solution.py:427
  6.6 6.8 %collective-permute-start.2 = (bf16[32,8,128]{2,1,0:T(8,128)(2,1)S(1)}, bf16[32,8,128]{2,1,0:T(8,128)(2,1)S(1)}, u32[]{:S(2)}, u32[]{:S(2)}) collective-permute-start(bf16[32,8,128]{2,1,0:T(8,128)(2,1)S(1)} %pad_maximum_fusion.1), channel_id=1, source_target_pairs={{0,12},{1,15},{2,14},{3,13},{4,8},{5,11},{6,10},{7,9},{8,4},{9,7},... | collective-permute-start | bytes 196616 | tf_op jit(solution)/shard_map/ppermute | solution.py:427
  7.9 6.3 %collective-permute-start.1 = (bf16[32,8,128]{2,1,0:T(8,128)(2,1)S(1)}, bf16[32,8,128]{2,1,0:T(8,128)(2,1)S(1)}, u32[]{:S(2)}, u32[]{:S(2)}) collective-permute-start(bf16[32,8,128]{2,1,0:T(8,128)(2,1)S(1)} %pad_maximum_fusion.1), channel_id=1, source_target_pairs={{0,4},{1,7},{2,6},{3,5},{4,0},{5,3},{6,2},{7,1},{8,12},{9,15},{10,... | collective-permute-start | bytes 196616 | tf_op jit(solution)/shard_map/ppermute | solution.py:427
  9.1 5.8 %copy-start = (s32[2]{0:T(128)S(1)}, s32[2]{0:T(128)}, u32[]{:S(2)}) copy-start(s32[2]{0:T(128)} %refs_1_.3) | copy-start | bytes 28
  9.1 7.3 %copy-start.1 = (s32[2]{0:T(128)S(1)}, s32[2]{0:T(128)}, u32[]{:S(2)}) copy-start(s32[2]{0:T(128)} %refs_2_.1) | copy-start | bytes 28
  9.1 7.3 %copy-start.2 = (s32[16]{0:T(128)S(1)}, s32[16]{0:T(128)}, u32[]{:S(2)}) copy-start(s32[16]{0:T(128)} %refs_3_.1) | copy-start | bytes 196
  9.1 7.3 %copy-start.3 = (s32[16]{0:T(128)S(1)}, s32[16]{0:T(128)}, u32[]{:S(2)}) copy-start(s32[16]{0:T(128)} %refs_4_.1) | copy-start | bytes 196
  14.2 2.1 %collective-permute-start.5 = (bf16[96,8,128]{2,1,0:T(8,128)(2,1)S(1)}, bf16[96,8,128]{2,1,0:T(8,128)(2,1)S(1)}, u32[]{:S(2)}, u32[]{:S(2)}) collective-permute-start(bf16[96,8,128]{2,1,0:T(8,128)(2,1)S(1)} %pad_maximum_fusion.refs_4_.refs_9_), channel_id=1, source_target_pairs={{0,1},{1,0},{2,3},{3,2},{4,5},{5,4},{6,7},{7,6},{8,9},{9,8},{10,11... | collective-permute-start | bytes 589832 | tf_op jit(solution)/shard_map/ppermute | solution.py:427
  14.5 1.9 %collective-permute-start.6 = (bf16[16,8,128]{2,1,0:T(8,128)(2,1)S(1)}, bf16[16,8,128]{2,1,0:T(8,128)(2,1)S(1)}, u32[]{:S(2)}, u32[]{:S(2)}) collective-permute-start(bf16[16,8,128]{2,1,0:T(8,128)(2,1)S(1)} %collective-permute-done.4.refs_3_.refs_7_), channel_id=1, source_target_pairs={{0,1},{1,0},{2,3},{3,2},{4,5},{5,4},{6,7},{7,6},{8,9},{9,8},{10,11... | collective-permute-start | bytes 98312 | tf_op jit(solution)/shard_map/ppermute | solution.py:427
  18.7 1.5 %collective-permute-start.8 = (bf16[528,128]{1,0:T(8,128)(2,1)S(1)}, bf16[528,128]{1,0:T(8,128)(2,1)S(1)}, u32[]{:S(2)}, u32[]{:S(2)}) collective-permute-start(bf16[528,128]{1,0:T(8,128)(2,1)S(1)} %get-tuple-element.51), channel_id=1, source_target_pairs={{0,1},{1,0},{2,3},{3,2},{4,5},{5,4},{6,7},{7,6},{8,9},{9,8},{10,11... | collective-permute-start | bytes 405512 | tf_op jit(solution)/shard_map/ppermute | solution.py:427
  19.0 1.2 %collective-permute-start.7 = (bf16[192,128]{1,0:T(8,128)(2,1)S(1)}, bf16[192,128]{1,0:T(8,128)(2,1)S(1)}, u32[]{:S(2)}, u32[]{:S(2)}) collective-permute-start(bf16[192,128]{1,0:T(8,128)(2,1)S(1)} %get-tuple-element.50), channel_id=1, source_target_pairs={{0,1},{1,0},{2,3},{3,2},{4,5},{5,4},{6,7},{7,6},{8,9},{9,8},{10,11... | collective-permute-start | bytes 147464 | tf_op jit(solution)/shard_map/ppermute | solution.py:427
  20.6 6.1 %collective-permute-start.10 = (bf16[160,128]{1,0:T(8,128)(2,1)S(1)}, bf16[160,128]{1,0:T(8,128)(2,1)S(1)}, u32[]{:S(2)}, u32[]{:S(2)}) collective-permute-start(bf16[160,128]{1,0:T(8,128)(2,1)S(1)} %get-tuple-element.54), channel_id=1, source_target_pairs={{0,8},{1,11},{2,10},{3,9},{4,12},{5,15},{6,14},{7,13},{8,0},{9,3},... | collective-permute-start | bytes 122888 | tf_op jit(solution)/shard_map/ppermute | solution.py:427
  23.1 6.2 %collective-permute-start.11 = (bf16[160,128]{1,0:T(8,128)(2,1)S(1)}, bf16[160,128]{1,0:T(8,128)(2,1)S(1)}, u32[]{:S(2)}, u32[]{:S(2)}) collective-permute-start(bf16[160,128]{1,0:T(8,128)(2,1)S(1)} %get-tuple-element.55), channel_id=1, source_target_pairs={{0,12},{1,15},{2,14},{3,13},{4,8},{5,11},{6,10},{7,9},{8,4},{9,7},... | collective-permute-start | bytes 122888 | tf_op jit(solution)/shard_map/ppermute | solution.py:427
  24.4 5.2 %collective-permute-start.12 = (bf16[160,128]{1,0:T(8,128)(2,1)S(1)}, bf16[160,128]{1,0:T(8,128)(2,1)S(1)}, u32[]{:S(2)}, u32[]{:S(2)}) collective-permute-start(bf16[160,128]{1,0:T(8,128)(2,1)S(1)} %get-tuple-element.56), channel_id=1, source_target_pairs={{0,4},{1,7},{2,6},{3,5},{4,0},{5,3},{6,2},{7,1},{8,12},{9,15},{10,... | collective-permute-start | bytes 122888 | tf_op jit(solution)/shard_map/ppermute | solution.py:427
  24.4 5.5 %collective-permute-start.9 = (bf16[96,128]{1,0:T(8,128)(2,1)S(1)}, bf16[96,128]{1,0:T(8,128)(2,1)S(1)}, u32[]{:S(2)}, u32[]{:S(2)}) collective-permute-start(bf16[96,128]{1,0:T(8,128)(2,1)S(1)} %get-tuple-element.53), channel_id=1, source_target_pairs={{0,2},{1,3},{2,0},{3,1},{4,6},{5,7},{6,4},{7,5},{8,10},{9,11},{10,... | collective-permute-start | bytes 73736 | tf_op jit(solution)/shard_map/ppermute | solution.py:427
  26.7 3.2 %collective-permute-start.13 = (bf16[96,128]{1,0:T(8,128)(2,1)S(1)}, bf16[96,128]{1,0:T(8,128)(2,1)S(1)}, u32[]{:S(2)}, u32[]{:S(2)}) collective-permute-start(bf16[96,128]{1,0:T(8,128)(2,1)S(1)} %slice.12), channel_id=1, source_target_pairs={{0,1},{1,0},{2,3},{3,2},{4,5},{5,4},{6,7},{7,6},{8,9},{9,8},{10,11... | collective-permute-start | bytes 73736 | tf_op jit(solution)/shard_map/ppermute | solution.py:427
  29.3 1.2 %collective-permute-start.14 = (bf16[96,128]{1,0:T(8,128)(2,1)S(1)}, bf16[96,128]{1,0:T(8,128)(2,1)S(1)}, u32[]{:S(2)}, u32[]{:S(2)}) collective-permute-start(bf16[96,128]{1,0:T(8,128)(2,1)S(1)} %slice.13), channel_id=1, source_target_pairs={{0,1},{1,0},{2,3},{3,2},{4,5},{5,4},{6,7},{7,6},{8,9},{9,8},{10,11... | collective-permute-start | bytes 73736 | tf_op jit(solution)/shard_map/ppermute | solution.py:427
  29.6 1.2 %collective-permute-start.15 = (bf16[96,128]{1,0:T(8,128)(2,1)S(1)}, bf16[96,128]{1,0:T(8,128)(2,1)S(1)}, u32[]{:S(2)}, u32[]{:S(2)}) collective-permute-start(bf16[96,128]{1,0:T(8,128)(2,1)S(1)} %slice.14), channel_id=1, source_target_pairs={{0,1},{1,0},{2,3},{3,2},{4,5},{5,4},{6,7},{7,6},{8,9},{9,8},{10,11... | collective-permute-start | bytes 73736 | tf_op jit(solution)/shard_map/ppermute | solution.py:427

commit v14 on v13

--- a/solution.py
+++ b/solution.py
@@ -34,16 +34,16 @@
         self.per_head = per_head = lanes // KEY_HEADS
         self.heads, self.chunks = QUERY_HEADS // devices, width // HEAD_WIDTH
         self.single = 1
-        self.pairs = [(m, m + 1) for m in range(2, lanes, 2)]
-        self.pairs[-2:] = self.pairs[:-3:-1]
+        self.pairs = [(m, m + 1) for m in range(lanes - 2, 0, -2)]
+        self.pairs[:2] = self.pairs[1::-1]
         size = self.heads + self.chunks
         self.own = ((0, 0), ((0, 0), (1, 0)))
         self.one = ((self.single,) * 2, ((2, 0), (3, 0)))
         self.mine, self.theirs = [], []
         for k, (a, b) in enumerate(self.pairs):
-            at = 2 * size * k
-            self.mine.append(((a, b), ((4, at), (4, at + size))))
-            self.theirs.append(((b, a), ((5, at + size), (5, at))))
+            at = size + 2 * size * k
+            self.mine.append(((a, b), ((2, at), (2, at + size))))
+            self.theirs.append(((b, a), ((3, at + size), (3, at))))
 
     def head_masks(self, unit):
         return tuple(mask // self.per_head for mask in unit[0][0])
@@ -116,6 +116,15 @@
     return total
 
 
+def tiles_of(refs, requests, out_ref, at):
+    for ref in refs:
+        rows = jnp.concatenate([ref[b].astype(jnp.float32) for b in range(requests)], axis=0)
+        for c in range(rows.shape[1] // HEAD_WIDTH):
+            tile = rows[:, c * HEAD_WIDTH : (c + 1) * HEAD_WIDTH]
+            out_ref[at] = tile.astype(jnp.bfloat16)
+            at += 1
+
+
 def pack_kernel(requests, query_ref, hidden_ref, own_ref, query_buf, hidden_buf, sems):
     loads = [
         pltpu.make_async_copy(query_ref, query_buf, sems.at[0]),
@@ -123,14 +132,16 @@
     ]
     for load in loads:
         load.start()
-    at = 0
-    for load, ref in zip(loads, (query_buf, hidden_buf)):
+    for load in loads:
         load.wait()
-        rows = jnp.concatenate([ref[b].astype(jnp.float32) for b in range(requests)], axis=0)
-        for c in range(rows.shape[1] // HEAD_WIDTH):
-            tile = rows[:, c * HEAD_WIDTH : (c + 1) * HEAD_WIDTH]
-            own_ref[at] = tile.astype(jnp.bfloat16)
-            at += 1
+    tiles_of((query_buf, hidden_buf), requests, own_ref, 0)
+
+
+def pack_other_kernel(requests, own_ref, query_ref, hidden_ref, other_ref, both_ref):
+    size = own_ref.shape[0]
+    both_ref[:size] = own_ref[...]
+    tiles_of((query_ref, hidden_ref), requests, both_ref, size)
+    other_ref[...] = both_ref[size:]
 
 
 def base_kernel(heads, sources, index_ref, own_ref, weight_ref, down_ref, *refs):
@@ -159,7 +170,7 @@
         load.wait()
 
 
-def attend(sizes, plan, keep, index_ref, length_ref, arrays, key_ref, value_ref, put):
+def attend(sizes, plan, keep, numbers, index_ref, length_ref, arrays, key_ref, value_ref, put):
     requests, tokens, devices = sizes
     here = index_ref[0]
     chip = here // 2
@@ -176,7 +187,8 @@
         place_request == (column // tokens) % requests
     )
     peaks, totals = [], []
-    for number, runs in enumerate(plan.attention_chunks(slot_rows, keep)):
+    chunks = plan.attention_chunks(slot_rows, keep)
+    for number, runs in enumerate(chunks[i] for i in numbers):
         places = [slot[1][side] for run in runs for slot, side in run]
         query = jnp.concatenate(
             [arrays[array][tile + h] for array, tile in places for h in range(plan.heads)], axis=0
@@ -211,8 +223,8 @@
 
 
 def send_kernel(sizes, plan, *refs):
-    (index_ref, length_ref, adapter_ref, rank_ref, pool_ref, *arrays) = refs[:-9]
-    (key_ref, value_ref, base_ref, up_ref, *halves, send_ref, own_ref, parts_ref) = refs[-9:]
+    (index_ref, length_ref, adapter_ref, rank_ref, pool_ref, *arrays) = refs[:-8]
+    (key_ref, value_ref, base_ref, up_ref, *halves, send_ref, own_ref) = refs[-8:]
     requests, tokens, devices = sizes
 
     def put(chunk, row, mix):
@@ -220,11 +232,11 @@
         send_ref[at : at + mix.shape[0]] = mix.astype(jnp.bfloat16)
 
     peaks, totals = attend(
-        sizes, plan, False, index_ref, length_ref, arrays, key_ref, value_ref, put
+        sizes, plan, False, range(CHUNKS), index_ref, length_ref, arrays, key_ref, value_ref, put
     )
     highs = [round_bf16(total) for total in totals]
     lows = [total - high for total, high in zip(totals, highs)]
-    send_ref[MIX_ROWS:] = rows_of(peaks + highs + lows, STAT_ROWS).astype(jnp.bfloat16)
+    send_ref[-STAT_ROWS:] = rows_of(peaks + highs + lows, STAT_ROWS).astype(jnp.bfloat16)
 
     rows = requests * tokens
     lowered = lower(sources_of(plan), arrays, halves)
@@ -251,28 +263,30 @@
     own_ref[0] = keys
     own_ref[1] = values
     high = keys.astype(jnp.bfloat16)
-    parts_ref[:step] = high
-    parts_ref[step : 2 * step] = (keys - high.astype(jnp.float32)).astype(jnp.bfloat16)
-    parts_ref[2 * step :] = values.astype(jnp.bfloat16)
-
-
-def keep_kernel(sizes, plan, *refs):
-    (index_ref, length_ref, own_ref, one_ref, pairs_ref) = refs[:5]
-    (key_ref, value_ref, mix_ref, stat_ref) = refs[5:]
-    arrays = {0: own_ref, 2: one_ref, 4: pairs_ref}
+    send_ref[MIX_ROWS : MIX_ROWS + step] = high
+    send_ref[MIX_ROWS + step : MIX_ROWS + 2 * step] = (keys - high.astype(jnp.float32)).astype(
+        jnp.bfloat16
+    )
+    send_ref[MIX_ROWS + 2 * step : MIX_ROWS + 3 * step] = values.astype(jnp.bfloat16)
+
+
+def keep_kernel(sizes, plan, numbers, *refs):
+    (index_ref, length_ref, own_ref, near_ref, key_ref, value_ref, mix_ref, stat_ref) = refs
+    arrays = {0: own_ref, 2: near_ref}
 
     def put(chunk, row, mix):
         at = chunk * 128 + row
         mix_ref[at : at + mix.shape[0]] = mix
 
     peaks, totals = attend(
-        sizes, plan, True, index_ref, length_ref, arrays, key_ref, value_ref, put
+        sizes, plan, True, numbers, index_ref, length_ref, arrays, key_ref, value_ref, put
     )
     stat_ref[...] = rows_of(peaks + totals, 8)
 
 
-def join_kernel(sizes, plan, index_ref, mix_ref, stat_ref, proj_ref, got_parts_ref, got_ref, *refs):
-    packet_refs, tail_ref = refs[:-1], refs[-1]
+def join_kernel(sizes, plan, index_ref, *refs):
+    mix_refs, stat_refs, (proj_ref, got_ref) = refs[:2], refs[2:4], refs[4:6]
+    packet_refs, tail_ref = refs[6:-1], refs[-1]
     requests, tokens, devices = sizes
     here = index_ref[0]
     chip = here // 2
@@ -280,22 +294,24 @@
     rows = requests * tokens
     slot_rows = plan.heads * rows
     step = KEY_HEADS * rows
-    got = got_ref[MIX_ROWS:].astype(jnp.float32)
-    own = stat_ref[...]
-    own_peak, got_peak = own[:CHUNKS], got[:CHUNKS]
+    got = got_ref[MIX_ROWS + 3 * step :].astype(jnp.float32)
+    half = CHUNKS // 2
+    own_peak = jnp.concatenate([ref[:half] for ref in stat_refs], axis=0)
+    own_total = jnp.concatenate([ref[half : 2 * half] for ref in stat_refs], axis=0)
+    got_peak = got[:CHUNKS]
     peak = jnp.maximum(own_peak, got_peak)
     own_factor = jnp.exp(own_peak - peak)
     got_factor = jnp.exp(got_peak - peak)
-    total = own_factor * own[CHUNKS : 2 * CHUNKS] + got_factor * (
+    total = own_factor * own_total + got_factor * (
         got[CHUNKS : 2 * CHUNKS] + got[2 * CHUNKS : 3 * CHUNKS]
     )
     high = round_bf16(total)
     low = total - high
     filler = jnp.zeros((128 - 2 * CHUNKS, 128), jnp.float32)
     table = jnp.transpose(jnp.concatenate([own_factor, got_factor, filler], axis=0))
-    keys = proj_ref[0] + got_parts_ref[:step].astype(jnp.float32)
-    keys += got_parts_ref[step : 2 * step].astype(jnp.float32)
-    values = proj_ref[1] + got_parts_ref[2 * step :].astype(jnp.float32)
+    parts = got_ref[MIX_ROWS : MIX_ROWS + 3 * step].astype(jnp.float32)
+    keys = proj_ref[0] + parts[:step] + parts[step : 2 * step]
+    values = proj_ref[1] + parts[2 * step :]
     keys_high = round_bf16(keys)
     for j in range(KEY_HEADS):
         part = slice(j * rows, (j + 1) * rows)
@@ -306,7 +322,8 @@
     packet = {id(slot): ref for slot, ref in zip([plan.own, plan.one] + plan.mine, packet_refs)}
     for c, runs in enumerate(plan.attention_chunks(slot_rows, True)):
         span = slice(c * 128, c * 128 + 128)
-        mix = mix_ref[span] * table[:, c : c + 1]
+        at = c % half * 128
+        mix = mix_refs[c // half][at : at + 128] * table[:, c : c + 1]
         mix += got_ref[span].astype(jnp.float32) * table[:, CHUNKS + c : CHUNKS + c + 1]
         stats = jnp.where(
             stat_row == 0,
@@ -477,10 +494,21 @@
         "pack",
     )
     flat = requests * cached_key_rows.shape[1]
-    one = trade(own, devices, plan.single, plan.single)
-    other, late_own, late_lengths = lax.optimization_barrier((core_swap(own), own, lengths))
-    both = jnp.concatenate([own, other], axis=0)
+    other_queries, other_hidden = core_swap(queries), core_swap(hidden)
+    other_queries, late_own, late_lengths = lax.optimization_barrier((other_queries, own, lengths))
+    shape = (heads + chunks, rows, HEAD_WIDTH)
+    other, both = call(
+        functools.partial(pack_other_kernel, requests),
+        (late_own, other_queries, other_hidden),
+        [vmem()] * 3,
+        [pltpu.VMEM(shape, jnp.bfloat16), pltpu.VMEM((2 * shape[0],) + shape[1:], jnp.bfloat16)],
+        [],
+        "pack_other",
+    )
+    both, late_own = lax.optimization_barrier((both, late_own))
+    one = trade(late_own, devices, plan.single, plan.single)
     mine = [trade(both, devices, a, b) for a, b in plan.pairs]
+    flat = requests * cached_key_rows.shape[1]
 
     out_width = key_value_weight.shape[1]
     parts = 4 if width % (4 * HEAD_WIDTH) == 0 else 1
@@ -506,50 +534,53 @@
         "base",
     )
     cosine, sine = rotation(late_lengths, tokens)
-    mine = jnp.concatenate(mine, axis=0)
-    mine, one, base, cosine, sine = lax.optimization_barrier((mine, one, base, cosine, sine))
-    other_one, other_mine = core_swap(one), core_swap(mine)
-    mix, stats = call(
-        functools.partial(keep_kernel, sizes, plan),
-        (index, lengths, own, one, mine, keys, values),
-        [smem()] * 2 + [vmem()] * 5,
-        [
-            pltpu.VMEM((MIX_ROWS, HEAD_WIDTH), jnp.float32),
-            pltpu.VMEM((8, HEAD_WIDTH), jnp.float32),
-        ],
-        [],
-        "keep_states",
-    )
-    other_mine, mix = lax.optimization_barrier((other_mine, mix))
-    arrays = (own, other, one, other_one, mine, other_mine)
+    near = jnp.concatenate([one] + mine, axis=0)
+    near, base, cosine, sine = lax.optimization_barrier((near, base, cosine, sine))
+    other_near = core_swap(near)
+
+    def keep(numbers):
+        return call(
+            functools.partial(keep_kernel, sizes, plan, numbers),
+            (index, lengths, own, near, keys, values),
+            [smem()] * 2 + [vmem()] * 4,
+            [
+                pltpu.VMEM((MIX_ROWS // 2, HEAD_WIDTH), jnp.float32),
+                pltpu.VMEM((8, HEAD_WIDTH), jnp.float32),
+            ],
+            [],
+            "keep_states",
+        )
+
+    first_mix, first_stats = keep(range(CHUNKS // 2))
+    other_near, first_mix = lax.optimization_barrier((other_near, first_mix))
+    arrays = (own, other, near, other_near)
     step = KEY_HEADS * rows
-    send, proj, proj_parts = call(
+    send, proj = call(
         functools.partial(send_kernel, sizes, plan),
         (index, lengths, request_adapter, adapter_rank_list, adapter_pool_row)
         + arrays
         + (keys, values, base, up, *halves),
         [smem()] * 5 + [vmem()] * (len(arrays) + 6),
         [
-            pltpu.VMEM((MIX_ROWS + STAT_ROWS, HEAD_WIDTH), jnp.bfloat16),
+            pltpu.VMEM((MIX_ROWS + 3 * step + STAT_ROWS, HEAD_WIDTH), jnp.bfloat16),
             pltpu.VMEM((2, step, HEAD_WIDTH), jnp.float32),
-            pltpu.VMEM((3 * step, HEAD_WIDTH), jnp.bfloat16),
         ],
         [],
         "send_states",
     )
-    got_parts = core_swap(proj_parts)
     got = core_swap(send)
+    second_mix, second_stats = keep(range(CHUNKS // 2, CHUNKS))
     packets = call(
         functools.partial(join_kernel, sizes, plan),
-        (index, mix, stats, proj, got_parts, got),
-        [smem()] + [vmem()] * 5,
+        (index, first_mix, second_mix, first_stats, second_stats, proj, got),
+        [smem()] + [vmem()] * 6,
         [pltpu.VMEM((slot_rows + 4 * rows, HEAD_WIDTH), jnp.bfloat16)] * 2
         + [pltpu.VMEM((2 * slot_rows + 4 * rows, HEAD_WIDTH), jnp.bfloat16)] * len(plan.pairs),
         [pltpu.VMEM((KEY_HEADS, 3 * rows, HEAD_WIDTH), jnp.float32)],
         "join",
     )
     heard = [packets[0], trade(packets[1], devices, plan.single, plan.single)]
-    heard += [trade(x, devices, a, b) for x, (a, b) in zip(packets[:1:-1], plan.pairs[::-1])]
+    heard += [trade(x, devices, a, b) for x, (a, b) in zip(packets[2:], plan.pairs)]
     heard += [core_swap(x[slot_rows:]) for x in heard[2:]]
     return pl.pallas_call(
         functools.partial(merge_kernel, devices, requests, tokens, 2 + len(plan.pairs)),

time: 32.3 us -> 32.1 us (level)
  waiting for transfers between devices: 7.13 us -> 4.93 us
  starting transfers between devices: 13.5 us -> 14.5 us
  Pallas kernels: 10.1 us -> 11 us
    ppermute x16 -> x15, waiting for transfers between devices: 7.13 us -> 4.93 us  [trade(): return lax.ppermute(x, 'tensor', pairs)]
    ppermute x16 -> x15, starting transfers between devices: 13.5 us -> 14.5 us  [trade(): return lax.ppermute(x, 'tensor', pairs)]
    pallas_call x5 -> x7, Pallas kernels: 8.98 us -> 9.92 us  [call(): pl.pallas_call(kernel, out_shape=tuple(out_shape), in_specs=in_specs, out...]
  transfers between devices with their start and end apart: 16 -> 15, of which waited for: 8 -> 5; matrix products, arithmetic and copies ran while one was open for 3% -> 3% of each run, Pallas kernels for 17% -> 23%
where the time goes in v14:
time: 32.1 us; the launch traced here: 31.7 us
  starting transfers between devices  14.5 us (45%)
  Pallas kernels  11 us (34%)
  waiting for transfers between devices  4.93 us (15%)
  other arithmetic  0.96 us (3%)
    ppermute x15, starting transfers between devices, trade(): return lax.ppermute(x, 'tensor', pairs)  14.5 us
    pallas_call x7, Pallas kernels, call(): pl.pallas_call(kernel, out_shape=tuple(out_shape), in_specs=in_specs, out...  9.92 us
    ppermute x15, waiting for transfers between devices, trade(): return lax.ppermute(x, 'tensor', pairs)  4.93 us
    pallas_call x1, Pallas kernels, per_device(): pl.pallas_call(functools.partial(merge_kernel, devices, requests, tokens,...  1.13 us
    convert_element_type x1, other arithmetic, rotation(): (lengths[:, None] + jnp.arange(tokens, dtype=jnp.int32)[None, :]).astype(...  0.73 us
  transfers between devices with their start and end apart: 15, of which 5 were waited for; matrix products, arithmetic and copies ran while one was open for 3% of the time, Pallas kernels for 23%

profile of v14, /device:TPU:0, one launch (start us, length us, event | category | flops | bytes accessed | tf_op | source)
XLA Modules:
  0.0 31.7 jit_solution(3958426602604031610)
XLA Ops:
  0.0 0.5 %collective-permute-start = (bf16[2,4,1024]{2,1,0:T(4,128)(2,1)}, bf16[2,4,1024]{2,1,0:T(4,128)(2,1)S(1)}, u32[]{:S(2)}, u32[]{:S(2)}) collective-permute-start(bf16[2,4,1024]{2,1,0:T(4,128)(2,1)} %query_ref.1), channel_id=1, source_target_pairs={{0,1},{1,0},{2,3},{3,2},{4,5},{5,4},{6,7},{7,6},{8,9},{9,8},{10,11... | collective-permute-start | bytes 49160 | tf_op jit(solution)/shard_map/ppermute | solution.py:444
  0.5 0.1 collective-permute-start.1
  0.5 0.8 %pack.1.own_ref.refs_2_.refs_5_ = bf16[16,8,128]{2,1,0:T(8,128)(2,1)S(1)} custom-call(bf16[2,4,1024]{2,1,0:T(4,128)(2,1)} %query_ref.1, bf16[2,4,1024]{2,1,0:T(4,128)(2,1)} %hidden_ref.1), custom_call_target="tpu_custom_call" | custom-call | flops 1000000 | tf_op jit(solution)/shard_map/pack/pallas_call | solution.py:470
  1.3 0.2 collective-permute-done.query_ref
  1.5 0.3 %collective-permute-done.1.hidden_ref = bf16[2,4,1024]{2,1,0:T(4,128)(2,1)S(1)} collective-permute-done((bf16[2,4,1024]{2,1,0:T(4,128)(2,1)}, bf16[2,4,1024]{2,1,0:T(4,128)(2,1)S(1)}, u32[]{:S(2)}, u32[]{:S(2)}) %collective-permute-start.1) | collective-permute-done | bytes 16416 | tf_op jit(solution)/shard_map/ppermute | solution.py:444
  1.9 3.8 %collective-permute-start.3 = (bf16[32,8,128]{2,1,0:T(8,128)(2,1)S(1)}, bf16[32,8,128]{2,1,0:T(8,128)(2,1)S(1)}, u32[]{:S(2)}, u32[]{:S(2)}) collective-permute-start(bf16[32,8,128]{2,1,0:T(8,128)(2,1)S(1)} %get-tuple-element.39), channel_id=1, source_target_pairs={{0,8},{1,11},{2,10},{3,9},{4,12},{5,15},{6,14},{7,13},{8,0},{9,3},... | collective-permute-start | bytes 196616 | tf_op jit(solution)/shard_map/ppermute | solution.py:444
  5.7 1.3 %collective-permute-start.4 = (bf16[32,8,128]{2,1,0:T(8,128)(2,1)S(1)}, bf16[32,8,128]{2,1,0:T(8,128)(2,1)S(1)}, u32[]{:S(2)}, u32[]{:S(2)}) collective-permute-start(bf16[32,8,128]{2,1,0:T(8,128)(2,1)S(1)} %get-tuple-element.39), channel_id=1, source_target_pairs={{0,12},{1,15},{2,14},{3,13},{4,8},{5,11},{6,10},{7,9},{8,4},{9,7},... | collective-permute-start | bytes 196616 | tf_op jit(solution)/shard_map/ppermute | solution.py:444
  7.0 0.2 collective-permute-start.5
  7.3 1.5 %collective-permute-start.2 = (bf16[16,8,128]{2,1,0:T(8,128)(2,1)S(1)}, bf16[16,8,128]{2,1,0:T(8,128)(2,1)S(1)}, u32[]{:S(2)}, u32[]{:S(2)}) collective-permute-start(bf16[16,8,128]{2,1,0:T(8,128)(2,1)S(1)} %pack.1.own_ref.refs_2_.refs_5_), channel_id=1, source_target_pairs={{0,2},{1,3},{2,0},{3,1},{4,6},{5,7},{6,4},{7,5},{8,10},{9,11},{10,... | collective-permute-start | bytes 98312 | tf_op jit(solution)/shard_map/ppermute | solution.py:444
  8.8 0.7 %add_convert_fusion = f32[2,4]{1,0:T(2,128)S(1)} fusion(s32[2]{0:T(128)} %refs_1_.5), kind=kLoop, calls=%fused_computation.5 | loop fusion | flops 16 | bytes 40 | tf_op jit(solution)/shard_map/convert_element_type | solution.py:413
  9.5 0.1 convert_element_type.11
  9.6 0.1 fusion
  9.7 0.1 pad_maximum_fusion.1
  9.8 0.0 copy-start.3
  9.8 4.1 %base.1 = (f32[8,2048]{1,0:T(8,128)S(1)}, bf16[256,1024]{1,0:T(8,128)(2,1)S(1)}, bf16[256,1024]{1,0:T(8,128)(2,1)S(1)}, bf16[128,2048]{1,0:T(8,128)(2,1)S(1)}, b...) custom-call(s32[1]{0:T(128)} %bitcast.index_ref.refs_0_, ...), custom_call_target="tpu_custom_call" | custom-call | flops 1000000 | tf_op jit(solution)/shard_map/base/pallas_call | solution.py:470
  13.9 0.0 collective-permute-done.4
  13.9 0.5 %collective-permute-start.6 = (bf16[112,8,128]{2,1,0:T(8,128)(2,1)S(1)}, bf16[112,8,128]{2,1,0:T(8,128)(2,1)S(1)}, u32[]{:S(2)}, u32[]{:S(2)}) collective-permute-start(bf16[112,8,128]{2,1,0:T(8,128)(2,1)S(1)} %pad_maximum_fusion.refs_3_.refs_7_), channel_id=1, source_target_pairs={{0,1},{1,0},{2,3},{3,2},{4,5},{5,4},{6,7},{7,6},{8,9},{9,8},{10,11... | collective-permute-start | bytes 688136 | tf_op jit(solution)/shard_map/ppermute | solution.py:444
  14.4 1.2 %keep_states.2 = (f32[256,128]{1,0:T(8,128)S(1)}, f32[8,128]{1,0:T(8,128)S(1)}) custom-call(s32[1]{0:T(128)} %bitcast.index_ref.refs_0_, s32[2]{0:T(128)S(1)} %copy-done, bf16[16,8,128]{2,1,0:T(8,128)(2,1)S(1)} %pack.1.own_ref.refs_2_.refs_5_, bf16[112,8,128]{2,1,0:T(8,128)(2,1)S(1)} %pad_maximum_fusion.refs_3_.refs_7_, ...), custom_call_target="tpu_custom_call" | custom-call | flops 1000000 | tf_op jit(solution)/shard_map/keep_states/pallas_call | solution.py:470
  15.7 2.3 %send_states.1 = (bf16[720,128]{1,0:T(8,128)(2,1)S(1)}, f32[2,64,128]{2,1,0:T(8,128)S(1)}) custom-call(s32[1]{0:T(128)} %bitcast.index_ref.refs_0_, s32[2]{0:T(128)S(1)} %copy-done, s32[2]{0:T(128)S(1)} %copy-done.1, s32[16]{0:T(128)S(1)} %copy-done.2, s32[16]{0:T(128)S(1)} %copy-done.3, bf16[16,8,128]{2,1,0:T(8,128)(2,1)S(1)} %pack.1.own_ref.refs_2_.refs_5_, ...), custom_call_target="tpu_custom_call" | custom-call | flops 1000000 | tf_op jit(solution)/shard_map/send_states/pallas_call | solution.py:470
  18.0 0.3 collective-permute-start.7
  18.3 1.2 %keep_states.3 = (f32[256,128]{1,0:T(8,128)S(1)}, f32[8,128]{1,0:T(8,128)S(1)}) custom-call(s32[1]{0:T(128)} %bitcast.index_ref.refs_0_, s32[2]{0:T(128)S(1)} %copy-done, bf16[16,8,128]{2,1,0:T(8,128)(2,1)S(1)} %pack.1.own_ref.refs_2_.refs_5_, bf16[112,8,128]{2,1,0:T(8,128)(2,1)S(1)} %pad_maximum_fusion.refs_3_.refs_7_, ...), custom_call_target="tpu_custom_call" | custom-call | flops 1000000 | tf_op jit(solution)/shard_map/keep_states/pallas_call | solution.py:470
  19.5 0.3 %join.1 = (bf16[96,128]{1,0:T(8,128)(2,1)S(1)}, bf16[96,128]{1,0:T(8,128)(2,1)S(1)}, bf16[160,128]{1,0:T(8,128)(2,1)S(1)}, bf16[160,128]{1,0:T(8,128)(2,1)S(1)}, bf16[160,128]{1,0:T(8,128)(2,1)S(1)}) custom-call(s32[1]{0:T(128)} %bitcast.index_ref.refs_0_, f32[256,128]{1,0:T(8,128)S(1)} %get-tuple-element.48.refs_0_, ...), custom_call_target="tpu_custom_call" | custom-call | flops 1000000 | tf_op jit(solution)/shard_map/join/pallas_call | solution.py:470
  19.8 2.8 %collective-permute-start.9 = (bf16[160,128]{1,0:T(8,128)(2,1)S(1)}, bf16[160,128]{1,0:T(8,128)(2,1)S(1)}, u32[]{:S(2)}, u32[]{:S(2)}) collective-permute-start(bf16[160,128]{1,0:T(8,128)(2,1)S(1)} %get-tuple-element.62), channel_id=1, source_target_pairs={{0,8},{1,11},{2,10},{3,9},{4,12},{5,15},{6,14},{7,13},{8,0},{9,3},... | collective-permute-start | bytes 122888 | tf_op jit(solution)/shard_map/ppermute | solution.py:444
  22.6 1.3 %collective-permute-start.10 = (bf16[160,128]{1,0:T(8,128)(2,1)S(1)}, bf16[160,128]{1,0:T(8,128)(2,1)S(1)}, u32[]{:S(2)}, u32[]{:S(2)}) collective-permute-start(bf16[160,128]{1,0:T(8,128)(2,1)S(1)} %get-tuple-element.63), channel_id=1, source_target_pairs={{0,12},{1,15},{2,14},{3,13},{4,8},{5,11},{6,10},{7,9},{8,4},{9,7},... | collective-permute-start | bytes 122888 | tf_op jit(solution)/shard_map/ppermute | solution.py:444
  24.0 1.3 %collective-permute-start.8 = (bf16[96,128]{1,0:T(8,128)(2,1)S(1)}, bf16[96,128]{1,0:T(8,128)(2,1)S(1)}, u32[]{:S(2)}, u32[]{:S(2)}) collective-permute-start(bf16[96,128]{1,0:T(8,128)(2,1)S(1)} %get-tuple-element.61), channel_id=1, source_target_pairs={{0,2},{1,3},{2,0},{3,1},{4,6},{5,7},{6,4},{7,5},{8,10},{9,11},{10,... | collective-permute-start | bytes 73736 | tf_op jit(solution)/shard_map/ppermute | solution.py:444
  25.2 0.4 %collective-permute-start.12 = (bf16[96,128]{1,0:T(8,128)(2,1)S(1)}, bf16[96,128]{1,0:T(8,128)(2,1)S(1)}, u32[]{:S(2)}, u32[]{:S(2)}) collective-permute-start(bf16[96,128]{1,0:T(8,128)(2,1)S(1)} %slice.12), channel_id=1, source_target_pairs={{0,1},{1,0},{2,3},{3,2},{4,5},{5,4},{6,7},{7,6},{8,9},{9,8},{10,11... | collective-permute-start | bytes 73736 | tf_op jit(solution)/shard_map/ppermute | solution.py:444
  25.6 3.2 %collective-permute-done.10.refs_3_ = bf16[160,128]{1,0:T(8,128)(2,1)S(1)} collective-permute-done((bf16[160,128]{1,0:T(8,128)(2,1)S(1)}, bf16[160,128]{1,0:T(8,128)(2,1)S(1)}, u32[]{:S(2)}, u32[]{:S(2)}) %collective-permute-start.10) | collective-permute-done | bytes 40992 | tf_op jit(solution)/shard_map/ppermute | solution.py:444
  28.8 0.5 %collective-permute-start.13 = (bf16[96,128]{1,0:T(8,128)(2,1)S(1)}, bf16[96,128]{1,0:T(8,128)(2,1)S(1)}, u32[]{:S(2)}, u32[]{:S(2)}) collective-permute-start(bf16[96,128]{1,0:T(8,128)(2,1)S(1)} %slice.13), channel_id=1, source_target_pairs={{0,1},{1,0},{2,3},{3,2},{4,5},{5,4},{6,7},{7,6},{8,9},{9,8},{10,11... | collective-permute-start | bytes 73736 | tf_op jit(solution)/shard_map/ppermute | solution.py:444
  29.4 0.1 collective-permute-start.14
  29.5 0.8 %collective-permute-done.13.refs_6_ = bf16[96,128]{1,0:T(8,128)(2,1)S(1)} collective-permute-done((bf16[96,128]{1,0:T(8,128)(2,1)S(1)}, bf16[96,128]{1,0:T(8,128)(2,1)S(1)}, u32[]{:S(2)}, u32[]{:S(2)}) %collective-permute-start.13) | collective-permute-done | bytes 24608 | tf_op jit(solution)/shard_map/ppermute | solution.py:444
  30.2 0.4 %collective-permute-done.14.refs_7_ = bf16[96,128]{1,0:T(8,128)(2,1)S(1)} collective-permute-done((bf16[96,128]{1,0:T(8,128)(2,1)S(1)}, bf16[96,128]{1,0:T(8,128)(2,1)S(1)}, u32[]{:S(2)}, u32[]{:S(2)}) %collective-permute-start.14) | collective-permute-done | bytes 24608 | tf_op jit(solution)/shard_map/ppermute | solution.py:444
  30.6 1.1 %merge_states.1 = bf16[2,4,1024]{2,1,0:T(4,128)(2,1)} custom-call(bf16[16,8,128]{2,1,0:T(8,128)(2,1)S(1)} %pack.1.own_ref.refs_2_.refs_5_, f32[8,128]{1,0:T(8,128)S(1)} %get-tuple-element.42.cos_ref, f32[8,128]{1,0:T(8,128)S(1)} %get-tuple-element.43.sin_ref, bf16[96,128]{1,0:T(8,128)(2,1)S(1)} %get-tuple-element.60.refs_0_, ...), custom_call_target="tpu_custom_call" | custom-call | tf_op jit(solution)/shard_map/merge_states/pallas_call | solution.py:585
  (23 shorter events, 0.1 us)
Async XLA Ops:
  0.0 1.5 %collective-permute-start = (bf16[2,4,1024]{2,1,0:T(4,128)(2,1)}, bf16[2,4,1024]{2,1,0:T(4,128)(2,1)S(1)}, u32[]{:S(2)}, u32[]{:S(2)}) collective-permute-start(bf16[2,4,1024]{2,1,0:T(4,128)(2,1)} %query_ref.1), channel_id=1, source_target_pairs={{0,1},{1,0},{2,3},{3,2},{4,5},{5,4},{6,7},{7,6},{8,9},{9,8},{10,11... | collective-permute-start | bytes 49160 | tf_op jit(solution)/shard_map/ppermute | solution.py:444
  0.5 1.4 %collective-permute-start.1 = (bf16[2,4,1024]{2,1,0:T(4,128)(2,1)}, bf16[2,4,1024]{2,1,0:T(4,128)(2,1)S(1)}, u32[]{:S(2)}, u32[]{:S(2)}) collective-permute-start(bf16[2,4,1024]{2,1,0:T(4,128)(2,1)} %hidden_ref.1), channel_id=1, source_target_pairs={{0,1},{1,0},{2,3},{3,2},{4,5},{5,4},{6,7},{7,6},{8,9},{9,8},{10,11... | collective-permute-start | bytes 49160 | tf_op jit(solution)/shard_map/ppermute | solution.py:444
  1.9 12.0 %collective-permute-start.3 = (bf16[32,8,128]{2,1,0:T(8,128)(2,1)S(1)}, bf16[32,8,128]{2,1,0:T(8,128)(2,1)S(1)}, u32[]{:S(2)}, u32[]{:S(2)}) collective-permute-start(bf16[32,8,128]{2,1,0:T(8,128)(2,1)S(1)} %get-tuple-element.39), channel_id=1, source_target_pairs={{0,8},{1,11},{2,10},{3,9},{4,12},{5,15},{6,14},{7,13},{8,0},{9,3},... | collective-permute-start | bytes 196616 | tf_op jit(solution)/shard_map/ppermute | solution.py:444
  5.7 8.2 %collective-permute-start.4 = (bf16[32,8,128]{2,1,0:T(8,128)(2,1)S(1)}, bf16[32,8,128]{2,1,0:T(8,128)(2,1)S(1)}, u32[]{:S(2)}, u32[]{:S(2)}) collective-permute-start(bf16[32,8,128]{2,1,0:T(8,128)(2,1)S(1)} %get-tuple-element.39), channel_id=1, source_target_pairs={{0,12},{1,15},{2,14},{3,13},{4,8},{5,11},{6,10},{7,9},{8,4},{9,7},... | collective-permute-start | bytes 196616 | tf_op jit(solution)/shard_map/ppermute | solution.py:444
  7.0 6.9 %collective-permute-start.5 = (bf16[32,8,128]{2,1,0:T(8,128)(2,1)S(1)}, bf16[32,8,128]{2,1,0:T(8,128)(2,1)S(1)}, u32[]{:S(2)}, u32[]{:S(2)}) collective-permute-start(bf16[32,8,128]{2,1,0:T(8,128)(2,1)S(1)} %get-tuple-element.39), channel_id=1, source_target_pairs={{0,4},{1,7},{2,6},{3,5},{4,0},{5,3},{6,2},{7,1},{8,12},{9,15},{10,... | collective-permute-start | bytes 196616 | tf_op jit(solution)/shard_map/ppermute | solution.py:444
  7.3 6.6 %collective-permute-start.2 = (bf16[16,8,128]{2,1,0:T(8,128)(2,1)S(1)}, bf16[16,8,128]{2,1,0:T(8,128)(2,1)S(1)}, u32[]{:S(2)}, u32[]{:S(2)}) collective-permute-start(bf16[16,8,128]{2,1,0:T(8,128)(2,1)S(1)} %pack.1.own_ref.refs_2_.refs_5_), channel_id=1, source_target_pairs={{0,2},{1,3},{2,0},{3,1},{4,6},{5,7},{6,4},{7,5},{8,10},{9,11},{10,... | collective-permute-start | bytes 98312 | tf_op jit(solution)/shard_map/ppermute | solution.py:444
  9.8 4.6 %copy-start = (s32[2]{0:T(128)S(1)}, s32[2]{0:T(128)}, u32[]{:S(2)}) copy-start(s32[2]{0:T(128)} %refs_1_.5) | copy-start | bytes 28
  9.8 5.9 %copy-start.1 = (s32[2]{0:T(128)S(1)}, s32[2]{0:T(128)}, u32[]{:S(2)}) copy-start(s32[2]{0:T(128)} %refs_2_.1) | copy-start | bytes 28
  9.8 5.9 %copy-start.2 = (s32[16]{0:T(128)S(1)}, s32[16]{0:T(128)}, u32[]{:S(2)}) copy-start(s32[16]{0:T(128)} %refs_3_.1) | copy-start | bytes 196
  9.8 5.9 %copy-start.3 = (s32[16]{0:T(128)S(1)}, s32[16]{0:T(128)}, u32[]{:S(2)}) copy-start(s32[16]{0:T(128)} %refs_4_.1) | copy-start | bytes 196
  13.9 1.7 %collective-permute-start.6 = (bf16[112,8,128]{2,1,0:T(8,128)(2,1)S(1)}, bf16[112,8,128]{2,1,0:T(8,128)(2,1)S(1)}, u32[]{:S(2)}, u32[]{:S(2)}) collective-permute-start(bf16[112,8,128]{2,1,0:T(8,128)(2,1)S(1)} %pad_maximum_fusion.refs_3_.refs_7_), channel_id=1, source_target_pairs={{0,1},{1,0},{2,3},{3,2},{4,5},{5,4},{6,7},{7,6},{8,9},{9,8},{10,11... | collective-permute-start | bytes 688136 | tf_op jit(solution)/shard_map/ppermute | solution.py:444
  18.0 1.5 %collective-permute-start.7 = (bf16[720,128]{1,0:T(8,128)(2,1)S(1)}, bf16[720,128]{1,0:T(8,128)(2,1)S(1)}, u32[]{:S(2)}, u32[]{:S(2)}) collective-permute-start(bf16[720,128]{1,0:T(8,128)(2,1)S(1)} %get-tuple-element.59), channel_id=1, source_target_pairs={{0,1},{1,0},{2,3},{3,2},{4,5},{5,4},{6,7},{7,6},{8,9},{9,8},{10,11... | collective-permute-start | bytes 552968 | tf_op jit(solution)/shard_map/ppermute | solution.py:444
  19.8 5.4 %collective-permute-start.9 = (bf16[160,128]{1,0:T(8,128)(2,1)S(1)}, bf16[160,128]{1,0:T(8,128)(2,1)S(1)}, u32[]{:S(2)}, u32[]{:S(2)}) collective-permute-start(bf16[160,128]{1,0:T(8,128)(2,1)S(1)} %get-tuple-element.62), channel_id=1, source_target_pairs={{0,8},{1,11},{2,10},{3,9},{4,12},{5,15},{6,14},{7,13},{8,0},{9,3},... | collective-permute-start | bytes 122888 | tf_op jit(solution)/shard_map/ppermute | solution.py:444
  22.6 6.2 %collective-permute-start.10 = (bf16[160,128]{1,0:T(8,128)(2,1)S(1)}, bf16[160,128]{1,0:T(8,128)(2,1)S(1)}, u32[]{:S(2)}, u32[]{:S(2)}) collective-permute-start(bf16[160,128]{1,0:T(8,128)(2,1)S(1)} %get-tuple-element.63), channel_id=1, source_target_pairs={{0,12},{1,15},{2,14},{3,13},{4,8},{5,11},{6,10},{7,9},{8,4},{9,7},... | collective-permute-start | bytes 122888 | tf_op jit(solution)/shard_map/ppermute | solution.py:444
  23.9 5.4 %collective-permute-start.11 = (bf16[160,128]{1,0:T(8,128)(2,1)S(1)}, bf16[160,128]{1,0:T(8,128)(2,1)S(1)}, u32[]{:S(2)}, u32[]{:S(2)}) collective-permute-start(bf16[160,128]{1,0:T(8,128)(2,1)S(1)} %get-tuple-element.64), channel_id=1, source_target_pairs={{0,4},{1,7},{2,6},{3,5},{4,0},{5,3},{6,2},{7,1},{8,12},{9,15},{10,... | collective-permute-start | bytes 122888 | tf_op jit(solution)/shard_map/ppermute | solution.py:444
  24.0 5.5 %collective-permute-start.8 = (bf16[96,128]{1,0:T(8,128)(2,1)S(1)}, bf16[96,128]{1,0:T(8,128)(2,1)S(1)}, u32[]{:S(2)}, u32[]{:S(2)}) collective-permute-start(bf16[96,128]{1,0:T(8,128)(2,1)S(1)} %get-tuple-element.61), channel_id=1, source_target_pairs={{0,2},{1,3},{2,0},{3,1},{4,6},{5,7},{6,4},{7,5},{8,10},{9,11},{10,... | collective-permute-start | bytes 73736 | tf_op jit(solution)/shard_map/ppermute | solution.py:444
  25.2 4.2 %collective-permute-start.12 = (bf16[96,128]{1,0:T(8,128)(2,1)S(1)}, bf16[96,128]{1,0:T(8,128)(2,1)S(1)}, u32[]{:S(2)}, u32[]{:S(2)}) collective-permute-start(bf16[96,128]{1,0:T(8,128)(2,1)S(1)} %slice.12), channel_id=1, source_target_pairs={{0,1},{1,0},{2,3},{3,2},{4,5},{5,4},{6,7},{7,6},{8,9},{9,8},{10,11... | collective-permute-start | bytes 73736 | tf_op jit(solution)/shard_map/ppermute | solution.py:444
  28.8 1.4 %collective-permute-start.13 = (bf16[96,128]{1,0:T(8,128)(2,1)S(1)}, bf16[96,128]{1,0:T(8,128)(2,1)S(1)}, u32[]{:S(2)}, u32[]{:S(2)}) collective-permute-start(bf16[96,128]{1,0:T(8,128)(2,1)S(1)} %slice.13), channel_id=1, source_target_pairs={{0,1},{1,0},{2,3},{3,2},{4,5},{5,4},{6,7},{7,6},{8,9},{9,8},{10,11... | collective-permute-start | bytes 73736 | tf_op jit(solution)/shard_map/ppermute | solution.py:444
  29.4 1.2 %collective-permute-start.14 = (bf16[96,128]{1,0:T(8,128)(2,1)S(1)}, bf16[96,128]{1,0:T(8,128)(2,1)S(1)}, u32[]{:S(2)}, u32[]{:S(2)}) collective-permute-start(bf16[96,128]{1,0:T(8,128)(2,1)S(1)} %slice.14), channel_id=1, source_target_pairs={{0,1},{1,0},{2,3},{3,2},{4,5},{5,4},{6,7},{7,6},{8,9},{9,8},{10,11... | collective-permute-start | bytes 73736 | tf_op jit(solution)/shard_map/ppermute | solution.py:444

commit v15 on v14

--- a/solution.py
+++ b/solution.py
@@ -125,16 +125,21 @@
             at += 1
 
 
-def pack_kernel(requests, query_ref, hidden_ref, own_ref, query_buf, hidden_buf, sems):
+def pack_kernel(requests, query_ref, hidden_ref, key_ref, value_ref, *refs):
+    own_ref, held_key_ref, held_value_ref, query_buf, hidden_buf, sems = refs
+    sources = (query_ref, hidden_ref, key_ref, value_ref)
+    places = (query_buf, hidden_buf, held_key_ref, held_value_ref)
     loads = [
-        pltpu.make_async_copy(query_ref, query_buf, sems.at[0]),
-        pltpu.make_async_copy(hidden_ref, hidden_buf, sems.at[1]),
+        pltpu.make_async_copy(source, place, sems.at[i])
+        for i, (source, place) in enumerate(zip(sources, places))
     ]
     for load in loads:
         load.start()
-    for load in loads:
+    for load in loads[:2]:
         load.wait()
     tiles_of((query_buf, hidden_buf), requests, own_ref, 0)
+    for load in loads[2:]:
+        load.wait()
 
 
 def pack_other_kernel(requests, own_ref, query_ref, hidden_ref, other_ref, both_ref):
@@ -145,17 +150,13 @@
 
 
 def base_kernel(heads, sources, index_ref, own_ref, weight_ref, down_ref, *refs):
-    others, (base_ref, *held) = refs[:3], refs[3:7]
-    *halves, buffer, sems, row_sems = refs[7:]
+    up_ref, base_ref, held_up_ref, *halves, buffer, sems, row_sems = refs
     parts, depth = buffer.shape[:2]
     loads = [
         pltpu.make_async_copy(weight_ref.at[pl.ds(p * depth, depth)], buffer.at[p], sems.at[p])
         for p in range(parts)
     ]
-    others = [
-        pltpu.make_async_copy(source, place, sems.at[parts + i])
-        for i, (source, place) in enumerate(zip(others, held))
-    ]
+    others = [pltpu.make_async_copy(up_ref, held_up_ref, sems.at[parts])]
     others += streams(sources, index_ref, down_ref, halves, row_sems)
     for load in loads + others:
         load.start()
@@ -481,21 +482,23 @@
     def core_swap(x):
         return trade(x, devices, 0, 0, core=1)
 
-    (own,) = call(
+    flat = requests * cached_key_rows.shape[1]
+    caches = (cached_key_rows.reshape(flat, -1), cached_value_rows.reshape(flat, -1))
+    own, keys, values = call(
         functools.partial(pack_kernel, requests),
-        (pinned(queries), pinned(hidden)),
-        [hbm()] * 2,
-        [pltpu.VMEM((heads + chunks, rows, HEAD_WIDTH), jnp.bfloat16)],
+        tuple(pinned(x) for x in (queries, hidden) + caches),
+        [hbm()] * 4,
+        [pltpu.VMEM((heads + chunks, rows, HEAD_WIDTH), jnp.bfloat16)]
+        + [pltpu.VMEM(x.shape, x.dtype) for x in caches],
         [
             pltpu.VMEM(queries.shape, jnp.bfloat16),
             pltpu.VMEM(hidden.shape, jnp.bfloat16),
-            pltpu.SemaphoreType.DMA((2,)),
+            pltpu.SemaphoreType.DMA((4,)),
         ],
         "pack",
     )
-    flat = requests * cached_key_rows.shape[1]
     other_queries, other_hidden = core_swap(queries), core_swap(hidden)
-    other_queries, late_own, late_lengths = lax.optimization_barrier((other_queries, own, lengths))
+    other_queries, late_own = lax.optimization_barrier((other_queries, own))
     shape = (heads + chunks, rows, HEAD_WIDTH)
     other, both = call(
         functools.partial(pack_other_kernel, requests),
@@ -508,34 +511,27 @@
     both, late_own = lax.optimization_barrier((both, late_own))
     one = trade(late_own, devices, plan.single, plan.single)
     mine = [trade(both, devices, a, b) for a, b in plan.pairs]
-    flat = requests * cached_key_rows.shape[1]
 
     out_width = key_value_weight.shape[1]
     parts = 4 if width % (4 * HEAD_WIDTH) == 0 else 1
     down = pinned(adapter_down_weight[0])
     rank = down.shape[1]
-    big = (
-        cached_key_rows.reshape(flat, -1),
-        cached_value_rows.reshape(flat, -1),
-        adapter_up_weight[0],
-    )
-    base, keys, values, up, *halves = call(
+    up = adapter_up_weight[0]
+    base, up, *halves = call(
         functools.partial(base_kernel, heads, sources_of(plan)),
-        (index, late_own, pinned(key_value_weight), down) + tuple(pinned(x) for x in big),
-        [smem(), vmem()] + [hbm()] * 5,
-        [pltpu.VMEM((rows, out_width), jnp.float32)]
-        + [pltpu.VMEM(x.shape, x.dtype) for x in big]
+        (index, late_own, pinned(key_value_weight), down, pinned(up)),
+        [smem(), vmem()] + [hbm()] * 3,
+        [pltpu.VMEM((rows, out_width), jnp.float32), pltpu.VMEM(up.shape, up.dtype)]
         + [pltpu.VMEM((devices // 2, width, rank), jnp.bfloat16)] * 2,
         [
             pltpu.VMEM((parts, width // parts, out_width), jnp.bfloat16),
-            pltpu.SemaphoreType.DMA((parts + 3,)),
+            pltpu.SemaphoreType.DMA((parts + 1,)),
             pltpu.SemaphoreType.DMA((devices,)),
         ],
         "base",
     )
-    cosine, sine = rotation(late_lengths, tokens)
     near = jnp.concatenate([one] + mine, axis=0)
-    near, base, cosine, sine = lax.optimization_barrier((near, base, cosine, sine))
+    near, base = lax.optimization_barrier((near, base))
     other_near = core_swap(near)
 
     def keep(numbers):
@@ -579,9 +575,12 @@
         [pltpu.VMEM((KEY_HEADS, 3 * rows, HEAD_WIDTH), jnp.float32)],
         "join",
     )
-    heard = [packets[0], trade(packets[1], devices, plan.single, plan.single)]
-    heard += [trade(x, devices, a, b) for x, (a, b) in zip(packets[2:], plan.pairs)]
-    heard += [core_swap(x[slot_rows:]) for x in heard[2:]]
+    sent = sorted(zip(packets[2:], plan.pairs), key=lambda item: -sum(item[1]))
+    back = [trade(x, devices, a, b) for x, (a, b) in sent]
+    back[0], late_lengths = lax.optimization_barrier((back[0], lengths))
+    cosine, sine = rotation(late_lengths, tokens)
+    heard = [packets[0], trade(packets[1], devices, plan.single, plan.single)] + back
+    heard += [core_swap(x[slot_rows:]) for x in back]
     return pl.pallas_call(
         functools.partial(merge_kernel, devices, requests, tokens, 2 + len(plan.pairs)),
         out_shape=jax.ShapeDtypeStruct((requests, tokens, heads * HEAD_WIDTH), jnp.bfloat16),

time: 32.1 us -> 30.9 us (0.963)
  other arithmetic: 0.96 us -> 0.3 us
  waiting for transfers between devices: 4.93 us -> 4.45 us
    convert_element_type x1, other arithmetic: 0.73 us -> 0.07 us  [rotation(): (lengths[:, None] + jnp.arange(tokens, dtype=jnp.int32)[None, :]).astype(...]
    ppermute x15, waiting for transfers between devices: 4.93 us -> 4.45 us  [trade(): return lax.ppermute(x, 'tensor', pairs)]
  transfers between devices with their start and end apart: 15 -> 15, of which waited for: 5 -> 7; matrix products, arithmetic and copies ran while one was open for 3% -> 1% of each run, Pallas kernels for 23% -> 24%
where the time goes in v15:
time: 30.9 us; the launch traced here: 30.7 us
  starting transfers between devices  14.4 us (47%)
  Pallas kernels  11.3 us (37%)
  waiting for transfers between devices  4.45 us (14%)
    ppermute x15, starting transfers between devices, trade(): return lax.ppermute(x, 'tensor', pairs)  14.4 us
    pallas_call x7, Pallas kernels, call(): pl.pallas_call(kernel, out_shape=tuple(out_shape), in_specs=in_specs, out...  10.1 us
    ppermute x15, waiting for transfers between devices, trade(): return lax.ppermute(x, 'tensor', pairs)  4.45 us
    pallas_call x1, Pallas kernels, per_device(): pl.pallas_call(functools.partial(merge_kernel, devices, requests, tokens,...  1.13 us
  transfers between devices with their start and end apart: 15, of which 7 were waited for; matrix products, arithmetic and copies ran while one was open for 1% of the time, Pallas kernels for 24%

profile of v15, /device:TPU:0, one launch (start us, length us, event | category | flops | bytes accessed | tf_op | source)
XLA Modules:
  0.0 30.7 jit_solution(4018865894421836835)
XLA Ops:
  0.0 0.5 %collective-permute-start = (bf16[2,4,1024]{2,1,0:T(4,128)(2,1)}, bf16[2,4,1024]{2,1,0:T(4,128)(2,1)S(1)}, u32[]{:S(2)}, u32[]{:S(2)}) collective-permute-start(bf16[2,4,1024]{2,1,0:T(4,128)(2,1)} %query_ref.1), channel_id=1, source_target_pairs={{0,1},{1,0},{2,3},{3,2},{4,5},{5,4},{6,7},{7,6},{8,9},{9,8},{10,11... | collective-permute-start | bytes 49160 | tf_op jit(solution)/shard_map/ppermute | solution.py:445
  0.5 0.1 collective-permute-start.1
  0.5 1.3 %pack.1 = (bf16[16,8,128]{2,1,0:T(8,128)(2,1)S(1)}, bf16[256,1024]{1,0:T(8,128)(2,1)S(1)}, bf16[256,1024]{1,0:T(8,128)(2,1)S(1)}) custom-call(bf16[2,4,1024]{2,1,0:T(4,128)(2,1)} %query_ref.1, bf16[2,4,1024]{2,1,0:T(4,128)(2,1)} %hidden_ref.1, bf16[256,1024]{1,0:T(8,128)(2,1)} %bitcast.7, bf16[256,1024]{1,0:T(8,128)(2,1)} %bitcast.8), custom_call_target="tpu_custom_call" | custom-call | flops 1000000 | tf_op jit(solution)/shard_map/pack/pallas_call | solution.py:471
  1.8 0.0 collective-permute-done.query_ref
  1.8 0.1 collective-permute-done.1.hidden_ref
  1.9 4.1 %collective-permute-start.3 = (bf16[32,8,128]{2,1,0:T(8,128)(2,1)S(1)}, bf16[32,8,128]{2,1,0:T(8,128)(2,1)S(1)}, u32[]{:S(2)}, u32[]{:S(2)}) collective-permute-start(bf16[32,8,128]{2,1,0:T(8,128)(2,1)S(1)} %get-tuple-element.40), channel_id=1, source_target_pairs={{0,8},{1,11},{2,10},{3,9},{4,12},{5,15},{6,14},{7,13},{8,0},{9,3},... | collective-permute-start | bytes 196616 | tf_op jit(solution)/shard_map/ppermute | solution.py:445
  5.9 1.3 %collective-permute-start.4 = (bf16[32,8,128]{2,1,0:T(8,128)(2,1)S(1)}, bf16[32,8,128]{2,1,0:T(8,128)(2,1)S(1)}, u32[]{:S(2)}, u32[]{:S(2)}) collective-permute-start(bf16[32,8,128]{2,1,0:T(8,128)(2,1)S(1)} %get-tuple-element.40), channel_id=1, source_target_pairs={{0,12},{1,15},{2,14},{3,13},{4,8},{5,11},{6,10},{7,9},{8,4},{9,7},... | collective-permute-start | bytes 196616 | tf_op jit(solution)/shard_map/ppermute | solution.py:445
  7.3 0.2 collective-permute-start.5
  7.5 1.5 %collective-permute-start.2 = (bf16[16,8,128]{2,1,0:T(8,128)(2,1)S(1)}, bf16[16,8,128]{2,1,0:T(8,128)(2,1)S(1)}, u32[]{:S(2)}, u32[]{:S(2)}) collective-permute-start(bf16[16,8,128]{2,1,0:T(8,128)(2,1)S(1)} %get-tuple-element.39.own_ref.refs_2_.refs_5_), channel_id=1, source_target_pairs={{0,2},{1,3},{2,0},{3,1},{4,6},{5,7},{6,4},{7,5},{8,10},{9,11},{10,... | collective-permute-start | bytes 98312 | tf_op jit(solution)/shard_map/ppermute | solution.py:445
  9.0 3.8 %base.1 = (f32[8,2048]{1,0:T(8,128)S(1)}, bf16[128,2048]{1,0:T(8,128)(2,1)S(1)}, bf16[8,1024,128]{2,1,0:T(8,128)(2,1)S(1)}, bf16[8,1024,128]{2,1,0:T(8,128)(2,1)S(1)}) custom-call(s32[1]{0:T(128)} %bitcast.2.index_ref.refs_0_, bf16[16,8,128]{2,1,0:T(8,128)(2,1)S(1)} %get-tuple-element.39.own_ref.refs_2_.refs_5_, bf16[1024,2048]{1,0:T(8,128)(2,1)} %weight_ref.1, ...), custom_call_target="tpu_custom_call" | custom-call | flops 1000000 | tf_op jit(solution)/shard_map/base/pallas_call | solution.py:471
  12.9 0.5 %collective-permute-done.5 = bf16[32,8,128]{2,1,0:T(8,128)(2,1)S(1)} collective-permute-done((bf16[32,8,128]{2,1,0:T(8,128)(2,1)S(1)}, bf16[32,8,128]{2,1,0:T(8,128)(2,1)S(1)}, u32[]{:S(2)}, u32[]{:S(2)}) %collective-permute-start.5) | collective-permute-done | bytes 65568 | tf_op jit(solution)/shard_map/ppermute | solution.py:445
  13.4 0.1 collective-permute-start.6
  13.5 1.2 %keep_states.2 = (f32[256,128]{1,0:T(8,128)S(1)}, f32[8,128]{1,0:T(8,128)S(1)}) custom-call(s32[1]{0:T(128)} %bitcast.2.index_ref.refs_0_, s32[2]{0:T(128)S(1)} %copy-done, bf16[16,8,128]{2,1,0:T(8,128)(2,1)S(1)} %get-tuple-element.39.own_ref.refs_2_.refs_5_, bf16[112,8,128]{2,1,0:T(8,128)(2,1)S(1)} %pad_maximum_fusion.refs_3_.refs_7_, ...), custom_call_target="tpu_custom_call" | custom-call | flops 1000000 | tf_op jit(solution)/shard_map/keep_states/pallas_call | solution.py:471
  14.8 0.2 collective-permute-done.6.refs_8_
  14.9 2.3 %send_states.1 = (bf16[720,128]{1,0:T(8,128)(2,1)S(1)}, f32[2,64,128]{2,1,0:T(8,128)S(1)}) custom-call(s32[1]{0:T(128)} %bitcast.2.index_ref.refs_0_, s32[2]{0:T(128)S(1)} %copy-done, s32[2]{0:T(128)S(1)} %copy-done.1, s32[16]{0:T(128)S(1)} %copy-done.2, s32[16]{0:T(128)S(1)} %copy-done.3, bf16[16,8,128]{2,1,0:T(8,128)(2,1)S(1)} %get-tuple-element.39.own_ref.refs_2_.refs_5_, ...), custom_call_target="tpu_custom_call" | custom-call | flops 1000000 | tf_op jit(solution)/shard_map/send_states/pallas_call | solution.py:471
  17.2 0.4 %collective-permute-start.7 = (bf16[720,128]{1,0:T(8,128)(2,1)S(1)}, bf16[720,128]{1,0:T(8,128)(2,1)S(1)}, u32[]{:S(2)}, u32[]{:S(2)}) collective-permute-start(bf16[720,128]{1,0:T(8,128)(2,1)S(1)} %get-tuple-element.57), channel_id=1, source_target_pairs={{0,1},{1,0},{2,3},{3,2},{4,5},{5,4},{6,7},{7,6},{8,9},{9,8},{10,11... | collective-permute-start | bytes 552968 | tf_op jit(solution)/shard_map/ppermute | solution.py:445
  17.6 1.2 %keep_states.3 = (f32[256,128]{1,0:T(8,128)S(1)}, f32[8,128]{1,0:T(8,128)S(1)}) custom-call(s32[1]{0:T(128)} %bitcast.2.index_ref.refs_0_, s32[2]{0:T(128)S(1)} %copy-done, bf16[16,8,128]{2,1,0:T(8,128)(2,1)S(1)} %get-tuple-element.39.own_ref.refs_2_.refs_5_, bf16[112,8,128]{2,1,0:T(8,128)(2,1)S(1)} %pad_maximum_fusion.refs_3_.refs_7_, ...), custom_call_target="tpu_custom_call" | custom-call | flops 1000000 | tf_op jit(solution)/shard_map/keep_states/pallas_call | solution.py:471
  18.8 0.3 %join.1 = (bf16[96,128]{1,0:T(8,128)(2,1)S(1)}, bf16[96,128]{1,0:T(8,128)(2,1)S(1)}, bf16[160,128]{1,0:T(8,128)(2,1)S(1)}, bf16[160,128]{1,0:T(8,128)(2,1)S(1)}, bf16[160,128]{1,0:T(8,128)(2,1)S(1)}) custom-call(s32[1]{0:T(128)} %bitcast.2.index_ref.refs_0_, f32[256,128]{1,0:T(8,128)S(1)} %get-tuple-element.46.refs_0_, ...), custom_call_target="tpu_custom_call" | custom-call | flops 1000000 | tf_op jit(solution)/shard_map/join/pallas_call | solution.py:471
  19.2 3.6 %collective-permute-start.8 = (bf16[160,128]{1,0:T(8,128)(2,1)S(1)}, bf16[160,128]{1,0:T(8,128)(2,1)S(1)}, u32[]{:S(2)}, u32[]{:S(2)}) collective-permute-start(bf16[160,128]{1,0:T(8,128)(2,1)S(1)} %get-tuple-element.58), channel_id=1, source_target_pairs={{0,12},{1,15},{2,14},{3,13},{4,8},{5,11},{6,10},{7,9},{8,4},{9,7},... | collective-permute-start | bytes 122888 | tf_op jit(solution)/shard_map/ppermute | solution.py:445
  22.8 0.9 %collective-permute-start.11 = (bf16[160,128]{1,0:T(8,128)(2,1)S(1)}, bf16[160,128]{1,0:T(8,128)(2,1)S(1)}, u32[]{:S(2)}, u32[]{:S(2)}) collective-permute-start(bf16[160,128]{1,0:T(8,128)(2,1)S(1)} %get-tuple-element.64), channel_id=1, source_target_pairs={{0,4},{1,7},{2,6},{3,5},{4,0},{5,3},{6,2},{7,1},{8,12},{9,15},{10,... | collective-permute-start | bytes 122888 | tf_op jit(solution)/shard_map/ppermute | solution.py:445
  23.6 1.3 %collective-permute-start.9 = (bf16[96,128]{1,0:T(8,128)(2,1)S(1)}, bf16[96,128]{1,0:T(8,128)(2,1)S(1)}, u32[]{:S(2)}, u32[]{:S(2)}) collective-permute-start(bf16[96,128]{1,0:T(8,128)(2,1)S(1)} %get-tuple-element.61), channel_id=1, source_target_pairs={{0,2},{1,3},{2,0},{3,1},{4,6},{5,7},{6,4},{7,5},{8,10},{9,11},{10,... | collective-permute-start | bytes 73736 | tf_op jit(solution)/shard_map/ppermute | solution.py:445
  24.9 0.5 %collective-permute-done.8.refs_2_ = bf16[160,128]{1,0:T(8,128)(2,1)S(1)} collective-permute-done((bf16[160,128]{1,0:T(8,128)(2,1)S(1)}, bf16[160,128]{1,0:T(8,128)(2,1)S(1)}, u32[]{:S(2)}, u32[]{:S(2)}) %collective-permute-start.8) | collective-permute-done | bytes 40992 | tf_op jit(solution)/shard_map/ppermute | solution.py:445
  25.4 2.6 %collective-permute-done.10.refs_3_ = bf16[160,128]{1,0:T(8,128)(2,1)S(1)} collective-permute-done((bf16[160,128]{1,0:T(8,128)(2,1)S(1)}, bf16[160,128]{1,0:T(8,128)(2,1)S(1)}, u32[]{:S(2)}, u32[]{:S(2)}) %collective-permute-start.10) | collective-permute-done | bytes 40992 | tf_op jit(solution)/shard_map/ppermute | solution.py:445
  28.0 0.3 %collective-permute-start.13 = (bf16[96,128]{1,0:T(8,128)(2,1)S(1)}, bf16[96,128]{1,0:T(8,128)(2,1)S(1)}, u32[]{:S(2)}, u32[]{:S(2)}) collective-permute-start(bf16[96,128]{1,0:T(8,128)(2,1)S(1)} %slice.12), channel_id=1, source_target_pairs={{0,1},{1,0},{2,3},{3,2},{4,5},{5,4},{6,7},{7,6},{8,9},{9,8},{10,11... | collective-permute-start | bytes 73736 | tf_op jit(solution)/shard_map/ppermute | solution.py:445
  28.3 0.2 collective-permute-start.14
  28.5 0.1 add_convert_fusion
  28.6 0.1 convert_element_type.11
  28.7 0.1 fusion
  28.8 0.1 pad_maximum_fusion.1
  28.9 0.3 %collective-permute-done.13.refs_6_ = bf16[96,128]{1,0:T(8,128)(2,1)S(1)} collective-permute-done((bf16[96,128]{1,0:T(8,128)(2,1)S(1)}, bf16[96,128]{1,0:T(8,128)(2,1)S(1)}, u32[]{:S(2)}, u32[]{:S(2)}) %collective-permute-start.13) | collective-permute-done | bytes 24608 | tf_op jit(solution)/shard_map/ppermute | solution.py:445
  29.2 0.3 %collective-permute-done.14.refs_7_ = bf16[96,128]{1,0:T(8,128)(2,1)S(1)} collective-permute-done((bf16[96,128]{1,0:T(8,128)(2,1)S(1)}, bf16[96,128]{1,0:T(8,128)(2,1)S(1)}, u32[]{:S(2)}, u32[]{:S(2)}) %collective-permute-start.14) | collective-permute-done | bytes 24608 | tf_op jit(solution)/shard_map/ppermute | solution.py:445
  29.5 1.1 %merge_states.1 = bf16[2,4,1024]{2,1,0:T(4,128)(2,1)} custom-call(bf16[16,8,128]{2,1,0:T(8,128)(2,1)S(1)} %get-tuple-element.39.own_ref.refs_2_.refs_5_, f32[8,128]{1,0:T(8,128)S(1)} %get-tuple-element.68.cos_ref, f32[8,128]{1,0:T(8,128)S(1)} %get-tuple-element.69.sin_ref, bf16[96,128]{1,0:T(8,128)(2,1)S(1)} %get-tuple-element.60.refs_0_, ...), custom_call_target="tpu_custom_call" | custom-call | tf_op jit(solution)/shard_map/merge_states/pallas_call | solution.py:584
  (23 shorter events, 0.1 us)
Async XLA Ops:
  0.0 1.8 %collective-permute-start = (bf16[2,4,1024]{2,1,0:T(4,128)(2,1)}, bf16[2,4,1024]{2,1,0:T(4,128)(2,1)S(1)}, u32[]{:S(2)}, u32[]{:S(2)}) collective-permute-start(bf16[2,4,1024]{2,1,0:T(4,128)(2,1)} %query_ref.1), channel_id=1, source_target_pairs={{0,1},{1,0},{2,3},{3,2},{4,5},{5,4},{6,7},{7,6},{8,9},{9,8},{10,11... | collective-permute-start | bytes 49160 | tf_op jit(solution)/shard_map/ppermute | solution.py:445
  0.5 1.4 %collective-permute-start.1 = (bf16[2,4,1024]{2,1,0:T(4,128)(2,1)}, bf16[2,4,1024]{2,1,0:T(4,128)(2,1)S(1)}, u32[]{:S(2)}, u32[]{:S(2)}) collective-permute-start(bf16[2,4,1024]{2,1,0:T(4,128)(2,1)} %hidden_ref.1), channel_id=1, source_target_pairs={{0,1},{1,0},{2,3},{3,2},{4,5},{5,4},{6,7},{7,6},{8,9},{9,8},{10,11... | collective-permute-start | bytes 49160 | tf_op jit(solution)/shard_map/ppermute | solution.py:445
  1.9 11.0 %collective-permute-start.3 = (bf16[32,8,128]{2,1,0:T(8,128)(2,1)S(1)}, bf16[32,8,128]{2,1,0:T(8,128)(2,1)S(1)}, u32[]{:S(2)}, u32[]{:S(2)}) collective-permute-start(bf16[32,8,128]{2,1,0:T(8,128)(2,1)S(1)} %get-tuple-element.40), channel_id=1, source_target_pairs={{0,8},{1,11},{2,10},{3,9},{4,12},{5,15},{6,14},{7,13},{8,0},{9,3},... | collective-permute-start | bytes 196616 | tf_op jit(solution)/shard_map/ppermute | solution.py:445
  5.9 6.9 %collective-permute-start.4 = (bf16[32,8,128]{2,1,0:T(8,128)(2,1)S(1)}, bf16[32,8,128]{2,1,0:T(8,128)(2,1)S(1)}, u32[]{:S(2)}, u32[]{:S(2)}) collective-permute-start(bf16[32,8,128]{2,1,0:T(8,128)(2,1)S(1)} %get-tuple-element.40), channel_id=1, source_target_pairs={{0,12},{1,15},{2,14},{3,13},{4,8},{5,11},{6,10},{7,9},{8,4},{9,7},... | collective-permute-start | bytes 196616 | tf_op jit(solution)/shard_map/ppermute | solution.py:445
  7.3 6.1 %collective-permute-start.5 = (bf16[32,8,128]{2,1,0:T(8,128)(2,1)S(1)}, bf16[32,8,128]{2,1,0:T(8,128)(2,1)S(1)}, u32[]{:S(2)}, u32[]{:S(2)}) collective-permute-start(bf16[32,8,128]{2,1,0:T(8,128)(2,1)S(1)} %get-tuple-element.40), channel_id=1, source_target_pairs={{0,4},{1,7},{2,6},{3,5},{4,0},{5,3},{6,2},{7,1},{8,12},{9,15},{10,... | collective-permute-start | bytes 196616 | tf_op jit(solution)/shard_map/ppermute | solution.py:445
  7.5 5.3 %collective-permute-start.2 = (bf16[16,8,128]{2,1,0:T(8,128)(2,1)S(1)}, bf16[16,8,128]{2,1,0:T(8,128)(2,1)S(1)}, u32[]{:S(2)}, u32[]{:S(2)}) collective-permute-start(bf16[16,8,128]{2,1,0:T(8,128)(2,1)S(1)} %get-tuple-element.39.own_ref.refs_2_.refs_5_), channel_id=1, source_target_pairs={{0,2},{1,3},{2,0},{3,1},{4,6},{5,7},{6,4},{7,5},{8,10},{9,11},{10,... | collective-permute-start | bytes 98312 | tf_op jit(solution)/shard_map/ppermute | solution.py:445
  9.0 4.5 %copy-start = (s32[2]{0:T(128)S(1)}, s32[2]{0:T(128)}, u32[]{:S(2)}) copy-start(s32[2]{0:T(128)} %refs_1_.5) | copy-start | bytes 28
  9.0 5.9 %copy-start.1 = (s32[2]{0:T(128)S(1)}, s32[2]{0:T(128)}, u32[]{:S(2)}) copy-start(s32[2]{0:T(128)} %refs_2_.1) | copy-start | bytes 28
  9.0 5.9 %copy-start.2 = (s32[16]{0:T(128)S(1)}, s32[16]{0:T(128)}, u32[]{:S(2)}) copy-start(s32[16]{0:T(128)} %refs_3_.1) | copy-start | bytes 196
  9.0 5.9 %copy-start.3 = (s32[16]{0:T(128)S(1)}, s32[16]{0:T(128)}, u32[]{:S(2)}) copy-start(s32[16]{0:T(128)} %refs_4_.1) | copy-start | bytes 196
  13.4 1.6 %collective-permute-start.6 = (bf16[112,8,128]{2,1,0:T(8,128)(2,1)S(1)}, bf16[112,8,128]{2,1,0:T(8,128)(2,1)S(1)}, u32[]{:S(2)}, u32[]{:S(2)}) collective-permute-start(bf16[112,8,128]{2,1,0:T(8,128)(2,1)S(1)} %pad_maximum_fusion.refs_3_.refs_7_), channel_id=1, source_target_pairs={{0,1},{1,0},{2,3},{3,2},{4,5},{5,4},{6,7},{7,6},{8,9},{9,8},{10,11... | collective-permute-start | bytes 688136 | tf_op jit(solution)/shard_map/ppermute | solution.py:445
  17.2 1.6 %collective-permute-start.7 = (bf16[720,128]{1,0:T(8,128)(2,1)S(1)}, bf16[720,128]{1,0:T(8,128)(2,1)S(1)}, u32[]{:S(2)}, u32[]{:S(2)}) collective-permute-start(bf16[720,128]{1,0:T(8,128)(2,1)S(1)} %get-tuple-element.57), channel_id=1, source_target_pairs={{0,1},{1,0},{2,3},{3,2},{4,5},{5,4},{6,7},{7,6},{8,9},{9,8},{10,11... | collective-permute-start | bytes 552968 | tf_op jit(solution)/shard_map/ppermute | solution.py:445
  19.2 6.2 %collective-permute-start.8 = (bf16[160,128]{1,0:T(8,128)(2,1)S(1)}, bf16[160,128]{1,0:T(8,128)(2,1)S(1)}, u32[]{:S(2)}, u32[]{:S(2)}) collective-permute-start(bf16[160,128]{1,0:T(8,128)(2,1)S(1)} %get-tuple-element.58), channel_id=1, source_target_pairs={{0,12},{1,15},{2,14},{3,13},{4,8},{5,11},{6,10},{7,9},{8,4},{9,7},... | collective-permute-start | bytes 122888 | tf_op jit(solution)/shard_map/ppermute | solution.py:445
  22.8 5.3 %collective-permute-start.10 = (bf16[160,128]{1,0:T(8,128)(2,1)S(1)}, bf16[160,128]{1,0:T(8,128)(2,1)S(1)}, u32[]{:S(2)}, u32[]{:S(2)}) collective-permute-start(bf16[160,128]{1,0:T(8,128)(2,1)S(1)} %get-tuple-element.63), channel_id=1, source_target_pairs={{0,8},{1,11},{2,10},{3,9},{4,12},{5,15},{6,14},{7,13},{8,0},{9,3},... | collective-permute-start | bytes 122888 | tf_op jit(solution)/shard_map/ppermute | solution.py:445
  22.8 5.6 %collective-permute-start.11 = (bf16[160,128]{1,0:T(8,128)(2,1)S(1)}, bf16[160,128]{1,0:T(8,128)(2,1)S(1)}, u32[]{:S(2)}, u32[]{:S(2)}) collective-permute-start(bf16[160,128]{1,0:T(8,128)(2,1)S(1)} %get-tuple-element.64), channel_id=1, source_target_pairs={{0,4},{1,7},{2,6},{3,5},{4,0},{5,3},{6,2},{7,1},{8,12},{9,15},{10,... | collective-permute-start | bytes 122888 | tf_op jit(solution)/shard_map/ppermute | solution.py:445
  23.6 5.3 %collective-permute-start.9 = (bf16[96,128]{1,0:T(8,128)(2,1)S(1)}, bf16[96,128]{1,0:T(8,128)(2,1)S(1)}, u32[]{:S(2)}, u32[]{:S(2)}) collective-permute-start(bf16[96,128]{1,0:T(8,128)(2,1)S(1)} %get-tuple-element.61), channel_id=1, source_target_pairs={{0,2},{1,3},{2,0},{3,1},{4,6},{5,7},{6,4},{7,5},{8,10},{9,11},{10,... | collective-permute-start | bytes 73736 | tf_op jit(solution)/shard_map/ppermute | solution.py:445
  25.4 3.5 %collective-permute-start.12 = (bf16[96,128]{1,0:T(8,128)(2,1)S(1)}, bf16[96,128]{1,0:T(8,128)(2,1)S(1)}, u32[]{:S(2)}, u32[]{:S(2)}) collective-permute-start(bf16[96,128]{1,0:T(8,128)(2,1)S(1)} %slice.9), channel_id=1, source_target_pairs={{0,1},{1,0},{2,3},{3,2},{4,5},{5,4},{6,7},{7,6},{8,9},{9,8},{10,11... | collective-permute-start | bytes 73736 | tf_op jit(solution)/shard_map/ppermute | solution.py:445
  28.0 1.2 %collective-permute-start.13 = (bf16[96,128]{1,0:T(8,128)(2,1)S(1)}, bf16[96,128]{1,0:T(8,128)(2,1)S(1)}, u32[]{:S(2)}, u32[]{:S(2)}) collective-permute-start(bf16[96,128]{1,0:T(8,128)(2,1)S(1)} %slice.12), channel_id=1, source_target_pairs={{0,1},{1,0},{2,3},{3,2},{4,5},{5,4},{6,7},{7,6},{8,9},{9,8},{10,11... | collective-permute-start | bytes 73736 | tf_op jit(solution)/shard_map/ppermute | solution.py:445
  28.3 1.2 %collective-permute-start.14 = (bf16[96,128]{1,0:T(8,128)(2,1)S(1)}, bf16[96,128]{1,0:T(8,128)(2,1)S(1)}, u32[]{:S(2)}, u32[]{:S(2)}) collective-permute-start(bf16[96,128]{1,0:T(8,128)(2,1)S(1)} %slice.13), channel_id=1, source_target_pairs={{0,1},{1,0},{2,3},{3,2},{4,5},{5,4},{6,7},{7,6},{8,9},{9,8},{10,11... | collective-permute-start | bytes 73736 | tf_op jit(solution)/shard_map/ppermute | solution.py:445

commit v16 on v15

--- a/solution.py
+++ b/solution.py
@@ -125,10 +125,10 @@
             at += 1
 
 
-def pack_kernel(requests, query_ref, hidden_ref, key_ref, value_ref, *refs):
-    own_ref, held_key_ref, held_value_ref, query_buf, hidden_buf, sems = refs
-    sources = (query_ref, hidden_ref, key_ref, value_ref)
-    places = (query_buf, hidden_buf, held_key_ref, held_value_ref)
+def pack_kernel(requests, query_ref, hidden_ref, key_ref, *refs):
+    own_ref, held_key_ref, query_buf, hidden_buf, sems = refs
+    sources = (query_ref, hidden_ref, key_ref)
+    places = (query_buf, hidden_buf, held_key_ref)
     loads = [
         pltpu.make_async_copy(source, place, sems.at[i])
         for i, (source, place) in enumerate(zip(sources, places))
@@ -150,13 +150,16 @@
 
 
 def base_kernel(heads, sources, index_ref, own_ref, weight_ref, down_ref, *refs):
-    up_ref, base_ref, held_up_ref, *halves, buffer, sems, row_sems = refs
+    up_ref, value_ref, base_ref, held_up_ref, held_value_ref, *halves, buffer, sems, row_sems = refs
     parts, depth = buffer.shape[:2]
     loads = [
         pltpu.make_async_copy(weight_ref.at[pl.ds(p * depth, depth)], buffer.at[p], sems.at[p])
         for p in range(parts)
     ]
-    others = [pltpu.make_async_copy(up_ref, held_up_ref, sems.at[parts])]
+    others = [
+        pltpu.make_async_copy(up_ref, held_up_ref, sems.at[parts]),
+        pltpu.make_async_copy(value_ref, held_value_ref, sems.at[parts + 1]),
+    ]
     others += streams(sources, index_ref, down_ref, halves, row_sems)
     for load in loads + others:
         load.start()
@@ -187,31 +190,36 @@
     allowed = (here * positions + place % positions < limit) & (
         place_request == (column // tokens) % requests
     )
-    peaks, totals = [], []
+    bias = jnp.where(allowed, 0.0, NEG_FILL)
     chunks = plan.attention_chunks(slot_rows, keep)
-    for number, runs in enumerate(chunks[i] for i in numbers):
+    chunks = [chunks[i] for i in numbers]
+    spots, scores = [], []
+    for runs in chunks:
         places = [slot[1][side] for run in runs for slot, side in run]
         query = jnp.concatenate(
             [arrays[array][tile + h] for array, tile in places for h in range(plan.heads)], axis=0
         )
-        spots = [
-            head_columns((chip // per_head) ^ (here_mask(run[0][0][0], here) // per_head))
-            for run in runs
-        ]
+        spots.append(
+            [
+                head_columns((chip // per_head) ^ (here_mask(run[0][0][0], here) // per_head))
+                for run in runs
+            ]
+        )
         share = HEAD_WIDTH // len(runs)
-        scores = None
-        for i, spot in enumerate(spots):
+        score = None
+        for i, spot in enumerate(spots[-1]):
             part = dot(key_ref[:, spot], query, ((1,), (1,)))
-            scores = part if scores is None else jnp.where(column < i * share, scores, part)
-        scores = jnp.where(allowed, scores * SCALE, NEG_FILL)
-        peak = round_bf16(jnp.max(scores, axis=0, keepdims=True))
-        weights = jnp.exp(scores - peak)
-        peaks.append(peak)
-        totals.append(jnp.sum(weights, axis=0, keepdims=True))
-        weights = jnp.transpose(weights.astype(jnp.bfloat16))
-        for i, spot in enumerate(spots):
+            score = part if score is None else jnp.where(column < i * share, score, part)
+        scores.append(score * SCALE + bias)
+    peaks = [round_bf16(jnp.max(score, axis=0, keepdims=True)) for score in scores]
+    weights = [jnp.exp(score - peak) for score, peak in zip(scores, peaks)]
+    totals = [jnp.sum(weight, axis=0, keepdims=True) for weight in weights]
+    weights = [jnp.transpose(weight.astype(jnp.bfloat16)) for weight in weights]
+    for number, weight in enumerate(weights):
+        share = HEAD_WIDTH // len(spots[number])
+        for i, spot in enumerate(spots[number]):
             own = slice(i * share, (i + 1) * share)
-            put(number, i * share, dot(weights[own], value_ref[:, spot], ((1,), (0,))))
+            put(number, i * share, dot(weight[own], value_ref[:, spot], ((1,), (0,))))
     return peaks, totals
 
 
@@ -483,17 +491,20 @@
         return trade(x, devices, 0, 0, core=1)
 
     flat = requests * cached_key_rows.shape[1]
-    caches = (cached_key_rows.reshape(flat, -1), cached_value_rows.reshape(flat, -1))
-    own, keys, values = call(
+    keys = cached_key_rows.reshape(flat, -1)
+    values = cached_value_rows.reshape(flat, -1)
+    own, keys = call(
         functools.partial(pack_kernel, requests),
-        tuple(pinned(x) for x in (queries, hidden) + caches),
-        [hbm()] * 4,
-        [pltpu.VMEM((heads + chunks, rows, HEAD_WIDTH), jnp.bfloat16)]
-        + [pltpu.VMEM(x.shape, x.dtype) for x in caches],
+        tuple(pinned(x) for x in (queries, hidden, keys)),
+        [hbm()] * 3,
+        [
+            pltpu.VMEM((heads + chunks, rows, HEAD_WIDTH), jnp.bfloat16),
+            pltpu.VMEM(keys.shape, keys.dtype),
+        ],
         [
             pltpu.VMEM(queries.shape, jnp.bfloat16),
             pltpu.VMEM(hidden.shape, jnp.bfloat16),
-            pltpu.SemaphoreType.DMA((4,)),
+            pltpu.SemaphoreType.DMA((3,)),
         ],
         "pack",
     )
@@ -517,15 +528,19 @@
     down = pinned(adapter_down_weight[0])
     rank = down.shape[1]
     up = adapter_up_weight[0]
-    base, up, *halves = call(
+    base, up, values, *halves = call(
         functools.partial(base_kernel, heads, sources_of(plan)),
-        (index, late_own, pinned(key_value_weight), down, pinned(up)),
-        [smem(), vmem()] + [hbm()] * 3,
-        [pltpu.VMEM((rows, out_width), jnp.float32), pltpu.VMEM(up.shape, up.dtype)]
+        (index, late_own, pinned(key_value_weight), down, pinned(up), pinned(values)),
+        [smem(), vmem()] + [hbm()] * 4,
+        [
+            pltpu.VMEM((rows, out_width), jnp.float32),
+            pltpu.VMEM(up.shape, up.dtype),
+            pltpu.VMEM(values.shape, values.dtype),
+        ]
         + [pltpu.VMEM((devices // 2, width, rank), jnp.bfloat16)] * 2,
         [
             pltpu.VMEM((parts, width // parts, out_width), jnp.bfloat16),
-            pltpu.SemaphoreType.DMA((parts + 1,)),
+            pltpu.SemaphoreType.DMA((parts + 2,)),
             pltpu.SemaphoreType.DMA((devices,)),
         ],
         "base",

time: 30.9 us -> 30.2 us (0.977)
  Pallas kernels: 11.3 us -> 10.3 us
  starting transfers between devices: 14.4 us -> 14.9 us
    pallas_call x7, Pallas kernels: 10.1 us -> 9.21 us  [call(): pl.pallas_call(kernel, out_shape=tuple(out_shape), in_specs=in_specs, out...]
    ppermute x15, starting transfers between devices: 14.4 us -> 14.9 us  [trade(): return lax.ppermute(x, 'tensor', pairs)]
  transfers between devices with their start and end apart: 15 -> 15, of which waited for: 7 -> 7; matrix products, arithmetic and copies ran while one was open for 1% -> 1% of each run, Pallas kernels for 24% -> 23%
where the time goes in v16:
time: 30.2 us; the launch traced here: 29.9 us
  starting transfers between devices  14.9 us (49%)
  Pallas kernels  10.3 us (34%)
  waiting for transfers between devices  4.17 us (14%)
    ppermute x15, starting transfers between devices, trade(): return lax.ppermute(x, 'tensor', pairs)  14.9 us
    pallas_call x7, Pallas kernels, call(): pl.pallas_call(kernel, out_shape=tuple(out_shape), in_specs=in_specs, out...  9.21 us
    ppermute x15, waiting for transfers between devices, trade(): return lax.ppermute(x, 'tensor', pairs)  4.17 us
    pallas_call x1, Pallas kernels, per_device(): pl.pallas_call(functools.partial(merge_kernel, devices, requests, tokens,...  1.13 us
  transfers between devices with their start and end apart: 15, of which 7 were waited for; matrix products, arithmetic and copies ran while one was open for 1% of the time, Pallas kernels for 23%

profile of v16, /device:TPU:0, one launch (start us, length us, event | category | flops | bytes accessed | tf_op | source)
XLA Modules:
  0.0 29.9 jit_solution(6493989063444451976)
XLA Ops:
  0.0 0.5 %collective-permute-start = (bf16[2,4,1024]{2,1,0:T(4,128)(2,1)}, bf16[2,4,1024]{2,1,0:T(4,128)(2,1)S(1)}, u32[]{:S(2)}, u32[]{:S(2)}) collective-permute-start(bf16[2,4,1024]{2,1,0:T(4,128)(2,1)} %query_ref.1), channel_id=1, source_target_pairs={{0,1},{1,0},{2,3},{3,2},{4,5},{5,4},{6,7},{7,6},{8,9},{9,8},{10,11... | collective-permute-start | bytes 49160 | tf_op jit(solution)/shard_map/ppermute | solution.py:453
  0.5 0.1 collective-permute-start.1
  0.5 1.1 %pack.1 = (bf16[16,8,128]{2,1,0:T(8,128)(2,1)S(1)}, bf16[256,1024]{1,0:T(8,128)(2,1)S(1)}) custom-call(bf16[2,4,1024]{2,1,0:T(4,128)(2,1)} %query_ref.1, bf16[2,4,1024]{2,1,0:T(4,128)(2,1)} %hidden_ref.1, bf16[256,1024]{1,0:T(8,128)(2,1)} %bitcast.8), custom_call_target="tpu_custom_call" | custom-call | flops 1000000 | tf_op jit(solution)/shard_map/pack/pallas_call | solution.py:479
  1.6 0.2 collective-permute-done.1.hidden_ref
  1.9 3.9 %collective-permute-start.3 = (bf16[32,8,128]{2,1,0:T(8,128)(2,1)S(1)}, bf16[32,8,128]{2,1,0:T(8,128)(2,1)S(1)}, u32[]{:S(2)}, u32[]{:S(2)}) collective-permute-start(bf16[32,8,128]{2,1,0:T(8,128)(2,1)S(1)} %get-tuple-element.40), channel_id=1, source_target_pairs={{0,8},{1,11},{2,10},{3,9},{4,12},{5,15},{6,14},{7,13},{8,0},{9,3},... | collective-permute-start | bytes 196616 | tf_op jit(solution)/shard_map/ppermute | solution.py:453
  5.8 1.3 %collective-permute-start.4 = (bf16[32,8,128]{2,1,0:T(8,128)(2,1)S(1)}, bf16[32,8,128]{2,1,0:T(8,128)(2,1)S(1)}, u32[]{:S(2)}, u32[]{:S(2)}) collective-permute-start(bf16[32,8,128]{2,1,0:T(8,128)(2,1)S(1)} %get-tuple-element.40), channel_id=1, source_target_pairs={{0,12},{1,15},{2,14},{3,13},{4,8},{5,11},{6,10},{7,9},{8,4},{9,7},... | collective-permute-start | bytes 196616 | tf_op jit(solution)/shard_map/ppermute | solution.py:453
  7.1 0.2 collective-permute-start.5
  7.3 1.5 %collective-permute-start.2 = (bf16[16,8,128]{2,1,0:T(8,128)(2,1)S(1)}, bf16[16,8,128]{2,1,0:T(8,128)(2,1)S(1)}, u32[]{:S(2)}, u32[]{:S(2)}) collective-permute-start(bf16[16,8,128]{2,1,0:T(8,128)(2,1)S(1)} %get-tuple-element.39.own_ref.refs_2_.refs_5_), channel_id=1, source_target_pairs={{0,2},{1,3},{2,0},{3,1},{4,6},{5,7},{6,4},{7,5},{8,10},{9,11},{10,... | collective-permute-start | bytes 98312 | tf_op jit(solution)/shard_map/ppermute | solution.py:453
  8.9 3.9 %base.1 = (f32[8,2048]{1,0:T(8,128)S(1)}, bf16[128,2048]{1,0:T(8,128)(2,1)S(1)}, bf16[256,1024]{1,0:T(8,128)(2,1)S(1)}, bf16[8,1024,128]{2,1,0:T(8,128)(2,1)S(1)}, bf16[8,1024,128]{2,1,0:T(8,128)(2,1)S(1)}) custom-call(s32[1]{0:T(128)} %bitcast.1.index_ref.refs_0_, bf16[16,8,128]{2,1,0:T(8,128)(2,1)S(1)} %get-tuple-element.39.own_ref.refs_2_.refs_5_, ...), custom_call_target="tpu_custom_call" | custom-call | flops 1000000 | tf_op jit(solution)/shard_map/base/pallas_call | solution.py:479
  12.8 0.3 collective-permute-done.5
  13.1 0.7 %collective-permute-start.6 = (bf16[112,8,128]{2,1,0:T(8,128)(2,1)S(1)}, bf16[112,8,128]{2,1,0:T(8,128)(2,1)S(1)}, u32[]{:S(2)}, u32[]{:S(2)}) collective-permute-start(bf16[112,8,128]{2,1,0:T(8,128)(2,1)S(1)} %pad_maximum_fusion.refs_3_.refs_7_), channel_id=1, source_target_pairs={{0,1},{1,0},{2,3},{3,2},{4,5},{5,4},{6,7},{7,6},{8,9},{9,8},{10,11... | collective-permute-start | bytes 688136 | tf_op jit(solution)/shard_map/ppermute | solution.py:453
  13.8 1.0 %keep_states.2 = (f32[256,128]{1,0:T(8,128)S(1)}, f32[8,128]{1,0:T(8,128)S(1)}) custom-call(s32[1]{0:T(128)} %bitcast.1.index_ref.refs_0_, s32[2]{0:T(128)S(1)} %copy-done, bf16[16,8,128]{2,1,0:T(8,128)(2,1)S(1)} %get-tuple-element.39.own_ref.refs_2_.refs_5_, bf16[112,8,128]{2,1,0:T(8,128)(2,1)S(1)} %pad_maximum_fusion.refs_3_.refs_7_, ...), custom_call_target="tpu_custom_call" | custom-call | flops 1000000 | tf_op jit(solution)/shard_map/keep_states/pallas_call | solution.py:479
  14.8 0.1 collective-permute-done.6.refs_8_
  14.9 1.8 %send_states.1 = (bf16[720,128]{1,0:T(8,128)(2,1)S(1)}, f32[2,64,128]{2,1,0:T(8,128)S(1)}) custom-call(s32[1]{0:T(128)} %bitcast.1.index_ref.refs_0_, s32[2]{0:T(128)S(1)} %copy-done, s32[2]{0:T(128)S(1)} %copy-done.1, s32[16]{0:T(128)S(1)} %copy-done.2, s32[16]{0:T(128)S(1)} %copy-done.3, bf16[16,8,128]{2,1,0:T(8,128)(2,1)S(1)} %get-tuple-element.39.own_ref.refs_2_.refs_5_, ...), custom_call_target="tpu_custom_call" | custom-call | flops 1000000 | tf_op jit(solution)/shard_map/send_states/pallas_call | solution.py:479
  16.7 0.4 %collective-permute-start.7 = (bf16[720,128]{1,0:T(8,128)(2,1)S(1)}, bf16[720,128]{1,0:T(8,128)(2,1)S(1)}, u32[]{:S(2)}, u32[]{:S(2)}) collective-permute-start(bf16[720,128]{1,0:T(8,128)(2,1)S(1)} %get-tuple-element.57), channel_id=1, source_target_pairs={{0,1},{1,0},{2,3},{3,2},{4,5},{5,4},{6,7},{7,6},{8,9},{9,8},{10,11... | collective-permute-start | bytes 552968 | tf_op jit(solution)/shard_map/ppermute | solution.py:453
  17.2 1.0 %keep_states.3 = (f32[256,128]{1,0:T(8,128)S(1)}, f32[8,128]{1,0:T(8,128)S(1)}) custom-call(s32[1]{0:T(128)} %bitcast.1.index_ref.refs_0_, s32[2]{0:T(128)S(1)} %copy-done, bf16[16,8,128]{2,1,0:T(8,128)(2,1)S(1)} %get-tuple-element.39.own_ref.refs_2_.refs_5_, bf16[112,8,128]{2,1,0:T(8,128)(2,1)S(1)} %pad_maximum_fusion.refs_3_.refs_7_, ...), custom_call_target="tpu_custom_call" | custom-call | flops 1000000 | tf_op jit(solution)/shard_map/keep_states/pallas_call | solution.py:479
  18.2 0.0 collective-permute-done.7.refs_5_
  18.2 0.3 %join.1 = (bf16[96,128]{1,0:T(8,128)(2,1)S(1)}, bf16[96,128]{1,0:T(8,128)(2,1)S(1)}, bf16[160,128]{1,0:T(8,128)(2,1)S(1)}, bf16[160,128]{1,0:T(8,128)(2,1)S(1)}, bf16[160,128]{1,0:T(8,128)(2,1)S(1)}) custom-call(s32[1]{0:T(128)} %bitcast.1.index_ref.refs_0_, f32[256,128]{1,0:T(8,128)S(1)} %get-tuple-element.46.refs_0_, ...), custom_call_target="tpu_custom_call" | custom-call | flops 1000000 | tf_op jit(solution)/shard_map/join/pallas_call | solution.py:479
  18.6 3.5 %collective-permute-start.8 = (bf16[160,128]{1,0:T(8,128)(2,1)S(1)}, bf16[160,128]{1,0:T(8,128)(2,1)S(1)}, u32[]{:S(2)}, u32[]{:S(2)}) collective-permute-start(bf16[160,128]{1,0:T(8,128)(2,1)S(1)} %get-tuple-element.58), channel_id=1, source_target_pairs={{0,12},{1,15},{2,14},{3,13},{4,8},{5,11},{6,10},{7,9},{8,4},{9,7},... | collective-permute-start | bytes 122888 | tf_op jit(solution)/shard_map/ppermute | solution.py:453
  22.0 1.0 %collective-permute-start.11 = (bf16[160,128]{1,0:T(8,128)(2,1)S(1)}, bf16[160,128]{1,0:T(8,128)(2,1)S(1)}, u32[]{:S(2)}, u32[]{:S(2)}) collective-permute-start(bf16[160,128]{1,0:T(8,128)(2,1)S(1)} %get-tuple-element.64), channel_id=1, source_target_pairs={{0,4},{1,7},{2,6},{3,5},{4,0},{5,3},{6,2},{7,1},{8,12},{9,15},{10,... | collective-permute-start | bytes 122888 | tf_op jit(solution)/shard_map/ppermute | solution.py:453
  23.0 1.4 %collective-permute-start.9 = (bf16[96,128]{1,0:T(8,128)(2,1)S(1)}, bf16[96,128]{1,0:T(8,128)(2,1)S(1)}, u32[]{:S(2)}, u32[]{:S(2)}) collective-permute-start(bf16[96,128]{1,0:T(8,128)(2,1)S(1)} %get-tuple-element.61), channel_id=1, source_target_pairs={{0,2},{1,3},{2,0},{3,1},{4,6},{5,7},{6,4},{7,5},{8,10},{9,11},{10,... | collective-permute-start | bytes 73736 | tf_op jit(solution)/shard_map/ppermute | solution.py:453
  24.4 0.4 %collective-permute-done.8.refs_2_ = bf16[160,128]{1,0:T(8,128)(2,1)S(1)} collective-permute-done((bf16[160,128]{1,0:T(8,128)(2,1)S(1)}, bf16[160,128]{1,0:T(8,128)(2,1)S(1)}, u32[]{:S(2)}, u32[]{:S(2)}) %collective-permute-start.8) | collective-permute-done | bytes 40992 | tf_op jit(solution)/shard_map/ppermute | solution.py:453
  24.8 2.4 %collective-permute-done.10.refs_3_ = bf16[160,128]{1,0:T(8,128)(2,1)S(1)} collective-permute-done((bf16[160,128]{1,0:T(8,128)(2,1)S(1)}, bf16[160,128]{1,0:T(8,128)(2,1)S(1)}, u32[]{:S(2)}, u32[]{:S(2)}) %collective-permute-start.10) | collective-permute-done | bytes 40992 | tf_op jit(solution)/shard_map/ppermute | solution.py:453
  27.2 0.4 %collective-permute-start.13 = (bf16[96,128]{1,0:T(8,128)(2,1)S(1)}, bf16[96,128]{1,0:T(8,128)(2,1)S(1)}, u32[]{:S(2)}, u32[]{:S(2)}) collective-permute-start(bf16[96,128]{1,0:T(8,128)(2,1)S(1)} %slice.12), channel_id=1, source_target_pairs={{0,1},{1,0},{2,3},{3,2},{4,5},{5,4},{6,7},{7,6},{8,9},{9,8},{10,11... | collective-permute-start | bytes 73736 | tf_op jit(solution)/shard_map/ppermute | solution.py:453
  27.6 0.1 collective-permute-start.14
  27.7 0.1 add_convert_fusion
  27.8 0.1 convert_element_type.11
  27.9 0.1 fusion
  28.0 0.1 pad_maximum_fusion.1
  28.1 0.4 %collective-permute-done.13.refs_6_ = bf16[96,128]{1,0:T(8,128)(2,1)S(1)} collective-permute-done((bf16[96,128]{1,0:T(8,128)(2,1)S(1)}, bf16[96,128]{1,0:T(8,128)(2,1)S(1)}, u32[]{:S(2)}, u32[]{:S(2)}) %collective-permute-start.13) | collective-permute-done | bytes 24608 | tf_op jit(solution)/shard_map/ppermute | solution.py:453
  28.5 0.4 %collective-permute-done.14.refs_7_ = bf16[96,128]{1,0:T(8,128)(2,1)S(1)} collective-permute-done((bf16[96,128]{1,0:T(8,128)(2,1)S(1)}, bf16[96,128]{1,0:T(8,128)(2,1)S(1)}, u32[]{:S(2)}, u32[]{:S(2)}) %collective-permute-start.14) | collective-permute-done | bytes 24608 | tf_op jit(solution)/shard_map/ppermute | solution.py:453
  28.8 1.1 %merge_states.1 = bf16[2,4,1024]{2,1,0:T(4,128)(2,1)} custom-call(bf16[16,8,128]{2,1,0:T(8,128)(2,1)S(1)} %get-tuple-element.39.own_ref.refs_2_.refs_5_, f32[8,128]{1,0:T(8,128)S(1)} %get-tuple-element.68.cos_ref, f32[8,128]{1,0:T(8,128)S(1)} %get-tuple-element.69.sin_ref, bf16[96,128]{1,0:T(8,128)(2,1)S(1)} %get-tuple-element.60.refs_0_, ...), custom_call_target="tpu_custom_call" | custom-call | tf_op jit(solution)/shard_map/merge_states/pallas_call | solution.py:599
  (23 shorter events, 0.1 us)
Async XLA Ops:
  0.0 1.6 %collective-permute-start = (bf16[2,4,1024]{2,1,0:T(4,128)(2,1)}, bf16[2,4,1024]{2,1,0:T(4,128)(2,1)S(1)}, u32[]{:S(2)}, u32[]{:S(2)}) collective-permute-start(bf16[2,4,1024]{2,1,0:T(4,128)(2,1)} %query_ref.1), channel_id=1, source_target_pairs={{0,1},{1,0},{2,3},{3,2},{4,5},{5,4},{6,7},{7,6},{8,9},{9,8},{10,11... | collective-permute-start | bytes 49160 | tf_op jit(solution)/shard_map/ppermute | solution.py:453
  0.5 1.4 %collective-permute-start.1 = (bf16[2,4,1024]{2,1,0:T(4,128)(2,1)}, bf16[2,4,1024]{2,1,0:T(4,128)(2,1)S(1)}, u32[]{:S(2)}, u32[]{:S(2)}) collective-permute-start(bf16[2,4,1024]{2,1,0:T(4,128)(2,1)} %hidden_ref.1), channel_id=1, source_target_pairs={{0,1},{1,0},{2,3},{3,2},{4,5},{5,4},{6,7},{7,6},{8,9},{9,8},{10,11... | collective-permute-start | bytes 49160 | tf_op jit(solution)/shard_map/ppermute | solution.py:453
  1.9 10.9 %collective-permute-start.3 = (bf16[32,8,128]{2,1,0:T(8,128)(2,1)S(1)}, bf16[32,8,128]{2,1,0:T(8,128)(2,1)S(1)}, u32[]{:S(2)}, u32[]{:S(2)}) collective-permute-start(bf16[32,8,128]{2,1,0:T(8,128)(2,1)S(1)} %get-tuple-element.40), channel_id=1, source_target_pairs={{0,8},{1,11},{2,10},{3,9},{4,12},{5,15},{6,14},{7,13},{8,0},{9,3},... | collective-permute-start | bytes 196616 | tf_op jit(solution)/shard_map/ppermute | solution.py:453
  5.8 7.0 %collective-permute-start.4 = (bf16[32,8,128]{2,1,0:T(8,128)(2,1)S(1)}, bf16[32,8,128]{2,1,0:T(8,128)(2,1)S(1)}, u32[]{:S(2)}, u32[]{:S(2)}) collective-permute-start(bf16[32,8,128]{2,1,0:T(8,128)(2,1)S(1)} %get-tuple-element.40), channel_id=1, source_target_pairs={{0,12},{1,15},{2,14},{3,13},{4,8},{5,11},{6,10},{7,9},{8,4},{9,7},... | collective-permute-start | bytes 196616 | tf_op jit(solution)/shard_map/ppermute | solution.py:453
  7.1 6.0 %collective-permute-start.5 = (bf16[32,8,128]{2,1,0:T(8,128)(2,1)S(1)}, bf16[32,8,128]{2,1,0:T(8,128)(2,1)S(1)}, u32[]{:S(2)}, u32[]{:S(2)}) collective-permute-start(bf16[32,8,128]{2,1,0:T(8,128)(2,1)S(1)} %get-tuple-element.40), channel_id=1, source_target_pairs={{0,4},{1,7},{2,6},{3,5},{4,0},{5,3},{6,2},{7,1},{8,12},{9,15},{10,... | collective-permute-start | bytes 196616 | tf_op jit(solution)/shard_map/ppermute | solution.py:453
  7.3 5.4 %collective-permute-start.2 = (bf16[16,8,128]{2,1,0:T(8,128)(2,1)S(1)}, bf16[16,8,128]{2,1,0:T(8,128)(2,1)S(1)}, u32[]{:S(2)}, u32[]{:S(2)}) collective-permute-start(bf16[16,8,128]{2,1,0:T(8,128)(2,1)S(1)} %get-tuple-element.39.own_ref.refs_2_.refs_5_), channel_id=1, source_target_pairs={{0,2},{1,3},{2,0},{3,1},{4,6},{5,7},{6,4},{7,5},{8,10},{9,11},{10,... | collective-permute-start | bytes 98312 | tf_op jit(solution)/shard_map/ppermute | solution.py:453
  8.9 4.9 %copy-start = (s32[2]{0:T(128)S(1)}, s32[2]{0:T(128)}, u32[]{:S(2)}) copy-start(s32[2]{0:T(128)} %refs_1_.5) | copy-start | bytes 28
  8.9 6.0 %copy-start.1 = (s32[2]{0:T(128)S(1)}, s32[2]{0:T(128)}, u32[]{:S(2)}) copy-start(s32[2]{0:T(128)} %refs_2_.1) | copy-start | bytes 28
  8.9 6.0 %copy-start.2 = (s32[16]{0:T(128)S(1)}, s32[16]{0:T(128)}, u32[]{:S(2)}) copy-start(s32[16]{0:T(128)} %refs_3_.1) | copy-start | bytes 196
  8.9 6.0 %copy-start.3 = (s32[16]{0:T(128)S(1)}, s32[16]{0:T(128)}, u32[]{:S(2)}) copy-start(s32[16]{0:T(128)} %refs_4_.1) | copy-start | bytes 196
  13.1 1.8 %collective-permute-start.6 = (bf16[112,8,128]{2,1,0:T(8,128)(2,1)S(1)}, bf16[112,8,128]{2,1,0:T(8,128)(2,1)S(1)}, u32[]{:S(2)}, u32[]{:S(2)}) collective-permute-start(bf16[112,8,128]{2,1,0:T(8,128)(2,1)S(1)} %pad_maximum_fusion.refs_3_.refs_7_), channel_id=1, source_target_pairs={{0,1},{1,0},{2,3},{3,2},{4,5},{5,4},{6,7},{7,6},{8,9},{9,8},{10,11... | collective-permute-start | bytes 688136 | tf_op jit(solution)/shard_map/ppermute | solution.py:453
  16.7 1.5 %collective-permute-start.7 = (bf16[720,128]{1,0:T(8,128)(2,1)S(1)}, bf16[720,128]{1,0:T(8,128)(2,1)S(1)}, u32[]{:S(2)}, u32[]{:S(2)}) collective-permute-start(bf16[720,128]{1,0:T(8,128)(2,1)S(1)} %get-tuple-element.57), channel_id=1, source_target_pairs={{0,1},{1,0},{2,3},{3,2},{4,5},{5,4},{6,7},{7,6},{8,9},{9,8},{10,11... | collective-permute-start | bytes 552968 | tf_op jit(solution)/shard_map/ppermute | solution.py:453
  18.6 6.3 %collective-permute-start.8 = (bf16[160,128]{1,0:T(8,128)(2,1)S(1)}, bf16[160,128]{1,0:T(8,128)(2,1)S(1)}, u32[]{:S(2)}, u32[]{:S(2)}) collective-permute-start(bf16[160,128]{1,0:T(8,128)(2,1)S(1)} %get-tuple-element.58), channel_id=1, source_target_pairs={{0,12},{1,15},{2,14},{3,13},{4,8},{5,11},{6,10},{7,9},{8,4},{9,7},... | collective-permute-start | bytes 122888 | tf_op jit(solution)/shard_map/ppermute | solution.py:453
  22.0 5.2 %collective-permute-start.10 = (bf16[160,128]{1,0:T(8,128)(2,1)S(1)}, bf16[160,128]{1,0:T(8,128)(2,1)S(1)}, u32[]{:S(2)}, u32[]{:S(2)}) collective-permute-start(bf16[160,128]{1,0:T(8,128)(2,1)S(1)} %get-tuple-element.63), channel_id=1, source_target_pairs={{0,8},{1,11},{2,10},{3,9},{4,12},{5,15},{6,14},{7,13},{8,0},{9,3},... | collective-permute-start | bytes 122888 | tf_op jit(solution)/shard_map/ppermute | solution.py:453
  22.0 5.6 %collective-permute-start.11 = (bf16[160,128]{1,0:T(8,128)(2,1)S(1)}, bf16[160,128]{1,0:T(8,128)(2,1)S(1)}, u32[]{:S(2)}, u32[]{:S(2)}) collective-permute-start(bf16[160,128]{1,0:T(8,128)(2,1)S(1)} %get-tuple-element.64), channel_id=1, source_target_pairs={{0,4},{1,7},{2,6},{3,5},{4,0},{5,3},{6,2},{7,1},{8,12},{9,15},{10,... | collective-permute-start | bytes 122888 | tf_op jit(solution)/shard_map/ppermute | solution.py:453
  23.0 5.1 %collective-permute-start.9 = (bf16[96,128]{1,0:T(8,128)(2,1)S(1)}, bf16[96,128]{1,0:T(8,128)(2,1)S(1)}, u32[]{:S(2)}, u32[]{:S(2)}) collective-permute-start(bf16[96,128]{1,0:T(8,128)(2,1)S(1)} %get-tuple-element.61), channel_id=1, source_target_pairs={{0,2},{1,3},{2,0},{3,1},{4,6},{5,7},{6,4},{7,5},{8,10},{9,11},{10,... | collective-permute-start | bytes 73736 | tf_op jit(solution)/shard_map/ppermute | solution.py:453
  24.8 3.2 %collective-permute-start.12 = (bf16[96,128]{1,0:T(8,128)(2,1)S(1)}, bf16[96,128]{1,0:T(8,128)(2,1)S(1)}, u32[]{:S(2)}, u32[]{:S(2)}) collective-permute-start(bf16[96,128]{1,0:T(8,128)(2,1)S(1)} %slice.9), channel_id=1, source_target_pairs={{0,1},{1,0},{2,3},{3,2},{4,5},{5,4},{6,7},{7,6},{8,9},{9,8},{10,11... | collective-permute-start | bytes 73736 | tf_op jit(solution)/shard_map/ppermute | solution.py:453
  27.2 1.3 %collective-permute-start.13 = (bf16[96,128]{1,0:T(8,128)(2,1)S(1)}, bf16[96,128]{1,0:T(8,128)(2,1)S(1)}, u32[]{:S(2)}, u32[]{:S(2)}) collective-permute-start(bf16[96,128]{1,0:T(8,128)(2,1)S(1)} %slice.12), channel_id=1, source_target_pairs={{0,1},{1,0},{2,3},{3,2},{4,5},{5,4},{6,7},{7,6},{8,9},{9,8},{10,11... | collective-permute-start | bytes 73736 | tf_op jit(solution)/shard_map/ppermute | solution.py:453
  27.6 1.2 %collective-permute-start.14 = (bf16[96,128]{1,0:T(8,128)(2,1)S(1)}, bf16[96,128]{1,0:T(8,128)(2,1)S(1)}, u32[]{:S(2)}, u32[]{:S(2)}) collective-permute-start(bf16[96,128]{1,0:T(8,128)(2,1)S(1)} %slice.13), channel_id=1, source_target_pairs={{0,1},{1,0},{2,3},{3,2},{4,5},{5,4},{6,7},{7,6},{8,9},{9,8},{10,11... | collective-permute-start | bytes 73736 | tf_op jit(solution)/shard_map/ppermute | solution.py:453

commit v17 on v16

--- a/solution.py
+++ b/solution.py
@@ -86,11 +86,12 @@
 
 
 def sources_of(plan):
-    return [
+    sources = [
         (array, tile + plan.heads, masks, side)
         for masks, places in plan.slots()
         for side, (array, tile) in enumerate(places)
     ]
+    return sorted(sources, key=lambda source: source[0] % 2)
 
 
 def streams(sources, index_ref, down_ref, halves, sems):
@@ -105,13 +106,13 @@
     return copies
 
 
-def lower(sources, arrays, halves):
+def lower(sources, arrays, half_ref):
     total = None
-    count, depth = halves[0].shape[:2]
+    depth = half_ref.shape[1]
     for at, (array, first, _, _) in enumerate(sources):
         tiles = range(first, first + depth // HEAD_WIDTH)
         hidden = jnp.concatenate([arrays[array][c] for c in tiles], axis=1)
-        term = dot(hidden, halves[at // count][at % count], ((1,), (0,)))
+        term = dot(hidden, half_ref[at], ((1,), (0,)))
         total = term if total is None else total + term
     return total
 
@@ -125,21 +126,16 @@
             at += 1
 
 
-def pack_kernel(requests, query_ref, hidden_ref, key_ref, *refs):
-    own_ref, held_key_ref, query_buf, hidden_buf, sems = refs
-    sources = (query_ref, hidden_ref, key_ref)
-    places = (query_buf, hidden_buf, held_key_ref)
+def pack_kernel(requests, query_ref, hidden_ref, own_ref, query_buf, hidden_buf, sems):
     loads = [
-        pltpu.make_async_copy(source, place, sems.at[i])
-        for i, (source, place) in enumerate(zip(sources, places))
+        pltpu.make_async_copy(query_ref, query_buf, sems.at[0]),
+        pltpu.make_async_copy(hidden_ref, hidden_buf, sems.at[1]),
     ]
     for load in loads:
         load.start()
-    for load in loads[:2]:
+    for load in loads:
         load.wait()
     tiles_of((query_buf, hidden_buf), requests, own_ref, 0)
-    for load in loads[2:]:
-        load.wait()
 
 
 def pack_other_kernel(requests, own_ref, query_ref, hidden_ref, other_ref, both_ref):
@@ -149,40 +145,30 @@
     other_ref[...] = both_ref[size:]
 
 
-def base_kernel(heads, sources, index_ref, own_ref, weight_ref, down_ref, *refs):
-    up_ref, value_ref, base_ref, held_up_ref, held_value_ref, *halves, buffer, sems, row_sems = refs
+def base_kernel(sizes, plan, *refs):
+    (index_ref, length_ref, adapter_ref, rank_ref, pool_ref) = refs[:5]
+    (own_ref, weight_ref, down_ref, *sources) = refs[5:11]
+    (base_ref, bias_ref, mask_ref, *held) = refs[11:17]
+    *halves, buffer, sems, row_sems = refs[17:]
+    requests, tokens, devices = sizes
+    rows = requests * tokens
+    here = index_ref[0]
     parts, depth = buffer.shape[:2]
     loads = [
         pltpu.make_async_copy(weight_ref.at[pl.ds(p * depth, depth)], buffer.at[p], sems.at[p])
         for p in range(parts)
     ]
     others = [
-        pltpu.make_async_copy(up_ref, held_up_ref, sems.at[parts]),
-        pltpu.make_async_copy(value_ref, held_value_ref, sems.at[parts + 1]),
+        pltpu.make_async_copy(source, place, sems.at[parts + i])
+        for i, (source, place) in enumerate(zip(sources, held))
     ]
-    others += streams(sources, index_ref, down_ref, halves, row_sems)
+    others += streams(sources_of(plan), index_ref, down_ref, halves, row_sems)
     for load in loads + others:
         load.start()
-    tiles = depth // HEAD_WIDTH
-    total = jnp.zeros(base_ref.shape, jnp.float32)
-    for p in range(parts):
-        hidden = jnp.concatenate([own_ref[heads + p * tiles + c] for c in range(tiles)], axis=1)
-        loads[p].wait()
-        total += dot(hidden, buffer[p], ((1,), (0,)))
-    base_ref[...] = total
-    for load in others:
-        load.wait()
-
-
-def attend(sizes, plan, keep, numbers, index_ref, length_ref, arrays, key_ref, value_ref, put):
-    requests, tokens, devices = sizes
-    here = index_ref[0]
-    chip = here // 2
-    per_head = plan.per_head
-    slot_rows = plan.heads * requests * tokens
-    positions = key_ref.shape[0] // requests
-    place = lax.broadcasted_iota(jnp.int32, (requests * positions, HEAD_WIDTH), 0)
-    column = lax.broadcasted_iota(jnp.int32, (requests * positions, HEAD_WIDTH), 1)
+
+    positions = bias_ref.shape[0] // requests
+    place = lax.broadcasted_iota(jnp.int32, bias_ref.shape, 0)
+    column = lax.broadcasted_iota(jnp.int32, bias_ref.shape, 1)
     place_request = place // positions
     limit = jnp.zeros_like(place)
     for b in range(requests):
@@ -190,7 +176,38 @@
     allowed = (here * positions + place % positions < limit) & (
         place_request == (column // tokens) % requests
     )
-    bias = jnp.where(allowed, 0.0, NEG_FILL)
+    bias_ref[...] = jnp.where(allowed, 0.0, NEG_FILL)
+    row_request = lax.broadcasted_iota(jnp.int32, (rows, HEAD_WIDTH), 0) // tokens
+    ranks = jnp.zeros((rows, HEAD_WIDTH), jnp.int32)
+    owners = jnp.zeros((rows, HEAD_WIDTH), jnp.int32)
+    for b in range(requests):
+        adapter = adapter_ref[b]
+        ranks = jnp.where(row_request == b, rank_ref[adapter], ranks)
+        owners = jnp.where(row_request == b, pool_ref[adapter], owners)
+    column = lax.broadcasted_iota(jnp.int32, ranks.shape, 1)
+    mask_ref[0] = jnp.where(column < ranks, 1.0, 0.0)
+    mask_ref[1] = jnp.where(owners == here, 1.0, 0.0)
+
+    tiles = depth // HEAD_WIDTH
+    total = jnp.zeros(base_ref.shape, jnp.float32)
+    for p in range(parts):
+        first = plan.heads + p * tiles
+        hidden = jnp.concatenate([own_ref[first + c] for c in range(tiles)], axis=1)
+        loads[p].wait()
+        total += dot(hidden, buffer[p], ((1,), (0,)))
+    base_ref[...] = total
+    for load in others:
+        load.wait()
+
+
+def attend(sizes, plan, keep, numbers, index_ref, bias_ref, arrays, key_ref, value_ref, put):
+    requests, tokens, devices = sizes
+    here = index_ref[0]
+    chip = here // 2
+    per_head = plan.per_head
+    slot_rows = plan.heads * requests * tokens
+    bias = bias_ref[...]
+    column = lax.broadcasted_iota(jnp.int32, bias.shape, 1)
     chunks = plan.attention_chunks(slot_rows, keep)
     chunks = [chunks[i] for i in numbers]
     spots, scores = [], []
@@ -232,8 +249,9 @@
 
 
 def send_kernel(sizes, plan, *refs):
-    (index_ref, length_ref, adapter_ref, rank_ref, pool_ref, *arrays) = refs[:-8]
-    (key_ref, value_ref, base_ref, up_ref, *halves, send_ref, own_ref) = refs[-8:]
+    (index_ref, bias_ref, *arrays) = refs[:6]
+    (key_ref, value_ref, base_ref, up_ref, half_ref, lowered_ref, mask_ref) = refs[6:13]
+    (send_ref, own_ref) = refs[13:]
     requests, tokens, devices = sizes
 
     def put(chunk, row, mix):
@@ -241,25 +259,18 @@
         send_ref[at : at + mix.shape[0]] = mix.astype(jnp.bfloat16)
 
     peaks, totals = attend(
-        sizes, plan, False, range(CHUNKS), index_ref, length_ref, arrays, key_ref, value_ref, put
+        sizes, plan, False, range(CHUNKS), index_ref, bias_ref, arrays, key_ref, value_ref, put
     )
     highs = [round_bf16(total) for total in totals]
     lows = [total - high for total, high in zip(totals, highs)]
     send_ref[-STAT_ROWS:] = rows_of(peaks + highs + lows, STAT_ROWS).astype(jnp.bfloat16)
 
     rows = requests * tokens
-    lowered = lower(sources_of(plan), arrays, halves)
-    row_request = lax.broadcasted_iota(jnp.int32, (rows, 1), 0) // tokens
-    ranks = jnp.zeros((rows, 1), jnp.int32)
-    owners = jnp.zeros((rows, 1), jnp.int32)
-    for b in range(requests):
-        adapter = adapter_ref[b]
-        ranks = jnp.where(row_request == b, rank_ref[adapter], ranks)
-        owners = jnp.where(row_request == b, pool_ref[adapter], owners)
-    column = lax.broadcasted_iota(jnp.int32, lowered.shape, 1)
-    lowered = jnp.where(column < ranks, lowered, 0.0).astype(jnp.bfloat16)
+    sources = sources_of(plan)
+    lowered = lowered_ref[...] + lower(sources[devices // 2 :], arrays, half_ref)
+    lowered = jnp.where(mask_ref[0] > 0.0, lowered, 0.0).astype(jnp.bfloat16)
     lifted = dot(lowered, up_ref[...], ((1,), (0,)))
-    projected = base_ref[...] + jnp.where(owners == index_ref[0], lifted, 0.0)
+    projected = base_ref[...] + jnp.where(mask_ref[1][:, :1] > 0.0, lifted, 0.0)
     split = KEY_HEADS * HEAD_WIDTH
     step = KEY_HEADS * rows
     keys, values = [
@@ -280,15 +291,20 @@
 
 
 def keep_kernel(sizes, plan, numbers, *refs):
-    (index_ref, length_ref, own_ref, near_ref, key_ref, value_ref, mix_ref, stat_ref) = refs
+    (index_ref, bias_ref, own_ref, near_ref, key_ref, value_ref) = refs[:6]
     arrays = {0: own_ref, 2: near_ref}
+    if len(refs) > 8:
+        half_ref, mix_ref, stat_ref, lowered_ref = refs[6:]
+        lowered_ref[...] = lower(sources_of(plan)[: half_ref.shape[0]], arrays, half_ref)
+    else:
+        mix_ref, stat_ref = refs[6:]
 
     def put(chunk, row, mix):
         at = chunk * 128 + row
         mix_ref[at : at + mix.shape[0]] = mix
 
     peaks, totals = attend(
-        sizes, plan, True, numbers, index_ref, length_ref, arrays, key_ref, value_ref, put
+        sizes, plan, True, numbers, index_ref, bias_ref, arrays, key_ref, value_ref, put
     )
     stat_ref[...] = rows_of(peaks + totals, 8)
 
@@ -379,36 +395,43 @@
     stats = [tail[3 * rows :] for tail in tails]
     for s in range(swapped, sources):
         stats[s] = pltpu.roll(stats[s], HEAD_WIDTH - mix_rows, 1)
-    peak = functools.reduce(jnp.maximum, [stat[0:1] for stat in stats], fresh_peak)
+    past_peak = functools.reduce(jnp.maximum, [stat[0:1] for stat in stats])
+    factors = [jnp.exp(stat[0:1] - past_peak) for stat in stats]
+    past_total = functools.reduce(
+        jnp.add, [factor * (stat[1:2] + stat[2:3]) for factor, stat in zip(factors, stats)]
+    )
+    table = jnp.concatenate(factors + [jnp.zeros((128 - sources, 128), jnp.float32)], axis=0)
+    table = jnp.transpose(table)[:mix_rows]
+    mix = None
+    for s, ref in enumerate(got_refs):
+        term = ref[:mix_rows].astype(jnp.float32) * table[:, s : s + 1]
+        mix = term if mix is None else mix + term
+    peak = jnp.maximum(past_peak, fresh_peak)
+    scale = jnp.exp(past_peak - peak)
     weights = jnp.where(allowed, jnp.exp(fresh - peak), 0.0)
-    factors = [jnp.exp(stat[0:1] - peak) for stat in stats]
-    total = functools.reduce(
-        jnp.add,
-        [factor * (stat[1:2] + stat[2:3]) for factor, stat in zip(factors, stats)],
-        jnp.sum(weights, axis=0, keepdims=True),
-    )
-    inverse = 1.0 / total
-    start = -(-(sources + 1) // rows) * rows
+    inverse = 1.0 / (past_total * scale + jnp.sum(weights, axis=0, keepdims=True))
     table = jnp.concatenate(
-        [factor * inverse for factor in factors]
-        + [inverse, jnp.zeros((start - sources - 1, 128), jnp.float32), weights]
-        + [jnp.zeros((128 - start - rows, 128), jnp.float32)],
+        [
+            scale * inverse,
+            inverse,
+            jnp.zeros((rows - 2, 128), jnp.float32),
+            weights,
+            jnp.zeros((128 - 2 * rows, 128), jnp.float32),
+        ],
         axis=0,
     )
     table = jnp.transpose(table)[:mix_rows]
     lane = lax.broadcasted_iota(jnp.int32, table.shape, 1)
-    weights = jnp.where((lane >= start) & (lane < start + rows), table, 0.0).astype(jnp.bfloat16)
+    weights = jnp.where((lane >= rows) & (lane < 2 * rows), table, 0.0).astype(jnp.bfloat16)
     values = jnp.concatenate(
         [
-            jnp.zeros((start, HEAD_WIDTH), jnp.bfloat16),
+            jnp.zeros((rows, HEAD_WIDTH), jnp.bfloat16),
             values,
-            jnp.zeros((128 - start - rows, HEAD_WIDTH), jnp.bfloat16),
+            jnp.zeros((128 - 2 * rows, HEAD_WIDTH), jnp.bfloat16),
         ],
         axis=0,
     )
-    mix = dot(weights, values, ((1,), (0,))) * table[:, sources : sources + 1]
-    for s, ref in enumerate(got_refs):
-        mix += ref[:mix_rows].astype(jnp.float32) * table[:, s : s + 1]
+    mix = mix * table[:, 0:1] + dot(weights, values, ((1,), (0,))) * table[:, 1:2]
     for h in range(heads):
         tile = mix[h * rows : (h + 1) * rows]
         for b in range(requests):
@@ -493,18 +516,15 @@
     flat = requests * cached_key_rows.shape[1]
     keys = cached_key_rows.reshape(flat, -1)
     values = cached_value_rows.reshape(flat, -1)
-    own, keys = call(
+    (own,) = call(
         functools.partial(pack_kernel, requests),
-        tuple(pinned(x) for x in (queries, hidden, keys)),
-        [hbm()] * 3,
-        [
-            pltpu.VMEM((heads + chunks, rows, HEAD_WIDTH), jnp.bfloat16),
-            pltpu.VMEM(keys.shape, keys.dtype),
-        ],
+        (pinned(queries), pinned(hidden)),
+        [hbm()] * 2,
+        [pltpu.VMEM((heads + chunks, rows, HEAD_WIDTH), jnp.bfloat16)],
         [
             pltpu.VMEM(queries.shape, jnp.bfloat16),
             pltpu.VMEM(hidden.shape, jnp.bfloat16),
-            pltpu.SemaphoreType.DMA((3,)),
+            pltpu.SemaphoreType.DMA((2,)),
         ],
         "pack",
     )
@@ -528,19 +548,23 @@
     down = pinned(adapter_down_weight[0])
     rank = down.shape[1]
     up = adapter_up_weight[0]
-    base, up, values, *halves = call(
-        functools.partial(base_kernel, heads, sources_of(plan)),
-        (index, late_own, pinned(key_value_weight), down, pinned(up), pinned(values)),
-        [smem(), vmem()] + [hbm()] * 4,
+    big = (keys, values, up)
+    base, bias, masks, keys, values, up, *halves = call(
+        functools.partial(base_kernel, sizes, plan),
+        (index, lengths, request_adapter, adapter_rank_list, adapter_pool_row)
+        + (late_own, pinned(key_value_weight), down)
+        + tuple(pinned(x) for x in big),
+        [smem()] * 5 + [vmem()] + [hbm()] * 5,
         [
             pltpu.VMEM((rows, out_width), jnp.float32),
-            pltpu.VMEM(up.shape, up.dtype),
-            pltpu.VMEM(values.shape, values.dtype),
+            pltpu.VMEM((flat, HEAD_WIDTH), jnp.float32),
+            pltpu.VMEM((2, rows, HEAD_WIDTH), jnp.float32),
         ]
+        + [pltpu.VMEM(x.shape, x.dtype) for x in big]
         + [pltpu.VMEM((devices // 2, width, rank), jnp.bfloat16)] * 2,
         [
             pltpu.VMEM((parts, width // parts, out_width), jnp.bfloat16),
-            pltpu.SemaphoreType.DMA((parts + 2,)),
+            pltpu.SemaphoreType.DMA((parts + 3,)),
             pltpu.SemaphoreType.DMA((devices,)),
         ],
         "base",
@@ -549,29 +573,28 @@
     near, base = lax.optimization_barrier((near, base))
     other_near = core_swap(near)
 
-    def keep(numbers):
+    def keep(numbers, *half):
         return call(
             functools.partial(keep_kernel, sizes, plan, numbers),
-            (index, lengths, own, near, keys, values),
-            [smem()] * 2 + [vmem()] * 4,
+            (index, bias, own, near, keys, values) + half,
+            [smem()] + [vmem()] * (5 + len(half)),
             [
                 pltpu.VMEM((MIX_ROWS // 2, HEAD_WIDTH), jnp.float32),
                 pltpu.VMEM((8, HEAD_WIDTH), jnp.float32),
-            ],
+            ]
+            + [pltpu.VMEM((rows, rank), jnp.float32)] * len(half),
             [],
             "keep_states",
         )
 
-    first_mix, first_stats = keep(range(CHUNKS // 2))
+    first_mix, first_stats, lowered = keep(range(CHUNKS // 2), halves[0])
     other_near, first_mix = lax.optimization_barrier((other_near, first_mix))
     arrays = (own, other, near, other_near)
     step = KEY_HEADS * rows
     send, proj = call(
         functools.partial(send_kernel, sizes, plan),
-        (index, lengths, request_adapter, adapter_rank_list, adapter_pool_row)
-        + arrays
-        + (keys, values, base, up, *halves),
-        [smem()] * 5 + [vmem()] * (len(arrays) + 6),
+        (index, bias) + arrays + (keys, values, base, up, halves[1], lowered, masks),
+        [smem()] + [vmem()] * 12,
         [
             pltpu.VMEM((MIX_ROWS + 3 * step + STAT_ROWS, HEAD_WIDTH), jnp.bfloat16),
             pltpu.VMEM((2, step, HEAD_WIDTH), jnp.float32),

time: 30.2 us -> 32.6 us (1.079)
  local copies, waits for them, and re-layouts: 0.11 us -> 2.71 us
  waiting for transfers between devices: 4.17 us -> 5.85 us
  Pallas kernels: 10.3 us -> 9 us
  starting transfers between devices: 14.9 us -> 14.3 us
    unnamed x8 -> x10, local copies, waits for them, and re-layouts: 0.01 us -> 2.62 us
    ppermute x15, waiting for transfers between devices: 4.17 us -> 5.85 us  [trade(): return lax.ppermute(x, 'tensor', pairs)]
    pallas_call x7, Pallas kernels: 9.21 us -> 7.96 us  [call(): pl.pallas_call(kernel, out_shape=tuple(out_shape), in_specs=in_specs, out...]
    ppermute x15, starting transfers between devices: 14.9 us -> 14.3 us  [trade(): return lax.ppermute(x, 'tensor', pairs)]
  transfers between devices with their start and end apart: 15 -> 15, of which waited for: 7 -> 8; matrix products, arithmetic and copies ran while one was open for 1% -> 1% of each run, Pallas kernels for 23% -> 20%
where the time goes in v17:
time: 32.6 us; the launch traced here: 32.3 us
  starting transfers between devices  14.3 us (44%)
  Pallas kernels  9 us (28%)
  waiting for transfers between devices  5.85 us (18%)
  local copies, waits for them, and re-layouts  2.71 us (8%)
    ppermute x15, starting transfers between devices, trade(): return lax.ppermute(x, 'tensor', pairs)  14.3 us
    pallas_call x7, Pallas kernels, call(): pl.pallas_call(kernel, out_shape=tuple(out_shape), in_specs=in_specs, out...  7.96 us
    ppermute x15, waiting for transfers between devices, trade(): return lax.ppermute(x, 'tensor', pairs)  5.85 us
    unnamed x10, local copies, waits for them, and re-layouts  2.62 us
    pallas_call x1, Pallas kernels, per_device(): pl.pallas_call(functools.partial(merge_kernel, devices, requests, tokens,...  1.04 us
  transfers between devices with their start and end apart: 15, of which 8 were waited for; matrix products, arithmetic and copies ran while one was open for 1% of the time, Pallas kernels for 20%

profile of v17, /device:TPU:0, one launch (start us, length us, event | category | flops | bytes accessed | tf_op | source)
XLA Modules:
  0.0 32.3 jit_solution(10765132235600001990)
XLA Ops:
  0.0 0.5 %collective-permute-start = (bf16[2,4,1024]{2,1,0:T(4,128)(2,1)}, bf16[2,4,1024]{2,1,0:T(4,128)(2,1)S(1)}, u32[]{:S(2)}, u32[]{:S(2)}) collective-permute-start(bf16[2,4,1024]{2,1,0:T(4,128)(2,1)} %query_ref.1), channel_id=1, source_target_pairs={{0,1},{1,0},{2,3},{3,2},{4,5},{5,4},{6,7},{7,6},{8,9},{9,8},{10,11... | collective-permute-start | bytes 49160 | tf_op jit(solution)/shard_map/ppermute | solution.py:476
  0.5 0.8 %pack.1.own_ref.refs_5_.refs_2_ = bf16[16,8,128]{2,1,0:T(8,128)(2,1)S(1)} custom-call(bf16[2,4,1024]{2,1,0:T(4,128)(2,1)} %query_ref.1, bf16[2,4,1024]{2,1,0:T(4,128)(2,1)} %hidden_ref.1), custom_call_target="tpu_custom_call" | custom-call | flops 1000000 | tf_op jit(solution)/shard_map/pack/pallas_call | solution.py:502
  1.3 0.2 collective-permute-done.query_ref
  1.5 0.3 %collective-permute-done.1.hidden_ref = bf16[2,4,1024]{2,1,0:T(4,128)(2,1)S(1)} collective-permute-done((bf16[2,4,1024]{2,1,0:T(4,128)(2,1)}, bf16[2,4,1024]{2,1,0:T(4,128)(2,1)S(1)}, u32[]{:S(2)}, u32[]{:S(2)}) %collective-permute-start.1) | collective-permute-done | bytes 16416 | tf_op jit(solution)/shard_map/ppermute | solution.py:476
  1.9 3.8 %collective-permute-start.3 = (bf16[32,8,128]{2,1,0:T(8,128)(2,1)S(1)}, bf16[32,8,128]{2,1,0:T(8,128)(2,1)S(1)}, u32[]{:S(2)}, u32[]{:S(2)}) collective-permute-start(bf16[32,8,128]{2,1,0:T(8,128)(2,1)S(1)} %get-tuple-element.41), channel_id=1, source_target_pairs={{0,8},{1,11},{2,10},{3,9},{4,12},{5,15},{6,14},{7,13},{8,0},{9,3},... | collective-permute-start | bytes 196616 | tf_op jit(solution)/shard_map/ppermute | solution.py:476
  5.7 1.3 %collective-permute-start.4 = (bf16[32,8,128]{2,1,0:T(8,128)(2,1)S(1)}, bf16[32,8,128]{2,1,0:T(8,128)(2,1)S(1)}, u32[]{:S(2)}, u32[]{:S(2)}) collective-permute-start(bf16[32,8,128]{2,1,0:T(8,128)(2,1)S(1)} %get-tuple-element.41), channel_id=1, source_target_pairs={{0,12},{1,15},{2,14},{3,13},{4,8},{5,11},{6,10},{7,9},{8,4},{9,7},... | collective-permute-start | bytes 196616 | tf_op jit(solution)/shard_map/ppermute | solution.py:476
  7.0 0.2 collective-permute-start.5
  7.3 1.5 %collective-permute-start.2 = (bf16[16,8,128]{2,1,0:T(8,128)(2,1)S(1)}, bf16[16,8,128]{2,1,0:T(8,128)(2,1)S(1)}, u32[]{:S(2)}, u32[]{:S(2)}) collective-permute-start(bf16[16,8,128]{2,1,0:T(8,128)(2,1)S(1)} %pack.1.own_ref.refs_5_.refs_2_), channel_id=1, source_target_pairs={{0,2},{1,3},{2,0},{3,1},{4,6},{5,7},{6,4},{7,5},{8,10},{9,11},{10,... | collective-permute-start | bytes 98312 | tf_op jit(solution)/shard_map/ppermute | solution.py:476
  8.8 0.7 %copy-done = s32[2]{0:T(128)S(1)} copy-done((s32[2]{0:T(128)S(1)}, s32[2]{0:T(128)}, u32[]{:S(2)}) %copy-start) | copy-done | bytes 32
  9.4 0.7 %copy-done.1 = s32[16]{0:T(128)S(1)} copy-done((s32[16]{0:T(128)S(1)}, s32[16]{0:T(128)}, u32[]{:S(2)}) %copy-start.1) | copy-done | bytes 88
  10.1 0.7 %copy-done.2 = s32[16]{0:T(128)S(1)} copy-done((s32[16]{0:T(128)S(1)}, s32[16]{0:T(128)}, u32[]{:S(2)}) %copy-start.2) | copy-done | bytes 88
  10.8 0.7 %copy-done.3 = s32[2]{0:T(128)S(1)} copy-done((s32[2]{0:T(128)S(1)}, s32[2]{0:T(128)}, u32[]{:S(2)}) %copy-start.3) | copy-done | bytes 32
  11.4 4.6 %base.1 = (f32[8,2048]{1,0:T(8,128)S(1)}, f32[256,128]{1,0:T(8,128)S(1)}, f32[2,8,128]{2,1,0:T(8,128)S(1)}, bf16[256,1024]{1,0:T(8,128)(2,1)S(1)}, bf16[256,1024...) custom-call(s32[1]{0:T(128)} %bitcast.refs_0_.index_ref, ...), custom_call_target="tpu_custom_call" | custom-call | flops 1000000 | tf_op jit(solution)/shard_map/base/pallas_call | solution.py:502
  16.1 0.5 %collective-permute-start.6 = (bf16[112,8,128]{2,1,0:T(8,128)(2,1)S(1)}, bf16[112,8,128]{2,1,0:T(8,128)(2,1)S(1)}, u32[]{:S(2)}, u32[]{:S(2)}) collective-permute-start(bf16[112,8,128]{2,1,0:T(8,128)(2,1)S(1)} %pad_maximum_fusion.refs_3_.refs_4_), channel_id=1, source_target_pairs={{0,1},{1,0},{2,3},{3,2},{4,5},{5,4},{6,7},{7,6},{8,9},{9,8},{10,11... | collective-permute-start | bytes 688136 | tf_op jit(solution)/shard_map/ppermute | solution.py:476
  16.6 0.8 %keep_states.2 = (f32[256,128]{1,0:T(8,128)S(1)}, f32[8,128]{1,0:T(8,128)S(1)}, f32[8,128]{1,0:T(8,128)S(1)}) custom-call(s32[1]{0:T(128)} %bitcast.refs_0_.index_ref, f32[256,128]{1,0:T(8,128)S(1)} %get-tuple-element.44.refs_1_, bf16[16,8,128]{2,1,0:T(8,128)(2,1)S(1)} %pack.1.own_ref.refs_5_.refs_2_, ...), custom_call_target="tpu_custom_call" | custom-call | flops 1000000 | tf_op jit(solution)/shard_map/keep_states/pallas_call | solution.py:502
  17.3 0.3 %collective-permute-done.6.refs_5_ = bf16[112,8,128]{2,1,0:T(8,128)(2,1)S(1)} collective-permute-done((bf16[112,8,128]{2,1,0:T(8,128)(2,1)S(1)}, bf16[112,8,128]{2,1,0:T(8,128)(2,1)S(1)}, u32[]{:S(2)}, u32[]{:S(2)}) %collective-permute-start.6) | collective-permute-done | bytes 229408 | tf_op jit(solution)/shard_map/ppermute | solution.py:476
  17.7 1.0 %send_states.1 = (bf16[720,128]{1,0:T(8,128)(2,1)S(1)}, f32[2,64,128]{2,1,0:T(8,128)S(1)}) custom-call(s32[1]{0:T(128)} %bitcast.refs_0_.index_ref, f32[256,128]{1,0:T(8,128)S(1)} %get-tuple-element.44.refs_1_, bf16[16,8,128]{2,1,0:T(8,128)(2,1)S(1)} %pack.1.own_ref.refs_5_.refs_2_, bf16[16,8,128]{2,1,0:T(8,128)(2,1)S(1)} %get-tuple-element.53.refs_3_, ...), custom_call_target="tpu_custom_call" | custom-call | flops 1000000 | tf_op jit(solution)/shard_map/send_states/pallas_call | solution.py:502
  18.7 0.4 %collective-permute-start.7 = (bf16[720,128]{1,0:T(8,128)(2,1)S(1)}, bf16[720,128]{1,0:T(8,128)(2,1)S(1)}, u32[]{:S(2)}, u32[]{:S(2)}) collective-permute-start(bf16[720,128]{1,0:T(8,128)(2,1)S(1)} %get-tuple-element.61), channel_id=1, source_target_pairs={{0,1},{1,0},{2,3},{3,2},{4,5},{5,4},{6,7},{7,6},{8,9},{9,8},{10,11... | collective-permute-start | bytes 552968 | tf_op jit(solution)/shard_map/ppermute | solution.py:476
  19.1 0.5 %keep_states.3 = (f32[256,128]{1,0:T(8,128)S(1)}, f32[8,128]{1,0:T(8,128)S(1)}) custom-call(s32[1]{0:T(128)} %bitcast.refs_0_.index_ref, f32[256,128]{1,0:T(8,128)S(1)} %get-tuple-element.44.refs_1_, bf16[16,8,128]{2,1,0:T(8,128)(2,1)S(1)} %pack.1.own_ref.refs_5_.refs_2_, bf16[112,8,128]{2,1,0:T(8,128)(2,1)S(1)} %pad_maximum_fusion.refs_3_.refs_4_, ...), custom_call_target="tpu_custom_call" | custom-call | flops 1000000 | tf_op jit(solution)/shard_map/keep_states/pallas_call | solution.py:502
  19.6 0.6 %collective-permute-done.7.refs_5_ = bf16[720,128]{1,0:T(8,128)(2,1)S(1)} collective-permute-done((bf16[720,128]{1,0:T(8,128)(2,1)S(1)}, bf16[720,128]{1,0:T(8,128)(2,1)S(1)}, u32[]{:S(2)}, u32[]{:S(2)}) %collective-permute-start.7) | collective-permute-done | bytes 184352 | tf_op jit(solution)/shard_map/ppermute | solution.py:476
  20.2 0.3 %join.1 = (bf16[96,128]{1,0:T(8,128)(2,1)S(1)}, bf16[96,128]{1,0:T(8,128)(2,1)S(1)}, bf16[160,128]{1,0:T(8,128)(2,1)S(1)}, bf16[160,128]{1,0:T(8,128)(2,1)S(1)}, bf16[160,128]{1,0:T(8,128)(2,1)S(1)}) custom-call(s32[1]{0:T(128)} %bitcast.refs_0_.index_ref, f32[256,128]{1,0:T(8,128)S(1)} %get-tuple-element.49.refs_0_, ...), custom_call_target="tpu_custom_call" | custom-call | flops 1000000 | tf_op jit(solution)/shard_map/join/pallas_call | solution.py:502
  20.5 2.9 %collective-permute-start.8 = (bf16[160,128]{1,0:T(8,128)(2,1)S(1)}, bf16[160,128]{1,0:T(8,128)(2,1)S(1)}, u32[]{:S(2)}, u32[]{:S(2)}) collective-permute-start(bf16[160,128]{1,0:T(8,128)(2,1)S(1)} %get-tuple-element.62), channel_id=1, source_target_pairs={{0,12},{1,15},{2,14},{3,13},{4,8},{5,11},{6,10},{7,9},{8,4},{9,7},... | collective-permute-start | bytes 122888 | tf_op jit(solution)/shard_map/ppermute | solution.py:476
  23.5 0.3 %collective-permute-start.10 = (bf16[160,128]{1,0:T(8,128)(2,1)S(1)}, bf16[160,128]{1,0:T(8,128)(2,1)S(1)}, u32[]{:S(2)}, u32[]{:S(2)}) collective-permute-start(bf16[160,128]{1,0:T(8,128)(2,1)S(1)} %get-tuple-element.67), channel_id=1, source_target_pairs={{0,8},{1,11},{2,10},{3,9},{4,12},{5,15},{6,14},{7,13},{8,0},{9,3},... | collective-permute-start | bytes 122888 | tf_op jit(solution)/shard_map/ppermute | solution.py:476
  23.8 1.2 %collective-permute-start.11 = (bf16[160,128]{1,0:T(8,128)(2,1)S(1)}, bf16[160,128]{1,0:T(8,128)(2,1)S(1)}, u32[]{:S(2)}, u32[]{:S(2)}) collective-permute-start(bf16[160,128]{1,0:T(8,128)(2,1)S(1)} %get-tuple-element.68), channel_id=1, source_target_pairs={{0,4},{1,7},{2,6},{3,5},{4,0},{5,3},{6,2},{7,1},{8,12},{9,15},{10,... | collective-permute-start | bytes 122888 | tf_op jit(solution)/shard_map/ppermute | solution.py:476
  25.0 0.5 %collective-permute-start.9 = (bf16[96,128]{1,0:T(8,128)(2,1)S(1)}, bf16[96,128]{1,0:T(8,128)(2,1)S(1)}, u32[]{:S(2)}, u32[]{:S(2)}) collective-permute-start(bf16[96,128]{1,0:T(8,128)(2,1)S(1)} %get-tuple-element.65), channel_id=1, source_target_pairs={{0,2},{1,3},{2,0},{3,1},{4,6},{5,7},{6,4},{7,5},{8,10},{9,11},{10,... | collective-permute-start | bytes 73736 | tf_op jit(solution)/shard_map/ppermute | solution.py:476
  25.5 0.9 %collective-permute-done.8.refs_2_ = bf16[160,128]{1,0:T(8,128)(2,1)S(1)} collective-permute-done((bf16[160,128]{1,0:T(8,128)(2,1)S(1)}, bf16[160,128]{1,0:T(8,128)(2,1)S(1)}, u32[]{:S(2)}, u32[]{:S(2)}) %collective-permute-start.8) | collective-permute-done | bytes 40992 | tf_op jit(solution)/shard_map/ppermute | solution.py:476
  26.4 0.3 collective-permute-start.12
  26.7 2.7 %collective-permute-done.10.refs_3_ = bf16[160,128]{1,0:T(8,128)(2,1)S(1)} collective-permute-done((bf16[160,128]{1,0:T(8,128)(2,1)S(1)}, bf16[160,128]{1,0:T(8,128)(2,1)S(1)}, u32[]{:S(2)}, u32[]{:S(2)}) %collective-permute-start.10) | collective-permute-done | bytes 40992 | tf_op jit(solution)/shard_map/ppermute | solution.py:476
  29.4 0.7 %collective-permute-start.13 = (bf16[96,128]{1,0:T(8,128)(2,1)S(1)}, bf16[96,128]{1,0:T(8,128)(2,1)S(1)}, u32[]{:S(2)}, u32[]{:S(2)}) collective-permute-start(bf16[96,128]{1,0:T(8,128)(2,1)S(1)} %slice.12), channel_id=1, source_target_pairs={{0,1},{1,0},{2,3},{3,2},{4,5},{5,4},{6,7},{7,6},{8,9},{9,8},{10,11... | collective-permute-start | bytes 73736 | tf_op jit(solution)/shard_map/ppermute | solution.py:476
  30.5 0.4 %collective-permute-done.13.refs_6_ = bf16[96,128]{1,0:T(8,128)(2,1)S(1)} collective-permute-done((bf16[96,128]{1,0:T(8,128)(2,1)S(1)}, bf16[96,128]{1,0:T(8,128)(2,1)S(1)}, u32[]{:S(2)}, u32[]{:S(2)}) %collective-permute-start.13) | collective-permute-done | bytes 24608 | tf_op jit(solution)/shard_map/ppermute | solution.py:476
  30.9 0.4 %collective-permute-done.14.refs_7_ = bf16[96,128]{1,0:T(8,128)(2,1)S(1)} collective-permute-done((bf16[96,128]{1,0:T(8,128)(2,1)S(1)}, bf16[96,128]{1,0:T(8,128)(2,1)S(1)}, u32[]{:S(2)}, u32[]{:S(2)}) %collective-permute-start.14) | collective-permute-done | bytes 24608 | tf_op jit(solution)/shard_map/ppermute | solution.py:476
  31.2 1.0 %merge_states.1 = bf16[2,4,1024]{2,1,0:T(4,128)(2,1)} custom-call(bf16[16,8,128]{2,1,0:T(8,128)(2,1)S(1)} %pack.1.own_ref.refs_5_.refs_2_, f32[8,128]{1,0:T(8,128)S(1)} %get-tuple-element.72.cos_ref, f32[8,128]{1,0:T(8,128)S(1)} %get-tuple-element.73.sin_ref, bf16[96,128]{1,0:T(8,128)(2,1)S(1)} %get-tuple-element.64.refs_0_, ...), custom_call_target="tpu_custom_call" | custom-call | tf_op jit(solution)/shard_map/merge_states/pallas_call | solution.py:622
  (25 shorter events, 0.6 us)
Async XLA Ops:
  0.0 1.5 %collective-permute-start = (bf16[2,4,1024]{2,1,0:T(4,128)(2,1)}, bf16[2,4,1024]{2,1,0:T(4,128)(2,1)S(1)}, u32[]{:S(2)}, u32[]{:S(2)}) collective-permute-start(bf16[2,4,1024]{2,1,0:T(4,128)(2,1)} %query_ref.1), channel_id=1, source_target_pairs={{0,1},{1,0},{2,3},{3,2},{4,5},{5,4},{6,7},{7,6},{8,9},{9,8},{10,11... | collective-permute-start | bytes 49160 | tf_op jit(solution)/shard_map/ppermute | solution.py:476
  0.5 1.4 %collective-permute-start.1 = (bf16[2,4,1024]{2,1,0:T(4,128)(2,1)}, bf16[2,4,1024]{2,1,0:T(4,128)(2,1)S(1)}, u32[]{:S(2)}, u32[]{:S(2)}) collective-permute-start(bf16[2,4,1024]{2,1,0:T(4,128)(2,1)} %hidden_ref.1), channel_id=1, source_target_pairs={{0,1},{1,0},{2,3},{3,2},{4,5},{5,4},{6,7},{7,6},{8,9},{9,8},{10,11... | collective-permute-start | bytes 49160 | tf_op jit(solution)/shard_map/ppermute | solution.py:476
  1.9 14.2 %collective-permute-start.3 = (bf16[32,8,128]{2,1,0:T(8,128)(2,1)S(1)}, bf16[32,8,128]{2,1,0:T(8,128)(2,1)S(1)}, u32[]{:S(2)}, u32[]{:S(2)}) collective-permute-start(bf16[32,8,128]{2,1,0:T(8,128)(2,1)S(1)} %get-tuple-element.41), channel_id=1, source_target_pairs={{0,8},{1,11},{2,10},{3,9},{4,12},{5,15},{6,14},{7,13},{8,0},{9,3},... | collective-permute-start | bytes 196616 | tf_op jit(solution)/shard_map/ppermute | solution.py:476
  5.7 10.4 %collective-permute-start.4 = (bf16[32,8,128]{2,1,0:T(8,128)(2,1)S(1)}, bf16[32,8,128]{2,1,0:T(8,128)(2,1)S(1)}, u32[]{:S(2)}, u32[]{:S(2)}) collective-permute-start(bf16[32,8,128]{2,1,0:T(8,128)(2,1)S(1)} %get-tuple-element.41), channel_id=1, source_target_pairs={{0,12},{1,15},{2,14},{3,13},{4,8},{5,11},{6,10},{7,9},{8,4},{9,7},... | collective-permute-start | bytes 196616 | tf_op jit(solution)/shard_map/ppermute | solution.py:476
  7.0 9.0 %collective-permute-start.5 = (bf16[32,8,128]{2,1,0:T(8,128)(2,1)S(1)}, bf16[32,8,128]{2,1,0:T(8,128)(2,1)S(1)}, u32[]{:S(2)}, u32[]{:S(2)}) collective-permute-start(bf16[32,8,128]{2,1,0:T(8,128)(2,1)S(1)} %get-tuple-element.41), channel_id=1, source_target_pairs={{0,4},{1,7},{2,6},{3,5},{4,0},{5,3},{6,2},{7,1},{8,12},{9,15},{10,... | collective-permute-start | bytes 196616 | tf_op jit(solution)/shard_map/ppermute | solution.py:476
  7.3 8.8 %collective-permute-start.2 = (bf16[16,8,128]{2,1,0:T(8,128)(2,1)S(1)}, bf16[16,8,128]{2,1,0:T(8,128)(2,1)S(1)}, u32[]{:S(2)}, u32[]{:S(2)}) collective-permute-start(bf16[16,8,128]{2,1,0:T(8,128)(2,1)S(1)} %pack.1.own_ref.refs_5_.refs_2_), channel_id=1, source_target_pairs={{0,2},{1,3},{2,0},{3,1},{4,6},{5,7},{6,4},{7,5},{8,10},{9,11},{10,... | collective-permute-start | bytes 98312 | tf_op jit(solution)/shard_map/ppermute | solution.py:476
  8.8 0.7 %copy-start = (s32[2]{0:T(128)S(1)}, s32[2]{0:T(128)}, u32[]{:S(2)}) copy-start(s32[2]{0:T(128)} %refs_2_.1) | copy-start | bytes 28
  9.4 0.7 %copy-start.1 = (s32[16]{0:T(128)S(1)}, s32[16]{0:T(128)}, u32[]{:S(2)}) copy-start(s32[16]{0:T(128)} %refs_3_.1) | copy-start | bytes 196
  10.1 0.7 %copy-start.2 = (s32[16]{0:T(128)S(1)}, s32[16]{0:T(128)}, u32[]{:S(2)}) copy-start(s32[16]{0:T(128)} %refs_4_.1) | copy-start | bytes 196
  10.7 0.7 %copy-start.3 = (s32[2]{0:T(128)S(1)}, s32[2]{0:T(128)}, u32[]{:S(2)}) copy-start(s32[2]{0:T(128)} %refs_1_.1) | copy-start | bytes 28
  16.1 1.6 %collective-permute-start.6 = (bf16[112,8,128]{2,1,0:T(8,128)(2,1)S(1)}, bf16[112,8,128]{2,1,0:T(8,128)(2,1)S(1)}, u32[]{:S(2)}, u32[]{:S(2)}) collective-permute-start(bf16[112,8,128]{2,1,0:T(8,128)(2,1)S(1)} %pad_maximum_fusion.refs_3_.refs_4_), channel_id=1, source_target_pairs={{0,1},{1,0},{2,3},{3,2},{4,5},{5,4},{6,7},{7,6},{8,9},{9,8},{10,11... | collective-permute-start | bytes 688136 | tf_op jit(solution)/shard_map/ppermute | solution.py:476
  16.6 13.6 %copy-start.4 = (s32[2]{0:T(128)S(1)}, s32[2]{0:T(128)}, u32[]{:S(2)}) copy-start(s32[2]{0:T(128)} %refs_1_.1) | copy-start | bytes 28
  18.7 1.5 %collective-permute-start.7 = (bf16[720,128]{1,0:T(8,128)(2,1)S(1)}, bf16[720,128]{1,0:T(8,128)(2,1)S(1)}, u32[]{:S(2)}, u32[]{:S(2)}) collective-permute-start(bf16[720,128]{1,0:T(8,128)(2,1)S(1)} %get-tuple-element.61), channel_id=1, source_target_pairs={{0,1},{1,0},{2,3},{3,2},{4,5},{5,4},{6,7},{7,6},{8,9},{9,8},{10,11... | collective-permute-start | bytes 552968 | tf_op jit(solution)/shard_map/ppermute | solution.py:476
  20.5 5.9 %collective-permute-start.8 = (bf16[160,128]{1,0:T(8,128)(2,1)S(1)}, bf16[160,128]{1,0:T(8,128)(2,1)S(1)}, u32[]{:S(2)}, u32[]{:S(2)}) collective-permute-start(bf16[160,128]{1,0:T(8,128)(2,1)S(1)} %get-tuple-element.62), channel_id=1, source_target_pairs={{0,12},{1,15},{2,14},{3,13},{4,8},{5,11},{6,10},{7,9},{8,4},{9,7},... | collective-permute-start | bytes 122888 | tf_op jit(solution)/shard_map/ppermute | solution.py:476
  23.5 5.9 %collective-permute-start.10 = (bf16[160,128]{1,0:T(8,128)(2,1)S(1)}, bf16[160,128]{1,0:T(8,128)(2,1)S(1)}, u32[]{:S(2)}, u32[]{:S(2)}) collective-permute-start(bf16[160,128]{1,0:T(8,128)(2,1)S(1)} %get-tuple-element.67), channel_id=1, source_target_pairs={{0,8},{1,11},{2,10},{3,9},{4,12},{5,15},{6,14},{7,13},{8,0},{9,3},... | collective-permute-start | bytes 122888 | tf_op jit(solution)/shard_map/ppermute | solution.py:476
  23.8 6.3 %collective-permute-start.11 = (bf16[160,128]{1,0:T(8,128)(2,1)S(1)}, bf16[160,128]{1,0:T(8,128)(2,1)S(1)}, u32[]{:S(2)}, u32[]{:S(2)}) collective-permute-start(bf16[160,128]{1,0:T(8,128)(2,1)S(1)} %get-tuple-element.68), channel_id=1, source_target_pairs={{0,4},{1,7},{2,6},{3,5},{4,0},{5,3},{6,2},{7,1},{8,12},{9,15},{10,... | collective-permute-start | bytes 122888 | tf_op jit(solution)/shard_map/ppermute | solution.py:476
  25.0 5.5 %collective-permute-start.9 = (bf16[96,128]{1,0:T(8,128)(2,1)S(1)}, bf16[96,128]{1,0:T(8,128)(2,1)S(1)}, u32[]{:S(2)}, u32[]{:S(2)}) collective-permute-start(bf16[96,128]{1,0:T(8,128)(2,1)S(1)} %get-tuple-element.65), channel_id=1, source_target_pairs={{0,2},{1,3},{2,0},{3,1},{4,6},{5,7},{6,4},{7,5},{8,10},{9,11},{10,... | collective-permute-start | bytes 73736 | tf_op jit(solution)/shard_map/ppermute | solution.py:476
  26.4 4.1 %collective-permute-start.12 = (bf16[96,128]{1,0:T(8,128)(2,1)S(1)}, bf16[96,128]{1,0:T(8,128)(2,1)S(1)}, u32[]{:S(2)}, u32[]{:S(2)}) collective-permute-start(bf16[96,128]{1,0:T(8,128)(2,1)S(1)} %slice.9), channel_id=1, source_target_pairs={{0,1},{1,0},{2,3},{3,2},{4,5},{5,4},{6,7},{7,6},{8,9},{9,8},{10,11... | collective-permute-start | bytes 73736 | tf_op jit(solution)/shard_map/ppermute | solution.py:476
  29.4 1.5 %collective-permute-start.13 = (bf16[96,128]{1,0:T(8,128)(2,1)S(1)}, bf16[96,128]{1,0:T(8,128)(2,1)S(1)}, u32[]{:S(2)}, u32[]{:S(2)}) collective-permute-start(bf16[96,128]{1,0:T(8,128)(2,1)S(1)} %slice.12), channel_id=1, source_target_pairs={{0,1},{1,0},{2,3},{3,2},{4,5},{5,4},{6,7},{7,6},{8,9},{9,8},{10,11... | collective-permute-start | bytes 73736 | tf_op jit(solution)/shard_map/ppermute | solution.py:476
  30.0 1.2 %collective-permute-start.14 = (bf16[96,128]{1,0:T(8,128)(2,1)S(1)}, bf16[96,128]{1,0:T(8,128)(2,1)S(1)}, u32[]{:S(2)}, u32[]{:S(2)}) collective-permute-start(bf16[96,128]{1,0:T(8,128)(2,1)S(1)} %slice.13), channel_id=1, source_target_pairs={{0,1},{1,0},{2,3},{3,2},{4,5},{5,4},{6,7},{7,6},{8,9},{9,8},{10,11... | collective-permute-start | bytes 73736 | tf_op jit(solution)/shard_map/ppermute | solution.py:476

commit v18 on v17

--- a/solution.py
+++ b/solution.py
@@ -146,10 +146,10 @@
 
 
 def base_kernel(sizes, plan, *refs):
-    (index_ref, length_ref, adapter_ref, rank_ref, pool_ref) = refs[:5]
+    index_ref, *scalars = refs[:5]
     (own_ref, weight_ref, down_ref, *sources) = refs[5:11]
     (base_ref, bias_ref, mask_ref, *held) = refs[11:17]
-    *halves, buffer, sems, row_sems = refs[17:]
+    *halves, buffer, length_ref, adapter_ref, rank_ref, pool_ref, sems, row_sems, scalar_sems = refs[17:]
     requests, tokens, devices = sizes
     rows = requests * tokens
     here = index_ref[0]
@@ -163,9 +163,24 @@
         for i, (source, place) in enumerate(zip(sources, held))
     ]
     others += streams(sources_of(plan), index_ref, down_ref, halves, row_sems)
-    for load in loads + others:
+    scalars = [
+        pltpu.make_async_copy(source, place, scalar_sems.at[i])
+        for i, (source, place) in enumerate(
+            zip(scalars, (length_ref, adapter_ref, rank_ref, pool_ref))
+        )
+    ]
+    for load in scalars + loads + others:
         load.start()
-
+    tiles = depth // HEAD_WIDTH
+    total = jnp.zeros(base_ref.shape, jnp.float32)
+    for p in range(parts):
+        first = plan.heads + p * tiles
+        hidden = jnp.concatenate([own_ref[first + c] for c in range(tiles)], axis=1)
+        loads[p].wait()
+        total += dot(hidden, buffer[p], ((1,), (0,)))
+    base_ref[...] = total
+    for load in scalars:
+        load.wait()
     positions = bias_ref.shape[0] // requests
     place = lax.broadcasted_iota(jnp.int32, bias_ref.shape, 0)
     column = lax.broadcasted_iota(jnp.int32, bias_ref.shape, 1)
@@ -187,15 +202,6 @@
     column = lax.broadcasted_iota(jnp.int32, ranks.shape, 1)
     mask_ref[0] = jnp.where(column < ranks, 1.0, 0.0)
     mask_ref[1] = jnp.where(owners == here, 1.0, 0.0)
-
-    tiles = depth // HEAD_WIDTH
-    total = jnp.zeros(base_ref.shape, jnp.float32)
-    for p in range(parts):
-        first = plan.heads + p * tiles
-        hidden = jnp.concatenate([own_ref[first + c] for c in range(tiles)], axis=1)
-        loads[p].wait()
-        total += dot(hidden, buffer[p], ((1,), (0,)))
-    base_ref[...] = total
     for load in others:
         load.wait()
 
@@ -549,12 +555,14 @@
     rank = down.shape[1]
     up = adapter_up_weight[0]
     big = (keys, values, up)
+    scalars = (lengths, request_adapter, adapter_rank_list, adapter_pool_row)
     base, bias, masks, keys, values, up, *halves = call(
         functools.partial(base_kernel, sizes, plan),
-        (index, lengths, request_adapter, adapter_rank_list, adapter_pool_row)
+        (index,)
+        + tuple(pinned(x) for x in scalars)
         + (late_own, pinned(key_value_weight), down)
         + tuple(pinned(x) for x in big),
-        [smem()] * 5 + [vmem()] + [hbm()] * 5,
+        [smem()] + [hbm()] * 4 + [vmem()] + [hbm()] * 5,
         [
             pltpu.VMEM((rows, out_width), jnp.float32),
             pltpu.VMEM((flat, HEAD_WIDTH), jnp.float32),
@@ -564,8 +572,10 @@
         + [pltpu.VMEM((devices // 2, width, rank), jnp.bfloat16)] * 2,
         [
             pltpu.VMEM((parts, width // parts, out_width), jnp.bfloat16),
+            *[pltpu.SMEM(x.shape, x.dtype) for x in scalars],
             pltpu.SemaphoreType.DMA((parts + 3,)),
             pltpu.SemaphoreType.DMA((devices,)),
+            pltpu.SemaphoreType.DMA((4,)),
         ],
         "base",
     )

time: 32.6 us -> 29.5 us (0.905)
  local copies, waits for them, and re-layouts: 2.71 us -> 0.1 us
  starting transfers between devices: 14.3 us -> 15.1 us
  waiting for transfers between devices: 5.85 us -> 5.08 us
  Pallas kernels: 9 us -> 8.49 us
    unnamed x10 -> x2, local copies, waits for them, and re-layouts: 2.62 us -> 0.01 us
    ppermute x15, starting transfers between devices: 14.3 us -> 15.1 us  [trade(): return lax.ppermute(x, 'tensor', pairs)]
    ppermute x15, waiting for transfers between devices: 5.85 us -> 5.08 us  [trade(): return lax.ppermute(x, 'tensor', pairs)]
    pallas_call x7, Pallas kernels: 7.96 us -> 7.45 us  [call(): pl.pallas_call(kernel, out_shape=tuple(out_shape), in_specs=in_specs, out...]
  transfers between devices with their start and end apart: 15 -> 15, of which waited for: 8 -> 8; matrix products, arithmetic and copies ran while one was open for 1% -> 1% of each run, Pallas kernels for 20% -> 21%
where the time goes in v18:
time: 29.5 us; the launch traced here: 29.2 us
  starting transfers between devices  15.1 us (51%)
  Pallas kernels  8.49 us (29%)
  waiting for transfers between devices  5.08 us (17%)
  other arithmetic  0.3 us (1%)
    ppermute x15, starting transfers between devices, trade(): return lax.ppermute(x, 'tensor', pairs)  15.1 us
    pallas_call x7, Pallas kernels, call(): pl.pallas_call(kernel, out_shape=tuple(out_shape), in_specs=in_specs, out...  7.45 us
    ppermute x15, waiting for transfers between devices, trade(): return lax.ppermute(x, 'tensor', pairs)  5.08 us
    pallas_call x1, Pallas kernels, per_device(): pl.pallas_call(functools.partial(merge_kernel, devices, requests, tokens,...  1.04 us
  transfers between devices with their start and end apart: 15, of which 8 were waited for; matrix products, arithmetic and copies ran while one was open for 1% of the time, Pallas kernels for 21%

profile of v18, /device:TPU:0, one launch (start us, length us, event | category | flops | bytes accessed | tf_op | source)
XLA Modules:
  0.0 29.2 jit_solution(3602072200433863555)
XLA Ops:
  0.0 0.5 %collective-permute-start = (bf16[2,4,1024]{2,1,0:T(4,128)(2,1)}, bf16[2,4,1024]{2,1,0:T(4,128)(2,1)S(1)}, u32[]{:S(2)}, u32[]{:S(2)}) collective-permute-start(bf16[2,4,1024]{2,1,0:T(4,128)(2,1)} %query_ref.1), channel_id=1, source_target_pairs={{0,1},{1,0},{2,3},{3,2},{4,5},{5,4},{6,7},{7,6},{8,9},{9,8},{10,11... | collective-permute-start | bytes 49160 | tf_op jit(solution)/shard_map/ppermute | solution.py:482
  0.5 0.1 collective-permute-start.1
  0.5 0.8 %pack.1.own_ref.refs_5_.refs_2_ = bf16[16,8,128]{2,1,0:T(8,128)(2,1)S(1)} custom-call(bf16[2,4,1024]{2,1,0:T(4,128)(2,1)} %query_ref.1, bf16[2,4,1024]{2,1,0:T(4,128)(2,1)} %hidden_ref.1), custom_call_target="tpu_custom_call" | custom-call | flops 1000000 | tf_op jit(solution)/shard_map/pack/pallas_call | solution.py:508
  1.3 0.2 collective-permute-done.query_ref
  1.5 0.3 %collective-permute-done.1.hidden_ref = bf16[2,4,1024]{2,1,0:T(4,128)(2,1)S(1)} collective-permute-done((bf16[2,4,1024]{2,1,0:T(4,128)(2,1)}, bf16[2,4,1024]{2,1,0:T(4,128)(2,1)S(1)}, u32[]{:S(2)}, u32[]{:S(2)}) %collective-permute-start.1) | collective-permute-done | bytes 16416 | tf_op jit(solution)/shard_map/ppermute | solution.py:482
  1.9 3.8 %collective-permute-start.3 = (bf16[32,8,128]{2,1,0:T(8,128)(2,1)S(1)}, bf16[32,8,128]{2,1,0:T(8,128)(2,1)S(1)}, u32[]{:S(2)}, u32[]{:S(2)}) collective-permute-start(bf16[32,8,128]{2,1,0:T(8,128)(2,1)S(1)} %get-tuple-element.41), channel_id=1, source_target_pairs={{0,8},{1,11},{2,10},{3,9},{4,12},{5,15},{6,14},{7,13},{8,0},{9,3},... | collective-permute-start | bytes 196616 | tf_op jit(solution)/shard_map/ppermute | solution.py:482
  5.7 1.3 %collective-permute-start.4 = (bf16[32,8,128]{2,1,0:T(8,128)(2,1)S(1)}, bf16[32,8,128]{2,1,0:T(8,128)(2,1)S(1)}, u32[]{:S(2)}, u32[]{:S(2)}) collective-permute-start(bf16[32,8,128]{2,1,0:T(8,128)(2,1)S(1)} %get-tuple-element.41), channel_id=1, source_target_pairs={{0,12},{1,15},{2,14},{3,13},{4,8},{5,11},{6,10},{7,9},{8,4},{9,7},... | collective-permute-start | bytes 196616 | tf_op jit(solution)/shard_map/ppermute | solution.py:482
  7.0 0.2 collective-permute-start.5
  7.3 1.5 %collective-permute-start.2 = (bf16[16,8,128]{2,1,0:T(8,128)(2,1)S(1)}, bf16[16,8,128]{2,1,0:T(8,128)(2,1)S(1)}, u32[]{:S(2)}, u32[]{:S(2)}) collective-permute-start(bf16[16,8,128]{2,1,0:T(8,128)(2,1)S(1)} %pack.1.own_ref.refs_5_.refs_2_), channel_id=1, source_target_pairs={{0,2},{1,3},{2,0},{3,1},{4,6},{5,7},{6,4},{7,5},{8,10},{9,11},{10,... | collective-permute-start | bytes 98312 | tf_op jit(solution)/shard_map/ppermute | solution.py:482
  8.8 4.1 %base.1 = (f32[8,2048]{1,0:T(8,128)S(1)}, f32[256,128]{1,0:T(8,128)S(1)}, f32[2,8,128]{2,1,0:T(8,128)S(1)}, bf16[256,1024]{1,0:T(8,128)(2,1)S(1)}, bf16[256,1024...) custom-call(s32[1]{0:T(128)} %bitcast.refs_0_.index_ref, ...), custom_call_target="tpu_custom_call" | custom-call | flops 1000000 | tf_op jit(solution)/shard_map/base/pallas_call | solution.py:508
  13.0 0.8 %collective-permute-start.6 = (bf16[112,8,128]{2,1,0:T(8,128)(2,1)S(1)}, bf16[112,8,128]{2,1,0:T(8,128)(2,1)S(1)}, u32[]{:S(2)}, u32[]{:S(2)}) collective-permute-start(bf16[112,8,128]{2,1,0:T(8,128)(2,1)S(1)} %pad_maximum_fusion.refs_3_.refs_4_), channel_id=1, source_target_pairs={{0,1},{1,0},{2,3},{3,2},{4,5},{5,4},{6,7},{7,6},{8,9},{9,8},{10,11... | collective-permute-start | bytes 688136 | tf_op jit(solution)/shard_map/ppermute | solution.py:482
  13.8 0.8 %keep_states.2 = (f32[256,128]{1,0:T(8,128)S(1)}, f32[8,128]{1,0:T(8,128)S(1)}, f32[8,128]{1,0:T(8,128)S(1)}) custom-call(s32[1]{0:T(128)} %bitcast.refs_0_.index_ref, f32[256,128]{1,0:T(8,128)S(1)} %get-tuple-element.44.refs_1_, bf16[16,8,128]{2,1,0:T(8,128)(2,1)S(1)} %pack.1.own_ref.refs_5_.refs_2_, ...), custom_call_target="tpu_custom_call" | custom-call | flops 1000000 | tf_op jit(solution)/shard_map/keep_states/pallas_call | solution.py:508
  14.5 0.3 %collective-permute-done.6.refs_5_ = bf16[112,8,128]{2,1,0:T(8,128)(2,1)S(1)} collective-permute-done((bf16[112,8,128]{2,1,0:T(8,128)(2,1)S(1)}, bf16[112,8,128]{2,1,0:T(8,128)(2,1)S(1)}, u32[]{:S(2)}, u32[]{:S(2)}) %collective-permute-start.6) | collective-permute-done | bytes 229408 | tf_op jit(solution)/shard_map/ppermute | solution.py:482
  14.9 1.0 %send_states.1 = (bf16[720,128]{1,0:T(8,128)(2,1)S(1)}, f32[2,64,128]{2,1,0:T(8,128)S(1)}) custom-call(s32[1]{0:T(128)} %bitcast.refs_0_.index_ref, f32[256,128]{1,0:T(8,128)S(1)} %get-tuple-element.44.refs_1_, bf16[16,8,128]{2,1,0:T(8,128)(2,1)S(1)} %pack.1.own_ref.refs_5_.refs_2_, bf16[16,8,128]{2,1,0:T(8,128)(2,1)S(1)} %get-tuple-element.53.refs_3_, ...), custom_call_target="tpu_custom_call" | custom-call | flops 1000000 | tf_op jit(solution)/shard_map/send_states/pallas_call | solution.py:508
  15.9 0.4 %collective-permute-start.7 = (bf16[720,128]{1,0:T(8,128)(2,1)S(1)}, bf16[720,128]{1,0:T(8,128)(2,1)S(1)}, u32[]{:S(2)}, u32[]{:S(2)}) collective-permute-start(bf16[720,128]{1,0:T(8,128)(2,1)S(1)} %get-tuple-element.61), channel_id=1, source_target_pairs={{0,1},{1,0},{2,3},{3,2},{4,5},{5,4},{6,7},{7,6},{8,9},{9,8},{10,11... | collective-permute-start | bytes 552968 | tf_op jit(solution)/shard_map/ppermute | solution.py:482
  16.3 0.5 %keep_states.3 = (f32[256,128]{1,0:T(8,128)S(1)}, f32[8,128]{1,0:T(8,128)S(1)}) custom-call(s32[1]{0:T(128)} %bitcast.refs_0_.index_ref, f32[256,128]{1,0:T(8,128)S(1)} %get-tuple-element.44.refs_1_, bf16[16,8,128]{2,1,0:T(8,128)(2,1)S(1)} %pack.1.own_ref.refs_5_.refs_2_, bf16[112,8,128]{2,1,0:T(8,128)(2,1)S(1)} %pad_maximum_fusion.refs_3_.refs_4_, ...), custom_call_target="tpu_custom_call" | custom-call | flops 1000000 | tf_op jit(solution)/shard_map/keep_states/pallas_call | solution.py:508
  16.8 0.6 %collective-permute-done.7.refs_5_ = bf16[720,128]{1,0:T(8,128)(2,1)S(1)} collective-permute-done((bf16[720,128]{1,0:T(8,128)(2,1)S(1)}, bf16[720,128]{1,0:T(8,128)(2,1)S(1)}, u32[]{:S(2)}, u32[]{:S(2)}) %collective-permute-start.7) | collective-permute-done | bytes 184352 | tf_op jit(solution)/shard_map/ppermute | solution.py:482
  17.3 0.3 %join.1 = (bf16[96,128]{1,0:T(8,128)(2,1)S(1)}, bf16[96,128]{1,0:T(8,128)(2,1)S(1)}, bf16[160,128]{1,0:T(8,128)(2,1)S(1)}, bf16[160,128]{1,0:T(8,128)(2,1)S(1)}, bf16[160,128]{1,0:T(8,128)(2,1)S(1)}) custom-call(s32[1]{0:T(128)} %bitcast.refs_0_.index_ref, f32[256,128]{1,0:T(8,128)S(1)} %get-tuple-element.49.refs_0_, ...), custom_call_target="tpu_custom_call" | custom-call | flops 1000000 | tf_op jit(solution)/shard_map/join/pallas_call | solution.py:508
  17.7 3.4 %collective-permute-start.8 = (bf16[160,128]{1,0:T(8,128)(2,1)S(1)}, bf16[160,128]{1,0:T(8,128)(2,1)S(1)}, u32[]{:S(2)}, u32[]{:S(2)}) collective-permute-start(bf16[160,128]{1,0:T(8,128)(2,1)S(1)} %get-tuple-element.62), channel_id=1, source_target_pairs={{0,12},{1,15},{2,14},{3,13},{4,8},{5,11},{6,10},{7,9},{8,4},{9,7},... | collective-permute-start | bytes 122888 | tf_op jit(solution)/shard_map/ppermute | solution.py:482
  21.1 1.1 %collective-permute-start.11 = (bf16[160,128]{1,0:T(8,128)(2,1)S(1)}, bf16[160,128]{1,0:T(8,128)(2,1)S(1)}, u32[]{:S(2)}, u32[]{:S(2)}) collective-permute-start(bf16[160,128]{1,0:T(8,128)(2,1)S(1)} %get-tuple-element.68), channel_id=1, source_target_pairs={{0,4},{1,7},{2,6},{3,5},{4,0},{5,3},{6,2},{7,1},{8,12},{9,15},{10,... | collective-permute-start | bytes 122888 | tf_op jit(solution)/shard_map/ppermute | solution.py:482
  22.2 1.4 %collective-permute-start.9 = (bf16[96,128]{1,0:T(8,128)(2,1)S(1)}, bf16[96,128]{1,0:T(8,128)(2,1)S(1)}, u32[]{:S(2)}, u32[]{:S(2)}) collective-permute-start(bf16[96,128]{1,0:T(8,128)(2,1)S(1)} %get-tuple-element.65), channel_id=1, source_target_pairs={{0,2},{1,3},{2,0},{3,1},{4,6},{5,7},{6,4},{7,5},{8,10},{9,11},{10,... | collective-permute-start | bytes 73736 | tf_op jit(solution)/shard_map/ppermute | solution.py:482
  23.5 0.4 %collective-permute-done.8.refs_2_ = bf16[160,128]{1,0:T(8,128)(2,1)S(1)} collective-permute-done((bf16[160,128]{1,0:T(8,128)(2,1)S(1)}, bf16[160,128]{1,0:T(8,128)(2,1)S(1)}, u32[]{:S(2)}, u32[]{:S(2)}) %collective-permute-start.8) | collective-permute-done | bytes 40992 | tf_op jit(solution)/shard_map/ppermute | solution.py:482
  24.0 2.4 %collective-permute-done.10.refs_3_ = bf16[160,128]{1,0:T(8,128)(2,1)S(1)} collective-permute-done((bf16[160,128]{1,0:T(8,128)(2,1)S(1)}, bf16[160,128]{1,0:T(8,128)(2,1)S(1)}, u32[]{:S(2)}, u32[]{:S(2)}) %collective-permute-start.10) | collective-permute-done | bytes 40992 | tf_op jit(solution)/shard_map/ppermute | solution.py:482
  26.4 0.5 %collective-permute-start.13 = (bf16[96,128]{1,0:T(8,128)(2,1)S(1)}, bf16[96,128]{1,0:T(8,128)(2,1)S(1)}, u32[]{:S(2)}, u32[]{:S(2)}) collective-permute-start(bf16[96,128]{1,0:T(8,128)(2,1)S(1)} %slice.12), channel_id=1, source_target_pairs={{0,1},{1,0},{2,3},{3,2},{4,5},{5,4},{6,7},{7,6},{8,9},{9,8},{10,11... | collective-permute-start | bytes 73736 | tf_op jit(solution)/shard_map/ppermute | solution.py:482
  26.9 0.1 collective-permute-start.14
  27.0 0.1 add_convert_fusion
  27.1 0.1 convert_element_type.11
  27.2 0.1 fusion
  27.3 0.1 pad_maximum_fusion.1
  27.4 0.4 %collective-permute-done.13.refs_6_ = bf16[96,128]{1,0:T(8,128)(2,1)S(1)} collective-permute-done((bf16[96,128]{1,0:T(8,128)(2,1)S(1)}, bf16[96,128]{1,0:T(8,128)(2,1)S(1)}, u32[]{:S(2)}, u32[]{:S(2)}) %collective-permute-start.13) | collective-permute-done | bytes 24608 | tf_op jit(solution)/shard_map/ppermute | solution.py:482
  27.8 0.4 %collective-permute-done.14.refs_7_ = bf16[96,128]{1,0:T(8,128)(2,1)S(1)} collective-permute-done((bf16[96,128]{1,0:T(8,128)(2,1)S(1)}, bf16[96,128]{1,0:T(8,128)(2,1)S(1)}, u32[]{:S(2)}, u32[]{:S(2)}) %collective-permute-start.14) | collective-permute-done | bytes 24608 | tf_op jit(solution)/shard_map/ppermute | solution.py:482
  28.1 1.0 %merge_states.1 = bf16[2,4,1024]{2,1,0:T(4,128)(2,1)} custom-call(bf16[16,8,128]{2,1,0:T(8,128)(2,1)S(1)} %pack.1.own_ref.refs_5_.refs_2_, f32[8,128]{1,0:T(8,128)S(1)} %get-tuple-element.72.cos_ref, f32[8,128]{1,0:T(8,128)S(1)} %get-tuple-element.73.sin_ref, bf16[96,128]{1,0:T(8,128)(2,1)S(1)} %get-tuple-element.64.refs_0_, ...), custom_call_target="tpu_custom_call" | custom-call | tf_op jit(solution)/shard_map/merge_states/pallas_call | solution.py:632
  (17 shorter events, 0.1 us)
Async XLA Ops:
  0.0 1.5 %collective-permute-start = (bf16[2,4,1024]{2,1,0:T(4,128)(2,1)}, bf16[2,4,1024]{2,1,0:T(4,128)(2,1)S(1)}, u32[]{:S(2)}, u32[]{:S(2)}) collective-permute-start(bf16[2,4,1024]{2,1,0:T(4,128)(2,1)} %query_ref.1), channel_id=1, source_target_pairs={{0,1},{1,0},{2,3},{3,2},{4,5},{5,4},{6,7},{7,6},{8,9},{9,8},{10,11... | collective-permute-start | bytes 49160 | tf_op jit(solution)/shard_map/ppermute | solution.py:482
  0.5 1.4 %collective-permute-start.1 = (bf16[2,4,1024]{2,1,0:T(4,128)(2,1)}, bf16[2,4,1024]{2,1,0:T(4,128)(2,1)S(1)}, u32[]{:S(2)}, u32[]{:S(2)}) collective-permute-start(bf16[2,4,1024]{2,1,0:T(4,128)(2,1)} %hidden_ref.1), channel_id=1, source_target_pairs={{0,1},{1,0},{2,3},{3,2},{4,5},{5,4},{6,7},{7,6},{8,9},{9,8},{10,11... | collective-permute-start | bytes 49160 | tf_op jit(solution)/shard_map/ppermute | solution.py:482
  1.9 11.0 %collective-permute-start.3 = (bf16[32,8,128]{2,1,0:T(8,128)(2,1)S(1)}, bf16[32,8,128]{2,1,0:T(8,128)(2,1)S(1)}, u32[]{:S(2)}, u32[]{:S(2)}) collective-permute-start(bf16[32,8,128]{2,1,0:T(8,128)(2,1)S(1)} %get-tuple-element.41), channel_id=1, source_target_pairs={{0,8},{1,11},{2,10},{3,9},{4,12},{5,15},{6,14},{7,13},{8,0},{9,3},... | collective-permute-start | bytes 196616 | tf_op jit(solution)/shard_map/ppermute | solution.py:482
  5.7 7.2 %collective-permute-start.4 = (bf16[32,8,128]{2,1,0:T(8,128)(2,1)S(1)}, bf16[32,8,128]{2,1,0:T(8,128)(2,1)S(1)}, u32[]{:S(2)}, u32[]{:S(2)}) collective-permute-start(bf16[32,8,128]{2,1,0:T(8,128)(2,1)S(1)} %get-tuple-element.41), channel_id=1, source_target_pairs={{0,12},{1,15},{2,14},{3,13},{4,8},{5,11},{6,10},{7,9},{8,4},{9,7},... | collective-permute-start | bytes 196616 | tf_op jit(solution)/shard_map/ppermute | solution.py:482
  7.0 5.9 %collective-permute-start.5 = (bf16[32,8,128]{2,1,0:T(8,128)(2,1)S(1)}, bf16[32,8,128]{2,1,0:T(8,128)(2,1)S(1)}, u32[]{:S(2)}, u32[]{:S(2)}) collective-permute-start(bf16[32,8,128]{2,1,0:T(8,128)(2,1)S(1)} %get-tuple-element.41), channel_id=1, source_target_pairs={{0,4},{1,7},{2,6},{3,5},{4,0},{5,3},{6,2},{7,1},{8,12},{9,15},{10,... | collective-permute-start | bytes 196616 | tf_op jit(solution)/shard_map/ppermute | solution.py:482
  7.3 5.6 %collective-permute-start.2 = (bf16[16,8,128]{2,1,0:T(8,128)(2,1)S(1)}, bf16[16,8,128]{2,1,0:T(8,128)(2,1)S(1)}, u32[]{:S(2)}, u32[]{:S(2)}) collective-permute-start(bf16[16,8,128]{2,1,0:T(8,128)(2,1)S(1)} %pack.1.own_ref.refs_5_.refs_2_), channel_id=1, source_target_pairs={{0,2},{1,3},{2,0},{3,1},{4,6},{5,7},{6,4},{7,5},{8,10},{9,11},{10,... | collective-permute-start | bytes 98312 | tf_op jit(solution)/shard_map/ppermute | solution.py:482
  13.0 1.9 %collective-permute-start.6 = (bf16[112,8,128]{2,1,0:T(8,128)(2,1)S(1)}, bf16[112,8,128]{2,1,0:T(8,128)(2,1)S(1)}, u32[]{:S(2)}, u32[]{:S(2)}) collective-permute-start(bf16[112,8,128]{2,1,0:T(8,128)(2,1)S(1)} %pad_maximum_fusion.refs_3_.refs_4_), channel_id=1, source_target_pairs={{0,1},{1,0},{2,3},{3,2},{4,5},{5,4},{6,7},{7,6},{8,9},{9,8},{10,11... | collective-permute-start | bytes 688136 | tf_op jit(solution)/shard_map/ppermute | solution.py:482
  13.8 13.2 %copy-start = (s32[2]{0:T(128)S(1)}, s32[2]{0:T(128)}, u32[]{:S(2)}) copy-start(s32[2]{0:T(128)} %refs_1_.1) | copy-start | bytes 28
  15.9 1.5 %collective-permute-start.7 = (bf16[720,128]{1,0:T(8,128)(2,1)S(1)}, bf16[720,128]{1,0:T(8,128)(2,1)S(1)}, u32[]{:S(2)}, u32[]{:S(2)}) collective-permute-start(bf16[720,128]{1,0:T(8,128)(2,1)S(1)} %get-tuple-element.61), channel_id=1, source_target_pairs={{0,1},{1,0},{2,3},{3,2},{4,5},{5,4},{6,7},{7,6},{8,9},{9,8},{10,11... | collective-permute-start | bytes 552968 | tf_op jit(solution)/shard_map/ppermute | solution.py:482
  17.7 6.3 %collective-permute-start.8 = (bf16[160,128]{1,0:T(8,128)(2,1)S(1)}, bf16[160,128]{1,0:T(8,128)(2,1)S(1)}, u32[]{:S(2)}, u32[]{:S(2)}) collective-permute-start(bf16[160,128]{1,0:T(8,128)(2,1)S(1)} %get-tuple-element.62), channel_id=1, source_target_pairs={{0,12},{1,15},{2,14},{3,13},{4,8},{5,11},{6,10},{7,9},{8,4},{9,7},... | collective-permute-start | bytes 122888 | tf_op jit(solution)/shard_map/ppermute | solution.py:482
  21.1 5.3 %collective-permute-start.10 = (bf16[160,128]{1,0:T(8,128)(2,1)S(1)}, bf16[160,128]{1,0:T(8,128)(2,1)S(1)}, u32[]{:S(2)}, u32[]{:S(2)}) collective-permute-start(bf16[160,128]{1,0:T(8,128)(2,1)S(1)} %get-tuple-element.67), channel_id=1, source_target_pairs={{0,8},{1,11},{2,10},{3,9},{4,12},{5,15},{6,14},{7,13},{8,0},{9,3},... | collective-permute-start | bytes 122888 | tf_op jit(solution)/shard_map/ppermute | solution.py:482
  21.1 5.8 %collective-permute-start.11 = (bf16[160,128]{1,0:T(8,128)(2,1)S(1)}, bf16[160,128]{1,0:T(8,128)(2,1)S(1)}, u32[]{:S(2)}, u32[]{:S(2)}) collective-permute-start(bf16[160,128]{1,0:T(8,128)(2,1)S(1)} %get-tuple-element.68), channel_id=1, source_target_pairs={{0,4},{1,7},{2,6},{3,5},{4,0},{5,3},{6,2},{7,1},{8,12},{9,15},{10,... | collective-permute-start | bytes 122888 | tf_op jit(solution)/shard_map/ppermute | solution.py:482
  22.2 5.2 %collective-permute-start.9 = (bf16[96,128]{1,0:T(8,128)(2,1)S(1)}, bf16[96,128]{1,0:T(8,128)(2,1)S(1)}, u32[]{:S(2)}, u32[]{:S(2)}) collective-permute-start(bf16[96,128]{1,0:T(8,128)(2,1)S(1)} %get-tuple-element.65), channel_id=1, source_target_pairs={{0,2},{1,3},{2,0},{3,1},{4,6},{5,7},{6,4},{7,5},{8,10},{9,11},{10,... | collective-permute-start | bytes 73736 | tf_op jit(solution)/shard_map/ppermute | solution.py:482
  24.0 3.4 %collective-permute-start.12 = (bf16[96,128]{1,0:T(8,128)(2,1)S(1)}, bf16[96,128]{1,0:T(8,128)(2,1)S(1)}, u32[]{:S(2)}, u32[]{:S(2)}) collective-permute-start(bf16[96,128]{1,0:T(8,128)(2,1)S(1)} %slice.9), channel_id=1, source_target_pairs={{0,1},{1,0},{2,3},{3,2},{4,5},{5,4},{6,7},{7,6},{8,9},{9,8},{10,11... | collective-permute-start | bytes 73736 | tf_op jit(solution)/shard_map/ppermute | solution.py:482
  26.4 1.4 %collective-permute-start.13 = (bf16[96,128]{1,0:T(8,128)(2,1)S(1)}, bf16[96,128]{1,0:T(8,128)(2,1)S(1)}, u32[]{:S(2)}, u32[]{:S(2)}) collective-permute-start(bf16[96,128]{1,0:T(8,128)(2,1)S(1)} %slice.12), channel_id=1, source_target_pairs={{0,1},{1,0},{2,3},{3,2},{4,5},{5,4},{6,7},{7,6},{8,9},{9,8},{10,11... | collective-permute-start | bytes 73736 | tf_op jit(solution)/shard_map/ppermute | solution.py:482
  26.9 1.2 %collective-permute-start.14 = (bf16[96,128]{1,0:T(8,128)(2,1)S(1)}, bf16[96,128]{1,0:T(8,128)(2,1)S(1)}, u32[]{:S(2)}, u32[]{:S(2)}) collective-permute-start(bf16[96,128]{1,0:T(8,128)(2,1)S(1)} %slice.13), channel_id=1, source_target_pairs={{0,1},{1,0},{2,3},{3,2},{4,5},{5,4},{6,7},{7,6},{8,9},{9,8},{10,11... | collective-permute-start | bytes 73736 | tf_op jit(solution)/shard_map/ppermute | solution.py:482

commit v19 on v18

--- a/solution.py
+++ b/solution.py
@@ -376,14 +376,47 @@
                 packet_ref[packet_ref.shape[0] - 4 * rows :] = tail.astype(jnp.bfloat16)
 
 
-def merge_kernel(devices, requests, tokens, swapped, own_ref, cos_ref, sin_ref, *refs):
-    got_refs, out_ref = refs[:-1], refs[-1]
+def fold_states(states, mix_rows):
+    peak = functools.reduce(jnp.maximum, [state[0] for state in states])
+    factors = [jnp.exp(state[0] - peak) for state in states]
+    total = functools.reduce(jnp.add, [f * state[1] for f, state in zip(factors, states)])
+    table = jnp.concatenate(factors + [jnp.zeros((128 - len(states), 128), jnp.float32)], axis=0)
+    table = jnp.transpose(table)[:mix_rows]
+    mix = None
+    for s, state in enumerate(states):
+        term = state[2].astype(jnp.float32) * table[:, s : s + 1]
+        mix = term if mix is None else mix + term
+    return peak, total, mix
+
+
+def packet_states(refs, rows, mix_rows, shift):
+    states, sums = [], None
+    for ref in refs:
+        tail = ref[ref.shape[0] - 4 * rows :].astype(jnp.float32)
+        stat = tail[3 * rows :]
+        if shift:
+            stat = pltpu.roll(stat, HEAD_WIDTH - shift, 1)
+        states.append((stat[0:1], stat[1:2] + stat[2:3], ref[:mix_rows]))
+        sums = tail[: 3 * rows] if sums is None else sums + tail[: 3 * rows]
+    return states, sums
+
+
+def fold_kernel(rows, mix_rows, *refs):
+    *got_refs, mix_ref, stat_ref, sum_ref = refs
+    states, sums = packet_states(got_refs, rows, mix_rows, 0)
+    peak, total, mix = fold_states(states, mix_rows)
+    mix_ref[...] = mix
+    stat_ref[...] = rows_of([peak, total], 8)
+    sum_ref[...] = sums
+
+
+def merge_kernel(devices, requests, tokens, own_ref, cos_ref, sin_ref, *refs):
+    mix_ref, stat_ref, sum_ref, *got_refs, out_ref = refs
     rows = requests * tokens
     heads = QUERY_HEADS // devices
     mix_rows = heads * rows
-    sources = len(got_refs)
-    tails = [ref[ref.shape[0] - 4 * rows :].astype(jnp.float32) for ref in got_refs]
-    sums = functools.reduce(jnp.add, [tail[: 3 * rows] for tail in tails])
+    states, sums = packet_states(got_refs, rows, mix_rows, mix_rows)
+    sums += sum_ref[...]
     keys = sums[:rows] + sums[rows : 2 * rows]
     values = sums[2 * rows :].astype(jnp.bfloat16)
     turned = pltpu.roll(keys, HEAD_WIDTH // 2, 1)
@@ -398,20 +431,8 @@
     column = lax.broadcasted_iota(jnp.int32, fresh.shape, 1) % rows
     allowed = (source // tokens == column // tokens) & (source % tokens <= column % tokens)
     fresh_peak = jnp.max(jnp.where(allowed, fresh, NEG_FILL), axis=0, keepdims=True)
-    stats = [tail[3 * rows :] for tail in tails]
-    for s in range(swapped, sources):
-        stats[s] = pltpu.roll(stats[s], HEAD_WIDTH - mix_rows, 1)
-    past_peak = functools.reduce(jnp.maximum, [stat[0:1] for stat in stats])
-    factors = [jnp.exp(stat[0:1] - past_peak) for stat in stats]
-    past_total = functools.reduce(
-        jnp.add, [factor * (stat[1:2] + stat[2:3]) for factor, stat in zip(factors, stats)]
-    )
-    table = jnp.concatenate(factors + [jnp.zeros((128 - sources, 128), jnp.float32)], axis=0)
-    table = jnp.transpose(table)[:mix_rows]
-    mix = None
-    for s, ref in enumerate(got_refs):
-        term = ref[:mix_rows].astype(jnp.float32) * table[:, s : s + 1]
-        mix = term if mix is None else mix + term
+    states = [(stat_ref[0:1], stat_ref[1:2], mix_ref[...])] + states
+    past_peak, past_total, mix = fold_states(states, mix_rows)
     peak = jnp.maximum(past_peak, fresh_peak)
     scale = jnp.exp(past_peak - peak)
     weights = jnp.where(allowed, jnp.exp(fresh - peak), 0.0)
@@ -624,19 +645,32 @@
         "join",
     )
     sent = sorted(zip(packets[2:], plan.pairs), key=lambda item: -sum(item[1]))
+    sent[1:] = sent[:0:-1]
     back = [trade(x, devices, a, b) for x, (a, b) in sent]
     back[0], late_lengths = lax.optimization_barrier((back[0], lengths))
     cosine, sine = rotation(late_lengths, tokens)
     heard = [packets[0], trade(packets[1], devices, plan.single, plan.single)] + back
-    heard += [core_swap(x[slot_rows:]) for x in back]
+    folded = call(
+        functools.partial(fold_kernel, rows, slot_rows),
+        tuple(heard),
+        [vmem()] * len(heard),
+        [
+            pltpu.VMEM((slot_rows, HEAD_WIDTH), jnp.float32),
+            pltpu.VMEM((8, HEAD_WIDTH), jnp.float32),
+            pltpu.VMEM((3 * rows, HEAD_WIDTH), jnp.float32),
+        ],
+        [],
+        "fold",
+    )
+    swapped = [core_swap(x[slot_rows:]) for x in back]
     return pl.pallas_call(
-        functools.partial(merge_kernel, devices, requests, tokens, 2 + len(plan.pairs)),
+        functools.partial(merge_kernel, devices, requests, tokens),
         out_shape=jax.ShapeDtypeStruct((requests, tokens, heads * HEAD_WIDTH), jnp.bfloat16),
-        in_specs=[vmem()] * (3 + len(heard)),
+        in_specs=[vmem()] * (6 + len(swapped)),
         out_specs=vmem(),
         compiler_params=pltpu.CompilerParams(vmem_limit_bytes=8 * MIB),
         name="merge_states",
-    )(own, cosine, sine, *heard)
+    )(own, cosine, sine, *folded, *swapped)
 
 
 def solution(mesh):

time: 29.5 us -> 28.9 us (0.980)
  waiting for transfers between devices: 5.08 us -> 3.75 us
  starting transfers between devices: 15.1 us -> 15.6 us
    ppermute x15, waiting for transfers between devices: 5.08 us -> 3.75 us  [trade(): return lax.ppermute(x, 'tensor', pairs)]
    ppermute x15, starting transfers between devices: 15.1 us -> 15.6 us  [trade(): return lax.ppermute(x, 'tensor', pairs)]
    pallas_call x7 -> x8, Pallas kernels: 7.45 us -> 7.68 us  [call(): pl.pallas_call(kernel, out_shape=tuple(out_shape), in_specs=in_specs, out...]
  transfers between devices with their start and end apart: 15 -> 15, of which waited for: 8 -> 8; matrix products, arithmetic and copies ran while one was open for 1% -> 1% of each run, Pallas kernels for 21% -> 22%
where the time goes in v19:
time: 28.9 us; the launch traced here: 28.5 us
  starting transfers between devices  15.6 us (54%)
  Pallas kernels  8.72 us (30%)
  waiting for transfers between devices  3.75 us (13%)
  other arithmetic  0.3 us (1%)
    ppermute x15, starting transfers between devices, trade(): return lax.ppermute(x, 'tensor', pairs)  15.6 us
    pallas_call x8, Pallas kernels, call(): pl.pallas_call(kernel, out_shape=tuple(out_shape), in_specs=in_specs, out...  7.68 us
    ppermute x15, waiting for transfers between devices, trade(): return lax.ppermute(x, 'tensor', pairs)  3.75 us
    pallas_call x1, Pallas kernels, per_device(): pl.pallas_call(functools.partial(merge_kernel, devices, requests, tokens)...  1.03 us
  transfers between devices with their start and end apart: 15, of which 8 were waited for; matrix products, arithmetic and copies ran while one was open for 1% of the time, Pallas kernels for 22%

profile of v19, /device:TPU:0, one launch (start us, length us, event | category | flops | bytes accessed | tf_op | source)
XLA Modules:
  0.0 28.5 jit_solution(11114543863169967582)
XLA Ops:
  0.0 0.5 %collective-permute-start = (bf16[2,4,1024]{2,1,0:T(4,128)(2,1)}, bf16[2,4,1024]{2,1,0:T(4,128)(2,1)S(1)}, u32[]{:S(2)}, u32[]{:S(2)}) collective-permute-start(bf16[2,4,1024]{2,1,0:T(4,128)(2,1)} %query_ref.1), channel_id=1, source_target_pairs={{0,1},{1,0},{2,3},{3,2},{4,5},{5,4},{6,7},{7,6},{8,9},{9,8},{10,11... | collective-permute-start | bytes 49160 | tf_op jit(solution)/shard_map/ppermute | solution.py:503
  0.5 0.8 %pack.1.own_ref.refs_5_.refs_2_ = bf16[16,8,128]{2,1,0:T(8,128)(2,1)S(1)} custom-call(bf16[2,4,1024]{2,1,0:T(4,128)(2,1)} %query_ref.1, bf16[2,4,1024]{2,1,0:T(4,128)(2,1)} %hidden_ref.1), custom_call_target="tpu_custom_call" | custom-call | flops 1000000 | tf_op jit(solution)/shard_map/pack/pallas_call | solution.py:529
  1.3 0.2 collective-permute-done.query_ref
  1.5 0.3 %collective-permute-done.1.hidden_ref = bf16[2,4,1024]{2,1,0:T(4,128)(2,1)S(1)} collective-permute-done((bf16[2,4,1024]{2,1,0:T(4,128)(2,1)}, bf16[2,4,1024]{2,1,0:T(4,128)(2,1)S(1)}, u32[]{:S(2)}, u32[]{:S(2)}) %collective-permute-start.1) | collective-permute-done | bytes 16416 | tf_op jit(solution)/shard_map/ppermute | solution.py:503
  1.9 3.8 %collective-permute-start.3 = (bf16[32,8,128]{2,1,0:T(8,128)(2,1)S(1)}, bf16[32,8,128]{2,1,0:T(8,128)(2,1)S(1)}, u32[]{:S(2)}, u32[]{:S(2)}) collective-permute-start(bf16[32,8,128]{2,1,0:T(8,128)(2,1)S(1)} %get-tuple-element.44), channel_id=1, source_target_pairs={{0,8},{1,11},{2,10},{3,9},{4,12},{5,15},{6,14},{7,13},{8,0},{9,3},... | collective-permute-start | bytes 196616 | tf_op jit(solution)/shard_map/ppermute | solution.py:503
  5.7 1.3 %collective-permute-start.4 = (bf16[32,8,128]{2,1,0:T(8,128)(2,1)S(1)}, bf16[32,8,128]{2,1,0:T(8,128)(2,1)S(1)}, u32[]{:S(2)}, u32[]{:S(2)}) collective-permute-start(bf16[32,8,128]{2,1,0:T(8,128)(2,1)S(1)} %get-tuple-element.44), channel_id=1, source_target_pairs={{0,12},{1,15},{2,14},{3,13},{4,8},{5,11},{6,10},{7,9},{8,4},{9,7},... | collective-permute-start | bytes 196616 | tf_op jit(solution)/shard_map/ppermute | solution.py:503
  7.0 0.2 collective-permute-start.5
  7.3 1.5 %collective-permute-start.2 = (bf16[16,8,128]{2,1,0:T(8,128)(2,1)S(1)}, bf16[16,8,128]{2,1,0:T(8,128)(2,1)S(1)}, u32[]{:S(2)}, u32[]{:S(2)}) collective-permute-start(bf16[16,8,128]{2,1,0:T(8,128)(2,1)S(1)} %pack.1.own_ref.refs_5_.refs_2_), channel_id=1, source_target_pairs={{0,2},{1,3},{2,0},{3,1},{4,6},{5,7},{6,4},{7,5},{8,10},{9,11},{10,... | collective-permute-start | bytes 98312 | tf_op jit(solution)/shard_map/ppermute | solution.py:503
  8.8 4.1 %base.1 = (f32[8,2048]{1,0:T(8,128)S(1)}, f32[256,128]{1,0:T(8,128)S(1)}, f32[2,8,128]{2,1,0:T(8,128)S(1)}, bf16[256,1024]{1,0:T(8,128)(2,1)S(1)}, bf16[256,1024...) custom-call(s32[1]{0:T(128)} %bitcast.refs_0_.index_ref, ...), custom_call_target="tpu_custom_call" | custom-call | flops 1000000 | tf_op jit(solution)/shard_map/base/pallas_call | solution.py:529
  13.0 0.8 %collective-permute-start.6 = (bf16[112,8,128]{2,1,0:T(8,128)(2,1)S(1)}, bf16[112,8,128]{2,1,0:T(8,128)(2,1)S(1)}, u32[]{:S(2)}, u32[]{:S(2)}) collective-permute-start(bf16[112,8,128]{2,1,0:T(8,128)(2,1)S(1)} %pad_maximum_fusion.refs_3_.refs_4_), channel_id=1, source_target_pairs={{0,1},{1,0},{2,3},{3,2},{4,5},{5,4},{6,7},{7,6},{8,9},{9,8},{10,11... | collective-permute-start | bytes 688136 | tf_op jit(solution)/shard_map/ppermute | solution.py:503
  13.8 0.8 %keep_states.2 = (f32[256,128]{1,0:T(8,128)S(1)}, f32[8,128]{1,0:T(8,128)S(1)}, f32[8,128]{1,0:T(8,128)S(1)}) custom-call(s32[1]{0:T(128)} %bitcast.refs_0_.index_ref, f32[256,128]{1,0:T(8,128)S(1)} %get-tuple-element.47.refs_1_, bf16[16,8,128]{2,1,0:T(8,128)(2,1)S(1)} %pack.1.own_ref.refs_5_.refs_2_, ...), custom_call_target="tpu_custom_call" | custom-call | flops 1000000 | tf_op jit(solution)/shard_map/keep_states/pallas_call | solution.py:529
  14.5 0.3 %collective-permute-done.6.refs_5_ = bf16[112,8,128]{2,1,0:T(8,128)(2,1)S(1)} collective-permute-done((bf16[112,8,128]{2,1,0:T(8,128)(2,1)S(1)}, bf16[112,8,128]{2,1,0:T(8,128)(2,1)S(1)}, u32[]{:S(2)}, u32[]{:S(2)}) %collective-permute-start.6) | collective-permute-done | bytes 229408 | tf_op jit(solution)/shard_map/ppermute | solution.py:503
  14.9 1.0 %send_states.1 = (bf16[720,128]{1,0:T(8,128)(2,1)S(1)}, f32[2,64,128]{2,1,0:T(8,128)S(1)}) custom-call(s32[1]{0:T(128)} %bitcast.refs_0_.index_ref, f32[256,128]{1,0:T(8,128)S(1)} %get-tuple-element.47.refs_1_, bf16[16,8,128]{2,1,0:T(8,128)(2,1)S(1)} %pack.1.own_ref.refs_5_.refs_2_, bf16[16,8,128]{2,1,0:T(8,128)(2,1)S(1)} %get-tuple-element.56.refs_3_, ...), custom_call_target="tpu_custom_call" | custom-call | flops 1000000 | tf_op jit(solution)/shard_map/send_states/pallas_call | solution.py:529
  15.9 0.4 %collective-permute-start.7 = (bf16[720,128]{1,0:T(8,128)(2,1)S(1)}, bf16[720,128]{1,0:T(8,128)(2,1)S(1)}, u32[]{:S(2)}, u32[]{:S(2)}) collective-permute-start(bf16[720,128]{1,0:T(8,128)(2,1)S(1)} %get-tuple-element.64), channel_id=1, source_target_pairs={{0,1},{1,0},{2,3},{3,2},{4,5},{5,4},{6,7},{7,6},{8,9},{9,8},{10,11... | collective-permute-start | bytes 552968 | tf_op jit(solution)/shard_map/ppermute | solution.py:503
  16.3 0.5 %keep_states.3 = (f32[256,128]{1,0:T(8,128)S(1)}, f32[8,128]{1,0:T(8,128)S(1)}) custom-call(s32[1]{0:T(128)} %bitcast.refs_0_.index_ref, f32[256,128]{1,0:T(8,128)S(1)} %get-tuple-element.47.refs_1_, bf16[16,8,128]{2,1,0:T(8,128)(2,1)S(1)} %pack.1.own_ref.refs_5_.refs_2_, bf16[112,8,128]{2,1,0:T(8,128)(2,1)S(1)} %pad_maximum_fusion.refs_3_.refs_4_, ...), custom_call_target="tpu_custom_call" | custom-call | flops 1000000 | tf_op jit(solution)/shard_map/keep_states/pallas_call | solution.py:529
  16.8 0.6 %collective-permute-done.7.refs_5_ = bf16[720,128]{1,0:T(8,128)(2,1)S(1)} collective-permute-done((bf16[720,128]{1,0:T(8,128)(2,1)S(1)}, bf16[720,128]{1,0:T(8,128)(2,1)S(1)}, u32[]{:S(2)}, u32[]{:S(2)}) %collective-permute-start.7) | collective-permute-done | bytes 184352 | tf_op jit(solution)/shard_map/ppermute | solution.py:503
  17.3 0.3 %join.1 = (bf16[96,128]{1,0:T(8,128)(2,1)S(1)}, bf16[96,128]{1,0:T(8,128)(2,1)S(1)}, bf16[160,128]{1,0:T(8,128)(2,1)S(1)}, bf16[160,128]{1,0:T(8,128)(2,1)S(1)}, bf16[160,128]{1,0:T(8,128)(2,1)S(1)}) custom-call(s32[1]{0:T(128)} %bitcast.refs_0_.index_ref, f32[256,128]{1,0:T(8,128)S(1)} %get-tuple-element.52.refs_0_, ...), custom_call_target="tpu_custom_call" | custom-call | flops 1000000 | tf_op jit(solution)/shard_map/join/pallas_call | solution.py:529
  17.7 3.4 %collective-permute-start.8 = (bf16[160,128]{1,0:T(8,128)(2,1)S(1)}, bf16[160,128]{1,0:T(8,128)(2,1)S(1)}, u32[]{:S(2)}, u32[]{:S(2)}) collective-permute-start(bf16[160,128]{1,0:T(8,128)(2,1)S(1)} %get-tuple-element.65), channel_id=1, source_target_pairs={{0,12},{1,15},{2,14},{3,13},{4,8},{5,11},{6,10},{7,9},{8,4},{9,7},... | collective-permute-start | bytes 122888 | tf_op jit(solution)/shard_map/ppermute | solution.py:503
  21.1 1.1 %collective-permute-start.11 = (bf16[160,128]{1,0:T(8,128)(2,1)S(1)}, bf16[160,128]{1,0:T(8,128)(2,1)S(1)}, u32[]{:S(2)}, u32[]{:S(2)}) collective-permute-start(bf16[160,128]{1,0:T(8,128)(2,1)S(1)} %get-tuple-element.71), channel_id=1, source_target_pairs={{0,8},{1,11},{2,10},{3,9},{4,12},{5,15},{6,14},{7,13},{8,0},{9,3},... | collective-permute-start | bytes 122888 | tf_op jit(solution)/shard_map/ppermute | solution.py:503
  22.2 1.4 %collective-permute-start.9 = (bf16[96,128]{1,0:T(8,128)(2,1)S(1)}, bf16[96,128]{1,0:T(8,128)(2,1)S(1)}, u32[]{:S(2)}, u32[]{:S(2)}) collective-permute-start(bf16[96,128]{1,0:T(8,128)(2,1)S(1)} %get-tuple-element.68), channel_id=1, source_target_pairs={{0,2},{1,3},{2,0},{3,1},{4,6},{5,7},{6,4},{7,5},{8,10},{9,11},{10,... | collective-permute-start | bytes 73736 | tf_op jit(solution)/shard_map/ppermute | solution.py:503
  23.5 0.5 %collective-permute-done.8.refs_2_ = bf16[160,128]{1,0:T(8,128)(2,1)S(1)} collective-permute-done((bf16[160,128]{1,0:T(8,128)(2,1)S(1)}, bf16[160,128]{1,0:T(8,128)(2,1)S(1)}, u32[]{:S(2)}, u32[]{:S(2)}) %collective-permute-start.8) | collective-permute-done | bytes 40992 | tf_op jit(solution)/shard_map/ppermute | solution.py:503
  24.0 1.3 %collective-permute-done.10.refs_3_ = bf16[160,128]{1,0:T(8,128)(2,1)S(1)} collective-permute-done((bf16[160,128]{1,0:T(8,128)(2,1)S(1)}, bf16[160,128]{1,0:T(8,128)(2,1)S(1)}, u32[]{:S(2)}, u32[]{:S(2)}) %collective-permute-start.10) | collective-permute-done | bytes 40992 | tf_op jit(solution)/shard_map/ppermute | solution.py:503
  25.3 0.7 %collective-permute-start.13 = (bf16[96,128]{1,0:T(8,128)(2,1)S(1)}, bf16[96,128]{1,0:T(8,128)(2,1)S(1)}, u32[]{:S(2)}, u32[]{:S(2)}) collective-permute-start(bf16[96,128]{1,0:T(8,128)(2,1)S(1)} %slice.12), channel_id=1, source_target_pairs={{0,1},{1,0},{2,3},{3,2},{4,5},{5,4},{6,7},{7,6},{8,9},{9,8},{10,11... | collective-permute-start | bytes 73736 | tf_op jit(solution)/shard_map/ppermute | solution.py:503
  26.0 0.3 collective-permute-done.11.refs_4_
  26.3 0.3 %collective-permute-start.14 = (bf16[96,128]{1,0:T(8,128)(2,1)S(1)}, bf16[96,128]{1,0:T(8,128)(2,1)S(1)}, u32[]{:S(2)}, u32[]{:S(2)}) collective-permute-start(bf16[96,128]{1,0:T(8,128)(2,1)S(1)} %slice.13), channel_id=1, source_target_pairs={{0,1},{1,0},{2,3},{3,2},{4,5},{5,4},{6,7},{7,6},{8,9},{9,8},{10,11... | collective-permute-start | bytes 73736 | tf_op jit(solution)/shard_map/ppermute | solution.py:503
  26.6 0.1 add_convert_fusion
  26.7 0.1 convert_element_type.11
  26.8 0.1 fusion
  26.9 0.1 pad_maximum_fusion.1
  27.0 0.2 fold.1
  27.3 0.2 collective-permute-done.14.refs_5_
  27.5 1.0 %merge_states.1 = bf16[2,4,1024]{2,1,0:T(4,128)(2,1)} custom-call(bf16[16,8,128]{2,1,0:T(8,128)(2,1)S(1)} %pack.1.own_ref.refs_5_.refs_2_, f32[8,128]{1,0:T(8,128)S(1)} %get-tuple-element.78.cos_ref, f32[8,128]{1,0:T(8,128)S(1)} %get-tuple-element.79.sin_ref, f32[64,128]{1,0:T(8,128)S(1)} %get-tuple-element.72.refs_0_, ...), custom_call_target="tpu_custom_call" | custom-call | tf_op jit(solution)/shard_map/merge_states/pallas_call | solution.py:666
  (18 shorter events, 0.2 us)
Async XLA Ops:
  0.0 1.5 %collective-permute-start = (bf16[2,4,1024]{2,1,0:T(4,128)(2,1)}, bf16[2,4,1024]{2,1,0:T(4,128)(2,1)S(1)}, u32[]{:S(2)}, u32[]{:S(2)}) collective-permute-start(bf16[2,4,1024]{2,1,0:T(4,128)(2,1)} %query_ref.1), channel_id=1, source_target_pairs={{0,1},{1,0},{2,3},{3,2},{4,5},{5,4},{6,7},{7,6},{8,9},{9,8},{10,11... | collective-permute-start | bytes 49160 | tf_op jit(solution)/shard_map/ppermute | solution.py:503
  0.5 1.4 %collective-permute-start.1 = (bf16[2,4,1024]{2,1,0:T(4,128)(2,1)}, bf16[2,4,1024]{2,1,0:T(4,128)(2,1)S(1)}, u32[]{:S(2)}, u32[]{:S(2)}) collective-permute-start(bf16[2,4,1024]{2,1,0:T(4,128)(2,1)} %hidden_ref.1), channel_id=1, source_target_pairs={{0,1},{1,0},{2,3},{3,2},{4,5},{5,4},{6,7},{7,6},{8,9},{9,8},{10,11... | collective-permute-start | bytes 49160 | tf_op jit(solution)/shard_map/ppermute | solution.py:503
  1.9 11.0 %collective-permute-start.3 = (bf16[32,8,128]{2,1,0:T(8,128)(2,1)S(1)}, bf16[32,8,128]{2,1,0:T(8,128)(2,1)S(1)}, u32[]{:S(2)}, u32[]{:S(2)}) collective-permute-start(bf16[32,8,128]{2,1,0:T(8,128)(2,1)S(1)} %get-tuple-element.44), channel_id=1, source_target_pairs={{0,8},{1,11},{2,10},{3,9},{4,12},{5,15},{6,14},{7,13},{8,0},{9,3},... | collective-permute-start | bytes 196616 | tf_op jit(solution)/shard_map/ppermute | solution.py:503
  5.7 7.2 %collective-permute-start.4 = (bf16[32,8,128]{2,1,0:T(8,128)(2,1)S(1)}, bf16[32,8,128]{2,1,0:T(8,128)(2,1)S(1)}, u32[]{:S(2)}, u32[]{:S(2)}) collective-permute-start(bf16[32,8,128]{2,1,0:T(8,128)(2,1)S(1)} %get-tuple-element.44), channel_id=1, source_target_pairs={{0,12},{1,15},{2,14},{3,13},{4,8},{5,11},{6,10},{7,9},{8,4},{9,7},... | collective-permute-start | bytes 196616 | tf_op jit(solution)/shard_map/ppermute | solution.py:503
  7.0 5.9 %collective-permute-start.5 = (bf16[32,8,128]{2,1,0:T(8,128)(2,1)S(1)}, bf16[32,8,128]{2,1,0:T(8,128)(2,1)S(1)}, u32[]{:S(2)}, u32[]{:S(2)}) collective-permute-start(bf16[32,8,128]{2,1,0:T(8,128)(2,1)S(1)} %get-tuple-element.44), channel_id=1, source_target_pairs={{0,4},{1,7},{2,6},{3,5},{4,0},{5,3},{6,2},{7,1},{8,12},{9,15},{10,... | collective-permute-start | bytes 196616 | tf_op jit(solution)/shard_map/ppermute | solution.py:503
  7.3 5.6 %collective-permute-start.2 = (bf16[16,8,128]{2,1,0:T(8,128)(2,1)S(1)}, bf16[16,8,128]{2,1,0:T(8,128)(2,1)S(1)}, u32[]{:S(2)}, u32[]{:S(2)}) collective-permute-start(bf16[16,8,128]{2,1,0:T(8,128)(2,1)S(1)} %pack.1.own_ref.refs_5_.refs_2_), channel_id=1, source_target_pairs={{0,2},{1,3},{2,0},{3,1},{4,6},{5,7},{6,4},{7,5},{8,10},{9,11},{10,... | collective-permute-start | bytes 98312 | tf_op jit(solution)/shard_map/ppermute | solution.py:503
  13.0 1.9 %collective-permute-start.6 = (bf16[112,8,128]{2,1,0:T(8,128)(2,1)S(1)}, bf16[112,8,128]{2,1,0:T(8,128)(2,1)S(1)}, u32[]{:S(2)}, u32[]{:S(2)}) collective-permute-start(bf16[112,8,128]{2,1,0:T(8,128)(2,1)S(1)} %pad_maximum_fusion.refs_3_.refs_4_), channel_id=1, source_target_pairs={{0,1},{1,0},{2,3},{3,2},{4,5},{5,4},{6,7},{7,6},{8,9},{9,8},{10,11... | collective-permute-start | bytes 688136 | tf_op jit(solution)/shard_map/ppermute | solution.py:503
  13.8 12.9 %copy-start = (s32[2]{0:T(128)S(1)}, s32[2]{0:T(128)}, u32[]{:S(2)}) copy-start(s32[2]{0:T(128)} %refs_1_.1) | copy-start | bytes 28
  15.9 1.5 %collective-permute-start.7 = (bf16[720,128]{1,0:T(8,128)(2,1)S(1)}, bf16[720,128]{1,0:T(8,128)(2,1)S(1)}, u32[]{:S(2)}, u32[]{:S(2)}) collective-permute-start(bf16[720,128]{1,0:T(8,128)(2,1)S(1)} %get-tuple-element.64), channel_id=1, source_target_pairs={{0,1},{1,0},{2,3},{3,2},{4,5},{5,4},{6,7},{7,6},{8,9},{9,8},{10,11... | collective-permute-start | bytes 552968 | tf_op jit(solution)/shard_map/ppermute | solution.py:503
  17.7 6.3 %collective-permute-start.8 = (bf16[160,128]{1,0:T(8,128)(2,1)S(1)}, bf16[160,128]{1,0:T(8,128)(2,1)S(1)}, u32[]{:S(2)}, u32[]{:S(2)}) collective-permute-start(bf16[160,128]{1,0:T(8,128)(2,1)S(1)} %get-tuple-element.65), channel_id=1, source_target_pairs={{0,12},{1,15},{2,14},{3,13},{4,8},{5,11},{6,10},{7,9},{8,4},{9,7},... | collective-permute-start | bytes 122888 | tf_op jit(solution)/shard_map/ppermute | solution.py:503
  21.1 4.2 %collective-permute-start.10 = (bf16[160,128]{1,0:T(8,128)(2,1)S(1)}, bf16[160,128]{1,0:T(8,128)(2,1)S(1)}, u32[]{:S(2)}, u32[]{:S(2)}) collective-permute-start(bf16[160,128]{1,0:T(8,128)(2,1)S(1)} %get-tuple-element.70), channel_id=1, source_target_pairs={{0,4},{1,7},{2,6},{3,5},{4,0},{5,3},{6,2},{7,1},{8,12},{9,15},{10,... | collective-permute-start | bytes 122888 | tf_op jit(solution)/shard_map/ppermute | solution.py:503
  21.1 5.2 %collective-permute-start.11 = (bf16[160,128]{1,0:T(8,128)(2,1)S(1)}, bf16[160,128]{1,0:T(8,128)(2,1)S(1)}, u32[]{:S(2)}, u32[]{:S(2)}) collective-permute-start(bf16[160,128]{1,0:T(8,128)(2,1)S(1)} %get-tuple-element.71), channel_id=1, source_target_pairs={{0,8},{1,11},{2,10},{3,9},{4,12},{5,15},{6,14},{7,13},{8,0},{9,3},... | collective-permute-start | bytes 122888 | tf_op jit(solution)/shard_map/ppermute | solution.py:503
  22.2 4.8 %collective-permute-start.9 = (bf16[96,128]{1,0:T(8,128)(2,1)S(1)}, bf16[96,128]{1,0:T(8,128)(2,1)S(1)}, u32[]{:S(2)}, u32[]{:S(2)}) collective-permute-start(bf16[96,128]{1,0:T(8,128)(2,1)S(1)} %get-tuple-element.68), channel_id=1, source_target_pairs={{0,2},{1,3},{2,0},{3,1},{4,6},{5,7},{6,4},{7,5},{8,10},{9,11},{10,... | collective-permute-start | bytes 73736 | tf_op jit(solution)/shard_map/ppermute | solution.py:503
  24.0 3.2 %collective-permute-start.12 = (bf16[96,128]{1,0:T(8,128)(2,1)S(1)}, bf16[96,128]{1,0:T(8,128)(2,1)S(1)}, u32[]{:S(2)}, u32[]{:S(2)}) collective-permute-start(bf16[96,128]{1,0:T(8,128)(2,1)S(1)} %slice.9), channel_id=1, source_target_pairs={{0,1},{1,0},{2,3},{3,2},{4,5},{5,4},{6,7},{7,6},{8,9},{9,8},{10,11... | collective-permute-start | bytes 73736 | tf_op jit(solution)/shard_map/ppermute | solution.py:503
  25.3 2.0 %collective-permute-start.13 = (bf16[96,128]{1,0:T(8,128)(2,1)S(1)}, bf16[96,128]{1,0:T(8,128)(2,1)S(1)}, u32[]{:S(2)}, u32[]{:S(2)}) collective-permute-start(bf16[96,128]{1,0:T(8,128)(2,1)S(1)} %slice.12), channel_id=1, source_target_pairs={{0,1},{1,0},{2,3},{3,2},{4,5},{5,4},{6,7},{7,6},{8,9},{9,8},{10,11... | collective-permute-start | bytes 73736 | tf_op jit(solution)/shard_map/ppermute | solution.py:503
  26.3 1.2 %collective-permute-start.14 = (bf16[96,128]{1,0:T(8,128)(2,1)S(1)}, bf16[96,128]{1,0:T(8,128)(2,1)S(1)}, u32[]{:S(2)}, u32[]{:S(2)}) collective-permute-start(bf16[96,128]{1,0:T(8,128)(2,1)S(1)} %slice.13), channel_id=1, source_target_pairs={{0,1},{1,0},{2,3},{3,2},{4,5},{5,4},{6,7},{7,6},{8,9},{9,8},{10,11... | collective-permute-start | bytes 73736 | tf_op jit(solution)/shard_map/ppermute | solution.py:503
